TPU v7x, 32 devices: a whole 2x2x4 slice. The times are simulated.
32 devices in a mesh: groups: 2 (over x), seq: 16 (over z, y, core).
Axes of the slice: x: 2, y: 2, z: 4, core: 2. Of those that a mesh axis runs over, the one named last changes fastest.
Arguments:
- queries: bfloat16 [8192, 2048], P(('groups', 'seq')), parts along dimension 0, may hold values from -400 to 400
- neighbours: bfloat16 [64, 128, 896], P(('groups', 'seq')), parts along dimension 0, may hold values from -500 to 500
- w_key: bfloat16 [896, 2048], replicated, may hold values from -0.1875 to 0.1875
- w_value: bfloat16 [896, 2048], replicated, may hold values from -0.1875 to 0.1875
- retrieval_owner: int32 [128, 2], P(('groups', 'seq')), parts along dimension 0, may hold values from 0 to 15, as said below
- retrieval_slot: int32 [128, 2], P(('groups', 'seq')), parts along dimension 0, may hold values from 0 to 1
- doc_starts: int32 [128], P(('groups', 'seq')), parts along dimension 0, may hold values 0 or 1
Outputs:
- attended: bfloat16 [8192, 2048], P(('groups', 'seq')), parts along dimension 0
There are 2 independent parts, one for each index of `groups`. A program takes and returns all parts, laid end to end along the dimension named above; an argument that names none is the same for every part. Nothing has to cross between parts.
Inputs may be any that keep to these rules, and one draw needn't show every extreme that they name: `retrieval_owner`: among the 8 owners named by the spans of one device, no owner appears more than 1 times, and some owner appears exactly 1 times.
All inputs are finite; a program needn't handle non-finite values. No bound on the sum of `doc_starts` on one device may be relied on, other than what follows from the above.
Results may differ from a plain program's by a relative error of at most 0.0071.
Values may be sent and summed in bfloat16 or wider, within the bound.
No kernel may reach another device: no remote copies, remote signals or barrier semaphores. Data moves between devices by JAX's collectives and lax.ppermute only.
A program may use at most 128 MiB of HBM per device.

v0:
```python
import math

import jax
import jax.numpy as jnp
from jax import lax
from jax.sharding import PartitionSpec as P

SPAN = 64
HEADS = 16
HEAD_DIM = 128


def from_behind(value, axis, steps):
    count = lax.axis_size(axis)
    first, last = (max(0, -steps), min(count, count - steps))
    return lax.ppermute(value, axis, [(source, source + steps) for source in range(first, last)])


def normalize(tokens_in):
    widened = tokens_in.astype(jnp.float32)
    factor = lax.rsqrt(jnp.mean(widened * widened, axis=-1, keepdims=True) + 1e-06)
    return (widened * factor).astype(jnp.bfloat16)


def ranks_of(owner_rows):
    count = owner_rows.shape[-1]
    same = owner_rows[..., :, None] == owner_rows[..., None, :]
    earlier = jnp.arange(count)[:, None] > jnp.arange(count)[None, :]
    return jnp.sum(jnp.where(same & earlier, 1, 0), axis=-1).astype(jnp.int32)


def project(chosen, w_key, w_value, span_count):
    model_width = w_key.shape[1]
    normed = normalize(chosen).reshape(-1, chosen.shape[-1])
    key_rows = jnp.dot(normed, w_key, preferred_element_type=jnp.float32).astype(jnp.bfloat16)
    value_rows = jnp.dot(normed, w_value, preferred_element_type=jnp.float32).astype(jnp.bfloat16)
    return (
        key_rows.reshape(span_count, -1, model_width),
        value_rows.reshape(span_count, -1, model_width),
    )


def attend(query_rows, key_rows, value_rows):
    windows = query_rows.shape[0]
    query_heads = query_rows.reshape(windows, SPAN, HEADS, HEAD_DIM)
    key_heads = key_rows.reshape(windows, -1, HEADS, HEAD_DIM)
    value_heads = value_rows.reshape(windows, -1, HEADS, HEAD_DIM)
    scores = jnp.einsum(
        "wqhd,wkhd->whqk", query_heads, key_heads, preferred_element_type=jnp.float32
    )
    scores = scores * (1.0 / math.sqrt(HEAD_DIM))
    highest = jnp.max(scores, axis=-1, keepdims=True)
    powers = jnp.exp(scores - highest)
    totals = jnp.sum(powers, axis=-1, keepdims=True)
    weights = (powers / totals).astype(jnp.bfloat16)
    result = jnp.einsum("whqk,wkhd->wqhd", weights, value_heads, preferred_element_type=jnp.float32)
    return result.reshape(windows * SPAN, HEADS * HEAD_DIM).astype(jnp.bfloat16)


def body(queries, neighbours, w_key, w_value, retrieval_owner, retrieval_slot, doc_starts):
    peer_count = lax.axis_size("seq")
    span_count = doc_starts.shape[0]
    token_count = queries.shape[0]
    model_width = queries.shape[1]
    request_count = 2 * span_count
    capacity = (request_count + peer_count - 1) // peer_count
    owners = retrieval_owner.reshape(-1)
    slot_ids = retrieval_slot.reshape(-1)
    destination = owners * capacity + ranks_of(owners)
    targets = jnp.arange(peer_count * capacity, dtype=jnp.int32)
    matches = destination[:, None] == targets[None, :]
    wanted = jnp.sum(jnp.where(matches, slot_ids[:, None] + 1, 0), axis=0) - 1
    asked_slot = lax.all_to_all(
        wanted.reshape(peer_count, capacity), "seq", split_axis=0, concat_axis=0, tiled=True
    ).reshape(-1)
    picked = jnp.take(neighbours, jnp.maximum(asked_slot, 0), axis=0)
    incoming = lax.all_to_all(picked, "seq", split_axis=0, concat_axis=0, tiled=True)
    chosen = jnp.take(incoming, destination, axis=0)
    key_rows, value_rows = project(chosen, w_key, w_value, span_count)
    tail_rows = from_behind(queries[: SPAN - 1], "seq", -1)
    query_rows = jnp.concatenate([queries[SPAN - 1 :], tail_rows], 0).reshape(
        span_count, SPAN, model_width
    )
    computed = attend(query_rows, key_rows, value_rows)
    head_rows = from_behind(computed[token_count - SPAN + 1 :], "seq", 1)
    attended = jnp.concatenate([head_rows, computed[: token_count - SPAN + 1]], 0)
    offsets = jnp.arange(SPAN)
    fresh_rows = (doc_starts[:, None] == 0) | (offsets[None, :] == SPAN - 1)
    opening = (
        (lax.axis_index("seq") == 0)
        & (jnp.arange(span_count)[:, None] == 0)
        & (offsets[None, :] < SPAN - 1)
    )
    kept_rows = (fresh_rows & jnp.logical_not(opening)).reshape(token_count)
    return jnp.where(kept_rows[:, None], attended, jnp.zeros((), jnp.bfloat16))


def solution(mesh):
    return jax.shard_map(
        body,
        mesh=mesh,
        in_specs=(
            P(("groups", "seq"), None),
            P(("groups", "seq"), None, None),
            P(),
            P(),
            P(("groups", "seq"), None),
            P(("groups", "seq"), None),
            P(("groups", "seq")),
        ),
        out_specs=P(("groups", "seq"), None),
        check_vma=False,
    )
```

profile of v0, /device:TPU:18, one launch (start us, length us, event | category | flops | bytes accessed | tf_op | source)
XLA Modules:
  0.0 157.6 jit_solution(7107284511529906446)
XLA Ops:
  0.0 0.0 copy-start
  0.0 0.8 copy.36
  0.8 0.1 reshape.159
  0.9 0.2 select_reduce_fusion.1
  1.1 0.7 broadcast_add_fusion
  1.8 0.1 copy.37
  1.9 0.1 add.70
  2.0 0.1 select_reduce_fusion
  2.1 0.1 copy.38
  2.2 10.1 %all_to_all.11 = s32[16,1,1]{2,1,0:T(1,128)S(1)} all-to-all(s32[16,1,1]{2,1,0:T(1,128)S(1)} %copy.38), channel_id=1, replica_groups=mesh['groups'=2,'seq'=16] {'seq'}, dimensions={0} | all-to-all | bytes 128 | tf_op jit(solution)/shard_map/all_to_all | solution.py:73
  12.2 0.4 maximum_reduce_fusion
  12.6 0.0 copy-done
  12.6 2.8 %gather_fusion = bf16[16,128,896]{2,1,0:T(8,128)(2,1)} fusion(bf16[2,128,896]{2,1,0:T(8,128)(2,1)S(1)} %copy-done, s32[1024]{0:T(1024)S(1)} %pad_clamp_fusion.1), kind=kCustom, calls=%fused_computation | custom fusion | bytes 7340096 | tf_op jit(solution)/shard_map/jit(_take)/gather | solution.py:76
  15.4 0.4 compare_reduce_fusion
  15.8 4.3 %broadcast_select_fusion = bf16[16,128,896]{2,1,0:T(8,128)(2,1)} fusion(bf16[16,128,896]{2,1,0:T(8,128)(2,1)} %gather_fusion, pred[16]{0:T(512)(128)(4,1)S(1)} %compare_reduce_fusion), kind=kLoop, calls=%fused_computation.15 | loop fusion | flops 1835008 | bytes 7340048 | tf_op jit(solution)/shard_map/jit(_take)/select_n | solution.py:76
  20.1 6.8 %all-to-all-start.1 = ((bf16[16,128,896]{2,1,0:T(8,128)(2,1)}), bf16[16,128,896]{2,1,0:T(8,128)(2,1)}, u32[]{:S(2)}, u32[]{:S(2)}) async-start(bf16[16,128,896]{2,1,0:T(8,128)(2,1)} %broadcast_select_fusion), calls=%async_computation.1 | async-start | bytes 7340032 | tf_op jit(solution)/shard_map/all_to_all | solution.py:77
  27.0 3.1 %collective-permute-start = (bf16[63,2048]{1,0:T(8,128)(2,1)S(1)}, bf16[63,2048]{1,0:T(8,128)(2,1)S(1)}, u32[]{:S(2)}, u32[]{:S(2)}) collective-permute-start(bf16[63,2048]{1,0:T(8,128)(2,1)S(1)} %slice.13), channel_id=1, source_target_pairs={{1,0},{2,1},{3,2},{4,3},{5,4},{6,5},{7,6},{8,7},{9,8},{10,9},{11,1... | collective-permute-start | bytes 774152 | tf_op jit(solution)/shard_map/ppermute | solution.py:16
  30.1 0.1 reshape.160
  30.2 0.1 broadcast_bitcast_fusion
  30.3 0.2 slice.12
  30.5 78.8 %collective-permute-done = bf16[63,2048]{1,0:T(8,128)(2,1)S(1)} collective-permute-done((bf16[63,2048]{1,0:T(8,128)(2,1)S(1)}, bf16[63,2048]{1,0:T(8,128)(2,1)S(1)}, u32[]{:S(2)}, u32[]{:S(2)}) %collective-permute-start) | collective-permute-done | bytes 258080 | tf_op jit(solution)/shard_map/ppermute | solution.py:16
  109.3 0.1 maximum_bitcast_fusion
  109.4 0.2 copy.44
  109.6 0.0 all-to-all-done.1
  109.6 2.9 %gather_fusion.1 = bf16[8,128,896]{2,1,0:T(8,128)(2,1)S(1)} fusion(bf16[16,128,896]{2,1,0:T(8,128)(2,1)} %all-to-all-done.1, s32[1024]{0:T(1024)S(1)} %pad_clamp_fusion), kind=kCustom, calls=%fused_computation.1 | custom fusion | bytes 3670048 | tf_op jit(solution)/shard_map/jit(_take)/gather | solution.py:78
  112.5 0.0 copy-start.4
  112.6 0.6 multiply_reduce_fusion.1
  113.2 0.5 multiply_convert_fusion
  113.7 0.9 copy-done.4
  114.6 4.7 %convert_bitcast_fusion = bf16[128,8,16,128]{3,1,2,0:T(8,128)(2,1)S(1)} fusion(bf16[1024,896]{1,0:T(8,128)(2,1)S(1)} %multiply_convert_fusion, bf16[896,2048]{1,0:T(8,128)(2,1)S(1)} %copy-done.4), kind=kOutput, calls=%fused_computation.9 | convolution fusion | flops 3760193536 | bytes 9699328 | tf_op jit(solution)/shard_map/dot_general | solution.py:35
  119.3 1.4 copy.45
  120.7 1.6 %fusion.3 = f32[4,16,64,256]{3,2,1,0:T(8,128)S(1)} fusion(bf16[4,256,16,128]{3,2,1,0:T(8,128)(2,1)S(1)} %bitcast.39, bf16[4,64,16,128]{3,2,1,0:T(8,128)(2,1)S(1)} %bitcast.42), kind=kOutput, calls=%fused_computation.5 | convolution fusion | flops 268435456 | bytes 9437184 | tf_op jit(solution)/shard_map/wqhd,wkhd->whqk/dot_general | solution.py:48
  122.3 0.0 copy-start.1
  122.3 2.0 %copy-done.1 = f32[4,16,64,256]{3,2,1,0:T(8,128)} copy-done((f32[4,16,64,256]{3,2,1,0:T(8,128)}, f32[4,16,64,256]{3,2,1,0:T(8,128)S(1)}, u32[]{:S(2)}) %copy-start.1) | copy-done | bytes 4194328
  124.3 1.6 %fusion.27 = f32[4,16,64]{2,1,0:T(8,128)S(1)} fusion(f32[4,16,64,256]{3,2,1,0:T(8,128)S(1)} %fusion.3), kind=kOutput, calls=%fused_computation.51 | output fusion | flops 4194559 | bytes 4210688 | tf_op jit(solution)/shard_map/sub | solution.py:53
  125.9 0.5 copy-done.5
  126.3 4.9 %convert_bitcast_fusion.1 = bf16[128,8,16,128]{3,1,2,0:T(8,128)(2,1)S(1)} fusion(bf16[1024,896]{1,0:T(8,128)(2,1)S(1)} %multiply_convert_fusion, bf16[896,2048]{1,0:T(8,128)(2,1)S(1)} %copy-done.5), kind=kOutput, calls=%fused_computation.10 | convolution fusion | flops 3760193536 | bytes 9699328 | tf_op jit(solution)/shard_map/dot_general | solution.py:36
  131.2 3.3 %copy.46 = bf16[128,8,16,128]{3,2,1,0:T(8,128)(2,1)} copy(bf16[128,8,16,128]{3,1,2,0:T(8,128)(2,1)S(1)} %convert_bitcast_fusion.1) | data formatting | bytes 8388608
  134.5 11.9 %fusion.13 = bf16[4,64,16,128]{3,1,2,0:T(8,128)(2,1)S(1)} fusion(bf16[4,256,16,128]{3,2,1,0:T(8,128)(2,1)} %bitcast.43, f32[4,16,64]{2,1,0:T(8,128)S(1)} %fusion.27, f32[4,16,64,256]{3,2,1,0:T(8,128)} %copy-done.1), kind=kOutput, calls=%fused_computation.20 | convolution fusion | flops 274206976 | bytes 9453568 | tf_op jit(solution)/shard_map/whqk,wkhd->wqhd/dot_general | solution.py:56
  146.5 0.7 copy.43
  147.1 0.3 copy.59
  147.4 0.1 slice.20
  147.5 1.9 %collective-permute-start.1 = (bf16[63,2048]{1,0:T(8,128)(2,1)S(1)}, bf16[63,2048]{1,0:T(8,128)(2,1)S(1)}, u32[]{:S(2)}, u32[]{:S(2)}) collective-permute-start(bf16[63,2048]{1,0:T(8,128)(2,1)S(1)} %slice.20), channel_id=1, source_target_pairs={{0,1},{1,2},{2,3},{3,4},{4,5},{5,6},{6,7},{7,8},{8,9},{9,10},{10,1... | collective-permute-start | bytes 774152 | tf_op jit(solution)/shard_map/ppermute | solution.py:16
  149.4 0.1 not_and_fusion
  149.5 0.1 and.61
  149.6 0.1 slice.21
  149.7 6.6 %collective-permute-done.1 = bf16[63,2048]{1,0:T(8,128)(2,1)S(1)} collective-permute-done((bf16[63,2048]{1,0:T(8,128)(2,1)S(1)}, bf16[63,2048]{1,0:T(8,128)(2,1)S(1)}, u32[]{:S(2)}, u32[]{:S(2)}) %collective-permute-start.1) | collective-permute-done | bytes 258080 | tf_op jit(solution)/shard_map/ppermute | solution.py:16
  156.3 1.3 maximum_select_fusion
  (14 shorter events, 0.1 us)
Async XLA Ops:
  0.0 12.6 %copy-start = (bf16[2,128,896]{2,1,0:T(8,128)(2,1)S(1)}, bf16[2,128,896]{2,1,0:T(8,128)(2,1)}, u32[]{:S(2)}) copy-start(bf16[2,128,896]{2,1,0:T(8,128)(2,1)} %param.8) | copy-start | bytes 1376260
  20.1 6.8 %copy-start.2 = (bf16[256,2048]{1,0:T(8,128)(2,1)S(1)}, bf16[256,2048]{1,0:T(8,128)(2,1)}, u32[]{:S(2)}) copy-start(bf16[256,2048]{1,0:T(8,128)(2,1)} %param.7) | copy-start | bytes 3145732
  20.1 10.3 %copy-start.3 = (s32[4]{0:T(128)S(1)}, s32[4]{0:T(128)}, u32[]{:S(2)}) copy-start(s32[4]{0:T(128)} %param.13) | copy-start | bytes 52
  20.1 89.5 %all-to-all-start.1 = ((bf16[16,128,896]{2,1,0:T(8,128)(2,1)}), bf16[16,128,896]{2,1,0:T(8,128)(2,1)}, u32[]{:S(2)}, u32[]{:S(2)}) async-start(bf16[16,128,896]{2,1,0:T(8,128)(2,1)} %broadcast_select_fusion), calls=%async_computation.1 | async-start | bytes 7340032 | tf_op jit(solution)/shard_map/all_to_all | solution.py:77
  27.0 82.3 %collective-permute-start = (bf16[63,2048]{1,0:T(8,128)(2,1)S(1)}, bf16[63,2048]{1,0:T(8,128)(2,1)S(1)}, u32[]{:S(2)}, u32[]{:S(2)}) collective-permute-start(bf16[63,2048]{1,0:T(8,128)(2,1)S(1)} %slice.13), channel_id=1, source_target_pairs={{1,0},{2,1},{3,2},{4,3},{5,4},{6,5},{7,6},{8,7},{9,8},{10,9},{11,1... | collective-permute-start | bytes 774152 | tf_op jit(solution)/shard_map/ppermute | solution.py:16
  112.5 2.0 %copy-start.4 = (bf16[896,2048]{1,0:T(8,128)(2,1)S(1)}, bf16[896,2048]{1,0:T(8,128)(2,1)}, u32[]{:S(2)}) copy-start(bf16[896,2048]{1,0:T(8,128)(2,1)} %param.9) | copy-start | bytes 11010052
  122.3 2.0 %copy-start.1 = (f32[4,16,64,256]{3,2,1,0:T(8,128)}, f32[4,16,64,256]{3,2,1,0:T(8,128)S(1)}, u32[]{:S(2)}) copy-start(f32[4,16,64,256]{3,2,1,0:T(8,128)S(1)} %fusion.3) | copy-start | bytes 12582916
  124.3 2.0 %copy-start.5 = (bf16[896,2048]{1,0:T(8,128)(2,1)S(1)}, bf16[896,2048]{1,0:T(8,128)(2,1)}, u32[]{:S(2)}) copy-start(bf16[896,2048]{1,0:T(8,128)(2,1)} %param.10) | copy-start | bytes 11010052
  147.5 8.8 %collective-permute-start.1 = (bf16[63,2048]{1,0:T(8,128)(2,1)S(1)}, bf16[63,2048]{1,0:T(8,128)(2,1)S(1)}, u32[]{:S(2)}, u32[]{:S(2)}) collective-permute-start(bf16[63,2048]{1,0:T(8,128)(2,1)S(1)} %slice.20), channel_id=1, source_target_pairs={{0,1},{1,2},{2,3},{3,4},{4,5},{5,6},{6,7},{7,8},{8,9},{9,10},{10,1... | collective-permute-start | bytes 774152 | tf_op jit(solution)/shard_map/ppermute | solution.py:16
where the time goes:
time: 158 us
  waiting for transfers between devices  85.4 us (54%)
  matrix products  23.1 us (15%)
  local copies, waits for them, and re-layouts  16.7 us (11%)
  starting transfers between devices  11.8 us (7%)
  other arithmetic  10.3 us (7%)
  blocking collectives  10.1 us (6%)
    ppermute x2, waiting for transfers between devices, from_behind(): lax.ppermute(value, axis, [(source, source + steps) for source in range(f...  85.4 us
    dot_general x1, matrix products, attend(): jnp.einsum('whqk,wkhd->wqhd', weights, value_heads, preferred_element_typ...  11.9 us
    all_to_all x1, blocking collectives, body(): lax.all_to_all(wanted.reshape(peer_count, capacity), 'seq', split_axis=0,...  10.1 us
    unnamed x17, local copies, waits for them, and re-layouts  9.37 us
    all_to_all x1, starting transfers between devices, body(): lax.all_to_all(picked, 'seq', split_axis=0, concat_axis=0, tiled=True)  6.81 us
    ppermute x2, starting transfers between devices, from_behind(): lax.ppermute(value, axis, [(source, source + steps) for source in range(f...  5.03 us
    dot_general x1, matrix products, project(): jnp.dot(normed, w_value, preferred_element_type=jnp.float32)  4.87 us
    dot_general x1, matrix products, project(): jnp.dot(normed, w_key, preferred_element_type=jnp.float32)  4.72 us
  transfers between devices with their start and end apart: 3, of which 2 were waited for; matrix products, arithmetic and copies ran while one was open for 1% of the time, Pallas kernels for 0%

commit v1 on v0

v1 whole, which is shorter than its diff:
```python
import functools
import math

import jax
import jax.numpy as jnp
from jax import lax
from jax.experimental import pallas as pl
from jax.experimental.pallas import tpu as pltpu
from jax.sharding import PartitionSpec as P

SPAN = 64
HEADS = 16
HEAD_DIM = 128
EPS = 1e-6
SCALE = math.log2(math.e) / math.sqrt(HEAD_DIM)


def contract(left, right, dims):
    return lax.dot_general(left, right, (dims, ((), ())), preferred_element_type=jnp.float32)


def fold_kernel(query_ref, key_ref, folded_ref, single_ref):
    blocks = folded_ref.shape[0]
    for head in range(HEADS):
        columns = slice(head * HEAD_DIM, (head + 1) * HEAD_DIM)
        rows = contract(query_ref[:, columns], key_ref[:, columns], ((1,), (1,))) * SCALE
        single_ref[head : head + 1, :] = rows[:1]
        rounded = rows.astype(jnp.bfloat16)
        for block in range(blocks):
            folded_ref[block, head] = rounded[block * SPAN : (block + 1) * SPAN]


def fold(rows, w_key):
    blocks, width = rows.shape[0] // SPAN, w_key.shape[0]
    return pl.pallas_call(
        fold_kernel,
        out_shape=(
            jax.ShapeDtypeStruct((blocks, HEADS, SPAN, width), jnp.bfloat16),
            jax.ShapeDtypeStruct((HEADS, width), jnp.float32),
        ),
        in_specs=[pl.BlockSpec(memory_space=pltpu.VMEM)] * 2,
        out_specs=(pl.BlockSpec(memory_space=pltpu.VMEM),) * 2,
        compiler_params=pltpu.CompilerParams(vmem_limit_bytes=48 * 2**20),
        cost_estimate=pl.CostEstimate(
            flops=2 * rows.size * width, bytes_accessed=16 * 2**20, transcendentals=0
        ),
        name="fold_queries",
    )(rows, w_key)


def mix(scores_of, tokens):
    scores = contract(scores_of, tokens, ((1,), (1,)))
    powers = jnp.exp2(scores - jnp.max(scores, axis=-1, keepdims=True))
    totals = jnp.sum(powers, axis=-1, keepdims=True)
    weights = (powers * (1.0 / totals)).astype(jnp.bfloat16)
    return contract(weights, tokens, ((1,), (0,)))


def attend_kernel(
    ids_ref, keep_ref, folded_hbm, single_ref, store_hbm, value_ref, out_ref,
    folded, raw, tokens, mixed, folded_sems, raw_sems,
):
    blocks = folded.shape[0]
    windows = blocks + 1
    length, width = raw.shape[2], raw.shape[3]

    def fetch_raw(window, part):
        return pltpu.make_async_copy(
            store_hbm.at[ids_ref[window, part]], raw.at[window, part], raw_sems.at[window, part]
        )

    def fetch_folded(block):
        return pltpu.make_async_copy(folded_hbm.at[block], folded.at[block], folded_sems.at[block])

    order = [blocks] + list(range(blocks))
    for window in order:
        for part in range(2):
            fetch_raw(window, part).start()
        if window < blocks:
            fetch_folded(window).start()

    lone = None
    for window in order:
        for part in range(2):
            fetch_raw(window, part).wait()
            widened = raw[window, part].astype(jnp.float32)
            factor = lax.rsqrt(jnp.mean(widened * widened, axis=-1, keepdims=True) + EPS)
            tokens[window, part * length : (part + 1) * length] = (widened * factor).astype(jnp.bfloat16)
        if window == blocks:
            lone = mix(single_ref[...].astype(jnp.bfloat16), tokens[window])
            continue
        fetch_folded(window).wait()
        rows = mix(folded[window].reshape(HEADS * SPAN, width), tokens[window]).reshape(HEADS, SPAN, width)
        if window == 0:
            first = lax.broadcasted_iota(jnp.int32, rows.shape, 1) == 0
            rows = jnp.where(first, lone[:, None, :], rows)
        mixed[:, window * SPAN : (window + 1) * SPAN] = rows.astype(jnp.bfloat16)

    count = blocks * SPAN
    place = lax.broadcasted_iota(jnp.int32, (count, HEAD_DIM), 0)
    kept = place % SPAN == 0
    for block in range(blocks):
        kept = kept | ((place // SPAN == block) & (keep_ref[block] > 0))
    for head in range(HEADS):
        columns = slice(head * HEAD_DIM, (head + 1) * HEAD_DIM)
        rows = contract(mixed[head], value_ref[:, columns], ((1,), (0,)))
        rows = jnp.where(kept, rows, 0.0)
        out_ref[:, columns] = pltpu.roll(rows, count - 1, 0).astype(jnp.bfloat16)


def attend(ids, keep, folded, single, store, w_value):
    blocks, _, _, width = folded.shape
    length = store.shape[1]
    count = blocks * SPAN
    model_width = w_value.shape[1]
    smem, vmem, anywhere = (
        pl.BlockSpec(memory_space=space) for space in (pltpu.SMEM, pltpu.VMEM, pl.ANY)
    )
    return pl.pallas_call(
        attend_kernel,
        out_shape=jax.ShapeDtypeStruct((count, model_width), jnp.bfloat16),
        in_specs=[smem, smem, anywhere, vmem, anywhere, vmem],
        out_specs=vmem,
        scratch_shapes=[
            pltpu.VMEM(folded.shape, jnp.bfloat16),
            pltpu.VMEM((blocks + 1, 2, length, width), jnp.bfloat16),
            pltpu.VMEM((blocks + 1, 2 * length, width), jnp.bfloat16),
            pltpu.VMEM((HEADS, count, width), jnp.bfloat16),
            pltpu.SemaphoreType.DMA((blocks,)),
            pltpu.SemaphoreType.DMA((blocks + 1, 2)),
        ],
        compiler_params=pltpu.CompilerParams(vmem_limit_bytes=56 * 2**20),
        cost_estimate=pl.CostEstimate(
            flops=2 * HEADS * count * width * (4 * length + HEAD_DIM),
            bytes_accessed=16 * 2**20,
            transcendentals=HEADS * count * 2 * length,
        ),
        name="attend_windows",
    )(ids, keep, folded, single, store, w_value)


def body(queries, neighbours, w_key, w_value, retrieval_owner, retrieval_slot, doc_starts):
    devices = lax.axis_size("seq")
    here = lax.axis_index("seq")
    store = lax.all_gather(neighbours, "seq", axis=0, tiled=True)
    own_ids = retrieval_owner * neighbours.shape[0] + retrieval_slot
    ids_before = lax.ppermute(own_ids[-1:], "seq", [(i, i + 1) for i in range(devices - 1)])
    ids = jnp.concatenate([ids_before, own_ids], 0)
    blocks = doc_starts.shape[0]
    opening = (here == 0) & (jnp.arange(blocks) == 0)
    keep = ((doc_starts == 0) & jnp.logical_not(opening)).astype(jnp.int32)
    rows = jnp.concatenate([queries[-1:], queries[:-1]], 0)
    folded, single = fold(rows, w_key)
    return attend(ids, keep, folded, single, store, w_value)


def solution(mesh):
    return jax.shard_map(
        body,
        mesh=mesh,
        in_specs=(
            P(("groups", "seq"), None),
            P(("groups", "seq"), None, None),
            P(),
            P(),
            P(("groups", "seq"), None),
            P(("groups", "seq"), None),
            P(("groups", "seq")),
        ),
        out_specs=P(("groups", "seq"), None),
        check_vma=False,
    )
```

time: 158 us -> 106 us (0.67)
  the two profiles are of different devices: /device:TPU:18 before, /device:TPU:0 now
where the time goes in v1:
time: 106 us
  waiting for transfers between devices  59.6 us (56%)
  Pallas kernels  23.4 us (22%)
  between operations  13.5 us (13%)
  local copies, waits for them, and re-layouts  4.16 us (4%)
  other arithmetic  2.85 us (3%)
  starting transfers between devices  2.35 us (2%)
    all_gather x1, waiting for transfers between devices, body(): store = lax.all_gather(neighbours, 'seq', axis=0, tiled=True)  58.9 us
    pallas_call x1, Pallas kernels, attend(): pl.pallas_call(attend_kernel, out_shape=jax.ShapeDtypeStruct((count, mode...  18.3 us
    pallas_call x1, Pallas kernels, fold(): pl.pallas_call(fold_kernel, out_shape=(jax.ShapeDtypeStruct((blocks, HEAD...  5.09 us
    unnamed x6, local copies, waits for them, and re-layouts  2.65 us
    ppermute x1, starting transfers between devices, body(): lax.ppermute(own_ids[-1:], 'seq', [(i, i + 1) for i in range(devices - 1)])  2.34 us
  transfers between devices with their start and end apart: 2, of which 1 were waited for; matrix products, arithmetic and copies ran while one was open for 4% of the time, Pallas kernels for 5%

profile of v1, /device:TPU:0, one launch (start us, length us, event | category | flops | bytes accessed | tf_op | source)
XLA Modules:
  0.0 105.8 jit_solution(9127133460549662672)
XLA Ops:
  6.5 0.0 copy-start.2
  6.5 0.0 all-gather.2.cloned.1.call-start
  6.5 0.7 all-gather.2.cloned.1.call-update
  7.3 0.7 multiply_add_fusion
  8.0 0.1 slice.9
  8.0 2.3 %collective-permute-start = (s32[1,2]{0,1:T(2,128)S(1)}, s32[1,2]{0,1:T(2,128)S(1)}, u32[]{:S(2)}, u32[]{:S(2)}) collective-permute-start(s32[1,2]{0,1:T(2,128)S(1)} %slice.9), channel_id=1, source_target_pairs={{0,1},{1,2},{2,3},{3,4},{4,5},{5,6},{6,7},{7,8},{8,9},{9,10},{10,1... | collective-permute-start | bytes 32 | tf_op jit(solution)/shard_map/ppermute | solution.py:147
  10.4 0.8 slice.10
  11.2 1.5 %pad_maximum_fusion.query_ref = bf16[256,2048]{1,0:T(8,128)(2,1)S(1)} fusion(bf16[255,2048]{1,0:T(8,128)(2,1)} %bitcast.1, bf16[1,2048]{1,0:T(2,128)(2,1)S(1)} %slice.10), kind=kLoop, calls=%fused_computation | loop fusion | flops 2097152 | bytes 2097152 | tf_op jit(solution)/shard_map/concatenate | solution.py:152
  12.7 0.0 copy-start
  12.7 2.0 %copy-done = bf16[896,2048]{1,0:T(8,128)(2,1)S(1)} copy-done((bf16[896,2048]{1,0:T(8,128)(2,1)S(1)}, bf16[896,2048]{1,0:T(8,128)(2,1)}, u32[]{:S(2)}) %copy-start) | copy-done | bytes 3670040
  14.7 5.1 %fold_queries.1 = (bf16[4,16,64,896]{3,2,1,0:T(8,128)(2,1)}, f32[16,896]{1,0:T(8,128)S(1)}) custom-call(bf16[256,2048]{1,0:T(8,128)(2,1)S(1)} %pad_maximum_fusion.query_ref, bf16[896,2048]{1,0:T(8,128)(2,1)S(1)} %copy-done), custom_call_target="tpu_custom_call" | custom-call | flops 939524096 | bytes 16777216 | tf_op jit(solution)/shard_map/fold_queries/pallas_call | solution.py:35
  19.8 0.0 copy-start.1
  19.8 0.6 copy-done.1
  20.4 0.0 copy-done.2
  20.4 0.6 and_convert_fusion.keep_ref
  21.0 0.0 collective-permute-done
  21.0 0.1 pad_add_fusion
  21.1 0.7 copy.10.ids_ref
  21.7 58.9 %all-gather.2.cloned.1.call-done.store_hbm = bf16[32,128,896]{2,1,0:T(8,128)(2,1)} async-done(((bf16[2,128,896]{2,1,0:T(8,128)(2,1)}), bf16[32,128,896]{2,1,0:T(8,128)(2,1)}) %all-gather.2.cloned.1.call-update) | async-done | bytes 7340048 | tf_op jit(solution)/shard_map/all_gather | solution.py:145
  80.6 18.3 %attend_windows.1 = bf16[256,2048]{1,0:T(8,128)(2,1)} custom-call(s32[5,2]{1,0:T(8,128)} %copy.10.ids_ref, s32[4]{0:T(128)} %and_convert_fusion.keep_ref, bf16[4,16,64,896]{3,2,1,0:T(8,128)(2,1)} %get-tuple-element.7.folded_hbm, f32[16,896]{1,0:T(8,128)} %copy-done.1, bf16[32,128,896]{2,1,0:T(8,128)(2,1)} %all-gather.2.cloned.1.call-done.store_hbm, ...), custom_call_target="tpu_custom_call" | custom-call | flops 4697620480 | bytes 16777216 | tf_op jit(solution)/shard_map/attend_windows/pallas_call | solution.py:119
Async XLA Ops:
  6.5 13.9 %copy-start.2 = (s32[4]{0:T(128)S(1)}, s32[4]{0:T(128)}, u32[]{:S(2)}) copy-start(s32[4]{0:T(128)} %param.13) | copy-start | bytes 52
  6.5 74.1 %all-gather.2.cloned.1.call-start = ((), (), s32[]{:S(2)}) async-start(), calls=%async_computation | async-start | bytes 7798784 | tf_op jit(solution)/shard_map/all_gather | solution.py:145
  8.0 13.0 %collective-permute-start = (s32[1,2]{0,1:T(2,128)S(1)}, s32[1,2]{0,1:T(2,128)S(1)}, u32[]{:S(2)}, u32[]{:S(2)}) collective-permute-start(s32[1,2]{0,1:T(2,128)S(1)} %slice.9), channel_id=1, source_target_pairs={{0,1},{1,2},{2,3},{3,4},{4,5},{5,6},{6,7},{7,8},{8,9},{9,10},{10,1... | collective-permute-start | bytes 32 | tf_op jit(solution)/shard_map/ppermute | solution.py:147
  12.7 2.0 %copy-start = (bf16[896,2048]{1,0:T(8,128)(2,1)S(1)}, bf16[896,2048]{1,0:T(8,128)(2,1)}, u32[]{:S(2)}) copy-start(bf16[896,2048]{1,0:T(8,128)(2,1)} %key_ref.1) | copy-start | bytes 11010052
  19.8 0.6 copy-start.1
Sparse Core Ops, SparseCore 0:
  9.6 70.9 all-gather.1

commit v2 on v1

--- a/solution.py
+++ b/solution.py
@@ -57,16 +57,16 @@
 
 
 def attend_kernel(
-    ids_ref, keep_ref, folded_hbm, single_ref, store_hbm, value_ref, out_ref,
-    folded, raw, tokens, mixed, folded_sems, raw_sems,
+    source_ref, block_ref, keep_ref, folded_hbm, single_ref, value_ref, *rest
 ):
+    *stores, out_ref, folded, raw, tokens, mixed, folded_sems, raw_sems = rest
     blocks = folded.shape[0]
     windows = blocks + 1
     length, width = raw.shape[2], raw.shape[3]
 
-    def fetch_raw(window, part):
+    def fetch_raw(window, part, store):
         return pltpu.make_async_copy(
-            store_hbm.at[ids_ref[window, part]], raw.at[window, part], raw_sems.at[window, part]
+            store.at[block_ref[window, part]], raw.at[window, part], raw_sems.at[window, part]
         )
 
     def fetch_folded(block):
@@ -75,14 +75,19 @@
     order = [blocks] + list(range(blocks))
     for window in order:
         for part in range(2):
-            fetch_raw(window, part).start()
+            for place, store in enumerate(stores):
+
+                @pl.when(source_ref[window, part] == place)
+                def _(store=store):
+                    fetch_raw(window, part, store).start()
+
         if window < blocks:
             fetch_folded(window).start()
 
     lone = None
     for window in order:
         for part in range(2):
-            fetch_raw(window, part).wait()
+            fetch_raw(window, part, stores[0]).wait()
             widened = raw[window, part].astype(jnp.float32)
             factor = lax.rsqrt(jnp.mean(widened * widened, axis=-1, keepdims=True) + EPS)
             tokens[window, part * length : (part + 1) * length] = (widened * factor).astype(jnp.bfloat16)
@@ -108,9 +113,9 @@
         out_ref[:, columns] = pltpu.roll(rows, count - 1, 0).astype(jnp.bfloat16)
 
 
-def attend(ids, keep, folded, single, store, w_value):
+def attend(source, block, keep, folded, single, stores, w_value):
     blocks, _, _, width = folded.shape
-    length = store.shape[1]
+    length = stores[0].shape[1]
     count = blocks * SPAN
     model_width = w_value.shape[1]
     smem, vmem, anywhere = (
@@ -119,7 +124,7 @@
     return pl.pallas_call(
         attend_kernel,
         out_shape=jax.ShapeDtypeStruct((count, model_width), jnp.bfloat16),
-        in_specs=[smem, smem, anywhere, vmem, anywhere, vmem],
+        in_specs=[smem, smem, smem, anywhere, vmem, vmem] + [anywhere] * len(stores),
         out_specs=vmem,
         scratch_shapes=[
             pltpu.VMEM(folded.shape, jnp.bfloat16),
@@ -136,22 +141,27 @@
             transcendentals=HEADS * count * 2 * length,
         ),
         name="attend_windows",
-    )(ids, keep, folded, single, store, w_value)
+    )(source, block, keep, folded, single, w_value, *stores)
 
 
 def body(queries, neighbours, w_key, w_value, retrieval_owner, retrieval_slot, doc_starts):
     devices = lax.axis_size("seq")
     here = lax.axis_index("seq")
-    store = lax.all_gather(neighbours, "seq", axis=0, tiled=True)
-    own_ids = retrieval_owner * neighbours.shape[0] + retrieval_slot
-    ids_before = lax.ppermute(own_ids[-1:], "seq", [(i, i + 1) for i in range(devices - 1)])
-    ids = jnp.concatenate([ids_before, own_ids], 0)
+    cores = 2
+    same_core = [list(range(core, devices, cores)) for core in range(cores)]
+    mine = lax.all_gather(neighbours, "seq", axis=0, tiled=True, axis_index_groups=same_core)
+    other = lax.ppermute(mine, "seq", [(i, i ^ 1) for i in range(devices)])
+    owner_slot = jnp.stack([retrieval_owner, retrieval_slot])
+    before = lax.ppermute(owner_slot[:, -1:], "seq", [(i, i + 1) for i in range(devices - 1)])
+    owner, slot = jnp.concatenate([before, owner_slot], 1)
+    source = jnp.where(owner % cores == here % cores, 0, 1)
+    block = owner // cores * neighbours.shape[0] + slot
     blocks = doc_starts.shape[0]
     opening = (here == 0) & (jnp.arange(blocks) == 0)
     keep = ((doc_starts == 0) & jnp.logical_not(opening)).astype(jnp.int32)
     rows = jnp.concatenate([queries[-1:], queries[:-1]], 0)
     folded, single = fold(rows, w_key)
-    return attend(ids, keep, folded, single, store, w_value)
+    return attend(source, block, keep, folded, single, (mine, other), w_value)
 
 
 def solution(mesh):

time: 106 us -> 119 us (1.12)
  waiting for transfers between devices: 59.6 us -> 72.5 us
    all_gather x1, waiting for transfers between devices: 58.9 us -> 71.8 us  [body(): lax.all_gather(neighbours, 'seq', axis=0, tiled=True, axis_index_groups=s...]
    ppermute x1 -> x2, starting transfers between devices: 2.34 us -> 2.4 us  [the longest x1 2.4 us: body(): lax.ppermute(owner_slot[:, -1:], 'seq', [(i, i + 1) for i in range(device...]
    unnamed x6 -> x10, local copies, waits for them, and re-layouts: 2.65 us -> 2.66 us
  transfers between devices with their start and end apart: 2 -> 3, of which waited for: 1 -> 1; matrix products, arithmetic and copies ran while one was open for 4% -> 4% of each run, Pallas kernels for 5% -> 4%
where the time goes in v2:
time: 119 us
  waiting for transfers between devices  72.5 us (61%)
  Pallas kernels  23.4 us (20%)
  between operations  13.5 us (11%)
  local copies, waits for them, and re-layouts  3.63 us (3%)
  other arithmetic  3.53 us (3%)
  starting transfers between devices  2.41 us (2%)
    all_gather x1, waiting for transfers between devices, body(): lax.all_gather(neighbours, 'seq', axis=0, tiled=True, axis_index_groups=s...  71.8 us
    pallas_call x1, Pallas kernels, attend(): pl.pallas_call(attend_kernel, out_shape=jax.ShapeDtypeStruct((count, mode...  18.4 us
    pallas_call x1, Pallas kernels, fold(): pl.pallas_call(fold_kernel, out_shape=(jax.ShapeDtypeStruct((blocks, HEAD...  5.03 us
    unnamed x10, local copies, waits for them, and re-layouts  2.66 us
    ppermute x1, starting transfers between devices, body(): lax.ppermute(owner_slot[:, -1:], 'seq', [(i, i + 1) for i in range(device...  2.4 us
  transfers between devices with their start and end apart: 3, of which 1 were waited for; matrix products, arithmetic and copies ran while one was open for 4% of the time, Pallas kernels for 4%

profile of v2, /device:TPU:0, one launch (start us, length us, event | category | flops | bytes accessed | tf_op | source)
XLA Modules:
  0.0 119.0 jit_solution(8187153833932842421)
XLA Ops:
  6.5 0.0 copy-start.3
  6.5 0.0 copy-start.2
  6.5 0.0 copy-start.4
  6.5 0.0 all-gather.2.cloned.1.call-start
  6.5 0.7 all-gather.2.cloned.1.call-update
  7.3 71.8 %all-gather.2.cloned.1.call-done.rest_0_ = bf16[16,128,896]{2,1,0:T(8,128)(2,1)} async-done(((bf16[2,128,896]{2,1,0:T(8,128)(2,1)}), bf16[16,128,896]{2,1,0:T(8,128)(2,1)}) %all-gather.2.cloned.1.call-update) | async-done | bytes 3670032 | tf_op jit(solution)/shard_map/all_gather | solution.py:152
  79.1 0.0 collective-permute-start.1
  79.1 0.8 pad_add_fusion
  79.9 2.4 %collective-permute-start = (s32[2,1,2]{1,2,0:T(2,128)S(1)}, s32[2,1,2]{1,2,0:T(2,128)S(1)}, u32[]{:S(2)}, u32[]{:S(2)}) collective-permute-start(s32[2,1,2]{1,2,0:T(2,128)S(1)} %pad_add_fusion), channel_id=1, source_target_pairs={{0,1},{1,2},{2,3},{3,4},{4,5},{5,6},{6,7},{7,8},{8,9},{9,10},{10,1... | collective-permute-start | bytes 56 | tf_op jit(solution)/shard_map/ppermute | solution.py:155
  82.3 0.8 slice.10
  83.1 1.5 %pad_maximum_fusion.query_ref = bf16[256,2048]{1,0:T(8,128)(2,1)S(1)} fusion(bf16[255,2048]{1,0:T(8,128)(2,1)} %bitcast.7, bf16[1,2048]{1,0:T(2,128)(2,1)S(1)} %slice.10), kind=kLoop, calls=%fused_computation | loop fusion | flops 2097152 | bytes 2097152 | tf_op jit(solution)/shard_map/concatenate | solution.py:162
  84.6 0.0 copy-start
  84.6 2.0 %copy-done = bf16[896,2048]{1,0:T(8,128)(2,1)S(1)} copy-done((bf16[896,2048]{1,0:T(8,128)(2,1)S(1)}, bf16[896,2048]{1,0:T(8,128)(2,1)}, u32[]{:S(2)}) %copy-start) | copy-done | bytes 3670040
  86.6 5.0 %fold_queries.1 = (bf16[4,16,64,896]{3,2,1,0:T(8,128)(2,1)}, f32[16,896]{1,0:T(8,128)S(1)}) custom-call(bf16[256,2048]{1,0:T(8,128)(2,1)S(1)} %pad_maximum_fusion.query_ref, bf16[896,2048]{1,0:T(8,128)(2,1)S(1)} %copy-done), custom_call_target="tpu_custom_call" | custom-call | flops 939524096 | bytes 16777216 | tf_op jit(solution)/shard_map/fold_queries/pallas_call | solution.py:35
  91.6 0.0 copy-start.1
  91.6 0.6 copy-done.1
  92.2 0.0 copy-done.4
  92.2 0.6 and_convert_fusion.keep_ref
  92.8 0.0 collective-permute-done
  92.8 0.0 copy-done.3
  92.8 0.0 copy-done.2
  92.9 0.1 add_add_fusion
  92.9 0.1 copy.13
  93.0 0.1 copy.17
  93.1 0.6 fusion.2
  93.7 0.0 collective-permute-done.1.rest_1_
  93.7 18.4 %attend_windows.1 = bf16[256,2048]{1,0:T(8,128)(2,1)} custom-call(s32[5,2]{1,0:T(8,128)} %get-tuple-element.10.source_ref, s32[5,2]{1,0:T(8,128)} %get-tuple-element.9.block_ref, s32[4]{0:T(128)} %and_convert_fusion.keep_ref, bf16[4,16,64,896]{3,2,1,0:T(8,128)(2,1)} %get-tuple-element.7.folded_hbm, f32[16,896]{1,0:T(8,128)} %copy-done.1, ...), custom_call_target="tpu_custom_call" | custom-call | flops 4697620480 | bytes 16777216 | tf_op jit(solution)/shard_map/attend_windows/pallas_call | solution.py:124
  (1 shorter events, 0.0 us)
Async XLA Ops:
  6.5 86.3 %copy-start.3 = (s32[4,2]{0,1:T(2,128)S(1)}, s32[4,2]{0,1:T(2,128)}, u32[]{:S(2)}) copy-start(s32[4,2]{0,1:T(2,128)} %param.11) | copy-start | bytes 100
  6.5 86.3 %copy-start.2 = (s32[4,2]{0,1:T(2,128)S(1)}, s32[4,2]{0,1:T(2,128)}, u32[]{:S(2)}) copy-start(s32[4,2]{0,1:T(2,128)} %param.12) | copy-start | bytes 100
  6.5 85.7 %copy-start.4 = (s32[4]{0:T(128)S(1)}, s32[4]{0:T(128)}, u32[]{:S(2)}) copy-start(s32[4]{0:T(128)} %param.13) | copy-start | bytes 52
  6.5 72.6 %all-gather.2.cloned.1.call-start = ((), (), s32[]{:S(2)}) async-start(), calls=%async_computation | async-start | bytes 4128768 | tf_op jit(solution)/shard_map/all_gather | solution.py:152
  79.1 14.6 %collective-permute-start.1 = (bf16[16,128,896]{2,1,0:T(8,128)(2,1)}, bf16[16,128,896]{2,1,0:T(8,128)(2,1)}, u32[]{:S(2)}, u32[]{:S(2)}) collective-permute-start(bf16[16,128,896]{2,1,0:T(8,128)(2,1)} %all-gather.2.cloned.1.call-done.rest_0_), channel_id=1, source_target_pairs={{0,1},{1,0},{2,3},{3,2},{4,5},{5,4},{6,7},{7,6},{8,9},{9,8},{10,11... | collective-permute-start | bytes 11010056 | tf_op jit(solution)/shard_map/ppermute | solution.py:153
  79.9 13.0 %collective-permute-start = (s32[2,1,2]{1,2,0:T(2,128)S(1)}, s32[2,1,2]{1,2,0:T(2,128)S(1)}, u32[]{:S(2)}, u32[]{:S(2)}) collective-permute-start(s32[2,1,2]{1,2,0:T(2,128)S(1)} %pad_add_fusion), channel_id=1, source_target_pairs={{0,1},{1,2},{2,3},{3,4},{4,5},{5,6},{6,7},{7,8},{8,9},{9,10},{10,1... | collective-permute-start | bytes 56 | tf_op jit(solution)/shard_map/ppermute | solution.py:155
  84.6 2.0 %copy-start = (bf16[896,2048]{1,0:T(8,128)(2,1)S(1)}, bf16[896,2048]{1,0:T(8,128)(2,1)}, u32[]{:S(2)}) copy-start(bf16[896,2048]{1,0:T(8,128)(2,1)} %key_ref.1) | copy-start | bytes 11010052
  91.6 0.6 copy-start.1
Sparse Core Ops, SparseCore 0:
  9.5 69.5 all-gather.1

commit v3 on v2

--- a/solution.py
+++ b/solution.py
@@ -144,29 +144,83 @@
     )(source, block, keep, folded, single, w_value, *stores)
 
 
-def body(queries, neighbours, w_key, w_value, retrieval_owner, retrieval_slot, doc_starts):
+CORES = 2
+
+
+def chip_ring(mesh):
+    row = mesh.devices.reshape(-1, mesh.shape["seq"])[0]
+    chips = list(range(len(row) // CORES))
+    columns = [tuple(getattr(row[CORES * chip], "coords", (0, 0))[:2]) for chip in chips]
+    if len(set(columns)) != 2:
+        return chips
+    up = [chip for chip in chips if columns[chip] == columns[0]]
+    return up + [chip for chip in reversed(chips) if columns[chip] != columns[0]]
+
+
+def gather(stored, ring):
+    size = len(ring)
+    half = size // 2
+
+    def turned(value, steps):
+        pairs = [
+            (CORES * ring[i] + core, CORES * ring[(i + steps) % size] + core)
+            for i in range(size)
+            for core in range(CORES)
+        ]
+        return lax.ppermute(value, "seq", pairs)
+
+    ahead, behind = [stored], [stored]
+    for _ in range((size - 1) // 2):
+        ahead.append(turned(ahead[-1], 1))
+        behind.append(turned(behind[-1], -1))
+    own = ahead + behind[1:]
+    if size % 2 == 0:
+        cut = stored.shape[0] // 2
+        own += [turned(ahead[-1][:cut], 1), turned(behind[-1][cut:], -1)]
+    swap = [(i, i ^ 1) for i in range(CORES * size)]
+    return own + [lax.ppermute(value, "seq", swap) for value in own]
+
+
+def locate(owner, slot, here, stored, ring):
+    size = len(ring)
+    reach = (size - 1) // 2
+    order = jnp.asarray([ring.index(chip) for chip in range(size)], jnp.int32)
+
+    def place_of(device):
+        chips = jnp.arange(size)
+        return jnp.sum(jnp.where((device // CORES)[..., None] == chips, order, 0), axis=-1)
+
+    away = (place_of(here) - place_of(owner)) % size
+    cut = stored // 2
+    source = jnp.where(away <= reach, away, reach + size - away)
+    block = slot
+    if size % 2 == 0:
+        middle, late = away == size // 2, slot >= cut
+        source = jnp.where(middle, 2 * reach + 1 + late, source)
+        block = jnp.where(middle & late, slot - cut, slot)
+    count = 2 * reach + 1 + 2 * (size % 2 == 0)
+    return source + jnp.where(owner % CORES == here % CORES, 0, count), block
+
+
+def body(ring, queries, neighbours, w_key, w_value, retrieval_owner, retrieval_slot, doc_starts):
     devices = lax.axis_size("seq")
     here = lax.axis_index("seq")
-    cores = 2
-    same_core = [list(range(core, devices, cores)) for core in range(cores)]
-    mine = lax.all_gather(neighbours, "seq", axis=0, tiled=True, axis_index_groups=same_core)
-    other = lax.ppermute(mine, "seq", [(i, i ^ 1) for i in range(devices)])
+    stores = gather(neighbours, ring)
     owner_slot = jnp.stack([retrieval_owner, retrieval_slot])
     before = lax.ppermute(owner_slot[:, -1:], "seq", [(i, i + 1) for i in range(devices - 1)])
     owner, slot = jnp.concatenate([before, owner_slot], 1)
-    source = jnp.where(owner % cores == here % cores, 0, 1)
-    block = owner // cores * neighbours.shape[0] + slot
+    source, block = locate(owner, slot, here, neighbours.shape[0], ring)
     blocks = doc_starts.shape[0]
     opening = (here == 0) & (jnp.arange(blocks) == 0)
     keep = ((doc_starts == 0) & jnp.logical_not(opening)).astype(jnp.int32)
     rows = jnp.concatenate([queries[-1:], queries[:-1]], 0)
     folded, single = fold(rows, w_key)
-    return attend(source, block, keep, folded, single, (mine, other), w_value)
+    return attend(source, block, keep, folded, single, stores, w_value)
 
 
 def solution(mesh):
     return jax.shard_map(
-        body,
+        functools.partial(body, chip_ring(mesh)),
         mesh=mesh,
         in_specs=(
             P(("groups", "seq"), None),

time: 119 us -> 77.4 us (0.65)
  waiting for transfers between devices: 72.5 us -> 28.5 us
  between operations: 13.5 us -> 0.31 us
  starting transfers between devices: 2.41 us -> 13 us
  local copies, waits for them, and re-layouts: 3.63 us -> 6.12 us
  other arithmetic: 3.53 us -> 5.58 us
    all_gather x1 -> x0, waiting for transfers between devices: 71.8 us -> none  [body(): lax.all_gather(neighbours, 'seq', axis=0, tiled=True, axis_index_groups=s...]
    ppermute x1 -> x17, waiting for transfers between devices: 0.01 us -> 28.5 us  [the longest x8 28.1 us: turned(): return lax.ppermute(value, 'seq', pairs)]
    ppermute x1 -> x17, starting transfers between devices: 0.01 us -> 10.6 us  [the longest x8 9.5 us: turned(): return lax.ppermute(value, 'seq', pairs)]
    slice x0 -> x2, local copies, waits for them, and re-layouts: none -> 1.41 us  [gather(): own += [turned(ahead[-1][:cut], 1), turned(behind[-1][cut:], -1)]]
    unnamed x10 -> x32, local copies, waits for them, and re-layouts: 2.66 us -> 3.74 us
  transfers between devices with their start and end apart: 3 -> 18, of which waited for: 1 -> 6; matrix products, arithmetic and copies ran while one was open for 4% -> 10% of each run, Pallas kernels for 4% -> 7%
where the time goes in v3:
time: 77.4 us; the launch traced here: 77 us
  waiting for transfers between devices  28.5 us (37%)
  Pallas kernels  23.5 us (30%)
  starting transfers between devices  13 us (17%)
  local copies, waits for them, and re-layouts  6.12 us (8%)
  other arithmetic  5.58 us (7%)
    ppermute x8, waiting for transfers between devices, turned(): return lax.ppermute(value, 'seq', pairs)  28.1 us
    pallas_call x1, Pallas kernels, attend(): pl.pallas_call(attend_kernel, out_shape=jax.ShapeDtypeStruct((count, mode...  18.5 us
    ppermute x8, starting transfers between devices, turned(): return lax.ppermute(value, 'seq', pairs)  9.5 us
    pallas_call x1, Pallas kernels, fold(): pl.pallas_call(fold_kernel, out_shape=(jax.ShapeDtypeStruct((blocks, HEAD...  5.01 us
    unnamed x32, local copies, waits for them, and re-layouts  3.74 us
    ppermute x1, starting transfers between devices, body(): lax.ppermute(owner_slot[:, -1:], 'seq', [(i, i + 1) for i in range(device...  2.4 us
  transfers between devices with their start and end apart: 18, of which 6 were waited for; matrix products, arithmetic and copies ran while one was open for 10% of the time, Pallas kernels for 7%

profile of v3, /device:TPU:0, one launch (start us, length us, event | category | flops | bytes accessed | tf_op | source)
XLA Modules:
  0.0 77.0 jit_solution(9334998700912794492)
XLA Ops:
  0.0 3.1 %collective-permute-start.1 = (bf16[2,128,896]{2,1,0:T(8,128)(2,1)}, bf16[2,128,896]{2,1,0:T(8,128)(2,1)S(1)}, u32[]{:S(2)}, u32[]{:S(2)}) collective-permute-start(bf16[2,128,896]{2,1,0:T(8,128)(2,1)} %rest_0_.1), channel_id=1, source_target_pairs={{0,4},{1,5},{4,8},{5,9},{8,12},{9,13},{12,14},{13,15},{14,10},{15,... | collective-permute-start | bytes 1376264 | tf_op jit(solution)/shard_map/ppermute | solution.py:170
  3.1 0.0 collective-permute-start.4
  3.1 10.7 %collective-permute-done.1.rest_1_ = bf16[2,128,896]{2,1,0:T(8,128)(2,1)S(1)} collective-permute-done((bf16[2,128,896]{2,1,0:T(8,128)(2,1)}, bf16[2,128,896]{2,1,0:T(8,128)(2,1)S(1)}, u32[]{:S(2)}, u32[]{:S(2)}) %collective-permute-start.1) | collective-permute-done | bytes 458784 | tf_op jit(solution)/shard_map/ppermute | solution.py:170
  13.8 1.8 %collective-permute-start.2 = (bf16[2,128,896]{2,1,0:T(8,128)(2,1)S(1)}, bf16[2,128,896]{2,1,0:T(8,128)(2,1)S(1)}, u32[]{:S(2)}, u32[]{:S(2)}) collective-permute-start(bf16[2,128,896]{2,1,0:T(8,128)(2,1)S(1)} %collective-permute-done.1.rest_1_), channel_id=1, source_target_pairs={{0,4},{1,5},{4,8},{5,9},{8,12},{9,13},{12,14},{13,15},{14,10},{15,... | collective-permute-start | bytes 1376264 | tf_op jit(solution)/shard_map/ppermute | solution.py:170
  15.6 0.0 collective-permute-done.4.rest_4_
  15.6 0.2 collective-permute-start.5
  15.8 0.8 pad_add_fusion
  16.6 2.4 %collective-permute-start = (s32[2,1,2]{1,2,0:T(2,128)S(1)}, s32[2,1,2]{1,2,0:T(2,128)S(1)}, u32[]{:S(2)}, u32[]{:S(2)}) collective-permute-start(s32[2,1,2]{1,2,0:T(2,128)S(1)} %pad_add_fusion), channel_id=1, source_target_pairs={{0,1},{1,2},{2,3},{3,4},{4,5},{5,6},{6,7},{7,8},{8,9},{9,10},{10,1... | collective-permute-start | bytes 56 | tf_op jit(solution)/shard_map/ppermute | solution.py:210
  19.0 0.8 %slice.16 = bf16[1,2048]{1,0:T(2,128)(2,1)S(1)} slice(bf16[256,2048]{1,0:T(8,128)(2,1)} %param.8), slice={[255:256], [0:2048]} | slice | bytes 8192 | tf_op jit(solution)/shard_map/slice | solution.py:216
  19.8 5.7 %collective-permute-done.2.rest_2_ = bf16[2,128,896]{2,1,0:T(8,128)(2,1)S(1)} collective-permute-done((bf16[2,128,896]{2,1,0:T(8,128)(2,1)S(1)}, bf16[2,128,896]{2,1,0:T(8,128)(2,1)S(1)}, u32[]{:S(2)}, u32[]{:S(2)}) %collective-permute-start.2) | collective-permute-done | bytes 458784 | tf_op jit(solution)/shard_map/ppermute | solution.py:170
  25.5 1.5 %collective-permute-start.3 = (bf16[2,128,896]{2,1,0:T(8,128)(2,1)S(1)}, bf16[2,128,896]{2,1,0:T(8,128)(2,1)S(1)}, u32[]{:S(2)}, u32[]{:S(2)}) collective-permute-start(bf16[2,128,896]{2,1,0:T(8,128)(2,1)S(1)} %collective-permute-done.2.rest_2_), channel_id=1, source_target_pairs={{0,4},{1,5},{4,8},{5,9},{8,12},{9,13},{12,14},{13,15},{14,10},{15,... | collective-permute-start | bytes 1376264 | tf_op jit(solution)/shard_map/ppermute | solution.py:170
  26.9 1.5 %pad_maximum_fusion.query_ref = bf16[256,2048]{1,0:T(8,128)(2,1)S(1)} fusion(bf16[255,2048]{1,0:T(8,128)(2,1)} %bitcast.7, bf16[1,2048]{1,0:T(2,128)(2,1)S(1)} %slice.16), kind=kLoop, calls=%fused_computation | loop fusion | flops 2097152 | bytes 2097152 | tf_op jit(solution)/shard_map/concatenate | solution.py:216
  28.4 0.0 collective-permute-done.5.rest_5_
  28.5 0.6 collective-permute-start.6
  29.1 1.2 %and_convert_fusion.keep_ref = s32[4]{0:T(128)} fusion(s32[4]{0:T(128)} %param.14, pred[]{:T(512)S(6)} %eq.53), kind=kLoop, calls=%fused_computation.24 | loop fusion | flops 24 | bytes 33 | tf_op jit(solution)/shard_map/convert_element_type | solution.py:215
  30.3 0.0 collective-permute-start.10
  30.3 0.0 collective-permute-done
  30.3 0.5 collective-permute-start.13
  30.8 5.4 %collective-permute-done.3.rest_3_ = bf16[2,128,896]{2,1,0:T(8,128)(2,1)S(1)} collective-permute-done((bf16[2,128,896]{2,1,0:T(8,128)(2,1)S(1)}, bf16[2,128,896]{2,1,0:T(8,128)(2,1)S(1)}, u32[]{:S(2)}, u32[]{:S(2)}) %collective-permute-start.3) | collective-permute-done | bytes 458784 | tf_op jit(solution)/shard_map/ppermute | solution.py:170
  36.3 0.0 collective-permute-start.11
  36.3 2.2 %copy-done = bf16[896,2048]{1,0:T(8,128)(2,1)S(1)} copy-done((bf16[896,2048]{1,0:T(8,128)(2,1)S(1)}, bf16[896,2048]{1,0:T(8,128)(2,1)}, u32[]{:S(2)}) %copy-start) | copy-done | bytes 3670040
  38.5 5.0 %fold_queries.1 = (bf16[4,16,64,896]{3,2,1,0:T(8,128)(2,1)}, f32[16,896]{1,0:T(8,128)S(1)}) custom-call(bf16[256,2048]{1,0:T(8,128)(2,1)S(1)} %pad_maximum_fusion.query_ref, bf16[896,2048]{1,0:T(8,128)(2,1)S(1)} %copy-done), custom_call_target="tpu_custom_call" | custom-call | flops 939524096 | bytes 16777216 | tf_op jit(solution)/shard_map/fold_queries/pallas_call | solution.py:35
  43.5 0.6 copy-done.1
  44.1 0.6 fusion.7
  44.7 0.1 add_add_fusion
  44.8 0.7 slice.20
  45.5 0.0 collective-permute-done.6.rest_6_
  45.5 1.2 %collective-permute-start.7 = (bf16[1,128,896]{2,1,0:T(8,128)(2,1)}, bf16[1,128,896]{2,1,0:T(8,128)(2,1)S(1)}, u32[]{:S(2)}, u32[]{:S(2)}) collective-permute-start(bf16[1,128,896]{2,1,0:T(8,128)(2,1)} %slice.20), channel_id=1, source_target_pairs={{0,4},{1,5},{4,8},{5,9},{8,12},{9,13},{12,14},{13,15},{14,10},{15,... | collective-permute-start | bytes 688136 | tf_op jit(solution)/shard_map/ppermute | solution.py:170
  46.7 0.7 slice.21
  47.4 1.1 %collective-permute-start.8 = (bf16[1,128,896]{2,1,0:T(8,128)(2,1)}, bf16[1,128,896]{2,1,0:T(8,128)(2,1)}, u32[]{:S(2)}, u32[]{:S(2)}) collective-permute-start(bf16[1,128,896]{2,1,0:T(8,128)(2,1)} %slice.21), channel_id=1, source_target_pairs={{0,2},{1,3},{4,0},{5,1},{8,4},{9,5},{12,8},{13,9},{14,12},{15,13},... | collective-permute-start | bytes 688136 | tf_op jit(solution)/shard_map/ppermute | solution.py:170
  48.5 0.1 copy.16
  48.6 0.0 collective-permute-done.10.rest_10_
  48.6 0.0 collective-permute-start.14
  48.6 0.0 collective-permute-done.13.rest_13_
  48.6 0.5 collective-permute-start.12
  49.1 0.0 collective-permute-done.11.rest_11_
  49.1 0.1 collective-permute-start.15
  49.2 4.4 %collective-permute-done.7.rest_7_ = bf16[1,128,896]{2,1,0:T(8,128)(2,1)S(1)} collective-permute-done((bf16[1,128,896]{2,1,0:T(8,128)(2,1)}, bf16[1,128,896]{2,1,0:T(8,128)(2,1)S(1)}, u32[]{:S(2)}, u32[]{:S(2)}) %collective-permute-start.7) | collective-permute-done | bytes 229408 | tf_op jit(solution)/shard_map/ppermute | solution.py:170
  53.6 0.0 collective-permute-start.16
  53.6 1.9 %collective-permute-done.8.rest_8_ = bf16[1,128,896]{2,1,0:T(8,128)(2,1)} collective-permute-done((bf16[1,128,896]{2,1,0:T(8,128)(2,1)}, bf16[1,128,896]{2,1,0:T(8,128)(2,1)}, u32[]{:S(2)}, u32[]{:S(2)}) %collective-permute-start.8) | collective-permute-done | bytes 229408 | tf_op jit(solution)/shard_map/ppermute | solution.py:170
  55.5 0.2 fusion
  55.8 0.1 copy.20
  55.9 1.2 %add_select_fusion = (s32[5,2]{1,0:T(8,128)}, s32[5,2]{1,0:T(8,128)}) fusion(s32[5,2]{1,0:T(8,128)S(1)} %copy.20, s32[5,2]{1,0:T(8,128)S(1)} %fusion, s32[]{:T(128)} %fusion.7, s32[]{:T(128)S(6)} %select_n.60, s32[5,2]{1,0:T(8,128)S(1)} %copy.16), kind=kLoop, calls=%fused_computation.3 | loop fusion | flops 370 | bytes 208 | tf_op jit(solution)/shard_map/jit(_where)/select_n | solution.py:200
  57.0 0.3 collective-permute-done.17.rest_17_
  57.4 0.4 copy-done.9
  57.9 0.3 copy-done.10
  58.2 0.2 copy-done.11
  58.3 18.5 %attend_windows.1 = bf16[256,2048]{1,0:T(8,128)(2,1)} custom-call(s32[5,2]{1,0:T(8,128)} %get-tuple-element.10.source_ref, s32[5,2]{1,0:T(8,128)} %get-tuple-element.9.block_ref, s32[4]{0:T(128)} %and_convert_fusion.keep_ref, bf16[4,16,64,896]{3,2,1,0:T(8,128)(2,1)} %get-tuple-element.7.folded_hbm, f32[16,896]{1,0:T(8,128)} %copy-done.1, ...), custom_call_target="tpu_custom_call" | custom-call | flops 4697620480 | bytes 16777216 | tf_op jit(solution)/shard_map/attend_windows/pallas_call | solution.py:124
  (36 shorter events, 0.1 us)
Async XLA Ops:
  0.0 44.1 %copy-start.15 = (s32[8]{0:T(128)S(1)}, s32[8]{0:T(128)}, u32[]{:S(2)}) copy-start(s32[8]{0:T(128)} %constant.71.clone) | copy-start | bytes 100
  0.0 44.7 %copy-start.14 = (s32[4,2]{0,1:T(2,128)S(1)}, s32[4,2]{0,1:T(2,128)}, u32[]{:S(2)}) copy-start(s32[4,2]{0,1:T(2,128)} %param.12) | copy-start | bytes 100
  0.0 44.7 %copy-start.13 = (s32[4,2]{0,1:T(2,128)S(1)}, s32[4,2]{0,1:T(2,128)}, u32[]{:S(2)}) copy-start(s32[4,2]{0,1:T(2,128)} %param.13) | copy-start | bytes 100
  0.0 13.8 %collective-permute-start.1 = (bf16[2,128,896]{2,1,0:T(8,128)(2,1)}, bf16[2,128,896]{2,1,0:T(8,128)(2,1)S(1)}, u32[]{:S(2)}, u32[]{:S(2)}) collective-permute-start(bf16[2,128,896]{2,1,0:T(8,128)(2,1)} %rest_0_.1), channel_id=1, source_target_pairs={{0,4},{1,5},{4,8},{5,9},{8,12},{9,13},{12,14},{13,15},{14,10},{15,... | collective-permute-start | bytes 1376264 | tf_op jit(solution)/shard_map/ppermute | solution.py:170
  3.1 12.5 %collective-permute-start.4 = (bf16[2,128,896]{2,1,0:T(8,128)(2,1)}, bf16[2,128,896]{2,1,0:T(8,128)(2,1)S(1)}, u32[]{:S(2)}, u32[]{:S(2)}) collective-permute-start(bf16[2,128,896]{2,1,0:T(8,128)(2,1)} %rest_0_.1), channel_id=1, source_target_pairs={{0,2},{1,3},{4,0},{5,1},{8,4},{9,5},{12,8},{13,9},{14,12},{15,13},... | collective-permute-start | bytes 1376264 | tf_op jit(solution)/shard_map/ppermute | solution.py:170
  13.8 31.7 %copy-start.4 = (bf16[2,128,896]{2,1,0:T(8,128)(2,1)}, bf16[2,128,896]{2,1,0:T(8,128)(2,1)S(1)}, u32[]{:S(2)}) copy-start(bf16[2,128,896]{2,1,0:T(8,128)(2,1)S(1)} %collective-permute-done.1.rest_1_) | copy-start | bytes 1376260
  13.8 11.7 %collective-permute-start.2 = (bf16[2,128,896]{2,1,0:T(8,128)(2,1)S(1)}, bf16[2,128,896]{2,1,0:T(8,128)(2,1)S(1)}, u32[]{:S(2)}, u32[]{:S(2)}) collective-permute-start(bf16[2,128,896]{2,1,0:T(8,128)(2,1)S(1)} %collective-permute-done.1.rest_1_), channel_id=1, source_target_pairs={{0,4},{1,5},{4,8},{5,9},{8,12},{9,13},{12,14},{13,15},{14,10},{15,... | collective-permute-start | bytes 1376264 | tf_op jit(solution)/shard_map/ppermute | solution.py:170
  15.6 29.9 %copy-start.5 = (bf16[2,128,896]{2,1,0:T(8,128)(2,1)}, bf16[2,128,896]{2,1,0:T(8,128)(2,1)S(1)}, u32[]{:S(2)}) copy-start(bf16[2,128,896]{2,1,0:T(8,128)(2,1)S(1)} %collective-permute-done.4.rest_4_) | copy-start | bytes 1376260
  15.6 12.9 %collective-permute-start.5 = (bf16[2,128,896]{2,1,0:T(8,128)(2,1)S(1)}, bf16[2,128,896]{2,1,0:T(8,128)(2,1)S(1)}, u32[]{:S(2)}, u32[]{:S(2)}) collective-permute-start(bf16[2,128,896]{2,1,0:T(8,128)(2,1)S(1)} %collective-permute-done.4.rest_4_), channel_id=1, source_target_pairs={{0,2},{1,3},{4,0},{5,1},{8,4},{9,5},{12,8},{13,9},{14,12},{15,13},... | collective-permute-start | bytes 1376264 | tf_op jit(solution)/shard_map/ppermute | solution.py:170
  15.8 31.6 %collective-permute-start.9 = (bf16[2,128,896]{2,1,0:T(8,128)(2,1)}, bf16[2,128,896]{2,1,0:T(8,128)(2,1)S(1)}, u32[]{:S(2)}, u32[]{:S(2)}) collective-permute-start(bf16[2,128,896]{2,1,0:T(8,128)(2,1)} %rest_0_.1), channel_id=1, source_target_pairs={{0,1},{1,0},{2,3},{3,2},{4,5},{5,4},{6,7},{7,6},{8,9},{9,8},{10,11... | collective-permute-start | bytes 1376264 | tf_op jit(solution)/shard_map/ppermute | solution.py:181
  16.6 13.7 %collective-permute-start = (s32[2,1,2]{1,2,0:T(2,128)S(1)}, s32[2,1,2]{1,2,0:T(2,128)S(1)}, u32[]{:S(2)}, u32[]{:S(2)}) collective-permute-start(s32[2,1,2]{1,2,0:T(2,128)S(1)} %pad_add_fusion), channel_id=1, source_target_pairs={{0,1},{1,2},{2,3},{3,4},{4,5},{5,6},{6,7},{7,8},{8,9},{9,10},{10,1... | collective-permute-start | bytes 56 | tf_op jit(solution)/shard_map/ppermute | solution.py:210
  25.5 21.9 %copy-start.6 = (bf16[2,128,896]{2,1,0:T(8,128)(2,1)}, bf16[2,128,896]{2,1,0:T(8,128)(2,1)S(1)}, u32[]{:S(2)}) copy-start(bf16[2,128,896]{2,1,0:T(8,128)(2,1)S(1)} %collective-permute-done.2.rest_2_) | copy-start | bytes 1376260
  25.5 10.8 %collective-permute-start.3 = (bf16[2,128,896]{2,1,0:T(8,128)(2,1)S(1)}, bf16[2,128,896]{2,1,0:T(8,128)(2,1)S(1)}, u32[]{:S(2)}, u32[]{:S(2)}) collective-permute-start(bf16[2,128,896]{2,1,0:T(8,128)(2,1)S(1)} %collective-permute-done.2.rest_2_), channel_id=1, source_target_pairs={{0,4},{1,5},{4,8},{5,9},{8,12},{9,13},{12,14},{13,15},{14,10},{15,... | collective-permute-start | bytes 1376264 | tf_op jit(solution)/shard_map/ppermute | solution.py:170
  28.4 28.9 %copy-start.7 = (bf16[2,128,896]{2,1,0:T(8,128)(2,1)}, bf16[2,128,896]{2,1,0:T(8,128)(2,1)S(1)}, u32[]{:S(2)}) copy-start(bf16[2,128,896]{2,1,0:T(8,128)(2,1)S(1)} %collective-permute-done.5.rest_5_) | copy-start | bytes 1376260
  28.5 17.0 %collective-permute-start.6 = (bf16[2,128,896]{2,1,0:T(8,128)(2,1)S(1)}, bf16[2,128,896]{2,1,0:T(8,128)(2,1)S(1)}, u32[]{:S(2)}, u32[]{:S(2)}) collective-permute-start(bf16[2,128,896]{2,1,0:T(8,128)(2,1)S(1)} %collective-permute-done.5.rest_5_), channel_id=1, source_target_pairs={{0,2},{1,3},{4,0},{5,1},{8,4},{9,5},{12,8},{13,9},{14,12},{15,13},... | collective-permute-start | bytes 1376264 | tf_op jit(solution)/shard_map/ppermute | solution.py:170
  30.3 18.3 %collective-permute-start.10 = (bf16[2,128,896]{2,1,0:T(8,128)(2,1)S(1)}, bf16[2,128,896]{2,1,0:T(8,128)(2,1)}, u32[]{:S(2)}, u32[]{:S(2)}) collective-permute-start(bf16[2,128,896]{2,1,0:T(8,128)(2,1)S(1)} %collective-permute-done.1.rest_1_), channel_id=1, source_target_pairs={{0,1},{1,0},{2,3},{3,2},{4,5},{5,4},{6,7},{7,6},{8,9},{9,8},{10,11... | collective-permute-start | bytes 1376264 | tf_op jit(solution)/shard_map/ppermute | solution.py:181
  30.3 18.3 %collective-permute-start.13 = (bf16[2,128,896]{2,1,0:T(8,128)(2,1)S(1)}, bf16[2,128,896]{2,1,0:T(8,128)(2,1)}, u32[]{:S(2)}, u32[]{:S(2)}) collective-permute-start(bf16[2,128,896]{2,1,0:T(8,128)(2,1)S(1)} %collective-permute-done.4.rest_4_), channel_id=1, source_target_pairs={{0,1},{1,0},{2,3},{3,2},{4,5},{5,4},{6,7},{7,6},{8,9},{9,8},{10,11... | collective-permute-start | bytes 1376264 | tf_op jit(solution)/shard_map/ppermute | solution.py:181
  36.3 21.1 %copy-start.2 = (bf16[2,128,896]{2,1,0:T(8,128)(2,1)}, bf16[2,128,896]{2,1,0:T(8,128)(2,1)S(1)}, u32[]{:S(2)}) copy-start(bf16[2,128,896]{2,1,0:T(8,128)(2,1)S(1)} %collective-permute-done.3.rest_3_) | copy-start | bytes 1376260
  36.3 12.9 %collective-permute-start.11 = (bf16[2,128,896]{2,1,0:T(8,128)(2,1)S(1)}, bf16[2,128,896]{2,1,0:T(8,128)(2,1)}, u32[]{:S(2)}, u32[]{:S(2)}) collective-permute-start(bf16[2,128,896]{2,1,0:T(8,128)(2,1)S(1)} %collective-permute-done.2.rest_2_), channel_id=1, source_target_pairs={{0,1},{1,0},{2,3},{3,2},{4,5},{5,4},{6,7},{7,6},{8,9},{9,8},{10,11... | collective-permute-start | bytes 1376264 | tf_op jit(solution)/shard_map/ppermute | solution.py:181
  36.3 2.2 %copy-start = (bf16[896,2048]{1,0:T(8,128)(2,1)S(1)}, bf16[896,2048]{1,0:T(8,128)(2,1)}, u32[]{:S(2)}) copy-start(bf16[896,2048]{1,0:T(8,128)(2,1)} %key_ref.1) | copy-start | bytes 11010052
  43.5 0.6 copy-start.1
  45.5 11.9 %copy-start.3 = (bf16[2,128,896]{2,1,0:T(8,128)(2,1)}, bf16[2,128,896]{2,1,0:T(8,128)(2,1)S(1)}, u32[]{:S(2)}) copy-start(bf16[2,128,896]{2,1,0:T(8,128)(2,1)S(1)} %collective-permute-done.6.rest_6_) | copy-start | bytes 1376260
  45.5 8.1 %collective-permute-start.7 = (bf16[1,128,896]{2,1,0:T(8,128)(2,1)}, bf16[1,128,896]{2,1,0:T(8,128)(2,1)S(1)}, u32[]{:S(2)}, u32[]{:S(2)}) collective-permute-start(bf16[1,128,896]{2,1,0:T(8,128)(2,1)} %slice.20), channel_id=1, source_target_pairs={{0,4},{1,5},{4,8},{5,9},{8,12},{9,13},{12,14},{13,15},{14,10},{15,... | collective-permute-start | bytes 688136 | tf_op jit(solution)/shard_map/ppermute | solution.py:170
  47.4 10.0 %copy-start.8 = (bf16[2,128,896]{2,1,0:T(8,128)(2,1)}, bf16[2,128,896]{2,1,0:T(8,128)(2,1)S(1)}, u32[]{:S(2)}) copy-start(bf16[2,128,896]{2,1,0:T(8,128)(2,1)S(1)} %collective-permute-done.9.rest_9_) | copy-start | bytes 1376260
  47.4 8.1 %collective-permute-start.8 = (bf16[1,128,896]{2,1,0:T(8,128)(2,1)}, bf16[1,128,896]{2,1,0:T(8,128)(2,1)}, u32[]{:S(2)}, u32[]{:S(2)}) collective-permute-start(bf16[1,128,896]{2,1,0:T(8,128)(2,1)} %slice.21), channel_id=1, source_target_pairs={{0,2},{1,3},{4,0},{5,1},{8,4},{9,5},{12,8},{13,9},{14,12},{15,13},... | collective-permute-start | bytes 688136 | tf_op jit(solution)/shard_map/ppermute | solution.py:170
  48.6 8.4 %collective-permute-start.14 = (bf16[2,128,896]{2,1,0:T(8,128)(2,1)S(1)}, bf16[2,128,896]{2,1,0:T(8,128)(2,1)S(1)}, u32[]{:S(2)}, u32[]{:S(2)}) collective-permute-start(bf16[2,128,896]{2,1,0:T(8,128)(2,1)S(1)} %collective-permute-done.5.rest_5_), channel_id=1, source_target_pairs={{0,1},{1,0},{2,3},{3,2},{4,5},{5,4},{6,7},{7,6},{8,9},{9,8},{10,11... | collective-permute-start | bytes 1376264 | tf_op jit(solution)/shard_map/ppermute | solution.py:181
  48.6 8.7 %collective-permute-start.12 = (bf16[2,128,896]{2,1,0:T(8,128)(2,1)S(1)}, bf16[2,128,896]{2,1,0:T(8,128)(2,1)S(1)}, u32[]{:S(2)}, u32[]{:S(2)}) collective-permute-start(bf16[2,128,896]{2,1,0:T(8,128)(2,1)S(1)} %collective-permute-done.3.rest_3_), channel_id=1, source_target_pairs={{0,1},{1,0},{2,3},{3,2},{4,5},{5,4},{6,7},{7,6},{8,9},{9,8},{10,11... | collective-permute-start | bytes 1376264 | tf_op jit(solution)/shard_map/ppermute | solution.py:181
  49.1 8.2 %collective-permute-start.15 = (bf16[2,128,896]{2,1,0:T(8,128)(2,1)S(1)}, bf16[2,128,896]{2,1,0:T(8,128)(2,1)S(1)}, u32[]{:S(2)}, u32[]{:S(2)}) collective-permute-start(bf16[2,128,896]{2,1,0:T(8,128)(2,1)S(1)} %collective-permute-done.6.rest_6_), channel_id=1, source_target_pairs={{0,1},{1,0},{2,3},{3,2},{4,5},{5,4},{6,7},{7,6},{8,9},{9,8},{10,11... | collective-permute-start | bytes 1376264 | tf_op jit(solution)/shard_map/ppermute | solution.py:181
  53.6 3.8 %copy-start.12 = (bf16[1,128,896]{2,1,0:T(8,128)(2,1)}, bf16[1,128,896]{2,1,0:T(8,128)(2,1)S(1)}, u32[]{:S(2)}) copy-start(bf16[1,128,896]{2,1,0:T(8,128)(2,1)S(1)} %collective-permute-done.7.rest_7_) | copy-start | bytes 688132
  53.6 3.4 %collective-permute-start.16 = (bf16[1,128,896]{2,1,0:T(8,128)(2,1)S(1)}, bf16[1,128,896]{2,1,0:T(8,128)(2,1)}, u32[]{:S(2)}, u32[]{:S(2)}) collective-permute-start(bf16[1,128,896]{2,1,0:T(8,128)(2,1)S(1)} %collective-permute-done.7.rest_7_), channel_id=1, source_target_pairs={{0,1},{1,0},{2,3},{3,2},{4,5},{5,4},{6,7},{7,6},{8,9},{9,8},{10,11... | collective-permute-start | bytes 688136 | tf_op jit(solution)/shard_map/ppermute | solution.py:181
  55.5 1.8 %collective-permute-start.17 = (bf16[1,128,896]{2,1,0:T(8,128)(2,1)}, bf16[1,128,896]{2,1,0:T(8,128)(2,1)}, u32[]{:S(2)}, u32[]{:S(2)}) collective-permute-start(bf16[1,128,896]{2,1,0:T(8,128)(2,1)} %collective-permute-done.8.rest_8_), channel_id=1, source_target_pairs={{0,1},{1,0},{2,3},{3,2},{4,5},{5,4},{6,7},{7,6},{8,9},{9,8},{10,11... | collective-permute-start | bytes 688136 | tf_op jit(solution)/shard_map/ppermute | solution.py:181
  57.0 0.8 %copy-start.9 = (bf16[2,128,896]{2,1,0:T(8,128)(2,1)}, bf16[2,128,896]{2,1,0:T(8,128)(2,1)S(1)}, u32[]{:S(2)}) copy-start(bf16[2,128,896]{2,1,0:T(8,128)(2,1)S(1)} %collective-permute-done.14.rest_14_) | copy-start | bytes 1376260
  57.4 0.8 %copy-start.10 = (bf16[2,128,896]{2,1,0:T(8,128)(2,1)}, bf16[2,128,896]{2,1,0:T(8,128)(2,1)S(1)}, u32[]{:S(2)}) copy-start(bf16[2,128,896]{2,1,0:T(8,128)(2,1)S(1)} %collective-permute-done.12.rest_12_) | copy-start | bytes 1376260
  57.4 0.9 %copy-start.11 = (bf16[2,128,896]{2,1,0:T(8,128)(2,1)}, bf16[2,128,896]{2,1,0:T(8,128)(2,1)S(1)}, u32[]{:S(2)}) copy-start(bf16[2,128,896]{2,1,0:T(8,128)(2,1)S(1)} %collective-permute-done.15.rest_15_) | copy-start | bytes 1376260

commit v4 on v1

v4 whole, which is shorter than its diff:
```python
import functools
import math

import jax
import jax.numpy as jnp
from jax import lax
from jax.experimental import pallas as pl
from jax.experimental.pallas import tpu as pltpu
from jax.sharding import PartitionSpec as P

SPAN = 64
HEADS = 16
HEAD_DIM = 128
EPS = 1e-6
SCALE = math.log2(math.e) / math.sqrt(HEAD_DIM)
CORES = 2
GROUP = 4
MIB = 2**20


SMEM_SPEC = pl.BlockSpec(memory_space=pltpu.SMEM)
VMEM_SPEC = pl.BlockSpec(memory_space=pltpu.VMEM)
ANY_SPEC = pl.BlockSpec(memory_space=pl.ANY)


def contract(left, right, dims):
    return lax.dot_general(left, right, (dims, ((), ())), preferred_element_type=jnp.float32)


def head_columns(head):
    return slice(head * HEAD_DIM, (head + 1) * HEAD_DIM)


def fold_kernel(query_ref, key_ref, folded_ref, single_ref):
    for head in range(HEADS):
        columns = head_columns(head)
        rows = contract(query_ref[:, columns], key_ref[:, columns], ((1,), (1,))) * SCALE
        single_ref[head : head + 1, :] = rows[:1]
        folded_ref[head] = rows.astype(jnp.bfloat16)


def fold(rows, w_key):
    count, width = rows.shape[0], w_key.shape[0]
    return pl.pallas_call(
        fold_kernel,
        out_shape=(
            jax.ShapeDtypeStruct((HEADS, count, width), jnp.bfloat16),
            jax.ShapeDtypeStruct((HEADS, width), jnp.float32),
        ),
        in_specs=[VMEM_SPEC] * 2,
        out_specs=(VMEM_SPEC,) * 2,
        compiler_params=pltpu.CompilerParams(vmem_limit_bytes=32 * MIB),
        cost_estimate=pl.CostEstimate(
            flops=2 * rows.size * width, bytes_accessed=16 * MIB, transcendentals=0
        ),
        name="fold_queries",
    )(rows, w_key)


def normalise(raw, tokens_ref, turned_ref):
    widened = raw.astype(jnp.float32)
    factor = lax.rsqrt(jnp.mean(widened * widened, axis=-1, keepdims=True) + EPS)
    scaled = widened * factor
    tokens_ref[...] = scaled.astype(jnp.bfloat16)
    turned_ref[...] = scaled.T.astype(jnp.bfloat16)


def collect_kernel(source_ref, block_ref, *rest):
    *stores, tokens_ref, turned_ref, raw, sems = rest
    requests = raw.shape[0]

    def fetch(request, store):
        return pltpu.make_async_copy(store.at[block_ref[request]], raw.at[request], sems.at[request])

    def begin(request, carry):
        for place, store in enumerate(stores):

            @pl.when(source_ref[request] == place)
            def _(store=store):
                fetch(request, store).start()

        return carry

    def finish(request, carry):
        @pl.when(source_ref[request] < len(stores))
        def _():
            fetch(request, stores[0]).wait()
            normalise(raw[request], tokens_ref.at[request], turned_ref.at[request])

        return carry

    lax.fori_loop(0, requests, begin, 0)
    lax.fori_loop(0, requests, finish, 0)


def collect(source, block, stores):
    requests = source.shape[0]
    length, width = stores[0].shape[1:]
    return pl.pallas_call(
        collect_kernel,
        out_shape=(
            jax.ShapeDtypeStruct((requests, length, width), jnp.bfloat16),
            jax.ShapeDtypeStruct((requests, width, length), jnp.bfloat16),
        ),
        in_specs=[SMEM_SPEC] * 2 + [ANY_SPEC] * len(stores),
        out_specs=(VMEM_SPEC,) * 2,
        scratch_shapes=[
            pltpu.VMEM((requests, length, width), jnp.bfloat16),
            pltpu.SemaphoreType.DMA((requests,)),
        ],
        compiler_params=pltpu.CompilerParams(vmem_limit_bytes=24 * MIB),
        cost_estimate=pl.CostEstimate(flops=4 * MIB, bytes_accessed=8 * MIB, transcendentals=0),
        name="collect_early",
    )(source, block, *stores)


def weigh(scores):
    powers = jnp.exp2(scores - jnp.max(scores, axis=-1, keepdims=True))
    totals = jnp.sum(powers, axis=-1, keepdims=True)
    return (powers * (1.0 / totals)).astype(jnp.bfloat16)


def attend_kernel(
    early, source_ref, block_ref, keep_ref, folded_ref, single_ref, tokens_in, turned_in, value_ref, *rest
):
    *late, out_ref, tokens, turned, raw, mixed, sems = rest
    requests, length, width = raw.shape
    windows = requests // 2
    blocks = windows - 1

    def fetch_early(request):
        return (
            pltpu.make_async_copy(tokens_in.at[request], tokens.at[request], sems.at[request, 0]),
            pltpu.make_async_copy(turned_in.at[request], turned.at[request], sems.at[request, 1]),
        )

    def fetch_late(request, store):
        return pltpu.make_async_copy(store.at[block_ref[request]], raw.at[request], sems.at[request, 0])

    order = [blocks] + list(range(blocks))
    for window in order:
        for request in (2 * window, 2 * window + 1):

            @pl.when(source_ref[request] < early)
            def _(request=request):
                for copy in fetch_early(request):
                    copy.start()

            for place, store in enumerate(late):

                @pl.when(source_ref[request] == early + place)
                def _(request=request, store=store):
                    fetch_late(request, store).start()

    lone = None
    for window in order:
        for request in (2 * window, 2 * window + 1):

            @pl.when(source_ref[request] < early)
            def _(request=request):
                for copy in fetch_early(request):
                    copy.wait()

            @pl.when(source_ref[request] >= early)
            def _(request=request):
                fetch_late(request, late[0]).wait()
                normalise(raw[request], tokens.at[request], turned.at[request])

        here = tokens[2 * window : 2 * window + 2].reshape(2 * length, width)
        across = jnp.concatenate([turned[2 * window], turned[2 * window + 1]], axis=1)
        if window == blocks:
            weights = weigh(contract(single_ref[...].astype(jnp.bfloat16), across, ((1,), (0,))))
            lone = contract(weights, here, ((1,), (0,)))
            continue
        rows = slice(window * SPAN, (window + 1) * SPAN)

        def score(group):
            taken = folded_ref[group * GROUP : (group + 1) * GROUP, rows].reshape(GROUP * SPAN, width)
            return contract(taken, across, ((1,), (0,)))

        groups = HEADS // GROUP
        scores = score(0)
        for group in range(groups):
            following = score(group + 1) if group + 1 < groups else None
            sums = contract(weigh(scores), here, ((1,), (0,))).reshape(GROUP, SPAN, width)
            heads = slice(group * GROUP, (group + 1) * GROUP)
            if window == 0:
                first = lax.broadcasted_iota(jnp.int32, sums.shape, 1) == 0
                sums = jnp.where(first, lone[heads][:, None, :], sums)
            mixed[heads, rows] = sums.astype(jnp.bfloat16)
            scores = following

    count = blocks * SPAN
    place = lax.broadcasted_iota(jnp.int32, (count, HEAD_DIM), 0)
    kept = place % SPAN == 0
    for block in range(blocks):
        kept = kept | ((place // SPAN == block) & (keep_ref[block] > 0))
    for head in range(HEADS):
        columns = head_columns(head)
        sums = contract(mixed[head], value_ref[:, columns], ((1,), (0,)))
        sums = jnp.where(kept, sums, 0.0)
        out_ref[:, columns] = pltpu.roll(sums, count - 1, 0).astype(jnp.bfloat16)


def attend(early, source, block, keep, folded, single, tokens, turned, w_value, late):
    requests, length, width = tokens.shape
    count = folded.shape[1]
    return pl.pallas_call(
        functools.partial(attend_kernel, early),
        out_shape=jax.ShapeDtypeStruct((count, w_value.shape[1]), jnp.bfloat16),
        in_specs=[SMEM_SPEC] * 3
        + [VMEM_SPEC] * 2
        + [ANY_SPEC] * 2
        + [VMEM_SPEC]
        + [ANY_SPEC] * len(late),
        out_specs=VMEM_SPEC,
        scratch_shapes=[
            pltpu.VMEM(tokens.shape, jnp.bfloat16),
            pltpu.VMEM(turned.shape, jnp.bfloat16),
            pltpu.VMEM(tokens.shape, jnp.bfloat16),
            pltpu.VMEM(folded.shape, jnp.bfloat16),
            pltpu.SemaphoreType.DMA((requests, 2)),
        ],
        compiler_params=pltpu.CompilerParams(vmem_limit_bytes=40 * MIB),
        cost_estimate=pl.CostEstimate(
            flops=2 * HEADS * count * width * (4 * length + HEAD_DIM),
            bytes_accessed=16 * MIB,
            transcendentals=HEADS * count * 2 * length,
        ),
        name="attend_windows",
    )(source, block, keep, folded, single, tokens, turned, w_value, *late)


def chip_ring(mesh):
    row = mesh.devices.reshape(-1, mesh.shape["seq"])[0]
    chips = list(range(len(row) // CORES))
    columns = [tuple(getattr(row[CORES * chip], "coords", (0, 0))[:2]) for chip in chips]
    if len(set(columns)) != 2:
        return chips
    up = [chip for chip in chips if columns[chip] == columns[0]]
    return up + [chip for chip in reversed(chips) if columns[chip] != columns[0]]


class Ring:
    def __init__(self, ring, slots):
        self.ring, self.slots = ring, slots
        self.size = len(ring)
        self.reach = (self.size - 1) // 2
        self.opposite = self.size % 2 == 0
        self.cut = slots // 2

    def turned(self, value, steps):
        size = self.size
        pairs = [
            (CORES * self.ring[i] + core, CORES * self.ring[(i + steps) % size] + core)
            for i in range(size)
            for core in range(CORES)
        ]
        return lax.ppermute(value, "seq", pairs)

    def swapped(self, value):
        return lax.ppermute(value, "seq", [(i, i ^ 1) for i in range(CORES * self.size)])

    def gather(self, stored, beside):
        slots = range(self.slots)
        waves = {1: [stored[slot : slot + 1] for slot in slots], -1: [stored[slot : slot + 1] for slot in slots]}
        early, late = [stored, self.swapped(stored)], []
        for step in range(self.reach):
            arrived = []
            for slot in slots:
                for way in (1, -1):
                    waves[way][slot] = self.turned(waves[way][slot], way)
                    arrived.append(waves[way][slot])
            if step == 0 and self.reach > 1:
                *arrived, beside = lax.optimization_barrier((*arrived, beside))
                for i, slot in enumerate(slots):
                    waves[1][slot], waves[-1][slot] = arrived[2 * i], arrived[2 * i + 1]
            early += arrived + [self.swapped(value) for value in arrived]
        if self.opposite:
            last = [self.turned(waves[1 if slot < self.cut else -1][slot], 1 if slot < self.cut else -1) for slot in slots]
            late = last + [self.swapped(value) for value in last]
        return early, late, beside

    def locate(self, owner, slot, here):
        order = jnp.asarray([self.ring.index(chip) for chip in range(self.size)], jnp.int32)

        def place_of(device):
            chips = jnp.arange(self.size)
            return jnp.sum(jnp.where((device // CORES)[..., None] == chips, order, 0), axis=-1)

        away = (place_of(here) - place_of(owner)) % self.size
        other = (owner % CORES != here % CORES).astype(jnp.int32)
        per_step = 2 * self.slots
        back = away > self.reach
        step = jnp.where(back, self.size - away, away)
        source = 2 + (step - 1) * 2 * per_step + other * per_step + 2 * slot + back
        if self.opposite:
            last = 2 + self.reach * 2 * per_step + other * self.slots + slot
            source = jnp.where(away == self.size // 2, last, source)
        return jnp.where(away == 0, other, source), jnp.where(away == 0, slot, 0)


def body(ring, queries, neighbours, w_key, w_value, retrieval_owner, retrieval_slot, doc_starts):
    devices = lax.axis_size("seq")
    here = lax.axis_index("seq")
    plan = Ring(ring, neighbours.shape[0])
    owner_slot = jnp.stack([retrieval_owner, retrieval_slot])
    before = lax.ppermute(owner_slot[:, -1:], "seq", [(i, i + 1) for i in range(devices - 1)])
    owner, slot = jnp.concatenate([before, owner_slot], 1).reshape(2, -1)
    source, block = plan.locate(owner, slot, here)
    blocks = doc_starts.shape[0]
    opening = (here == 0) & (jnp.arange(blocks) == 0)
    keep = ((doc_starts == 0) & jnp.logical_not(opening)).astype(jnp.int32)
    rows = jnp.concatenate([queries[-1:], queries[:-1]], 0)
    early, late, (folded, single, source, block, keep) = plan.gather(
        neighbours, (*fold(rows, w_key), source, block, keep)
    )
    tokens, turned = collect(source, block, early)
    return attend(len(early), source, block, keep, folded, single, tokens, turned, w_value, late)


def solution(mesh):
    return jax.shard_map(
        functools.partial(body, chip_ring(mesh)),
        mesh=mesh,
        in_specs=(
            P(("groups", "seq"), None),
            P(("groups", "seq"), None, None),
            P(),
            P(),
            P(("groups", "seq"), None),
            P(("groups", "seq"), None),
            P(("groups", "seq")),
        ),
        out_specs=P(("groups", "seq"), None),
        check_vma=False,
    )
```

time: 106 us -> 84.9 us (0.80)
  waiting for transfers between devices: 59.6 us -> 21.3 us
  starting transfers between devices: 2.35 us -> 20.8 us
  between operations: 13.5 us -> 0.39 us
  Pallas kernels: 23.4 us -> 31 us
  local copies, waits for them, and re-layouts: 4.16 us -> 7.18 us
    all_gather x1 -> x0, waiting for transfers between devices: 58.9 us -> none  [body(): store = lax.all_gather(neighbours, 'seq', axis=0, tiled=True)]
    ppermute x1 -> x30, waiting for transfers between devices: 0.01 us -> 21.3 us  [the longest x14 21.3 us: turned(): return lax.ppermute(value, 'seq', pairs)]
    ppermute x1 -> x30, starting transfers between devices: 2.34 us -> 20.8 us  [the longest x14 15.3 us: turned(): return lax.ppermute(value, 'seq', pairs)]
    pallas_call x2 -> x3, Pallas kernels: 23.4 us -> 31 us  [the longest x1 20.7 us: attend(): pl.pallas_call(functools.partial(attend_kernel, early), out_shape=jax.Sha...]
    unnamed x6 -> x16, local copies, waits for them, and re-layouts: 2.65 us -> 4.96 us
  transfers between devices with their start and end apart: 2 -> 30, of which waited for: 1 -> 8; matrix products, arithmetic and copies ran while one was open for 4% -> 6% of each run, Pallas kernels for 5% -> 12%
where the time goes in v4:
time: 84.9 us; the launch traced here: 84.5 us
  Pallas kernels  31 us (37%)
  waiting for transfers between devices  21.3 us (25%)
  starting transfers between devices  20.8 us (24%)
  local copies, waits for them, and re-layouts  7.18 us (8%)
  other arithmetic  3.74 us (4%)
    ppermute x14, waiting for transfers between devices, turned(): return lax.ppermute(value, 'seq', pairs)  21.3 us
    pallas_call x1, Pallas kernels, attend(): pl.pallas_call(functools.partial(attend_kernel, early), out_shape=jax.Sha...  20.7 us
    ppermute x14, starting transfers between devices, turned(): return lax.ppermute(value, 'seq', pairs)  15.3 us
    pallas_call x1, Pallas kernels, collect(): pl.pallas_call(collect_kernel, out_shape=(jax.ShapeDtypeStruct((requests,...  8.26 us
    unnamed x16, local copies, waits for them, and re-layouts  4.96 us
    ppermute x15, starting transfers between devices, swapped(): lax.ppermute(value, 'seq', [(i, i ^ 1) for i in range(CORES * self.size)])  4.25 us
    pallas_call x1, Pallas kernels, fold(): pl.pallas_call(fold_kernel, out_shape=(jax.ShapeDtypeStruct((HEADS, count...  2.08 us
  transfers between devices with their start and end apart: 30, of which 8 were waited for; matrix products, arithmetic and copies ran while one was open for 6% of the time, Pallas kernels for 12%

profile of v4, /device:TPU:0, one launch (start us, length us, event | category | flops | bytes accessed | tf_op | source)
XLA Modules:
  0.0 84.5 jit_solution(15208800340219790697)
XLA Ops:
  0.0 1.1 %fusion.9 = (bf16[1,128,896]{2,1,0:T(8,128)(2,1)S(1)}, bf16[1,128,896]{2,1,0:T(8,128)(2,1)S(1)}) fusion(bf16[2,128,896]{2,1,0:T(8,128)(2,1)} %rest_0_.1), kind=kLoop, calls=%fused_computation.29 | loop fusion | bytes 917504 | tf_op jit(solution)/shard_map/slice | solution.py:266
  1.1 3.1 %collective-permute-start = (bf16[1,128,896]{2,1,0:T(8,128)(2,1)S(1)}, bf16[1,128,896]{2,1,0:T(8,128)(2,1)S(1)}, u32[]{:S(2)}, u32[]{:S(2)}) collective-permute-start(bf16[1,128,896]{2,1,0:T(8,128)(2,1)S(1)} %get-tuple-element.34), channel_id=1, source_target_pairs={{0,4},{1,5},{4,8},{5,9},{8,12},{9,13},{12,14},{13,15},{14,10},{15,... | collective-permute-start | bytes 688136 | tf_op jit(solution)/shard_map/ppermute | solution.py:259
  4.2 0.0 collective-permute-start.1
  4.2 2.0 %collective-permute-start.2 = (bf16[1,128,896]{2,1,0:T(8,128)(2,1)S(1)}, bf16[1,128,896]{2,1,0:T(8,128)(2,1)S(1)}, u32[]{:S(2)}, u32[]{:S(2)}) collective-permute-start(bf16[1,128,896]{2,1,0:T(8,128)(2,1)S(1)} %get-tuple-element.33), channel_id=1, source_target_pairs={{0,4},{1,5},{4,8},{5,9},{8,12},{9,13},{12,14},{13,15},{14,10},{15,... | collective-permute-start | bytes 688136 | tf_op jit(solution)/shard_map/ppermute | solution.py:259
  6.2 0.0 collective-permute-start.3
  6.2 0.8 pad_add_fusion
  7.0 1.3 %collective-permute-start.4 = (s32[2,1,2]{1,2,0:T(2,128)S(1)}, s32[2,1,2]{1,2,0:T(2,128)S(1)}, u32[]{:S(2)}, u32[]{:S(2)}) collective-permute-start(s32[2,1,2]{1,2,0:T(2,128)S(1)} %pad_add_fusion), channel_id=1, source_target_pairs={{0,1},{1,2},{2,3},{3,4},{4,5},{5,6},{6,7},{7,8},{8,9},{9,10},{10,1... | collective-permute-start | bytes 56 | tf_op jit(solution)/shard_map/ppermute | solution.py:308
  8.3 0.8 slice.21
  9.1 1.5 %pad_maximum_fusion.query_ref = bf16[256,2048]{1,0:T(8,128)(2,1)S(1)} fusion(bf16[255,2048]{1,0:T(8,128)(2,1)} %bitcast.3, bf16[1,2048]{1,0:T(2,128)(2,1)S(1)} %slice.21), kind=kLoop, calls=%fused_computation | loop fusion | flops 2097152 | bytes 2097152 | tf_op jit(solution)/shard_map/concatenate | solution.py:314
  10.6 2.0 %copy-done.1 = bf16[896,2048]{1,0:T(8,128)(2,1)S(1)} copy-done((bf16[896,2048]{1,0:T(8,128)(2,1)S(1)}, bf16[896,2048]{1,0:T(8,128)(2,1)}, u32[]{:S(2)}) %copy-start.1) | copy-done | bytes 3670040
  12.6 0.0 copy-start.5
  12.6 2.1 %fold_queries.1 = (bf16[16,256,896]{2,1,0:T(8,128)(2,1)S(1)}, f32[16,896]{1,0:T(8,128)S(1)}) custom-call(bf16[256,2048]{1,0:T(8,128)(2,1)S(1)} %pad_maximum_fusion.query_ref, bf16[896,2048]{1,0:T(8,128)(2,1)S(1)} %copy-done.1), custom_call_target="tpu_custom_call" | custom-call | flops 939524096 | bytes 16777216 | tf_op jit(solution)/shard_map/fold_queries/pallas_call | solution.py:44
  14.7 2.9 %copy-done = bf16[16,256,896]{2,1,0:T(8,128)(2,1)} copy-done((bf16[16,256,896]{2,1,0:T(8,128)(2,1)}, bf16[16,256,896]{2,1,0:T(8,128)(2,1)S(1)}, u32[]{:S(2)}) %copy-start) | copy-done | bytes 7340056
  17.6 0.6 fusion
  18.3 2.8 %collective-permute-start.5 = (bf16[2,128,896]{2,1,0:T(8,128)(2,1)S(1)}, bf16[2,128,896]{2,1,0:T(8,128)(2,1)S(1)}, u32[]{:S(2)}, u32[]{:S(2)}) collective-permute-start(bf16[2,128,896]{2,1,0:T(8,128)(2,1)S(1)} %copy-done.3), channel_id=1, source_target_pairs={{0,1},{1,0},{2,3},{3,2},{4,5},{5,4},{6,7},{7,6},{8,9},{9,8},{10,11... | collective-permute-start | bytes 1376264 | tf_op jit(solution)/shard_map/ppermute | solution.py:262
  21.1 0.1 add_add_fusion
  21.1 0.1 copy.14
  21.2 0.1 unstack.15
  21.3 0.1 copy.13
  21.4 0.1 unstack.13
  21.5 0.1 select_reduce_fusion
  21.6 0.7 compare_select_fusion.8
  22.3 0.1 collective-permute-start.6
  22.4 0.5 collective-permute-start.7
  22.9 0.1 collective-permute-start.8
  23.0 1.6 %collective-permute-start.10 = (bf16[1,128,896]{2,1,0:T(8,128)(2,1)S(1)}, bf16[1,128,896]{2,1,0:T(8,128)(2,1)S(1)}, u32[]{:S(2)}, u32[]{:S(2)}) collective-permute-start(bf16[1,128,896]{2,1,0:T(8,128)(2,1)S(1)} %collective-permute-done.rest_2_), channel_id=1, source_target_pairs={{0,4},{1,5},{4,8},{5,9},{8,12},{9,13},{12,14},{13,15},{14,10},{15,... | collective-permute-start | bytes 688136 | tf_op jit(solution)/shard_map/ppermute | solution.py:259
  24.6 0.5 collective-permute-start.11
  25.0 1.6 %collective-permute-start.12 = (bf16[1,128,896]{2,1,0:T(8,128)(2,1)S(1)}, bf16[1,128,896]{2,1,0:T(8,128)(2,1)S(1)}, u32[]{:S(2)}, u32[]{:S(2)}) collective-permute-start(bf16[1,128,896]{2,1,0:T(8,128)(2,1)S(1)} %collective-permute-done.2.rest_4_), channel_id=1, source_target_pairs={{0,4},{1,5},{4,8},{5,9},{8,12},{9,13},{12,14},{13,15},{14,10},{15,... | collective-permute-start | bytes 688136 | tf_op jit(solution)/shard_map/ppermute | solution.py:259
  26.6 0.5 collective-permute-start.13
  27.1 4.3 %collective-permute-done.10.rest_10_ = bf16[1,128,896]{2,1,0:T(8,128)(2,1)S(1)} collective-permute-done((bf16[1,128,896]{2,1,0:T(8,128)(2,1)S(1)}, bf16[1,128,896]{2,1,0:T(8,128)(2,1)S(1)}, u32[]{:S(2)}, u32[]{:S(2)}) %collective-permute-start.10) | collective-permute-done | bytes 229408 | tf_op jit(solution)/shard_map/ppermute | solution.py:259
  31.4 1.6 %collective-permute-done.11.rest_11_ = bf16[1,128,896]{2,1,0:T(8,128)(2,1)S(1)} collective-permute-done((bf16[1,128,896]{2,1,0:T(8,128)(2,1)S(1)}, bf16[1,128,896]{2,1,0:T(8,128)(2,1)S(1)}, u32[]{:S(2)}, u32[]{:S(2)}) %collective-permute-start.11) | collective-permute-done | bytes 229408 | tf_op jit(solution)/shard_map/ppermute | solution.py:259
  33.0 2.8 %collective-permute-done.12.rest_12_ = bf16[1,128,896]{2,1,0:T(8,128)(2,1)S(1)} collective-permute-done((bf16[1,128,896]{2,1,0:T(8,128)(2,1)S(1)}, bf16[1,128,896]{2,1,0:T(8,128)(2,1)S(1)}, u32[]{:S(2)}, u32[]{:S(2)}) %collective-permute-start.12) | collective-permute-done | bytes 229408 | tf_op jit(solution)/shard_map/ppermute | solution.py:259
  35.9 1.6 %collective-permute-start.18 = (bf16[1,128,896]{2,1,0:T(8,128)(2,1)S(1)}, bf16[1,128,896]{2,1,0:T(8,128)(2,1)S(1)}, u32[]{:S(2)}, u32[]{:S(2)}) collective-permute-start(bf16[1,128,896]{2,1,0:T(8,128)(2,1)S(1)} %collective-permute-done.10.rest_10_), channel_id=1, source_target_pairs={{0,4},{1,5},{4,8},{5,9},{8,12},{9,13},{12,14},{13,15},{14,10},{15,... | collective-permute-start | bytes 688136 | tf_op jit(solution)/shard_map/ppermute | solution.py:259
  37.4 0.2 collective-permute-start.17
  37.7 0.5 collective-permute-start.21
  38.1 1.5 %collective-permute-start.19 = (bf16[1,128,896]{2,1,0:T(8,128)(2,1)S(1)}, bf16[1,128,896]{2,1,0:T(8,128)(2,1)S(1)}, u32[]{:S(2)}, u32[]{:S(2)}) collective-permute-start(bf16[1,128,896]{2,1,0:T(8,128)(2,1)S(1)} %collective-permute-done.11.rest_11_), channel_id=1, source_target_pairs={{0,2},{1,3},{4,0},{5,1},{8,4},{9,5},{12,8},{13,9},{14,12},{15,13},... | collective-permute-start | bytes 688136 | tf_op jit(solution)/shard_map/ppermute | solution.py:259
  39.6 0.5 collective-permute-start.20
  40.2 4.1 %collective-permute-done.18.rest_18_ = bf16[1,128,896]{2,1,0:T(8,128)(2,1)S(1)} collective-permute-done((bf16[1,128,896]{2,1,0:T(8,128)(2,1)S(1)}, bf16[1,128,896]{2,1,0:T(8,128)(2,1)S(1)}, u32[]{:S(2)}, u32[]{:S(2)}) %collective-permute-start.18) | collective-permute-done | bytes 229408 | tf_op jit(solution)/shard_map/ppermute | solution.py:259
  44.3 1.6 %collective-permute-start.26 = (bf16[1,128,896]{2,1,0:T(8,128)(2,1)S(1)}, bf16[1,128,896]{2,1,0:T(8,128)(2,1)S(1)}, u32[]{:S(2)}, u32[]{:S(2)}) collective-permute-start(bf16[1,128,896]{2,1,0:T(8,128)(2,1)S(1)} %collective-permute-done.18.rest_18_), channel_id=1, source_target_pairs={{0,4},{1,5},{4,8},{5,9},{8,12},{9,13},{12,14},{13,15},{14,10},{15,... | collective-permute-start | bytes 688136 | tf_op jit(solution)/shard_map/ppermute | solution.py:259
  45.8 0.3 collective-permute-done.21.rest_21_
  46.1 0.4 collective-permute-start.27
  46.6 4.5 %collective-permute-done.19.rest_19_ = bf16[1,128,896]{2,1,0:T(8,128)(2,1)S(1)} collective-permute-done((bf16[1,128,896]{2,1,0:T(8,128)(2,1)S(1)}, bf16[1,128,896]{2,1,0:T(8,128)(2,1)S(1)}, u32[]{:S(2)}, u32[]{:S(2)}) %collective-permute-start.19) | collective-permute-done | bytes 229408 | tf_op jit(solution)/shard_map/ppermute | solution.py:259
  51.0 0.5 collective-permute-start.24
  51.5 0.1 collective-permute-start.25
  51.6 2.1 %collective-permute-done.26.rest_0_ = bf16[1,128,896]{2,1,0:T(8,128)(2,1)S(1)} collective-permute-done((bf16[1,128,896]{2,1,0:T(8,128)(2,1)S(1)}, bf16[1,128,896]{2,1,0:T(8,128)(2,1)S(1)}, u32[]{:S(2)}, u32[]{:S(2)}) %collective-permute-start.26) | collective-permute-done | bytes 229408 | tf_op jit(solution)/shard_map/ppermute | solution.py:259
  53.7 1.6 %collective-permute-done.27.rest_1_ = bf16[1,128,896]{2,1,0:T(8,128)(2,1)S(1)} collective-permute-done((bf16[1,128,896]{2,1,0:T(8,128)(2,1)S(1)}, bf16[1,128,896]{2,1,0:T(8,128)(2,1)S(1)}, u32[]{:S(2)}, u32[]{:S(2)}) %collective-permute-start.27) | collective-permute-done | bytes 229408 | tf_op jit(solution)/shard_map/ppermute | solution.py:259
  55.3 8.3 %collect_early.1 = (bf16[10,128,896]{2,1,0:T(8,128)(2,1)S(1)}, bf16[10,896,128]{2,1,0:T(8,128)(2,1)S(1)}) custom-call(s32[10]{0:T(128)S(1)} %compare_select_fusion.9.source_ref, s32[10]{0:T(128)S(1)} %get-tuple-element.21.block_ref, bf16[2,128,896]{2,1,0:T(8,128)(2,1)S(1)} %copy-done.3, bf16[2,128,896]{2,1,0:T(8,128)(2,1)S(1)} %collective-permute-done.5.rest_1_, ...), custom_call_target="tpu_custom_call" | custom-call | flops 4194304 | bytes 8388608 | tf_op jit(solution)/shard_map/collect_early/pallas_call | solution.py:99
  63.6 20.7 %attend_windows.1 = bf16[256,2048]{1,0:T(8,128)(2,1)} custom-call(s32[10]{0:T(128)S(1)} %compare_select_fusion.9.source_ref, s32[10]{0:T(128)S(1)} %get-tuple-element.21.block_ref, s32[4]{0:T(128)S(1)} %and_convert_fusion.keep_ref, bf16[16,256,896]{2,1,0:T(8,128)(2,1)} %copy-done, f32[16,896]{1,0:T(8,128)S(1)} %get-tuple-element.24.single_ref, ...), custom_call_target="tpu_custom_call" | custom-call | flops 4697620480 | bytes 16777216 | tf_op jit(solution)/shard_map/attend_windows/pallas_call | solution.py:208
  (47 shorter events, 0.1 us)
Async XLA Ops:
  1.1 21.2 %collective-permute-start = (bf16[1,128,896]{2,1,0:T(8,128)(2,1)S(1)}, bf16[1,128,896]{2,1,0:T(8,128)(2,1)S(1)}, u32[]{:S(2)}, u32[]{:S(2)}) collective-permute-start(bf16[1,128,896]{2,1,0:T(8,128)(2,1)S(1)} %get-tuple-element.34), channel_id=1, source_target_pairs={{0,4},{1,5},{4,8},{5,9},{8,12},{9,13},{12,14},{13,15},{14,10},{15,... | collective-permute-start | bytes 688136 | tf_op jit(solution)/shard_map/ppermute | solution.py:259
  4.2 18.1 %collective-permute-start.1 = (bf16[1,128,896]{2,1,0:T(8,128)(2,1)S(1)}, bf16[1,128,896]{2,1,0:T(8,128)(2,1)S(1)}, u32[]{:S(2)}, u32[]{:S(2)}) collective-permute-start(bf16[1,128,896]{2,1,0:T(8,128)(2,1)S(1)} %get-tuple-element.34), channel_id=1, source_target_pairs={{0,2},{1,3},{4,0},{5,1},{8,4},{9,5},{12,8},{13,9},{14,12},{15,13},... | collective-permute-start | bytes 688136 | tf_op jit(solution)/shard_map/ppermute | solution.py:259
  4.2 18.1 %collective-permute-start.2 = (bf16[1,128,896]{2,1,0:T(8,128)(2,1)S(1)}, bf16[1,128,896]{2,1,0:T(8,128)(2,1)S(1)}, u32[]{:S(2)}, u32[]{:S(2)}) collective-permute-start(bf16[1,128,896]{2,1,0:T(8,128)(2,1)S(1)} %get-tuple-element.33), channel_id=1, source_target_pairs={{0,4},{1,5},{4,8},{5,9},{8,12},{9,13},{12,14},{13,15},{14,10},{15,... | collective-permute-start | bytes 688136 | tf_op jit(solution)/shard_map/ppermute | solution.py:259
  6.2 16.1 %collective-permute-start.3 = (bf16[1,128,896]{2,1,0:T(8,128)(2,1)S(1)}, bf16[1,128,896]{2,1,0:T(8,128)(2,1)S(1)}, u32[]{:S(2)}, u32[]{:S(2)}) collective-permute-start(bf16[1,128,896]{2,1,0:T(8,128)(2,1)S(1)} %get-tuple-element.33), channel_id=1, source_target_pairs={{0,2},{1,3},{4,0},{5,1},{8,4},{9,5},{12,8},{13,9},{14,12},{15,13},... | collective-permute-start | bytes 688136 | tf_op jit(solution)/shard_map/ppermute | solution.py:259
  7.0 11.3 %collective-permute-start.4 = (s32[2,1,2]{1,2,0:T(2,128)S(1)}, s32[2,1,2]{1,2,0:T(2,128)S(1)}, u32[]{:S(2)}, u32[]{:S(2)}) collective-permute-start(s32[2,1,2]{1,2,0:T(2,128)S(1)} %pad_add_fusion), channel_id=1, source_target_pairs={{0,1},{1,2},{2,3},{3,4},{4,5},{5,6},{6,7},{7,8},{8,9},{9,10},{10,1... | collective-permute-start | bytes 56 | tf_op jit(solution)/shard_map/ppermute | solution.py:308
  10.6 2.0 %copy-start.1 = (bf16[896,2048]{1,0:T(8,128)(2,1)S(1)}, bf16[896,2048]{1,0:T(8,128)(2,1)}, u32[]{:S(2)}) copy-start(bf16[896,2048]{1,0:T(8,128)(2,1)} %key_ref.1) | copy-start | bytes 11010052
  12.6 5.0 %copy-start.7 = (s32[8]{0:T(128)S(1)}, s32[8]{0:T(128)}, u32[]{:S(2)}) copy-start(s32[8]{0:T(128)} %constant.74.clone) | copy-start | bytes 100
  12.6 5.7 %copy-start.6 = (s32[4]{0:T(128)S(1)}, s32[4]{0:T(128)}, u32[]{:S(2)}) copy-start(s32[4]{0:T(128)} %param.14) | copy-start | bytes 52
  12.6 5.7 %copy-start.3 = (bf16[2,128,896]{2,1,0:T(8,128)(2,1)S(1)}, bf16[2,128,896]{2,1,0:T(8,128)(2,1)}, u32[]{:S(2)}) copy-start(bf16[2,128,896]{2,1,0:T(8,128)(2,1)} %rest_0_.1) | copy-start | bytes 1376260
  12.6 8.4 %copy-start.4 = (s32[4,2]{0,1:T(2,128)S(1)}, s32[4,2]{0,1:T(2,128)}, u32[]{:S(2)}) copy-start(s32[4,2]{0,1:T(2,128)} %param.13) | copy-start | bytes 100
  12.6 8.4 %copy-start.5 = (s32[4,2]{0,1:T(2,128)S(1)}, s32[4,2]{0,1:T(2,128)}, u32[]{:S(2)}) copy-start(s32[4,2]{0,1:T(2,128)} %param.12) | copy-start | bytes 100
  14.7 2.9 %copy-start = (bf16[16,256,896]{2,1,0:T(8,128)(2,1)}, bf16[16,256,896]{2,1,0:T(8,128)(2,1)S(1)}, u32[]{:S(2)}) copy-start(bf16[16,256,896]{2,1,0:T(8,128)(2,1)S(1)} %get-tuple-element.23.folded_ref) | copy-start | bytes 22020100
  18.3 6.3 %collective-permute-start.5 = (bf16[2,128,896]{2,1,0:T(8,128)(2,1)S(1)}, bf16[2,128,896]{2,1,0:T(8,128)(2,1)S(1)}, u32[]{:S(2)}, u32[]{:S(2)}) collective-permute-start(bf16[2,128,896]{2,1,0:T(8,128)(2,1)S(1)} %copy-done.3), channel_id=1, source_target_pairs={{0,1},{1,0},{2,3},{3,2},{4,5},{5,4},{6,7},{7,6},{8,9},{9,8},{10,11... | collective-permute-start | bytes 1376264 | tf_op jit(solution)/shard_map/ppermute | solution.py:262
  22.3 41.3 %copy-start.2 = (bf16[896,2048]{1,0:T(8,128)(2,1)S(1)}, bf16[896,2048]{1,0:T(8,128)(2,1)}, u32[]{:S(2)}) copy-start(bf16[896,2048]{1,0:T(8,128)(2,1)} %value_ref.1) | copy-start | bytes 11010052
  22.3 2.7 %collective-permute-start.6 = (bf16[1,128,896]{2,1,0:T(8,128)(2,1)S(1)}, bf16[1,128,896]{2,1,0:T(8,128)(2,1)S(1)}, u32[]{:S(2)}, u32[]{:S(2)}) collective-permute-start(bf16[1,128,896]{2,1,0:T(8,128)(2,1)S(1)} %collective-permute-done.rest_2_), channel_id=1, source_target_pairs={{0,1},{1,0},{2,3},{3,2},{4,5},{5,4},{6,7},{7,6},{8,9},{9,8},{10,11... | collective-permute-start | bytes 688136 | tf_op jit(solution)/shard_map/ppermute | solution.py:262
  22.4 4.2 %collective-permute-start.7 = (bf16[1,128,896]{2,1,0:T(8,128)(2,1)S(1)}, bf16[1,128,896]{2,1,0:T(8,128)(2,1)S(1)}, u32[]{:S(2)}, u32[]{:S(2)}) collective-permute-start(bf16[1,128,896]{2,1,0:T(8,128)(2,1)S(1)} %collective-permute-done.1.rest_3_), channel_id=1, source_target_pairs={{0,1},{1,0},{2,3},{3,2},{4,5},{5,4},{6,7},{7,6},{8,9},{9,8},{10,11... | collective-permute-start | bytes 688136 | tf_op jit(solution)/shard_map/ppermute | solution.py:262
  22.9 3.7 %collective-permute-start.8 = (bf16[1,128,896]{2,1,0:T(8,128)(2,1)S(1)}, bf16[1,128,896]{2,1,0:T(8,128)(2,1)S(1)}, u32[]{:S(2)}, u32[]{:S(2)}) collective-permute-start(bf16[1,128,896]{2,1,0:T(8,128)(2,1)S(1)} %collective-permute-done.2.rest_4_), channel_id=1, source_target_pairs={{0,1},{1,0},{2,3},{3,2},{4,5},{5,4},{6,7},{7,6},{8,9},{9,8},{10,11... | collective-permute-start | bytes 688136 | tf_op jit(solution)/shard_map/ppermute | solution.py:262
  23.0 8.4 %collective-permute-start.10 = (bf16[1,128,896]{2,1,0:T(8,128)(2,1)S(1)}, bf16[1,128,896]{2,1,0:T(8,128)(2,1)S(1)}, u32[]{:S(2)}, u32[]{:S(2)}) collective-permute-start(bf16[1,128,896]{2,1,0:T(8,128)(2,1)S(1)} %collective-permute-done.rest_2_), channel_id=1, source_target_pairs={{0,4},{1,5},{4,8},{5,9},{8,12},{9,13},{12,14},{13,15},{14,10},{15,... | collective-permute-start | bytes 688136 | tf_op jit(solution)/shard_map/ppermute | solution.py:259
  24.6 8.4 %collective-permute-start.11 = (bf16[1,128,896]{2,1,0:T(8,128)(2,1)S(1)}, bf16[1,128,896]{2,1,0:T(8,128)(2,1)S(1)}, u32[]{:S(2)}, u32[]{:S(2)}) collective-permute-start(bf16[1,128,896]{2,1,0:T(8,128)(2,1)S(1)} %collective-permute-done.1.rest_3_), channel_id=1, source_target_pairs={{0,2},{1,3},{4,0},{5,1},{8,4},{9,5},{12,8},{13,9},{14,12},{15,13},... | collective-permute-start | bytes 688136 | tf_op jit(solution)/shard_map/ppermute | solution.py:259
  25.0 10.8 %collective-permute-start.12 = (bf16[1,128,896]{2,1,0:T(8,128)(2,1)S(1)}, bf16[1,128,896]{2,1,0:T(8,128)(2,1)S(1)}, u32[]{:S(2)}, u32[]{:S(2)}) collective-permute-start(bf16[1,128,896]{2,1,0:T(8,128)(2,1)S(1)} %collective-permute-done.2.rest_4_), channel_id=1, source_target_pairs={{0,4},{1,5},{4,8},{5,9},{8,12},{9,13},{12,14},{13,15},{14,10},{15,... | collective-permute-start | bytes 688136 | tf_op jit(solution)/shard_map/ppermute | solution.py:259
  26.6 9.3 %collective-permute-start.9 = (bf16[1,128,896]{2,1,0:T(8,128)(2,1)S(1)}, bf16[1,128,896]{2,1,0:T(8,128)(2,1)S(1)}, u32[]{:S(2)}, u32[]{:S(2)}) collective-permute-start(bf16[1,128,896]{2,1,0:T(8,128)(2,1)S(1)} %collective-permute-done.3.rest_5_), channel_id=1, source_target_pairs={{0,1},{1,0},{2,3},{3,2},{4,5},{5,4},{6,7},{7,6},{8,9},{9,8},{10,11... | collective-permute-start | bytes 688136 | tf_op jit(solution)/shard_map/ppermute | solution.py:262
  26.6 10.8 %collective-permute-start.13 = (bf16[1,128,896]{2,1,0:T(8,128)(2,1)S(1)}, bf16[1,128,896]{2,1,0:T(8,128)(2,1)S(1)}, u32[]{:S(2)}, u32[]{:S(2)}) collective-permute-start(bf16[1,128,896]{2,1,0:T(8,128)(2,1)S(1)} %collective-permute-done.3.rest_5_), channel_id=1, source_target_pairs={{0,2},{1,3},{4,0},{5,1},{8,4},{9,5},{12,8},{13,9},{14,12},{15,13},... | collective-permute-start | bytes 688136 | tf_op jit(solution)/shard_map/ppermute | solution.py:259
  31.4 6.3 %collective-permute-start.14 = (bf16[1,128,896]{2,1,0:T(8,128)(2,1)S(1)}, bf16[1,128,896]{2,1,0:T(8,128)(2,1)S(1)}, u32[]{:S(2)}, u32[]{:S(2)}) collective-permute-start(bf16[1,128,896]{2,1,0:T(8,128)(2,1)S(1)} %collective-permute-done.10.rest_10_), channel_id=1, source_target_pairs={{0,1},{1,0},{2,3},{3,2},{4,5},{5,4},{6,7},{7,6},{8,9},{9,8},{10,11... | collective-permute-start | bytes 688136 | tf_op jit(solution)/shard_map/ppermute | solution.py:262
  33.0 5.1 %collective-permute-start.15 = (bf16[1,128,896]{2,1,0:T(8,128)(2,1)S(1)}, bf16[1,128,896]{2,1,0:T(8,128)(2,1)S(1)}, u32[]{:S(2)}, u32[]{:S(2)}) collective-permute-start(bf16[1,128,896]{2,1,0:T(8,128)(2,1)S(1)} %collective-permute-done.11.rest_11_), channel_id=1, source_target_pairs={{0,1},{1,0},{2,3},{3,2},{4,5},{5,4},{6,7},{7,6},{8,9},{9,8},{10,11... | collective-permute-start | bytes 688136 | tf_op jit(solution)/shard_map/ppermute | solution.py:262
  35.8 3.8 %collective-permute-start.16 = (bf16[1,128,896]{2,1,0:T(8,128)(2,1)S(1)}, bf16[1,128,896]{2,1,0:T(8,128)(2,1)S(1)}, u32[]{:S(2)}, u32[]{:S(2)}) collective-permute-start(bf16[1,128,896]{2,1,0:T(8,128)(2,1)S(1)} %collective-permute-done.12.rest_12_), channel_id=1, source_target_pairs={{0,1},{1,0},{2,3},{3,2},{4,5},{5,4},{6,7},{7,6},{8,9},{9,8},{10,11... | collective-permute-start | bytes 688136 | tf_op jit(solution)/shard_map/ppermute | solution.py:262
  35.9 8.4 %collective-permute-start.18 = (bf16[1,128,896]{2,1,0:T(8,128)(2,1)S(1)}, bf16[1,128,896]{2,1,0:T(8,128)(2,1)S(1)}, u32[]{:S(2)}, u32[]{:S(2)}) collective-permute-start(bf16[1,128,896]{2,1,0:T(8,128)(2,1)S(1)} %collective-permute-done.10.rest_10_), channel_id=1, source_target_pairs={{0,4},{1,5},{4,8},{5,9},{8,12},{9,13},{12,14},{13,15},{14,10},{15,... | collective-permute-start | bytes 688136 | tf_op jit(solution)/shard_map/ppermute | solution.py:259
  37.4 6.8 %collective-permute-start.17 = (bf16[1,128,896]{2,1,0:T(8,128)(2,1)S(1)}, bf16[1,128,896]{2,1,0:T(8,128)(2,1)S(1)}, u32[]{:S(2)}, u32[]{:S(2)}) collective-permute-start(bf16[1,128,896]{2,1,0:T(8,128)(2,1)S(1)} %collective-permute-done.13.rest_13_), channel_id=1, source_target_pairs={{0,1},{1,0},{2,3},{3,2},{4,5},{5,4},{6,7},{7,6},{8,9},{9,8},{10,11... | collective-permute-start | bytes 688136 | tf_op jit(solution)/shard_map/ppermute | solution.py:262
  37.7 8.4 %collective-permute-start.21 = (bf16[1,128,896]{2,1,0:T(8,128)(2,1)S(1)}, bf16[1,128,896]{2,1,0:T(8,128)(2,1)S(1)}, u32[]{:S(2)}, u32[]{:S(2)}) collective-permute-start(bf16[1,128,896]{2,1,0:T(8,128)(2,1)S(1)} %collective-permute-done.13.rest_13_), channel_id=1, source_target_pairs={{0,2},{1,3},{4,0},{5,1},{8,4},{9,5},{12,8},{13,9},{14,12},{15,13},... | collective-permute-start | bytes 688136 | tf_op jit(solution)/shard_map/ppermute | solution.py:259
  38.1 12.9 %collective-permute-start.19 = (bf16[1,128,896]{2,1,0:T(8,128)(2,1)S(1)}, bf16[1,128,896]{2,1,0:T(8,128)(2,1)S(1)}, u32[]{:S(2)}, u32[]{:S(2)}) collective-permute-start(bf16[1,128,896]{2,1,0:T(8,128)(2,1)S(1)} %collective-permute-done.11.rest_11_), channel_id=1, source_target_pairs={{0,2},{1,3},{4,0},{5,1},{8,4},{9,5},{12,8},{13,9},{14,12},{15,13},... | collective-permute-start | bytes 688136 | tf_op jit(solution)/shard_map/ppermute | solution.py:259
  39.6 11.4 %collective-permute-start.20 = (bf16[1,128,896]{2,1,0:T(8,128)(2,1)S(1)}, bf16[1,128,896]{2,1,0:T(8,128)(2,1)S(1)}, u32[]{:S(2)}, u32[]{:S(2)}) collective-permute-start(bf16[1,128,896]{2,1,0:T(8,128)(2,1)S(1)} %collective-permute-done.12.rest_12_), channel_id=1, source_target_pairs={{0,4},{1,5},{4,8},{5,9},{8,12},{9,13},{12,14},{13,15},{14,10},{15,... | collective-permute-start | bytes 688136 | tf_op jit(solution)/shard_map/ppermute | solution.py:259
  44.3 7.3 %collective-permute-start.22 = (bf16[1,128,896]{2,1,0:T(8,128)(2,1)S(1)}, bf16[1,128,896]{2,1,0:T(8,128)(2,1)S(1)}, u32[]{:S(2)}, u32[]{:S(2)}) collective-permute-start(bf16[1,128,896]{2,1,0:T(8,128)(2,1)S(1)} %collective-permute-done.18.rest_18_), channel_id=1, source_target_pairs={{0,1},{1,0},{2,3},{3,2},{4,5},{5,4},{6,7},{7,6},{8,9},{9,8},{10,11... | collective-permute-start | bytes 688136 | tf_op jit(solution)/shard_map/ppermute | solution.py:262
  44.3 9.4 %collective-permute-start.26 = (bf16[1,128,896]{2,1,0:T(8,128)(2,1)S(1)}, bf16[1,128,896]{2,1,0:T(8,128)(2,1)S(1)}, u32[]{:S(2)}, u32[]{:S(2)}) collective-permute-start(bf16[1,128,896]{2,1,0:T(8,128)(2,1)S(1)} %collective-permute-done.18.rest_18_), channel_id=1, source_target_pairs={{0,4},{1,5},{4,8},{5,9},{8,12},{9,13},{12,14},{13,15},{14,10},{15,... | collective-permute-start | bytes 688136 | tf_op jit(solution)/shard_map/ppermute | solution.py:259
  46.1 9.2 %collective-permute-start.27 = (bf16[1,128,896]{2,1,0:T(8,128)(2,1)S(1)}, bf16[1,128,896]{2,1,0:T(8,128)(2,1)S(1)}, u32[]{:S(2)}, u32[]{:S(2)}) collective-permute-start(bf16[1,128,896]{2,1,0:T(8,128)(2,1)S(1)} %collective-permute-done.21.rest_21_), channel_id=1, source_target_pairs={{0,2},{1,3},{4,0},{5,1},{8,4},{9,5},{12,8},{13,9},{14,12},{15,13},... | collective-permute-start | bytes 688136 | tf_op jit(solution)/shard_map/ppermute | solution.py:259
  51.0 4.3 %collective-permute-start.23 = (bf16[1,128,896]{2,1,0:T(8,128)(2,1)S(1)}, bf16[1,128,896]{2,1,0:T(8,128)(2,1)S(1)}, u32[]{:S(2)}, u32[]{:S(2)}) collective-permute-start(bf16[1,128,896]{2,1,0:T(8,128)(2,1)S(1)} %collective-permute-done.19.rest_19_), channel_id=1, source_target_pairs={{0,1},{1,0},{2,3},{3,2},{4,5},{5,4},{6,7},{7,6},{8,9},{9,8},{10,11... | collective-permute-start | bytes 688136 | tf_op jit(solution)/shard_map/ppermute | solution.py:262
  51.0 4.3 %collective-permute-start.24 = (bf16[1,128,896]{2,1,0:T(8,128)(2,1)S(1)}, bf16[1,128,896]{2,1,0:T(8,128)(2,1)S(1)}, u32[]{:S(2)}, u32[]{:S(2)}) collective-permute-start(bf16[1,128,896]{2,1,0:T(8,128)(2,1)S(1)} %collective-permute-done.20.rest_20_), channel_id=1, source_target_pairs={{0,1},{1,0},{2,3},{3,2},{4,5},{5,4},{6,7},{7,6},{8,9},{9,8},{10,11... | collective-permute-start | bytes 688136 | tf_op jit(solution)/shard_map/ppermute | solution.py:262
  51.5 3.8 %collective-permute-start.25 = (bf16[1,128,896]{2,1,0:T(8,128)(2,1)S(1)}, bf16[1,128,896]{2,1,0:T(8,128)(2,1)S(1)}, u32[]{:S(2)}, u32[]{:S(2)}) collective-permute-start(bf16[1,128,896]{2,1,0:T(8,128)(2,1)S(1)} %collective-permute-done.21.rest_21_), channel_id=1, source_target_pairs={{0,1},{1,0},{2,3},{3,2},{4,5},{5,4},{6,7},{7,6},{8,9},{9,8},{10,11... | collective-permute-start | bytes 688136 | tf_op jit(solution)/shard_map/ppermute | solution.py:262
  53.7 9.9 %collective-permute-start.28 = (bf16[1,128,896]{2,1,0:T(8,128)(2,1)S(1)}, bf16[1,128,896]{2,1,0:T(8,128)(2,1)S(1)}, u32[]{:S(2)}, u32[]{:S(2)}) collective-permute-start(bf16[1,128,896]{2,1,0:T(8,128)(2,1)S(1)} %collective-permute-done.26.rest_0_), channel_id=1, source_target_pairs={{0,1},{1,0},{2,3},{3,2},{4,5},{5,4},{6,7},{7,6},{8,9},{9,8},{10,11... | collective-permute-start | bytes 688136 | tf_op jit(solution)/shard_map/ppermute | solution.py:262
  55.3 8.3 %collective-permute-start.29 = (bf16[1,128,896]{2,1,0:T(8,128)(2,1)S(1)}, bf16[1,128,896]{2,1,0:T(8,128)(2,1)S(1)}, u32[]{:S(2)}, u32[]{:S(2)}) collective-permute-start(bf16[1,128,896]{2,1,0:T(8,128)(2,1)S(1)} %collective-permute-done.27.rest_1_), channel_id=1, source_target_pairs={{0,1},{1,0},{2,3},{3,2},{4,5},{5,4},{6,7},{7,6},{8,9},{9,8},{10,11... | collective-permute-start | bytes 688136 | tf_op jit(solution)/shard_map/ppermute | solution.py:262

commit v5 on v4

v5 whole, which is shorter than its diff:
```python
import functools
import math

import jax
import jax.numpy as jnp
from jax import lax
from jax.experimental import pallas as pl
from jax.experimental.pallas import tpu as pltpu
from jax.sharding import PartitionSpec as P

SPAN = 64
HEADS = 16
HEAD_DIM = 128
EPS = 1e-6
SCALE = math.log2(math.e) / math.sqrt(HEAD_DIM)
CORES = 2
GROUP = 4
MIB = 2**20


SMEM_SPEC = pl.BlockSpec(memory_space=pltpu.SMEM)
VMEM_SPEC = pl.BlockSpec(memory_space=pltpu.VMEM)
ANY_SPEC = pl.BlockSpec(memory_space=pl.ANY)


def contract(left, right, dims):
    return lax.dot_general(left, right, (dims, ((), ())), preferred_element_type=jnp.float32)


def head_columns(head):
    return slice(head * HEAD_DIM, (head + 1) * HEAD_DIM)


def fold_kernel(query_ref, key_hbm, folded_ref, single_ref, key, sems):
    groups = HEADS // GROUP

    def fetch(group):
        columns = slice(group * GROUP * HEAD_DIM, (group + 1) * GROUP * HEAD_DIM)
        return pltpu.make_async_copy(key_hbm.at[:, columns], key.at[:, columns], sems.at[group])

    for group in range(groups):
        fetch(group).start()
    for head in range(HEADS):
        if head % GROUP == 0:
            fetch(head // GROUP).wait()
        columns = head_columns(head)
        queries = pltpu.roll(query_ref[:, columns].astype(jnp.float32), 1, 0).astype(jnp.bfloat16)
        rows = contract(queries, key[:, columns], ((1,), (1,))) * SCALE
        single_ref[head : head + 1, :] = rows[:1]
        folded_ref[head] = rows.astype(jnp.bfloat16)


def fold(queries, w_key):
    count, width = queries.shape[0], w_key.shape[0]
    return pl.pallas_call(
        fold_kernel,
        out_shape=(
            jax.ShapeDtypeStruct((HEADS, count, width), jnp.bfloat16),
            jax.ShapeDtypeStruct((HEADS, width), jnp.float32),
        ),
        in_specs=[VMEM_SPEC, ANY_SPEC],
        out_specs=(VMEM_SPEC,) * 2,
        scratch_shapes=[
            pltpu.VMEM(w_key.shape, jnp.bfloat16),
            pltpu.SemaphoreType.DMA((HEADS // GROUP,)),
        ],
        compiler_params=pltpu.CompilerParams(vmem_limit_bytes=28 * MIB),
        cost_estimate=pl.CostEstimate(
            flops=2 * queries.size * width, bytes_accessed=8 * MIB, transcendentals=0
        ),
        name="fold_queries",
    )(queries, w_key)


def normalise(raw, tokens_ref, turned_ref):
    widened = raw.astype(jnp.float32)
    factor = lax.rsqrt(jnp.mean(widened * widened, axis=-1, keepdims=True) + EPS)
    scaled = widened * factor
    tokens_ref[...] = scaled.astype(jnp.bfloat16)
    turned_ref[...] = scaled.T.astype(jnp.bfloat16)


def among(stores, first, source, act):
    if len(stores) == 1:
        pl.when(source == first)(lambda: act(stores[0]))
        return
    half = len(stores) // 2
    pl.when(source < first + half)(lambda: among(stores[:half], first, source, act))
    pl.when(source >= first + half)(lambda: among(stores[half:], first + half, source, act))


def collect_kernel(source_ref, block_ref, *rest):
    *stores, tokens_ref, turned_ref, raw, sems = rest
    requests = raw.shape[0]

    def fetch(request, store):
        return pltpu.make_async_copy(store.at[block_ref[request]], raw.at[request], sems.at[request])

    def begin(request, carry):
        among(stores, 0, source_ref[request], lambda store: fetch(request, store).start())
        return carry

    def finish(request, carry):
        @pl.when(source_ref[request] < len(stores))
        def _():
            fetch(request, stores[0]).wait()
            normalise(raw[request], tokens_ref.at[request], turned_ref.at[request])

        return carry

    lax.fori_loop(0, requests, begin, 0)
    lax.fori_loop(0, requests, finish, 0)


def collect(source, block, stores):
    requests = source.shape[0]
    length, width = stores[0].shape[1:]
    return pl.pallas_call(
        collect_kernel,
        out_shape=(
            jax.ShapeDtypeStruct((requests, length, width), jnp.bfloat16),
            jax.ShapeDtypeStruct((requests, width, length), jnp.bfloat16),
        ),
        in_specs=[SMEM_SPEC] * 2 + [ANY_SPEC] * len(stores),
        out_specs=(VMEM_SPEC,) * 2,
        scratch_shapes=[
            pltpu.VMEM((requests, length, width), jnp.bfloat16),
            pltpu.SemaphoreType.DMA((requests,)),
        ],
        compiler_params=pltpu.CompilerParams(vmem_limit_bytes=16 * MIB),
        cost_estimate=pl.CostEstimate(flops=4 * MIB, bytes_accessed=8 * MIB, transcendentals=0),
        name="collect_early",
    )(source, block, *stores)


def weigh(scores):
    powers = jnp.exp2(scores - jnp.max(scores, axis=-1, keepdims=True))
    totals = jnp.sum(powers, axis=-1, keepdims=True)
    return (powers * (1.0 / totals)).astype(jnp.bfloat16)


def attend_kernel(
    early, source_ref, block_ref, keep_ref, folded_ref, single_ref, tokens_in, turned_in, value_ref, *rest
):
    *late, out_ref, tokens, turned, raw, scores, weights, mixed, sems = rest
    requests, length, width = raw.shape
    blocks = requests // 2 - 1
    count = blocks * SPAN
    rows_at_once = GROUP * SPAN

    def fetch_early(request):
        return (
            pltpu.make_async_copy(tokens_in.at[request], tokens.at[request], sems.at[request, 0]),
            pltpu.make_async_copy(turned_in.at[request], turned.at[request], sems.at[request, 1]),
        )

    def fetch_late(request, store):
        return pltpu.make_async_copy(store.at[block_ref[request]], raw.at[request], sems.at[request, 0])

    def begin(request, carry):
        @pl.when(source_ref[request] < early)
        def _():
            for copy in fetch_early(request):
                copy.start()

        if late:
            among(late, early, source_ref[request], lambda store: fetch_late(request, store).start())
        return carry

    def finish(request, carry):
        @pl.when(source_ref[request] < early)
        def _():
            for copy in fetch_early(request):
                copy.wait()

        if late:

            @pl.when(source_ref[request] >= early)
            def _():
                fetch_late(request, late[0]).wait()
                normalise(raw[request], tokens.at[request], turned.at[request])

        return carry

    lax.fori_loop(0, requests, begin, 0)
    lax.fori_loop(0, requests, finish, 0)

    def across(window):
        return jnp.concatenate([turned[2 * window], turned[2 * window + 1]], axis=1)

    def along(window):
        return tokens[2 * window : 2 * window + 2].reshape(2 * length, width)

    lone = weigh(contract(single_ref[...].astype(jnp.bfloat16), across(blocks), ((1,), (0,))))
    lone = contract(lone, along(blocks), ((1,), (0,)))

    place = lax.broadcasted_iota(jnp.int32, (count, HEAD_DIM), 0)
    kept = place % SPAN == 0
    for block in range(blocks):
        kept = kept | ((place // SPAN == block) & (keep_ref[block] > 0))

    units = [(group, window) for group in range(HEADS // GROUP) for window in range(blocks)]

    def score(unit):
        group, window = units[unit]
        heads, rows = slice(group * GROUP, (group + 1) * GROUP), slice(window * SPAN, (window + 1) * SPAN)
        taken = folded_ref[heads, rows].reshape(rows_at_once, width)
        scores[unit] = contract(taken, across(window), ((1,), (0,)))

    def soften(unit):
        for part in range(GROUP):
            rows = slice(part * SPAN, (part + 1) * SPAN)
            weights[unit, rows] = weigh(scores[unit, rows])

    def combine(unit):
        group, window = units[unit]
        heads, rows = slice(group * GROUP, (group + 1) * GROUP), slice(window * SPAN, (window + 1) * SPAN)
        sums = contract(weights[unit], along(window), ((1,), (0,))).reshape(GROUP, SPAN, width)
        if window == 0:
            first = lax.broadcasted_iota(jnp.int32, sums.shape, 1) == 0
            sums = jnp.where(first, lone[heads][:, None, :], sums)
        mixed[heads, rows] = sums.astype(jnp.bfloat16)

    def project(group):
        for head in range(group * GROUP, (group + 1) * GROUP):
            columns = head_columns(head)
            sums = contract(mixed[head], value_ref[:, columns], ((1,), (0,)))
            sums = jnp.where(kept, sums, 0.0)
            out_ref[:, columns] = pltpu.roll(sums, count - 1, 0).astype(jnp.bfloat16)

    for step in range(len(units) + 2):
        if step < len(units):
            score(step)
        if step >= 2:
            combine(step - 2)
        if 1 <= step <= len(units):
            soften(step - 1)
        if step >= 2 and units[step - 2][1] == blocks - 1:
            project(units[step - 2][0])


def attend(early, source, block, keep, folded, single, tokens, turned, w_value, late):
    requests, length, width = tokens.shape
    count = folded.shape[1]
    units = HEADS // GROUP * (count // SPAN)
    return pl.pallas_call(
        functools.partial(attend_kernel, early),
        out_shape=jax.ShapeDtypeStruct((count, w_value.shape[1]), jnp.bfloat16),
        in_specs=[SMEM_SPEC] * 3
        + [VMEM_SPEC] * 2
        + [ANY_SPEC] * 2
        + [VMEM_SPEC]
        + [ANY_SPEC] * len(late),
        out_specs=VMEM_SPEC,
        scratch_shapes=[
            pltpu.VMEM(tokens.shape, jnp.bfloat16),
            pltpu.VMEM(turned.shape, jnp.bfloat16),
            pltpu.VMEM(tokens.shape, jnp.bfloat16),
            pltpu.VMEM((units, GROUP * SPAN, 2 * length), jnp.float32),
            pltpu.VMEM((units, GROUP * SPAN, 2 * length), jnp.bfloat16),
            pltpu.VMEM(folded.shape, jnp.bfloat16),
            pltpu.SemaphoreType.DMA((requests, 2)),
        ],
        compiler_params=pltpu.CompilerParams(vmem_limit_bytes=32 * MIB),
        cost_estimate=pl.CostEstimate(
            flops=2 * HEADS * count * width * (4 * length + HEAD_DIM),
            bytes_accessed=16 * MIB,
            transcendentals=HEADS * count * 2 * length,
        ),
        name="attend_windows",
    )(source, block, keep, folded, single, tokens, turned, w_value, *late)


def chip_ring(mesh):
    row = mesh.devices.reshape(-1, mesh.shape["seq"])[0]
    chips = list(range(len(row) // CORES))
    columns = [tuple(getattr(row[CORES * chip], "coords", (0, 0))[:2]) for chip in chips]
    if len(set(columns)) != 2:
        return chips
    up = [chip for chip in chips if columns[chip] == columns[0]]
    return up + [chip for chip in reversed(chips) if columns[chip] != columns[0]]


class Ring:
    def __init__(self, ring, slots):
        self.ring, self.slots = ring, slots
        self.size = len(ring)
        self.reach = (self.size - 1) // 2
        self.opposite = self.size % 2 == 0
        self.cut = slots // 2

    def turned(self, value, steps):
        size = self.size
        pairs = [
            (CORES * self.ring[i] + core, CORES * self.ring[(i + steps) % size] + core)
            for i in range(size)
            for core in range(CORES)
        ]
        return lax.ppermute(value, "seq", pairs)

    def swapped(self, value):
        return lax.ppermute(value, "seq", [(i, i ^ 1) for i in range(CORES * self.size)])

    def gather(self, stored, beside):
        slots = range(self.slots)
        own = self.swapped(stored)
        early, late, swaps = [stored, own], [], []
        waves = {way: [stored[slot : slot + 1] for slot in slots] for way in (1, -1)}
        waiting = []
        for step in range(self.reach + self.opposite):
            last = step == self.reach
            for slot in slots:
                ways = (1, -1) if not last else (1,) if slot < self.cut else (-1,)
                sent = [waves[way][slot] for way in ways]
                if step == 0 and slot == 1:
                    *sent, own = lax.optimization_barrier((*sent, own))
                if step == 1 and slot == self.slots - 1:
                    *sent, beside = lax.optimization_barrier((*sent, beside))
                arrived = [self.turned(value, way) for value, way in zip(sent, ways)]
                for way, value in zip(ways, arrived):
                    waves[way][slot] = value
                if waiting:
                    *waiting, arrived[0] = lax.optimization_barrier((*waiting, arrived[0]))
                    swaps += [self.swapped(value) for value in waiting]
                    waves[ways[0]][slot] = arrived[0]
                waiting = arrived
                (late if last else early).append(arrived)
        swaps += [self.swapped(value) for value in waiting]
        stored, own, *early = early
        count = sum(map(len, early))
        early = [value for arrived in early for value in arrived]
        late = [value for arrived in late for value in arrived]
        return [stored, own, *early, *swaps[:count]], late + swaps[count:], beside

    def locate(self, owner, slot, here):
        order = jnp.asarray([self.ring.index(chip) for chip in range(self.size)], jnp.int32)

        def place_of(device):
            chips = jnp.arange(self.size)
            return jnp.sum(jnp.where((device // CORES)[..., None] == chips, order, 0), axis=-1)

        away = (place_of(here) - place_of(owner)) % self.size
        other = (owner % CORES != here % CORES).astype(jnp.int32)
        per_step = 2 * self.slots
        back = away > self.reach
        step = jnp.where(back, self.size - away, away)
        source = 2 + other * self.reach * per_step + (step - 1) * per_step + 2 * slot + back
        if self.opposite:
            last = 2 + CORES * self.reach * per_step + other * self.slots + slot
            source = jnp.where(away == self.size // 2, last, source)
        return jnp.where(away == 0, other, source), jnp.where(away == 0, slot, 0)


def body(ring, queries, neighbours, w_key, w_value, retrieval_owner, retrieval_slot, doc_starts):
    devices = lax.axis_size("seq")
    here = lax.axis_index("seq")
    plan = Ring(ring, neighbours.shape[0])
    owner_slot = jnp.stack([retrieval_owner, retrieval_slot])
    before = lax.ppermute(owner_slot[:, -1:], "seq", [(i, i + 1) for i in range(devices - 1)])
    owner, slot = jnp.concatenate([before, owner_slot], 1).reshape(2, -1)
    source, block = plan.locate(owner, slot, here)
    blocks = doc_starts.shape[0]
    opening = (here == 0) & (jnp.arange(blocks) == 0)
    keep = ((doc_starts == 0) & jnp.logical_not(opening)).astype(jnp.int32)
    early, late, (folded, single, source, block, keep) = plan.gather(
        neighbours, (*fold(queries, w_key), source, block, keep)
    )
    tokens, turned = collect(source, block, early)
    return attend(len(early), source, block, keep, folded, single, tokens, turned, w_value, late)


def solution(mesh):
    return jax.shard_map(
        functools.partial(body, chip_ring(mesh)),
        mesh=mesh,
        in_specs=(
            P(("groups", "seq"), None),
            P(("groups", "seq"), None, None),
            P(),
            P(),
            P(("groups", "seq"), None),
            P(("groups", "seq"), None),
            P(("groups", "seq")),
        ),
        out_specs=P(("groups", "seq"), None),
        check_vma=False,
    )
```

time: 84.9 us -> 89.4 us (1.053)
  Pallas kernels: 31 us -> 25.1 us
  local copies, waits for them, and re-layouts: 7.18 us -> 10.8 us
  starting transfers between devices: 20.8 us -> 24.4 us
  waiting for transfers between devices: 21.3 us -> 24.9 us
    pallas_call x1, Pallas kernels: 20.7 us -> 15.1 us  [attend(): pl.pallas_call(functools.partial(attend_kernel, early), out_shape=jax.Sha...]
    unnamed x16 -> x18, local copies, waits for them, and re-layouts: 4.96 us -> 9.26 us
    ppermute x14, starting transfers between devices: 15.3 us -> 19.2 us  [turned(): return lax.ppermute(value, 'seq', pairs)]
    ppermute x14, waiting for transfers between devices: 21.3 us -> 23.9 us  [turned(): return lax.ppermute(value, 'seq', pairs)]
    pallas_call x1, Pallas kernels: 8.26 us -> 6.42 us  [collect(): pl.pallas_call(collect_kernel, out_shape=(jax.ShapeDtypeStruct((requests,...]
    pallas_call x1, Pallas kernels: 2.08 us -> 3.58 us  [fold(): pl.pallas_call(fold_kernel, out_shape=(jax.ShapeDtypeStruct((HEADS, count...]
    concatenate x1 -> x0, other arithmetic: 1.48 us -> none  [body(): rows = jnp.concatenate([queries[-1:], queries[:-1]], 0)]
    ppermute x15, starting transfers between devices: 4.25 us -> 2.85 us  [swapped(): lax.ppermute(value, 'seq', [(i, i ^ 1) for i in range(CORES * self.size)])]
  transfers between devices with their start and end apart: 30 -> 30, of which waited for: 8 -> 11; matrix products, arithmetic and copies ran while one was open for 6% -> 4% of each run, Pallas kernels for 12% -> 11%
where the time goes in v5:
time: 89.4 us; the launch traced here: 89.1 us
  Pallas kernels  25.1 us (28%)
  waiting for transfers between devices  24.9 us (28%)
  starting transfers between devices  24.4 us (27%)
  local copies, waits for them, and re-layouts  10.8 us (12%)
  other arithmetic  3.58 us (4%)
    ppermute x14, waiting for transfers between devices, turned(): return lax.ppermute(value, 'seq', pairs)  23.9 us
    ppermute x14, starting transfers between devices, turned(): return lax.ppermute(value, 'seq', pairs)  19.2 us
    pallas_call x1, Pallas kernels, attend(): pl.pallas_call(functools.partial(attend_kernel, early), out_shape=jax.Sha...  15.1 us
    unnamed x18, local copies, waits for them, and re-layouts  9.26 us
    pallas_call x1, Pallas kernels, collect(): pl.pallas_call(collect_kernel, out_shape=(jax.ShapeDtypeStruct((requests,...  6.42 us
    pallas_call x1, Pallas kernels, fold(): pl.pallas_call(fold_kernel, out_shape=(jax.ShapeDtypeStruct((HEADS, count...  3.58 us
    ppermute x15, starting transfers between devices, swapped(): lax.ppermute(value, 'seq', [(i, i ^ 1) for i in range(CORES * self.size)])  2.85 us
    ppermute x1, starting transfers between devices, body(): lax.ppermute(owner_slot[:, -1:], 'seq', [(i, i + 1) for i in range(device...  2.4 us
  transfers between devices with their start and end apart: 30, of which 11 were waited for; matrix products, arithmetic and copies ran while one was open for 4% of the time, Pallas kernels for 11%

profile of v5, /device:TPU:0, one launch (start us, length us, event | category | flops | bytes accessed | tf_op | source)
XLA Modules:
  0.0 89.1 jit_solution(13483221217163288310)
XLA Ops:
  0.0 1.1 %fusion.8 = (bf16[1,128,896]{2,1,0:T(8,128)(2,1)S(1)}, bf16[1,128,896]{2,1,0:T(8,128)(2,1)S(1)}) fusion(bf16[2,128,896]{2,1,0:T(8,128)(2,1)} %rest_0_.1), kind=kLoop, calls=%fused_computation.27 | loop fusion | bytes 917504 | tf_op jit(solution)/shard_map/slice | solution.py:308
  1.2 3.0 %collective-permute-start.1 = (bf16[1,128,896]{2,1,0:T(8,128)(2,1)S(1)}, bf16[1,128,896]{2,1,0:T(8,128)(2,1)S(1)}, u32[]{:S(2)}, u32[]{:S(2)}) collective-permute-start(bf16[1,128,896]{2,1,0:T(8,128)(2,1)S(1)} %get-tuple-element.74), channel_id=1, source_target_pairs={{0,2},{1,3},{4,0},{5,1},{8,4},{9,5},{12,8},{13,9},{14,12},{15,13},... | collective-permute-start | bytes 688136 | tf_op jit(solution)/shard_map/ppermute | solution.py:299
  4.2 0.1 collective-permute-start
  4.3 0.8 pad_add_fusion
  5.1 2.4 %collective-permute-start.5 = (s32[2,1,2]{1,2,0:T(2,128)S(1)}, s32[2,1,2]{1,2,0:T(2,128)S(1)}, u32[]{:S(2)}, u32[]{:S(2)}) collective-permute-start(s32[2,1,2]{1,2,0:T(2,128)S(1)} %pad_add_fusion), channel_id=1, source_target_pairs={{0,1},{1,2},{2,3},{3,4},{4,5},{5,6},{6,7},{7,8},{8,9},{9,10},{10,1... | collective-permute-start | bytes 56 | tf_op jit(solution)/shard_map/ppermute | solution.py:359
  7.5 1.3 %fusion = s32[]{:T(128)} fusion(s32[8]{0:T(128)} %constant.73.clone, s32[]{:T(128)S(6)} %select_n.51), kind=kLoop, calls=%fused_computation.19 | loop fusion | flops 23 | bytes 40 | tf_op jit(solution)/shard_map/reduce_sum | solution.py:340
  8.8 0.7 and_convert_fusion.keep_ref
  9.5 2.0 %copy-done.2 = bf16[896,2048]{1,0:T(8,128)(2,1)S(1)} copy-done((bf16[896,2048]{1,0:T(8,128)(2,1)S(1)}, bf16[896,2048]{1,0:T(8,128)(2,1)}, u32[]{:S(2)}) %copy-start.2) | copy-done | bytes 3670040
  11.5 1.2 %copy-done.5 = bf16[256,2048]{1,0:T(8,128)(2,1)S(1)} copy-done((bf16[256,2048]{1,0:T(8,128)(2,1)S(1)}, bf16[256,2048]{1,0:T(8,128)(2,1)}, u32[]{:S(2)}) %copy-start.5) | copy-done | bytes 1048600
  12.7 3.6 %fold_queries.1 = (bf16[16,256,896]{2,1,0:T(8,128)(2,1)S(1)}, f32[16,896]{1,0:T(8,128)S(1)}) custom-call(bf16[256,2048]{1,0:T(8,128)(2,1)S(1)} %copy-done.5, bf16[896,2048]{1,0:T(8,128)(2,1)S(1)} %copy-done.2), custom_call_target="tpu_custom_call" | custom-call | flops 939524096 | bytes 8388608 | tf_op jit(solution)/shard_map/fold_queries/pallas_call | solution.py:55
  16.3 2.9 %copy-done = bf16[16,256,896]{2,1,0:T(8,128)(2,1)} copy-done((bf16[16,256,896]{2,1,0:T(8,128)(2,1)}, bf16[16,256,896]{2,1,0:T(8,128)(2,1)S(1)}, u32[]{:S(2)}) %copy-start) | copy-done | bytes 7340056
  19.3 0.1 copy.13
  19.4 0.1 unstack.13
  19.5 0.1 select_reduce_fusion
  19.6 0.1 copy.14
  19.8 2.0 %collective-permute-start.7 = (bf16[1,128,896]{2,1,0:T(8,128)(2,1)S(1)}, bf16[1,128,896]{2,1,0:T(8,128)(2,1)S(1)}, u32[]{:S(2)}, u32[]{:S(2)}) collective-permute-start(bf16[1,128,896]{2,1,0:T(8,128)(2,1)S(1)} %collective-permute-done.1.rest_3_), channel_id=1, source_target_pairs={{0,2},{1,3},{4,0},{5,1},{8,4},{9,5},{12,8},{13,9},{14,12},{15,13},... | collective-permute-start | bytes 688136 | tf_op jit(solution)/shard_map/ppermute | solution.py:299
  21.8 0.1 collective-permute-start.3
  21.9 1.9 %collective-permute-start.4 = (bf16[1,128,896]{2,1,0:T(8,128)(2,1)S(1)}, bf16[1,128,896]{2,1,0:T(8,128)(2,1)S(1)}, u32[]{:S(2)}, u32[]{:S(2)}) collective-permute-start(bf16[1,128,896]{2,1,0:T(8,128)(2,1)S(1)} %get-tuple-element.40), channel_id=1, source_target_pairs={{0,2},{1,3},{4,0},{5,1},{8,4},{9,5},{12,8},{13,9},{14,12},{15,13},... | collective-permute-start | bytes 688136 | tf_op jit(solution)/shard_map/ppermute | solution.py:299
  23.8 0.7 compare_select_fusion.8
  24.4 0.2 collective-permute-start.6
  24.6 3.2 %collective-permute-done.7.rest_7_ = bf16[1,128,896]{2,1,0:T(8,128)(2,1)S(1)} collective-permute-done((bf16[1,128,896]{2,1,0:T(8,128)(2,1)S(1)}, bf16[1,128,896]{2,1,0:T(8,128)(2,1)S(1)}, u32[]{:S(2)}, u32[]{:S(2)}) %collective-permute-start.7) | collective-permute-done | bytes 229408 | tf_op jit(solution)/shard_map/ppermute | solution.py:299
  27.8 2.3 %collective-permute-start.11 = (bf16[1,128,896]{2,1,0:T(8,128)(2,1)S(1)}, bf16[1,128,896]{2,1,0:T(8,128)(2,1)S(1)}, u32[]{:S(2)}, u32[]{:S(2)}) collective-permute-start(bf16[1,128,896]{2,1,0:T(8,128)(2,1)S(1)} %collective-permute-done.7.rest_7_), channel_id=1, source_target_pairs={{0,2},{1,3},{4,0},{5,1},{8,4},{9,5},{12,8},{13,9},{14,12},{15,13},... | collective-permute-start | bytes 688136 | tf_op jit(solution)/shard_map/ppermute | solution.py:299
  30.1 0.1 collective-permute-done.3.rest_4_
  30.2 2.5 %collective-permute-done.4.rest_5_ = bf16[1,128,896]{2,1,0:T(8,128)(2,1)S(1)} collective-permute-done((bf16[1,128,896]{2,1,0:T(8,128)(2,1)S(1)}, bf16[1,128,896]{2,1,0:T(8,128)(2,1)S(1)}, u32[]{:S(2)}, u32[]{:S(2)}) %collective-permute-start.4) | collective-permute-done | bytes 229408 | tf_op jit(solution)/shard_map/ppermute | solution.py:299
  32.7 2.3 %collective-permute-start.8 = (bf16[1,128,896]{2,1,0:T(8,128)(2,1)S(1)}, bf16[1,128,896]{2,1,0:T(8,128)(2,1)S(1)}, u32[]{:S(2)}, u32[]{:S(2)}) collective-permute-start(bf16[1,128,896]{2,1,0:T(8,128)(2,1)S(1)} %collective-permute-done.3.rest_4_), channel_id=1, source_target_pairs={{0,4},{1,5},{4,8},{5,9},{8,12},{9,13},{12,14},{13,15},{14,10},{15,... | collective-permute-start | bytes 688136 | tf_op jit(solution)/shard_map/ppermute | solution.py:299
  35.0 0.2 collective-permute-start.14
  35.2 1.6 %collective-permute-start.10 = (bf16[1,128,896]{2,1,0:T(8,128)(2,1)S(1)}, bf16[1,128,896]{2,1,0:T(8,128)(2,1)S(1)}, u32[]{:S(2)}, u32[]{:S(2)}) collective-permute-start(bf16[1,128,896]{2,1,0:T(8,128)(2,1)S(1)} %collective-permute-done.6.rest_6_), channel_id=1, source_target_pairs={{0,4},{1,5},{4,8},{5,9},{8,12},{9,13},{12,14},{13,15},{14,10},{15,... | collective-permute-start | bytes 688136 | tf_op jit(solution)/shard_map/ppermute | solution.py:299
  36.8 0.4 collective-permute-start.9
  37.2 0.4 collective-permute-done.11.rest_11_
  37.7 0.6 collective-permute-start.15
  38.3 3.2 %collective-permute-done.8.rest_8_ = bf16[1,128,896]{2,1,0:T(8,128)(2,1)S(1)} collective-permute-done((bf16[1,128,896]{2,1,0:T(8,128)(2,1)S(1)}, bf16[1,128,896]{2,1,0:T(8,128)(2,1)S(1)}, u32[]{:S(2)}, u32[]{:S(2)}) %collective-permute-start.8) | collective-permute-done | bytes 229408 | tf_op jit(solution)/shard_map/ppermute | solution.py:299
  41.5 0.5 collective-permute-start.17
  42.0 4.3 %collective-permute-done.10.rest_10_ = bf16[1,128,896]{2,1,0:T(8,128)(2,1)S(1)} collective-permute-done((bf16[1,128,896]{2,1,0:T(8,128)(2,1)S(1)}, bf16[1,128,896]{2,1,0:T(8,128)(2,1)S(1)}, u32[]{:S(2)}, u32[]{:S(2)}) %collective-permute-start.10) | collective-permute-done | bytes 229408 | tf_op jit(solution)/shard_map/ppermute | solution.py:299
  46.2 1.7 %collective-permute-start.12 = (bf16[1,128,896]{2,1,0:T(8,128)(2,1)S(1)}, bf16[1,128,896]{2,1,0:T(8,128)(2,1)S(1)}, u32[]{:S(2)}, u32[]{:S(2)}) collective-permute-start(bf16[1,128,896]{2,1,0:T(8,128)(2,1)S(1)} %collective-permute-done.8.rest_8_), channel_id=1, source_target_pairs={{0,4},{1,5},{4,8},{5,9},{8,12},{9,13},{12,14},{13,15},{14,10},{15,... | collective-permute-start | bytes 688136 | tf_op jit(solution)/shard_map/ppermute | solution.py:299
  47.9 0.4 collective-permute-start.13
  48.3 1.7 %collective-permute-start.24 = (bf16[1,128,896]{2,1,0:T(8,128)(2,1)S(1)}, bf16[1,128,896]{2,1,0:T(8,128)(2,1)S(1)}, u32[]{:S(2)}, u32[]{:S(2)}) collective-permute-start(bf16[1,128,896]{2,1,0:T(8,128)(2,1)S(1)} %collective-permute-done.10.rest_10_), channel_id=1, source_target_pairs={{0,4},{1,5},{4,8},{5,9},{8,12},{9,13},{12,14},{13,15},{14,10},{15,... | collective-permute-start | bytes 688136 | tf_op jit(solution)/shard_map/ppermute | solution.py:299
  50.0 0.2 collective-permute-start.19
  50.2 4.5 %collective-permute-done.12.rest_12_ = bf16[1,128,896]{2,1,0:T(8,128)(2,1)S(1)} collective-permute-done((bf16[1,128,896]{2,1,0:T(8,128)(2,1)S(1)}, bf16[1,128,896]{2,1,0:T(8,128)(2,1)S(1)}, u32[]{:S(2)}, u32[]{:S(2)}) %collective-permute-start.12) | collective-permute-done | bytes 229408 | tf_op jit(solution)/shard_map/ppermute | solution.py:299
  54.8 1.6 %collective-permute-start.27 = (bf16[1,128,896]{2,1,0:T(8,128)(2,1)S(1)}, bf16[1,128,896]{2,1,0:T(8,128)(2,1)S(1)}, u32[]{:S(2)}, u32[]{:S(2)}) collective-permute-start(bf16[1,128,896]{2,1,0:T(8,128)(2,1)S(1)} %collective-permute-done.13.rest_13_), channel_id=1, source_target_pairs={{0,2},{1,3},{4,0},{5,1},{8,4},{9,5},{12,8},{13,9},{14,12},{15,13},... | collective-permute-start | bytes 688136 | tf_op jit(solution)/shard_map/ppermute | solution.py:299
  56.4 0.2 collective-permute-start.21
  56.6 2.0 %collective-permute-done.24.rest_0_ = bf16[1,128,896]{2,1,0:T(8,128)(2,1)S(1)} collective-permute-done((bf16[1,128,896]{2,1,0:T(8,128)(2,1)S(1)}, bf16[1,128,896]{2,1,0:T(8,128)(2,1)S(1)}, u32[]{:S(2)}, u32[]{:S(2)}) %collective-permute-start.24) | collective-permute-done | bytes 229408 | tf_op jit(solution)/shard_map/ppermute | solution.py:299
  58.7 0.5 collective-permute-start.23
  59.2 3.5 %collective-permute-done.27.rest_1_ = bf16[1,128,896]{2,1,0:T(8,128)(2,1)S(1)} collective-permute-done((bf16[1,128,896]{2,1,0:T(8,128)(2,1)S(1)}, bf16[1,128,896]{2,1,0:T(8,128)(2,1)S(1)}, u32[]{:S(2)}, u32[]{:S(2)}) %collective-permute-start.27) | collective-permute-done | bytes 229408 | tf_op jit(solution)/shard_map/ppermute | solution.py:299
  62.8 0.5 collective-permute-start.28
  63.3 0.9 %collective-permute-done.26.rest_25_ = bf16[1,128,896]{2,1,0:T(8,128)(2,1)S(1)} collective-permute-done((bf16[1,128,896]{2,1,0:T(8,128)(2,1)S(1)}, bf16[1,128,896]{2,1,0:T(8,128)(2,1)S(1)}, u32[]{:S(2)}, u32[]{:S(2)}) %collective-permute-start.26) | collective-permute-done | bytes 229408 | tf_op jit(solution)/shard_map/ppermute | solution.py:302
  64.2 6.4 %collect_early.1 = (bf16[10,128,896]{2,1,0:T(8,128)(2,1)S(1)}, bf16[10,896,128]{2,1,0:T(8,128)(2,1)S(1)}) custom-call(s32[10]{0:T(128)S(1)} %compare_select_fusion.9.source_ref, s32[10]{0:T(128)S(1)} %get-tuple-element.44.block_ref, bf16[2,128,896]{2,1,0:T(8,128)(2,1)S(1)} %copy-done.4, bf16[2,128,896]{2,1,0:T(8,128)(2,1)S(1)} %collective-permute-done.2.rest_1_, ...), custom_call_target="tpu_custom_call" | custom-call | flops 4194304 | bytes 8388608 | tf_op jit(solution)/shard_map/collect_early/pallas_call | solution.py:118
  70.7 3.1 %copy-done.1 = bf16[16,256,896]{2,1,0:T(8,128)(2,1)S(1)} copy-done((bf16[16,256,896]{2,1,0:T(8,128)(2,1)S(1)}, bf16[16,256,896]{2,1,0:T(8,128)(2,1)}, u32[]{:S(2)}) %copy-start.1) | copy-done | bytes 7340056
  73.8 15.1 %attend_windows.1 = bf16[256,2048]{1,0:T(8,128)(2,1)} custom-call(s32[10]{0:T(128)S(1)} %compare_select_fusion.9.source_ref, s32[10]{0:T(128)S(1)} %get-tuple-element.44.block_ref, s32[4]{0:T(128)S(1)} %and_convert_fusion.keep_ref, bf16[16,256,896]{2,1,0:T(8,128)(2,1)S(1)} %copy-done.1, f32[16,896]{1,0:T(8,128)S(1)} %get-tuple-element.47.single_ref, ...), custom_call_target="tpu_custom_call" | custom-call | flops 4697620480 | bytes 16777216 | tf_op jit(solution)/shard_map/attend_windows/pallas_call | solution.py:246
  (47 shorter events, 0.5 us)
Async XLA Ops:
  0.0 19.5 %copy-start.8 = (s32[8]{0:T(128)S(1)}, s32[8]{0:T(128)}, u32[]{:S(2)}) copy-start(s32[8]{0:T(128)} %constant.73.clone) | copy-start | bytes 100
  0.0 64.2 %copy-start.4 = (bf16[2,128,896]{2,1,0:T(8,128)(2,1)S(1)}, bf16[2,128,896]{2,1,0:T(8,128)(2,1)}, u32[]{:S(2)}) copy-start(bf16[2,128,896]{2,1,0:T(8,128)(2,1)} %rest_0_.1) | copy-start | bytes 1376260
  0.0 19.2 %copy-start.6 = (s32[4,2]{0,1:T(2,128)S(1)}, s32[4,2]{0,1:T(2,128)}, u32[]{:S(2)}) copy-start(s32[4,2]{0,1:T(2,128)} %param.13) | copy-start | bytes 100
  0.0 19.2 %copy-start.7 = (s32[4,2]{0,1:T(2,128)S(1)}, s32[4,2]{0,1:T(2,128)}, u32[]{:S(2)}) copy-start(s32[4,2]{0,1:T(2,128)} %param.12) | copy-start | bytes 100
  1.2 18.6 %collective-permute-start.1 = (bf16[1,128,896]{2,1,0:T(8,128)(2,1)S(1)}, bf16[1,128,896]{2,1,0:T(8,128)(2,1)S(1)}, u32[]{:S(2)}, u32[]{:S(2)}) collective-permute-start(bf16[1,128,896]{2,1,0:T(8,128)(2,1)S(1)} %get-tuple-element.74), channel_id=1, source_target_pairs={{0,2},{1,3},{4,0},{5,1},{8,4},{9,5},{12,8},{13,9},{14,12},{15,13},... | collective-permute-start | bytes 688136 | tf_op jit(solution)/shard_map/ppermute | solution.py:299
  4.2 20.3 %collective-permute-start = (bf16[1,128,896]{2,1,0:T(8,128)(2,1)S(1)}, bf16[1,128,896]{2,1,0:T(8,128)(2,1)S(1)}, u32[]{:S(2)}, u32[]{:S(2)}) collective-permute-start(bf16[1,128,896]{2,1,0:T(8,128)(2,1)S(1)} %get-tuple-element.74), channel_id=1, source_target_pairs={{0,4},{1,5},{4,8},{5,9},{8,12},{9,13},{12,14},{13,15},{14,10},{15,... | collective-permute-start | bytes 688136 | tf_op jit(solution)/shard_map/ppermute | solution.py:299
  4.3 17.4 %collective-permute-start.2 = (bf16[2,128,896]{2,1,0:T(8,128)(2,1)}, bf16[2,128,896]{2,1,0:T(8,128)(2,1)S(1)}, u32[]{:S(2)}, u32[]{:S(2)}) collective-permute-start(bf16[2,128,896]{2,1,0:T(8,128)(2,1)} %rest_0_.1), channel_id=1, source_target_pairs={{0,1},{1,0},{2,3},{3,2},{4,5},{5,4},{6,7},{7,6},{8,9},{9,8},{10,11... | collective-permute-start | bytes 1376264 | tf_op jit(solution)/shard_map/ppermute | solution.py:302
  5.1 14.2 %collective-permute-start.5 = (s32[2,1,2]{1,2,0:T(2,128)S(1)}, s32[2,1,2]{1,2,0:T(2,128)S(1)}, u32[]{:S(2)}, u32[]{:S(2)}) collective-permute-start(s32[2,1,2]{1,2,0:T(2,128)S(1)} %pad_add_fusion), channel_id=1, source_target_pairs={{0,1},{1,2},{2,3},{3,4},{4,5},{5,6},{6,7},{7,8},{8,9},{9,10},{10,1... | collective-permute-start | bytes 56 | tf_op jit(solution)/shard_map/ppermute | solution.py:359
  9.5 2.0 %copy-start.2 = (bf16[896,2048]{1,0:T(8,128)(2,1)S(1)}, bf16[896,2048]{1,0:T(8,128)(2,1)}, u32[]{:S(2)}) copy-start(bf16[896,2048]{1,0:T(8,128)(2,1)} %key_hbm.1) | copy-start | bytes 11010052
  11.5 1.2 %copy-start.5 = (bf16[256,2048]{1,0:T(8,128)(2,1)S(1)}, bf16[256,2048]{1,0:T(8,128)(2,1)}, u32[]{:S(2)}) copy-start(bf16[256,2048]{1,0:T(8,128)(2,1)} %query_ref.1) | copy-start | bytes 3145732
  16.3 2.9 %copy-start = (bf16[16,256,896]{2,1,0:T(8,128)(2,1)}, bf16[16,256,896]{2,1,0:T(8,128)(2,1)S(1)}, u32[]{:S(2)}) copy-start(bf16[16,256,896]{2,1,0:T(8,128)(2,1)S(1)} %get-tuple-element.46.folded_ref) | copy-start | bytes 22020100
  19.8 50.9 %copy-start.3 = (bf16[896,2048]{1,0:T(8,128)(2,1)S(1)}, bf16[896,2048]{1,0:T(8,128)(2,1)}, u32[]{:S(2)}) copy-start(bf16[896,2048]{1,0:T(8,128)(2,1)} %value_ref.1) | copy-start | bytes 11010052
  19.8 8.0 %collective-permute-start.7 = (bf16[1,128,896]{2,1,0:T(8,128)(2,1)S(1)}, bf16[1,128,896]{2,1,0:T(8,128)(2,1)S(1)}, u32[]{:S(2)}, u32[]{:S(2)}) collective-permute-start(bf16[1,128,896]{2,1,0:T(8,128)(2,1)S(1)} %collective-permute-done.1.rest_3_), channel_id=1, source_target_pairs={{0,2},{1,3},{4,0},{5,1},{8,4},{9,5},{12,8},{13,9},{14,12},{15,13},... | collective-permute-start | bytes 688136 | tf_op jit(solution)/shard_map/ppermute | solution.py:299
  21.8 8.5 %collective-permute-start.3 = (bf16[1,128,896]{2,1,0:T(8,128)(2,1)S(1)}, bf16[1,128,896]{2,1,0:T(8,128)(2,1)S(1)}, u32[]{:S(2)}, u32[]{:S(2)}) collective-permute-start(bf16[1,128,896]{2,1,0:T(8,128)(2,1)S(1)} %get-tuple-element.40), channel_id=1, source_target_pairs={{0,4},{1,5},{4,8},{5,9},{8,12},{9,13},{12,14},{13,15},{14,10},{15,... | collective-permute-start | bytes 688136 | tf_op jit(solution)/shard_map/ppermute | solution.py:299
  21.9 10.9 %collective-permute-start.4 = (bf16[1,128,896]{2,1,0:T(8,128)(2,1)S(1)}, bf16[1,128,896]{2,1,0:T(8,128)(2,1)S(1)}, u32[]{:S(2)}, u32[]{:S(2)}) collective-permute-start(bf16[1,128,896]{2,1,0:T(8,128)(2,1)S(1)} %get-tuple-element.40), channel_id=1, source_target_pairs={{0,2},{1,3},{4,0},{5,1},{8,4},{9,5},{12,8},{13,9},{14,12},{15,13},... | collective-permute-start | bytes 688136 | tf_op jit(solution)/shard_map/ppermute | solution.py:299
  24.4 10.7 %collective-permute-start.6 = (bf16[1,128,896]{2,1,0:T(8,128)(2,1)S(1)}, bf16[1,128,896]{2,1,0:T(8,128)(2,1)S(1)}, u32[]{:S(2)}, u32[]{:S(2)}) collective-permute-start(bf16[1,128,896]{2,1,0:T(8,128)(2,1)S(1)} %collective-permute-done.rest_2_), channel_id=1, source_target_pairs={{0,4},{1,5},{4,8},{5,9},{8,12},{9,13},{12,14},{13,15},{14,10},{15,... | collective-permute-start | bytes 688136 | tf_op jit(solution)/shard_map/ppermute | solution.py:299
  27.8 9.8 %collective-permute-start.11 = (bf16[1,128,896]{2,1,0:T(8,128)(2,1)S(1)}, bf16[1,128,896]{2,1,0:T(8,128)(2,1)S(1)}, u32[]{:S(2)}, u32[]{:S(2)}) collective-permute-start(bf16[1,128,896]{2,1,0:T(8,128)(2,1)S(1)} %collective-permute-done.7.rest_7_), channel_id=1, source_target_pairs={{0,2},{1,3},{4,0},{5,1},{8,4},{9,5},{12,8},{13,9},{14,12},{15,13},... | collective-permute-start | bytes 688136 | tf_op jit(solution)/shard_map/ppermute | solution.py:299
  32.7 8.7 %collective-permute-start.8 = (bf16[1,128,896]{2,1,0:T(8,128)(2,1)S(1)}, bf16[1,128,896]{2,1,0:T(8,128)(2,1)S(1)}, u32[]{:S(2)}, u32[]{:S(2)}) collective-permute-start(bf16[1,128,896]{2,1,0:T(8,128)(2,1)S(1)} %collective-permute-done.3.rest_4_), channel_id=1, source_target_pairs={{0,4},{1,5},{4,8},{5,9},{8,12},{9,13},{12,14},{13,15},{14,10},{15,... | collective-permute-start | bytes 688136 | tf_op jit(solution)/shard_map/ppermute | solution.py:299
  35.0 6.4 %collective-permute-start.14 = (bf16[1,128,896]{2,1,0:T(8,128)(2,1)S(1)}, bf16[1,128,896]{2,1,0:T(8,128)(2,1)S(1)}, u32[]{:S(2)}, u32[]{:S(2)}) collective-permute-start(bf16[1,128,896]{2,1,0:T(8,128)(2,1)S(1)} %collective-permute-done.rest_2_), channel_id=1, source_target_pairs={{0,1},{1,0},{2,3},{3,2},{4,5},{5,4},{6,7},{7,6},{8,9},{9,8},{10,11... | collective-permute-start | bytes 688136 | tf_op jit(solution)/shard_map/ppermute | solution.py:302
  35.2 11.0 %collective-permute-start.10 = (bf16[1,128,896]{2,1,0:T(8,128)(2,1)S(1)}, bf16[1,128,896]{2,1,0:T(8,128)(2,1)S(1)}, u32[]{:S(2)}, u32[]{:S(2)}) collective-permute-start(bf16[1,128,896]{2,1,0:T(8,128)(2,1)S(1)} %collective-permute-done.6.rest_6_), channel_id=1, source_target_pairs={{0,4},{1,5},{4,8},{5,9},{8,12},{9,13},{12,14},{13,15},{14,10},{15,... | collective-permute-start | bytes 688136 | tf_op jit(solution)/shard_map/ppermute | solution.py:299
  36.8 11.1 %collective-permute-start.9 = (bf16[1,128,896]{2,1,0:T(8,128)(2,1)S(1)}, bf16[1,128,896]{2,1,0:T(8,128)(2,1)S(1)}, u32[]{:S(2)}, u32[]{:S(2)}) collective-permute-start(bf16[1,128,896]{2,1,0:T(8,128)(2,1)S(1)} %collective-permute-done.4.rest_5_), channel_id=1, source_target_pairs={{0,2},{1,3},{4,0},{5,1},{8,4},{9,5},{12,8},{13,9},{14,12},{15,13},... | collective-permute-start | bytes 688136 | tf_op jit(solution)/shard_map/ppermute | solution.py:299
  37.7 10.6 %collective-permute-start.15 = (bf16[1,128,896]{2,1,0:T(8,128)(2,1)S(1)}, bf16[1,128,896]{2,1,0:T(8,128)(2,1)S(1)}, u32[]{:S(2)}, u32[]{:S(2)}) collective-permute-start(bf16[1,128,896]{2,1,0:T(8,128)(2,1)S(1)} %collective-permute-done.1.rest_3_), channel_id=1, source_target_pairs={{0,1},{1,0},{2,3},{3,2},{4,5},{5,4},{6,7},{7,6},{8,9},{9,8},{10,11... | collective-permute-start | bytes 688136 | tf_op jit(solution)/shard_map/ppermute | solution.py:302
  41.5 6.8 %collective-permute-start.16 = (bf16[1,128,896]{2,1,0:T(8,128)(2,1)S(1)}, bf16[1,128,896]{2,1,0:T(8,128)(2,1)S(1)}, u32[]{:S(2)}, u32[]{:S(2)}) collective-permute-start(bf16[1,128,896]{2,1,0:T(8,128)(2,1)S(1)} %collective-permute-done.3.rest_4_), channel_id=1, source_target_pairs={{0,1},{1,0},{2,3},{3,2},{4,5},{5,4},{6,7},{7,6},{8,9},{9,8},{10,11... | collective-permute-start | bytes 688136 | tf_op jit(solution)/shard_map/ppermute | solution.py:302
  41.5 8.5 %collective-permute-start.17 = (bf16[1,128,896]{2,1,0:T(8,128)(2,1)S(1)}, bf16[1,128,896]{2,1,0:T(8,128)(2,1)S(1)}, u32[]{:S(2)}, u32[]{:S(2)}) collective-permute-start(bf16[1,128,896]{2,1,0:T(8,128)(2,1)S(1)} %collective-permute-done.4.rest_5_), channel_id=1, source_target_pairs={{0,1},{1,0},{2,3},{3,2},{4,5},{5,4},{6,7},{7,6},{8,9},{9,8},{10,11... | collective-permute-start | bytes 688136 | tf_op jit(solution)/shard_map/ppermute | solution.py:302
  46.2 8.5 %collective-permute-start.12 = (bf16[1,128,896]{2,1,0:T(8,128)(2,1)S(1)}, bf16[1,128,896]{2,1,0:T(8,128)(2,1)S(1)}, u32[]{:S(2)}, u32[]{:S(2)}) collective-permute-start(bf16[1,128,896]{2,1,0:T(8,128)(2,1)S(1)} %collective-permute-done.8.rest_8_), channel_id=1, source_target_pairs={{0,4},{1,5},{4,8},{5,9},{8,12},{9,13},{12,14},{13,15},{14,10},{15,... | collective-permute-start | bytes 688136 | tf_op jit(solution)/shard_map/ppermute | solution.py:299
  47.9 6.9 %collective-permute-start.13 = (bf16[1,128,896]{2,1,0:T(8,128)(2,1)S(1)}, bf16[1,128,896]{2,1,0:T(8,128)(2,1)S(1)}, u32[]{:S(2)}, u32[]{:S(2)}) collective-permute-start(bf16[1,128,896]{2,1,0:T(8,128)(2,1)S(1)} %collective-permute-done.9.rest_9_), channel_id=1, source_target_pairs={{0,2},{1,3},{4,0},{5,1},{8,4},{9,5},{12,8},{13,9},{14,12},{15,13},... | collective-permute-start | bytes 688136 | tf_op jit(solution)/shard_map/ppermute | solution.py:299
  48.3 8.1 %collective-permute-start.18 = (bf16[1,128,896]{2,1,0:T(8,128)(2,1)S(1)}, bf16[1,128,896]{2,1,0:T(8,128)(2,1)S(1)}, u32[]{:S(2)}, u32[]{:S(2)}) collective-permute-start(bf16[1,128,896]{2,1,0:T(8,128)(2,1)S(1)} %collective-permute-done.6.rest_6_), channel_id=1, source_target_pairs={{0,1},{1,0},{2,3},{3,2},{4,5},{5,4},{6,7},{7,6},{8,9},{9,8},{10,11... | collective-permute-start | bytes 688136 | tf_op jit(solution)/shard_map/ppermute | solution.py:302
  48.3 10.4 %collective-permute-start.24 = (bf16[1,128,896]{2,1,0:T(8,128)(2,1)S(1)}, bf16[1,128,896]{2,1,0:T(8,128)(2,1)S(1)}, u32[]{:S(2)}, u32[]{:S(2)}) collective-permute-start(bf16[1,128,896]{2,1,0:T(8,128)(2,1)S(1)} %collective-permute-done.10.rest_10_), channel_id=1, source_target_pairs={{0,4},{1,5},{4,8},{5,9},{8,12},{9,13},{12,14},{13,15},{14,10},{15,... | collective-permute-start | bytes 688136 | tf_op jit(solution)/shard_map/ppermute | solution.py:299
  50.0 8.7 %collective-permute-start.19 = (bf16[1,128,896]{2,1,0:T(8,128)(2,1)S(1)}, bf16[1,128,896]{2,1,0:T(8,128)(2,1)S(1)}, u32[]{:S(2)}, u32[]{:S(2)}) collective-permute-start(bf16[1,128,896]{2,1,0:T(8,128)(2,1)S(1)} %collective-permute-done.7.rest_7_), channel_id=1, source_target_pairs={{0,1},{1,0},{2,3},{3,2},{4,5},{5,4},{6,7},{7,6},{8,9},{9,8},{10,11... | collective-permute-start | bytes 688136 | tf_op jit(solution)/shard_map/ppermute | solution.py:302
  54.7 4.5 %collective-permute-start.20 = (bf16[1,128,896]{2,1,0:T(8,128)(2,1)S(1)}, bf16[1,128,896]{2,1,0:T(8,128)(2,1)S(1)}, u32[]{:S(2)}, u32[]{:S(2)}) collective-permute-start(bf16[1,128,896]{2,1,0:T(8,128)(2,1)S(1)} %collective-permute-done.8.rest_8_), channel_id=1, source_target_pairs={{0,1},{1,0},{2,3},{3,2},{4,5},{5,4},{6,7},{7,6},{8,9},{9,8},{10,11... | collective-permute-start | bytes 688136 | tf_op jit(solution)/shard_map/ppermute | solution.py:302
  54.8 8.0 %collective-permute-start.27 = (bf16[1,128,896]{2,1,0:T(8,128)(2,1)S(1)}, bf16[1,128,896]{2,1,0:T(8,128)(2,1)S(1)}, u32[]{:S(2)}, u32[]{:S(2)}) collective-permute-start(bf16[1,128,896]{2,1,0:T(8,128)(2,1)S(1)} %collective-permute-done.13.rest_13_), channel_id=1, source_target_pairs={{0,2},{1,3},{4,0},{5,1},{8,4},{9,5},{12,8},{13,9},{14,12},{15,13},... | collective-permute-start | bytes 688136 | tf_op jit(solution)/shard_map/ppermute | solution.py:299
  56.4 6.4 %collective-permute-start.21 = (bf16[1,128,896]{2,1,0:T(8,128)(2,1)S(1)}, bf16[1,128,896]{2,1,0:T(8,128)(2,1)S(1)}, u32[]{:S(2)}, u32[]{:S(2)}) collective-permute-start(bf16[1,128,896]{2,1,0:T(8,128)(2,1)S(1)} %collective-permute-done.9.rest_9_), channel_id=1, source_target_pairs={{0,1},{1,0},{2,3},{3,2},{4,5},{5,4},{6,7},{7,6},{8,9},{9,8},{10,11... | collective-permute-start | bytes 688136 | tf_op jit(solution)/shard_map/ppermute | solution.py:302
  58.7 4.6 %collective-permute-start.22 = (bf16[1,128,896]{2,1,0:T(8,128)(2,1)S(1)}, bf16[1,128,896]{2,1,0:T(8,128)(2,1)S(1)}, u32[]{:S(2)}, u32[]{:S(2)}) collective-permute-start(bf16[1,128,896]{2,1,0:T(8,128)(2,1)S(1)} %collective-permute-done.10.rest_10_), channel_id=1, source_target_pairs={{0,1},{1,0},{2,3},{3,2},{4,5},{5,4},{6,7},{7,6},{8,9},{9,8},{10,11... | collective-permute-start | bytes 688136 | tf_op jit(solution)/shard_map/ppermute | solution.py:302
  58.7 4.7 %collective-permute-start.23 = (bf16[1,128,896]{2,1,0:T(8,128)(2,1)S(1)}, bf16[1,128,896]{2,1,0:T(8,128)(2,1)S(1)}, u32[]{:S(2)}, u32[]{:S(2)}) collective-permute-start(bf16[1,128,896]{2,1,0:T(8,128)(2,1)S(1)} %collective-permute-done.11.rest_11_), channel_id=1, source_target_pairs={{0,1},{1,0},{2,3},{3,2},{4,5},{5,4},{6,7},{7,6},{8,9},{9,8},{10,11... | collective-permute-start | bytes 688136 | tf_op jit(solution)/shard_map/ppermute | solution.py:302
  59.2 4.2 %collective-permute-start.25 = (bf16[1,128,896]{2,1,0:T(8,128)(2,1)S(1)}, bf16[1,128,896]{2,1,0:T(8,128)(2,1)S(1)}, u32[]{:S(2)}, u32[]{:S(2)}) collective-permute-start(bf16[1,128,896]{2,1,0:T(8,128)(2,1)S(1)} %collective-permute-done.12.rest_12_), channel_id=1, source_target_pairs={{0,1},{1,0},{2,3},{3,2},{4,5},{5,4},{6,7},{7,6},{8,9},{9,8},{10,11... | collective-permute-start | bytes 688136 | tf_op jit(solution)/shard_map/ppermute | solution.py:302
  62.8 1.5 %collective-permute-start.26 = (bf16[1,128,896]{2,1,0:T(8,128)(2,1)S(1)}, bf16[1,128,896]{2,1,0:T(8,128)(2,1)S(1)}, u32[]{:S(2)}, u32[]{:S(2)}) collective-permute-start(bf16[1,128,896]{2,1,0:T(8,128)(2,1)S(1)} %collective-permute-done.13.rest_13_), channel_id=1, source_target_pairs={{0,1},{1,0},{2,3},{3,2},{4,5},{5,4},{6,7},{7,6},{8,9},{9,8},{10,11... | collective-permute-start | bytes 688136 | tf_op jit(solution)/shard_map/ppermute | solution.py:302
  62.8 7.9 %collective-permute-start.28 = (bf16[1,128,896]{2,1,0:T(8,128)(2,1)S(1)}, bf16[1,128,896]{2,1,0:T(8,128)(2,1)S(1)}, u32[]{:S(2)}, u32[]{:S(2)}) collective-permute-start(bf16[1,128,896]{2,1,0:T(8,128)(2,1)S(1)} %collective-permute-done.24.rest_0_), channel_id=1, source_target_pairs={{0,1},{1,0},{2,3},{3,2},{4,5},{5,4},{6,7},{7,6},{8,9},{9,8},{10,11... | collective-permute-start | bytes 688136 | tf_op jit(solution)/shard_map/ppermute | solution.py:302
  63.3 7.4 %collective-permute-start.29 = (bf16[1,128,896]{2,1,0:T(8,128)(2,1)S(1)}, bf16[1,128,896]{2,1,0:T(8,128)(2,1)S(1)}, u32[]{:S(2)}, u32[]{:S(2)}) collective-permute-start(bf16[1,128,896]{2,1,0:T(8,128)(2,1)S(1)} %collective-permute-done.27.rest_1_), channel_id=1, source_target_pairs={{0,1},{1,0},{2,3},{3,2},{4,5},{5,4},{6,7},{7,6},{8,9},{9,8},{10,11... | collective-permute-start | bytes 688136 | tf_op jit(solution)/shard_map/ppermute | solution.py:302
  70.7 3.1 %copy-start.1 = (bf16[16,256,896]{2,1,0:T(8,128)(2,1)S(1)}, bf16[16,256,896]{2,1,0:T(8,128)(2,1)}, u32[]{:S(2)}) copy-start(bf16[16,256,896]{2,1,0:T(8,128)(2,1)} %copy-done) | copy-start | bytes 22020100

commit v6 on v5

v6 whole, which is shorter than its diff:
```python
import functools
import math

import jax
import jax.numpy as jnp
from jax import lax
from jax.experimental import pallas as pl
from jax.experimental.pallas import tpu as pltpu
from jax.sharding import PartitionSpec as P

SPAN = 64
HEADS = 16
HEAD_DIM = 128
EPS = 1e-6
SCALE = math.log2(math.e) / math.sqrt(HEAD_DIM)
CORES = 2
GROUP = 4
MIB = 2**20


SMEM_SPEC = pl.BlockSpec(memory_space=pltpu.SMEM)
VMEM_SPEC = pl.BlockSpec(memory_space=pltpu.VMEM)
ANY_SPEC = pl.BlockSpec(memory_space=pl.ANY)
HBM_SPEC = pl.BlockSpec(memory_space=pltpu.HBM)


def contract(left, right, dims):
    return lax.dot_general(left, right, (dims, ((), ())), preferred_element_type=jnp.float32)


def in_hbm(value):
    return pltpu.with_memory_space_constraint(value, pltpu.HBM)


def head_columns(head):
    return slice(head * HEAD_DIM, (head + 1) * HEAD_DIM)


def fold_kernel(query_hbm, key_hbm, folded_hbm, single_ref, query, key, folded, in_sems, out_sems):
    groups = HEADS // GROUP

    def fetch(group):
        columns = slice(group * GROUP * HEAD_DIM, (group + 1) * GROUP * HEAD_DIM)
        return (
            pltpu.make_async_copy(query_hbm.at[:, columns], query.at[:, columns], in_sems.at[group, 0]),
            pltpu.make_async_copy(key_hbm.at[:, columns], key.at[:, columns], in_sems.at[group, 1]),
        )

    def put(head):
        return pltpu.make_async_copy(folded.at[head], folded_hbm.at[head], out_sems.at[head])

    for group in range(groups):
        for copy in fetch(group):
            copy.start()
    for head in range(HEADS):
        if head % GROUP == 0:
            for copy in fetch(head // GROUP):
                copy.wait()
        columns = head_columns(head)
        queries = pltpu.roll(query[:, columns].astype(jnp.float32), 1, 0).astype(jnp.bfloat16)
        rows = contract(queries, key[:, columns], ((1,), (1,))) * SCALE
        single_ref[head : head + 1, :] = rows[:1]
        folded[head] = rows.astype(jnp.bfloat16)
        put(head).start()
    for head in range(HEADS):
        put(head).wait()


def fold(queries, w_key):
    count, width = queries.shape[0], w_key.shape[0]
    shape = (HEADS, count, width)
    return pl.pallas_call(
        fold_kernel,
        out_shape=(
            pltpu.HBM(shape, jnp.bfloat16),
            jax.ShapeDtypeStruct((HEADS, width), jnp.float32),
        ),
        in_specs=[HBM_SPEC] * 2,
        out_specs=(HBM_SPEC, VMEM_SPEC),
        scratch_shapes=[
            pltpu.VMEM(queries.shape, jnp.bfloat16),
            pltpu.VMEM(w_key.shape, jnp.bfloat16),
            pltpu.VMEM(shape, jnp.bfloat16),
            pltpu.SemaphoreType.DMA((HEADS // GROUP, 2)),
            pltpu.SemaphoreType.DMA((HEADS,)),
        ],
        compiler_params=pltpu.CompilerParams(vmem_limit_bytes=28 * MIB),
        cost_estimate=pl.CostEstimate(
            flops=2 * queries.size * width, bytes_accessed=12 * MIB, transcendentals=0
        ),
        name="fold_queries",
    )(in_hbm(queries), in_hbm(w_key))


def normalise(raw, tokens_ref):
    widened = raw.astype(jnp.float32)
    factor = lax.rsqrt(jnp.mean(widened * widened, axis=-1, keepdims=True) + EPS)
    tokens_ref[...] = (widened * factor).astype(jnp.bfloat16)


def among(stores, first, source, act):
    if len(stores) == 1:
        pl.when(source == first)(lambda: act(stores[0]))
        return
    half = len(stores) // 2
    pl.when(source < first + half)(lambda: among(stores[:half], first, source, act))
    pl.when(source >= first + half)(lambda: among(stores[half:], first + half, source, act))


def collect_kernel(first, source_ref, block_ref, *rest):
    *stores, tokens_ref, raw, sems = rest
    before_ref = stores.pop() if first else None
    requests = raw.shape[0]

    def fetch(request, store):
        return pltpu.make_async_copy(store.at[block_ref[request]], raw.at[request], sems.at[request])

    def begin(request, carry):
        among(stores, first, source_ref[request], lambda store: fetch(request, store).start())
        return carry

    def finish(request, carry):
        source = source_ref[request]
        here = (source >= first) & (source < first + len(stores))

        @pl.when(here)
        def _():
            fetch(request, stores[0]).wait()
            normalise(raw[request], tokens_ref.at[request])

        if before_ref is not None:

            @pl.when(jnp.logical_not(here))
            def _():
                tokens_ref[request] = before_ref[request]

        return carry

    lax.fori_loop(0, requests, begin, 0)
    lax.fori_loop(0, requests, finish, 0)


def collect(first, source, block, stores, before):
    requests = source.shape[0]
    length, width = stores[0].shape[1:]
    shape = (requests, length, width)
    before = [before] if first else []
    return pl.pallas_call(
        functools.partial(collect_kernel, first),
        out_shape=jax.ShapeDtypeStruct(shape, jnp.bfloat16),
        in_specs=[SMEM_SPEC] * 2 + [ANY_SPEC] * len(stores) + [VMEM_SPEC] * len(before),
        out_specs=VMEM_SPEC,
        scratch_shapes=[pltpu.VMEM(shape, jnp.bfloat16), pltpu.SemaphoreType.DMA((requests,))],
        compiler_params=pltpu.CompilerParams(vmem_limit_bytes=16 * MIB),
        cost_estimate=pl.CostEstimate(flops=4 * MIB, bytes_accessed=8 * MIB, transcendentals=0),
        name="collect_blocks",
    )(source, block, *stores, *before)


def weigh(scores):
    powers = jnp.exp2(scores - jnp.max(scores, axis=-1, keepdims=True))
    totals = jnp.sum(powers, axis=-1, keepdims=True)
    return (powers * (1.0 / totals)).astype(jnp.bfloat16)


def attend_kernel(
    early, source_ref, block_ref, keep_ref, folded_hbm, single_ref, tokens_in, value_ref, *rest
):
    *late, out_ref, tokens, raw, folded, scores, weights, mixed, sems, folded_sems = rest
    requests, length, width = raw.shape
    blocks = requests // 2 - 1
    count = blocks * SPAN
    rows_at_once = GROUP * SPAN

    def fetch_folded(group):
        heads = pl.ds(group * GROUP, GROUP)
        return pltpu.make_async_copy(folded_hbm.at[heads], folded.at[heads], folded_sems.at[group])

    def fetch_late(request, store):
        return pltpu.make_async_copy(store.at[block_ref[request]], raw.at[request], sems.at[request])

    def begin(request, carry):
        among(late, early, source_ref[request], lambda store: fetch_late(request, store).start())
        return carry

    def finish(request, carry):
        @pl.when(source_ref[request] < early)
        def _():
            tokens[request] = tokens_in[request]

        if late:

            @pl.when(source_ref[request] >= early)
            def _():
                fetch_late(request, late[0]).wait()
                normalise(raw[request], tokens.at[request])

        return carry

    if late:
        lax.fori_loop(0, requests, begin, 0)
    for group in range(HEADS // GROUP):
        fetch_folded(group).start()
    lax.fori_loop(0, requests, finish, 0)

    def along(window):
        return tokens[2 * window : 2 * window + 2].reshape(2 * length, width)

    lone = weigh(contract(single_ref[...].astype(jnp.bfloat16), along(blocks), ((1,), (1,))))
    lone = contract(lone, along(blocks), ((1,), (0,)))

    place = lax.broadcasted_iota(jnp.int32, (count, HEAD_DIM), 0)
    kept = place % SPAN == 0
    for block in range(blocks):
        kept = kept | ((place // SPAN == block) & (keep_ref[block] > 0))

    units = [(group, window) for group in range(HEADS // GROUP) for window in range(blocks)]

    def score(unit):
        group, window = units[unit]
        heads, rows = slice(group * GROUP, (group + 1) * GROUP), slice(window * SPAN, (window + 1) * SPAN)
        if window == 0:
            fetch_folded(group).wait()
        taken = folded[heads, rows].reshape(rows_at_once, width)
        scores[unit] = contract(taken, along(window), ((1,), (1,)))

    def soften(unit):
        for part in range(GROUP):
            rows = slice(part * SPAN, (part + 1) * SPAN)
            weights[unit, rows] = weigh(scores[unit, rows])

    def combine(unit):
        group, window = units[unit]
        heads, rows = slice(group * GROUP, (group + 1) * GROUP), slice(window * SPAN, (window + 1) * SPAN)
        sums = contract(weights[unit], along(window), ((1,), (0,))).reshape(GROUP, SPAN, width)
        if window == 0:
            first = lax.broadcasted_iota(jnp.int32, sums.shape, 1) == 0
            sums = jnp.where(first, lone[heads][:, None, :], sums)
        mixed[heads, rows] = sums.astype(jnp.bfloat16)

    def project(group):
        for head in range(group * GROUP, (group + 1) * GROUP):
            columns = head_columns(head)
            sums = contract(mixed[head], value_ref[:, columns], ((1,), (0,)))
            sums = jnp.where(kept, sums, 0.0)
            out_ref[:, columns] = pltpu.roll(sums, count - 1, 0).astype(jnp.bfloat16)

    for step in range(len(units) + 2):
        if step < len(units):
            score(step)
        if step >= 2:
            combine(step - 2)
        if 1 <= step <= len(units):
            soften(step - 1)
        if step >= 2 and units[step - 2][1] == blocks - 1:
            project(units[step - 2][0])


def attend(early, source, block, keep, folded, single, tokens, w_value, late):
    requests, length, width = tokens.shape
    count = folded.shape[1]
    units = HEADS // GROUP * (count // SPAN)
    return pl.pallas_call(
        functools.partial(attend_kernel, early),
        out_shape=jax.ShapeDtypeStruct((count, w_value.shape[1]), jnp.bfloat16),
        in_specs=[SMEM_SPEC] * 3
        + [HBM_SPEC]
        + [VMEM_SPEC] * 3
        + [ANY_SPEC] * len(late),
        out_specs=VMEM_SPEC,
        scratch_shapes=[
            pltpu.VMEM(tokens.shape, jnp.bfloat16),
            pltpu.VMEM(tokens.shape, jnp.bfloat16),
            pltpu.VMEM(folded.shape, jnp.bfloat16),
            pltpu.VMEM((units, GROUP * SPAN, 2 * length), jnp.float32),
            pltpu.VMEM((units, GROUP * SPAN, 2 * length), jnp.bfloat16),
            pltpu.VMEM(folded.shape, jnp.bfloat16),
            pltpu.SemaphoreType.DMA((requests,)),
            pltpu.SemaphoreType.DMA((HEADS // GROUP,)),
        ],
        compiler_params=pltpu.CompilerParams(vmem_limit_bytes=40 * MIB),
        cost_estimate=pl.CostEstimate(
            flops=2 * HEADS * count * width * (4 * length + HEAD_DIM),
            bytes_accessed=16 * MIB,
            transcendentals=HEADS * count * 2 * length,
        ),
        name="attend_windows",
    )(source, block, keep, in_hbm(folded), single, tokens, w_value, *late)


def chip_ring(mesh):
    row = mesh.devices.reshape(-1, mesh.shape["seq"])[0]
    chips = list(range(len(row) // CORES))
    columns = [tuple(getattr(row[CORES * chip], "coords", (0, 0))[:2]) for chip in chips]
    if len(set(columns)) != 2:
        return chips
    up = [chip for chip in chips if columns[chip] == columns[0]]
    return up + [chip for chip in reversed(chips) if columns[chip] != columns[0]]


class Ring:
    def __init__(self, ring):
        self.ring = ring
        self.size = len(ring)
        self.reach = (self.size - 1) // 2
        self.opposite = self.size % 2 == 0

    def turned(self, value, steps, cores=range(CORES)):
        size = self.size
        pairs = [
            (CORES * self.ring[i] + core, CORES * self.ring[(i + steps) % size] + core)
            for i in range(size)
            for core in cores
        ]
        return lax.ppermute(value, "seq", pairs)

    def swapped(self, value, cores=range(CORES)):
        return lax.ppermute(value, "seq", [(CORES * i + core, CORES * i + 1 - core) for i in range(self.size) for core in cores])

    def locate(self, owner, here):
        order = jnp.asarray([self.ring.index(chip) for chip in range(self.size)], jnp.int32)

        def place_of(device):
            chips = jnp.arange(self.size)
            return jnp.sum(jnp.where((device // CORES)[..., None] == chips, order, 0), axis=-1)

        away = (place_of(here) - place_of(owner)) % self.size
        back = away > self.reach
        arrival = jnp.where(back, 2 * (self.size - away), jnp.maximum(2 * away - 1, 0))
        if self.opposite:
            arrival = jnp.where(away == self.size // 2, 2 * self.reach + 1 + owner % CORES, arrival)
        return CORES * arrival + (owner % CORES != here % CORES)


def tie(values, others):
    values, others = lax.optimization_barrier((tuple(values), tuple(others)))
    return list(values), list(others)


def body(ring, queries, neighbours, w_key, w_value, retrieval_owner, retrieval_slot, doc_starts):
    devices = lax.axis_size("seq")
    here = lax.axis_index("seq")
    plan = Ring(ring)
    owner_slot = jnp.stack([retrieval_owner, retrieval_slot])
    before = lax.ppermute(owner_slot[:, -1:], "seq", [(i, i + 1) for i in range(devices - 1)])
    owner, slot = jnp.concatenate([before, owner_slot], 1).reshape(2, -1)
    source, block = plan.locate(owner, here), slot
    blocks = doc_starts.shape[0]
    opening = (here == 0) & (jnp.arange(blocks) == 0)
    keep = ((doc_starts == 0) & jnp.logical_not(opening)).astype(jnp.int32)
    beside = [*fold(queries, w_key), source, block, keep]
    ahead = behind = neighbours
    stores, tokens, done = [neighbours, plan.swapped(neighbours)], None, 0
    for step in range(plan.reach):
        if step == 1:
            (ahead, behind), beside = tie((ahead, behind), beside)
        if step == 2:
            done = 6
            tokens = collect(0, beside[2], beside[3], stores[:done], None)
            (ahead, behind), (tokens,) = tie((ahead, behind), (tokens,))
        ahead, behind = plan.turned(ahead, 1), plan.turned(behind, -1)
        stores += [ahead, plan.swapped(ahead), behind, plan.swapped(behind)]
    folded, single, source, block, keep = beside
    late = []
    if plan.opposite:
        ahead, behind = plan.turned(ahead, 1, (0,)), plan.turned(behind, -1, (1,))
        late = [ahead, plan.swapped(ahead, (0,)), behind, plan.swapped(behind, (1,))]
    tokens = collect(done, source, block, stores[done:], tokens)
    return attend(len(stores), source, block, keep, folded, single, tokens, w_value, late)


def solution(mesh):
    return jax.shard_map(
        functools.partial(body, chip_ring(mesh)),
        mesh=mesh,
        in_specs=(
            P(("groups", "seq"), None),
            P(("groups", "seq"), None, None),
            P(),
            P(),
            P(("groups", "seq"), None),
            P(("groups", "seq"), None),
            P(("groups", "seq")),
        ),
        out_specs=P(("groups", "seq"), None),
        check_vma=False,
    )
```

time: 89.4 us -> 71.5 us (0.80)
  local copies, waits for them, and re-layouts: 10.8 us -> 0.38 us
  starting transfers between devices: 24.4 us -> 17.5 us
  waiting for transfers between devices: 24.9 us -> 27.7 us
  Pallas kernels: 25.1 us -> 22.5 us
  other arithmetic: 3.58 us -> 2.25 us
    unnamed x18 -> x12, local copies, waits for them, and re-layouts: 9.26 us -> 0.02 us
    ppermute x14 -> x8, starting transfers between devices: 19.2 us -> 11.3 us  [turned(): return lax.ppermute(value, 'seq', pairs)]
    pallas_call x1, Pallas kernels: 15.1 us -> 11.3 us  [attend(): pl.pallas_call(functools.partial(attend_kernel, early), out_shape=jax.Sha...]
    ppermute x14 -> x8, waiting for transfers between devices: 23.9 us -> 27.7 us  [turned(): return lax.ppermute(value, 'seq', pairs)]
    pallas_call x2 -> x3, Pallas kernels: 10 us -> 11.2 us  [the longest x2 6.1 us: collect(): pl.pallas_call(functools.partial(collect_kernel, first), out_shape=jax.Sh...]
    slice x1 -> x0, local copies, waits for them, and re-layouts: 1.14 us -> none  [gather(): waves = {way: [stored[slot:slot + 1] for slot in slots] for way in (1, -1)}]
    ppermute x15 -> x9, waiting for transfers between devices: 0.93 us -> 0.02 us  [swapped(): lax.ppermute(value, 'seq', [(CORES * i + core, CORES * i + 1 - core) for...]
    ppermute x15 -> x9, starting transfers between devices: 2.85 us -> 3.75 us  [swapped(): lax.ppermute(value, 'seq', [(CORES * i + core, CORES * i + 1 - core) for...]
  transfers between devices with their start and end apart: 30 -> 18, of which waited for: 11 -> 6; matrix products, arithmetic and copies ran while one was open for 4% -> 4% of each run, Pallas kernels for 11% -> 16%
where the time goes in v6:
time: 71.5 us; the launch traced here: 70.6 us
  waiting for transfers between devices  27.7 us (39%)
  Pallas kernels  22.5 us (31%)
  starting transfers between devices  17.5 us (24%)
  other arithmetic  2.25 us (3%)
    ppermute x8, waiting for transfers between devices, turned(): return lax.ppermute(value, 'seq', pairs)  27.7 us
    ppermute x8, starting transfers between devices, turned(): return lax.ppermute(value, 'seq', pairs)  11.3 us
    pallas_call x1, Pallas kernels, attend(): pl.pallas_call(functools.partial(attend_kernel, early), out_shape=jax.Sha...  11.3 us
    pallas_call x2, Pallas kernels, collect(): pl.pallas_call(functools.partial(collect_kernel, first), out_shape=jax.Sh...  6.1 us
    pallas_call x1, Pallas kernels, fold(): pl.pallas_call(fold_kernel, out_shape=(pltpu.HBM(shape, jnp.bfloat16), ja...  5.07 us
    ppermute x9, starting transfers between devices, swapped(): lax.ppermute(value, 'seq', [(CORES * i + core, CORES * i + 1 - core) for...  3.75 us
    ppermute x1, starting transfers between devices, body(): lax.ppermute(owner_slot[:, -1:], 'seq', [(i, i + 1) for i in range(device...  2.4 us
  transfers between devices with their start and end apart: 18, of which 6 were waited for; matrix products, arithmetic and copies ran while one was open for 4% of the time, Pallas kernels for 16%

profile of v6, /device:TPU:0, one launch (start us, length us, event | category | flops | bytes accessed | tf_op | source)
XLA Modules:
  0.0 70.6 jit_solution(2667253215531542041)
XLA Ops:
  0.0 3.1 %collective-permute-start = (bf16[2,128,896]{2,1,0:T(8,128)(2,1)}, bf16[2,128,896]{2,1,0:T(8,128)(2,1)S(1)}, u32[]{:S(2)}, u32[]{:S(2)}) collective-permute-start(bf16[2,128,896]{2,1,0:T(8,128)(2,1)} %rest_0_.1), channel_id=1, source_target_pairs={{0,4},{1,5},{4,8},{5,9},{8,12},{9,13},{12,14},{13,15},{14,10},{15,... | collective-permute-start | bytes 1376264 | tf_op jit(solution)/shard_map/ppermute | solution.py:315
  3.1 0.0 collective-permute-start.1
  3.1 0.0 collective-permute-start.7
  3.1 0.8 %pad_add_fusion = s32[2,1,2]{1,2,0:T(2,128)S(1)} fusion(s32[1,4,2]{1,2,0:T(2,128)} %bitcast.2, s32[1,4,2]{1,2,0:T(2,128)} %bitcast.4), kind=kLoop, calls=%fused_computation.4 | loop fusion | flops 4 | bytes 80 | tf_op jit(solution)/shard_map/stack | solution.py:344
  3.9 2.4 %collective-permute-start.2 = (s32[2,1,2]{1,2,0:T(2,128)S(1)}, s32[2,1,2]{1,2,0:T(2,128)S(1)}, u32[]{:S(2)}, u32[]{:S(2)}) collective-permute-start(s32[2,1,2]{1,2,0:T(2,128)S(1)} %pad_add_fusion), channel_id=1, source_target_pairs={{0,1},{1,2},{2,3},{3,4},{4,5},{5,6},{6,7},{7,8},{8,9},{9,10},{10,1... | collective-permute-start | bytes 56 | tf_op jit(solution)/shard_map/ppermute | solution.py:345
  6.3 5.1 %fold_queries.1 = (bf16[16,256,896]{2,1,0:T(8,128)(2,1)}, f32[16,896]{1,0:T(8,128)S(1)}) custom-call(bf16[256,2048]{1,0:T(8,128)(2,1)} %query_hbm.1, bf16[896,2048]{1,0:T(8,128)(2,1)} %key_hbm.1), custom_call_target="tpu_custom_call" | custom-call | flops 939524096 | bytes 12582912 | tf_op jit(solution)/shard_map/fold_queries/pallas_call | solution.py:72
  11.4 0.6 fusion
  12.1 0.0 collective-permute-done.2
  12.1 0.1 add_add_fusion
  12.2 0.1 copy.13
  12.3 0.1 unstack.13
  12.4 0.1 select_reduce_fusion
  12.5 1.3 %collective-permute-done.rest_2_ = bf16[2,128,896]{2,1,0:T(8,128)(2,1)S(1)} collective-permute-done((bf16[2,128,896]{2,1,0:T(8,128)(2,1)}, bf16[2,128,896]{2,1,0:T(8,128)(2,1)S(1)}, u32[]{:S(2)}, u32[]{:S(2)}) %collective-permute-start) | collective-permute-done | bytes 458784 | tf_op jit(solution)/shard_map/ppermute | solution.py:315
  13.8 0.3 collective-permute-start.8
  14.1 1.2 %collective-permute-done.1.rest_4_ = bf16[2,128,896]{2,1,0:T(8,128)(2,1)S(1)} collective-permute-done((bf16[2,128,896]{2,1,0:T(8,128)(2,1)}, bf16[2,128,896]{2,1,0:T(8,128)(2,1)S(1)}, u32[]{:S(2)}, u32[]{:S(2)}) %collective-permute-start.1) | collective-permute-done | bytes 458784 | tf_op jit(solution)/shard_map/ppermute | solution.py:315
  15.3 0.0 collective-permute-start.9
  15.3 0.7 fusion.2.source_ref
  16.0 0.1 copy.14
  16.1 0.1 unstack.15.block_ref
  16.1 1.6 %collective-permute-start.3 = (bf16[2,128,896]{2,1,0:T(8,128)(2,1)S(1)}, bf16[2,128,896]{2,1,0:T(8,128)(2,1)S(1)}, u32[]{:S(2)}, u32[]{:S(2)}) collective-permute-start(bf16[2,128,896]{2,1,0:T(8,128)(2,1)S(1)} %collective-permute-done.rest_2_), channel_id=1, source_target_pairs={{0,4},{1,5},{4,8},{5,9},{8,12},{9,13},{12,14},{13,15},{14,10},{15,... | collective-permute-start | bytes 1376264 | tf_op jit(solution)/shard_map/ppermute | solution.py:315
  17.7 0.4 collective-permute-start.5
  18.2 0.0 collective-permute-done.7.rest_1_
  18.2 0.0 collective-permute-done.8.rest_3_
  18.2 0.0 collective-permute-done.9.rest_5_
  18.2 2.4 %collect_blocks.2.rest_8_ = bf16[10,128,896]{2,1,0:T(8,128)(2,1)S(1)} custom-call(s32[10]{0:T(128)S(1)} %fusion.2.source_ref, s32[10]{0:T(128)S(1)} %unstack.15.block_ref, bf16[2,128,896]{2,1,0:T(8,128)(2,1)S(1)} %copy-done, bf16[2,128,896]{2,1,0:T(8,128)(2,1)S(1)} %collective-permute-done.7.rest_1_, bf16[2,128,896]{2,1,0:T(8,128)(2,1)S(1)} %collective-permute-done.rest_2_, ...), custom_call_target="tpu_custom_call" | custom-call | flops 4194304 | bytes 8388608 | tf_op jit(solution)/shard_map/collect_blocks/pallas_call | solution.py:148
  20.6 0.0 copy-start.1
  20.6 8.5 %collective-permute-done.3.rest_0_ = bf16[2,128,896]{2,1,0:T(8,128)(2,1)S(1)} collective-permute-done((bf16[2,128,896]{2,1,0:T(8,128)(2,1)S(1)}, bf16[2,128,896]{2,1,0:T(8,128)(2,1)S(1)}, u32[]{:S(2)}, u32[]{:S(2)}) %collective-permute-start.3) | collective-permute-done | bytes 458784 | tf_op jit(solution)/shard_map/ppermute | solution.py:315
  29.1 1.3 %collective-permute-done.5.rest_2_ = bf16[2,128,896]{2,1,0:T(8,128)(2,1)S(1)} collective-permute-done((bf16[2,128,896]{2,1,0:T(8,128)(2,1)S(1)}, bf16[2,128,896]{2,1,0:T(8,128)(2,1)S(1)}, u32[]{:S(2)}, u32[]{:S(2)}) %collective-permute-start.5) | collective-permute-done | bytes 458784 | tf_op jit(solution)/shard_map/ppermute | solution.py:315
  30.4 1.6 %collective-permute-start.10 = (bf16[2,128,896]{2,1,0:T(8,128)(2,1)S(1)}, bf16[2,128,896]{2,1,0:T(8,128)(2,1)S(1)}, u32[]{:S(2)}, u32[]{:S(2)}) collective-permute-start(bf16[2,128,896]{2,1,0:T(8,128)(2,1)S(1)} %collective-permute-done.3.rest_0_), channel_id=1, source_target_pairs={{0,4},{1,5},{4,8},{5,9},{8,12},{9,13},{12,14},{13,15},{14,10},{15,... | collective-permute-start | bytes 1376264 | tf_op jit(solution)/shard_map/ppermute | solution.py:315
  31.9 0.4 collective-permute-start.12
  32.4 0.0 collective-permute-start.4
  32.4 9.8 %collective-permute-done.10.rest_4_ = bf16[2,128,896]{2,1,0:T(8,128)(2,1)S(1)} collective-permute-done((bf16[2,128,896]{2,1,0:T(8,128)(2,1)S(1)}, bf16[2,128,896]{2,1,0:T(8,128)(2,1)S(1)}, u32[]{:S(2)}, u32[]{:S(2)}) %collective-permute-start.10) | collective-permute-done | bytes 458784 | tf_op jit(solution)/shard_map/ppermute | solution.py:315
  42.2 3.5 %collective-permute-start.14 = (bf16[2,128,896]{2,1,0:T(8,128)(2,1)S(1)}, bf16[2,128,896]{2,1,0:T(8,128)(2,1)S(1)}, u32[]{:S(2)}, u32[]{:S(2)}) collective-permute-start(bf16[2,128,896]{2,1,0:T(8,128)(2,1)S(1)} %collective-permute-done.10.rest_4_), channel_id=1, source_target_pairs={{0,4},{4,8},{8,12},{12,14},{14,10},{10,6},{6,2},{2,0},{16,20},{20,... | collective-permute-start | bytes 1376264 | tf_op jit(solution)/shard_map/ppermute | solution.py:315
  45.7 0.0 collective-permute-done.12.rest_6_
  45.7 0.7 collective-permute-start.16
  46.4 0.1 collective-permute-start.6
  46.5 0.5 collective-permute-start.11
  47.0 0.0 collective-permute-done.4.rest_1_
  47.0 0.1 collective-permute-start.13
  47.1 5.5 %collective-permute-done.14.rest_0_ = bf16[2,128,896]{2,1,0:T(8,128)(2,1)S(1)} collective-permute-done((bf16[2,128,896]{2,1,0:T(8,128)(2,1)S(1)}, bf16[2,128,896]{2,1,0:T(8,128)(2,1)S(1)}, u32[]{:S(2)}, u32[]{:S(2)}) %collective-permute-start.14) | collective-permute-done | bytes 458784 | tf_op jit(solution)/shard_map/ppermute | solution.py:315
  52.6 1.3 %collective-permute-start.15 = (bf16[2,128,896]{2,1,0:T(8,128)(2,1)S(1)}, bf16[2,128,896]{2,1,0:T(8,128)(2,1)S(1)}, u32[]{:S(2)}, u32[]{:S(2)}) collective-permute-start(bf16[2,128,896]{2,1,0:T(8,128)(2,1)S(1)} %collective-permute-done.14.rest_0_), channel_id=1, source_target_pairs={{0,1},{2,3},{4,5},{6,7},{8,9},{10,11},{12,13},{14,15},{16,17},{18,... | collective-permute-start | bytes 1376264 | tf_op jit(solution)/shard_map/ppermute | solution.py:318
  53.9 0.0 collective-permute-done.16.rest_2_
  53.9 1.5 %collective-permute-start.17 = (bf16[2,128,896]{2,1,0:T(8,128)(2,1)S(1)}, bf16[2,128,896]{2,1,0:T(8,128)(2,1)S(1)}, u32[]{:S(2)}, u32[]{:S(2)}) collective-permute-start(bf16[2,128,896]{2,1,0:T(8,128)(2,1)S(1)} %collective-permute-done.16.rest_2_), channel_id=1, source_target_pairs={{1,0},{3,2},{5,4},{7,6},{9,8},{11,10},{13,12},{15,14},{17,16},{19,... | collective-permute-start | bytes 1376264 | tf_op jit(solution)/shard_map/ppermute | solution.py:318
  55.4 0.0 collective-permute-done.6.rest_3_
  55.4 0.0 collective-permute-done.13.rest_7_
  55.4 3.7 %collect_blocks.3.tokens_in = bf16[10,128,896]{2,1,0:T(8,128)(2,1)S(1)} custom-call(s32[10]{0:T(128)S(1)} %fusion.2.source_ref, s32[10]{0:T(128)S(1)} %unstack.15.block_ref, bf16[2,128,896]{2,1,0:T(8,128)(2,1)S(1)} %collective-permute-done.3.rest_0_, bf16[2,128,896]{2,1,0:T(8,128)(2,1)S(1)} %collective-permute-done.4.rest_1_, ...), custom_call_target="tpu_custom_call" | custom-call | flops 4194304 | bytes 8388608 | tf_op jit(solution)/shard_map/collect_blocks/pallas_call | solution.py:148
  59.2 0.0 collective-permute-done.17.rest_3_
  59.2 11.3 %attend_windows.1 = bf16[256,2048]{1,0:T(8,128)(2,1)} custom-call(s32[10]{0:T(128)S(1)} %fusion.2.source_ref, s32[10]{0:T(128)S(1)} %unstack.15.block_ref, s32[4]{0:T(128)S(1)} %and_convert_fusion.keep_ref, bf16[16,256,896]{2,1,0:T(8,128)(2,1)} %get-tuple-element.22.folded_hbm, f32[16,896]{1,0:T(8,128)S(1)} %get-tuple-element.23.single_ref, ...), custom_call_target="tpu_custom_call" | custom-call | flops 4697620480 | bytes 16777216 | tf_op jit(solution)/shard_map/attend_windows/pallas_call | solution.py:263
  (16 shorter events, 0.0 us)
Async XLA Ops:
  0.0 11.4 %copy-start.5 = (s32[8]{0:T(128)S(1)}, s32[8]{0:T(128)}, u32[]{:S(2)}) copy-start(s32[8]{0:T(128)} %constant.73.clone) | copy-start | bytes 100
  0.0 18.2 %copy-start = (bf16[2,128,896]{2,1,0:T(8,128)(2,1)S(1)}, bf16[2,128,896]{2,1,0:T(8,128)(2,1)}, u32[]{:S(2)}) copy-start(bf16[2,128,896]{2,1,0:T(8,128)(2,1)} %rest_0_.1) | copy-start | bytes 1376260
  0.0 12.1 %copy-start.2 = (s32[4,2]{0,1:T(2,128)S(1)}, s32[4,2]{0,1:T(2,128)}, u32[]{:S(2)}) copy-start(s32[4,2]{0,1:T(2,128)} %param.13) | copy-start | bytes 100
  0.0 12.1 %copy-start.3 = (s32[4,2]{0,1:T(2,128)S(1)}, s32[4,2]{0,1:T(2,128)}, u32[]{:S(2)}) copy-start(s32[4,2]{0,1:T(2,128)} %param.12) | copy-start | bytes 100
  0.0 12.1 %copy-start.4 = (s32[4]{0:T(128)S(1)}, s32[4]{0:T(128)}, u32[]{:S(2)}) copy-start(s32[4]{0:T(128)} %param.14) | copy-start | bytes 52
  0.0 13.8 %collective-permute-start = (bf16[2,128,896]{2,1,0:T(8,128)(2,1)}, bf16[2,128,896]{2,1,0:T(8,128)(2,1)S(1)}, u32[]{:S(2)}, u32[]{:S(2)}) collective-permute-start(bf16[2,128,896]{2,1,0:T(8,128)(2,1)} %rest_0_.1), channel_id=1, source_target_pairs={{0,4},{1,5},{4,8},{5,9},{8,12},{9,13},{12,14},{13,15},{14,10},{15,... | collective-permute-start | bytes 1376264 | tf_op jit(solution)/shard_map/ppermute | solution.py:315
  3.1 12.2 %collective-permute-start.1 = (bf16[2,128,896]{2,1,0:T(8,128)(2,1)}, bf16[2,128,896]{2,1,0:T(8,128)(2,1)S(1)}, u32[]{:S(2)}, u32[]{:S(2)}) collective-permute-start(bf16[2,128,896]{2,1,0:T(8,128)(2,1)} %rest_0_.1), channel_id=1, source_target_pairs={{0,2},{1,3},{4,0},{5,1},{8,4},{9,5},{12,8},{13,9},{14,12},{15,13},... | collective-permute-start | bytes 1376264 | tf_op jit(solution)/shard_map/ppermute | solution.py:315
  3.1 15.1 %collective-permute-start.7 = (bf16[2,128,896]{2,1,0:T(8,128)(2,1)}, bf16[2,128,896]{2,1,0:T(8,128)(2,1)S(1)}, u32[]{:S(2)}, u32[]{:S(2)}) collective-permute-start(bf16[2,128,896]{2,1,0:T(8,128)(2,1)} %rest_0_.1), channel_id=1, source_target_pairs={{0,1},{1,0},{2,3},{3,2},{4,5},{5,4},{6,7},{7,6},{8,9},{9,8},{10,11... | collective-permute-start | bytes 1376264 | tf_op jit(solution)/shard_map/ppermute | solution.py:318
  3.9 8.2 %collective-permute-start.2 = (s32[2,1,2]{1,2,0:T(2,128)S(1)}, s32[2,1,2]{1,2,0:T(2,128)S(1)}, u32[]{:S(2)}, u32[]{:S(2)}) collective-permute-start(s32[2,1,2]{1,2,0:T(2,128)S(1)} %pad_add_fusion), channel_id=1, source_target_pairs={{0,1},{1,2},{2,3},{3,4},{4,5},{5,6},{6,7},{7,8},{8,9},{9,10},{10,1... | collective-permute-start | bytes 56 | tf_op jit(solution)/shard_map/ppermute | solution.py:345
  13.8 4.4 %collective-permute-start.8 = (bf16[2,128,896]{2,1,0:T(8,128)(2,1)S(1)}, bf16[2,128,896]{2,1,0:T(8,128)(2,1)S(1)}, u32[]{:S(2)}, u32[]{:S(2)}) collective-permute-start(bf16[2,128,896]{2,1,0:T(8,128)(2,1)S(1)} %collective-permute-done.rest_2_), channel_id=1, source_target_pairs={{0,1},{1,0},{2,3},{3,2},{4,5},{5,4},{6,7},{7,6},{8,9},{9,8},{10,11... | collective-permute-start | bytes 1376264 | tf_op jit(solution)/shard_map/ppermute | solution.py:318
  15.3 2.9 %collective-permute-start.9 = (bf16[2,128,896]{2,1,0:T(8,128)(2,1)S(1)}, bf16[2,128,896]{2,1,0:T(8,128)(2,1)S(1)}, u32[]{:S(2)}, u32[]{:S(2)}) collective-permute-start(bf16[2,128,896]{2,1,0:T(8,128)(2,1)S(1)} %collective-permute-done.1.rest_4_), channel_id=1, source_target_pairs={{0,1},{1,0},{2,3},{3,2},{4,5},{5,4},{6,7},{7,6},{8,9},{9,8},{10,11... | collective-permute-start | bytes 1376264 | tf_op jit(solution)/shard_map/ppermute | solution.py:318
  16.1 12.9 %collective-permute-start.3 = (bf16[2,128,896]{2,1,0:T(8,128)(2,1)S(1)}, bf16[2,128,896]{2,1,0:T(8,128)(2,1)S(1)}, u32[]{:S(2)}, u32[]{:S(2)}) collective-permute-start(bf16[2,128,896]{2,1,0:T(8,128)(2,1)S(1)} %collective-permute-done.rest_2_), channel_id=1, source_target_pairs={{0,4},{1,5},{4,8},{5,9},{8,12},{9,13},{12,14},{13,15},{14,10},{15,... | collective-permute-start | bytes 1376264 | tf_op jit(solution)/shard_map/ppermute | solution.py:315
  17.7 12.7 %collective-permute-start.5 = (bf16[2,128,896]{2,1,0:T(8,128)(2,1)S(1)}, bf16[2,128,896]{2,1,0:T(8,128)(2,1)S(1)}, u32[]{:S(2)}, u32[]{:S(2)}) collective-permute-start(bf16[2,128,896]{2,1,0:T(8,128)(2,1)S(1)} %collective-permute-done.1.rest_4_), channel_id=1, source_target_pairs={{0,2},{1,3},{4,0},{5,1},{8,4},{9,5},{12,8},{13,9},{14,12},{15,13},... | collective-permute-start | bytes 1376264 | tf_op jit(solution)/shard_map/ppermute | solution.py:315
  20.6 38.6 %copy-start.1 = (bf16[896,2048]{1,0:T(8,128)(2,1)S(1)}, bf16[896,2048]{1,0:T(8,128)(2,1)}, u32[]{:S(2)}) copy-start(bf16[896,2048]{1,0:T(8,128)(2,1)} %value_ref.1) | copy-start | bytes 11010052
  30.4 11.8 %collective-permute-start.10 = (bf16[2,128,896]{2,1,0:T(8,128)(2,1)S(1)}, bf16[2,128,896]{2,1,0:T(8,128)(2,1)S(1)}, u32[]{:S(2)}, u32[]{:S(2)}) collective-permute-start(bf16[2,128,896]{2,1,0:T(8,128)(2,1)S(1)} %collective-permute-done.3.rest_0_), channel_id=1, source_target_pairs={{0,4},{1,5},{4,8},{5,9},{8,12},{9,13},{12,14},{13,15},{14,10},{15,... | collective-permute-start | bytes 1376264 | tf_op jit(solution)/shard_map/ppermute | solution.py:315
  31.9 13.7 %collective-permute-start.12 = (bf16[2,128,896]{2,1,0:T(8,128)(2,1)S(1)}, bf16[2,128,896]{2,1,0:T(8,128)(2,1)S(1)}, u32[]{:S(2)}, u32[]{:S(2)}) collective-permute-start(bf16[2,128,896]{2,1,0:T(8,128)(2,1)S(1)} %collective-permute-done.5.rest_2_), channel_id=1, source_target_pairs={{0,2},{1,3},{4,0},{5,1},{8,4},{9,5},{12,8},{13,9},{14,12},{15,13},... | collective-permute-start | bytes 1376264 | tf_op jit(solution)/shard_map/ppermute | solution.py:315
  32.4 14.6 %collective-permute-start.4 = (bf16[2,128,896]{2,1,0:T(8,128)(2,1)S(1)}, bf16[2,128,896]{2,1,0:T(8,128)(2,1)S(1)}, u32[]{:S(2)}, u32[]{:S(2)}) collective-permute-start(bf16[2,128,896]{2,1,0:T(8,128)(2,1)S(1)} %collective-permute-done.3.rest_0_), channel_id=1, source_target_pairs={{0,1},{1,0},{2,3},{3,2},{4,5},{5,4},{6,7},{7,6},{8,9},{9,8},{10,11... | collective-permute-start | bytes 1376264 | tf_op jit(solution)/shard_map/ppermute | solution.py:318
  42.2 10.4 %collective-permute-start.14 = (bf16[2,128,896]{2,1,0:T(8,128)(2,1)S(1)}, bf16[2,128,896]{2,1,0:T(8,128)(2,1)S(1)}, u32[]{:S(2)}, u32[]{:S(2)}) collective-permute-start(bf16[2,128,896]{2,1,0:T(8,128)(2,1)S(1)} %collective-permute-done.10.rest_4_), channel_id=1, source_target_pairs={{0,4},{4,8},{8,12},{12,14},{14,10},{10,6},{6,2},{2,0},{16,20},{20,... | collective-permute-start | bytes 1376264 | tf_op jit(solution)/shard_map/ppermute | solution.py:315
  45.7 8.2 %collective-permute-start.16 = (bf16[2,128,896]{2,1,0:T(8,128)(2,1)S(1)}, bf16[2,128,896]{2,1,0:T(8,128)(2,1)S(1)}, u32[]{:S(2)}, u32[]{:S(2)}) collective-permute-start(bf16[2,128,896]{2,1,0:T(8,128)(2,1)S(1)} %collective-permute-done.12.rest_6_), channel_id=1, source_target_pairs={{1,3},{5,1},{9,5},{13,9},{15,13},{11,15},{7,11},{3,7},{17,19},{21,... | collective-permute-start | bytes 1376264 | tf_op jit(solution)/shard_map/ppermute | solution.py:315
  46.4 9.0 %collective-permute-start.6 = (bf16[2,128,896]{2,1,0:T(8,128)(2,1)S(1)}, bf16[2,128,896]{2,1,0:T(8,128)(2,1)S(1)}, u32[]{:S(2)}, u32[]{:S(2)}) collective-permute-start(bf16[2,128,896]{2,1,0:T(8,128)(2,1)S(1)} %collective-permute-done.5.rest_2_), channel_id=1, source_target_pairs={{0,1},{1,0},{2,3},{3,2},{4,5},{5,4},{6,7},{7,6},{8,9},{9,8},{10,11... | collective-permute-start | bytes 1376264 | tf_op jit(solution)/shard_map/ppermute | solution.py:318
  46.5 8.9 %collective-permute-start.11 = (bf16[2,128,896]{2,1,0:T(8,128)(2,1)S(1)}, bf16[2,128,896]{2,1,0:T(8,128)(2,1)S(1)}, u32[]{:S(2)}, u32[]{:S(2)}) collective-permute-start(bf16[2,128,896]{2,1,0:T(8,128)(2,1)S(1)} %collective-permute-done.10.rest_4_), channel_id=1, source_target_pairs={{0,1},{1,0},{2,3},{3,2},{4,5},{5,4},{6,7},{7,6},{8,9},{9,8},{10,11... | collective-permute-start | bytes 1376264 | tf_op jit(solution)/shard_map/ppermute | solution.py:318
  47.0 8.4 %collective-permute-start.13 = (bf16[2,128,896]{2,1,0:T(8,128)(2,1)S(1)}, bf16[2,128,896]{2,1,0:T(8,128)(2,1)S(1)}, u32[]{:S(2)}, u32[]{:S(2)}) collective-permute-start(bf16[2,128,896]{2,1,0:T(8,128)(2,1)S(1)} %collective-permute-done.12.rest_6_), channel_id=1, source_target_pairs={{0,1},{1,0},{2,3},{3,2},{4,5},{5,4},{6,7},{7,6},{8,9},{9,8},{10,11... | collective-permute-start | bytes 1376264 | tf_op jit(solution)/shard_map/ppermute | solution.py:318
  52.6 6.6 %collective-permute-start.15 = (bf16[2,128,896]{2,1,0:T(8,128)(2,1)S(1)}, bf16[2,128,896]{2,1,0:T(8,128)(2,1)S(1)}, u32[]{:S(2)}, u32[]{:S(2)}) collective-permute-start(bf16[2,128,896]{2,1,0:T(8,128)(2,1)S(1)} %collective-permute-done.14.rest_0_), channel_id=1, source_target_pairs={{0,1},{2,3},{4,5},{6,7},{8,9},{10,11},{12,13},{14,15},{16,17},{18,... | collective-permute-start | bytes 1376264 | tf_op jit(solution)/shard_map/ppermute | solution.py:318
  53.9 5.3 %collective-permute-start.17 = (bf16[2,128,896]{2,1,0:T(8,128)(2,1)S(1)}, bf16[2,128,896]{2,1,0:T(8,128)(2,1)S(1)}, u32[]{:S(2)}, u32[]{:S(2)}) collective-permute-start(bf16[2,128,896]{2,1,0:T(8,128)(2,1)S(1)} %collective-permute-done.16.rest_2_), channel_id=1, source_target_pairs={{1,0},{3,2},{5,4},{7,6},{9,8},{11,10},{13,12},{15,14},{17,16},{19,... | collective-permute-start | bytes 1376264 | tf_op jit(solution)/shard_map/ppermute | solution.py:318

commit v7 on v6

--- a/solution.py
+++ b/solution.py
@@ -299,25 +299,30 @@
 
 
 class Ring:
-    def __init__(self, ring):
-        self.ring = ring
+    def __init__(self, ring, slots):
+        self.ring, self.slots = ring, slots
         self.size = len(ring)
         self.reach = (self.size - 1) // 2
         self.opposite = self.size % 2 == 0
 
-    def turned(self, value, steps, cores=range(CORES)):
+    def turned(self, value, steps):
         size = self.size
         pairs = [
             (CORES * self.ring[i] + core, CORES * self.ring[(i + steps) % size] + core)
             for i in range(size)
-            for core in cores
+            for core in range(CORES)
         ]
         return lax.ppermute(value, "seq", pairs)
 
-    def swapped(self, value, cores=range(CORES)):
-        return lax.ppermute(value, "seq", [(CORES * i + core, CORES * i + 1 - core) for i in range(self.size) for core in cores])
-
-    def locate(self, owner, here):
+    def swapped(self, value):
+        return lax.ppermute(value, "seq", [(i, i ^ 1) for i in range(CORES * self.size)])
+
+    def ways(self, step, slot):
+        if step < self.reach:
+            return (1, -1)
+        return (1,) if slot < self.slots // 2 else (-1,)
+
+    def locate(self, owner, slot, here):
         order = jnp.asarray([self.ring.index(chip) for chip in range(self.size)], jnp.int32)
 
         def place_of(device):
@@ -326,47 +331,58 @@
 
         away = (place_of(here) - place_of(owner)) % self.size
         back = away > self.reach
-        arrival = jnp.where(back, 2 * (self.size - away), jnp.maximum(2 * away - 1, 0))
+        step = jnp.where(back, self.size - away, away) - 1
+        arrival = 1 + 2 * self.slots * step + 2 * slot + back
         if self.opposite:
-            arrival = jnp.where(away == self.size // 2, 2 * self.reach + 1 + owner % CORES, arrival)
-        return CORES * arrival + (owner % CORES != here % CORES)
-
-
-def tie(values, others):
-    values, others = lax.optimization_barrier((tuple(values), tuple(others)))
-    return list(values), list(others)
+            arrival = jnp.where(away == self.size // 2, 1 + 2 * self.slots * self.reach + slot, arrival)
+        arrival = jnp.where(away == 0, 0, arrival)
+        return CORES * arrival + (owner % CORES != here % CORES), jnp.where(away == 0, slot, 0)
+
+
+def after(values, others):
+    return list(lax.optimization_barrier((tuple(values), tuple(others)))[0])
 
 
 def body(ring, queries, neighbours, w_key, w_value, retrieval_owner, retrieval_slot, doc_starts):
     devices = lax.axis_size("seq")
     here = lax.axis_index("seq")
-    plan = Ring(ring)
+    plan = Ring(ring, neighbours.shape[0])
     owner_slot = jnp.stack([retrieval_owner, retrieval_slot])
     before = lax.ppermute(owner_slot[:, -1:], "seq", [(i, i + 1) for i in range(devices - 1)])
     owner, slot = jnp.concatenate([before, owner_slot], 1).reshape(2, -1)
-    source, block = plan.locate(owner, here), slot
+    source, block = plan.locate(owner, slot, here)
     blocks = doc_starts.shape[0]
     opening = (here == 0) & (jnp.arange(blocks) == 0)
     keep = ((doc_starts == 0) & jnp.logical_not(opening)).astype(jnp.int32)
-    beside = [*fold(queries, w_key), source, block, keep]
-    ahead = behind = neighbours
-    stores, tokens, done = [neighbours, plan.swapped(neighbours)], None, 0
-    for step in range(plan.reach):
-        if step == 1:
-            (ahead, behind), beside = tie((ahead, behind), beside)
-        if step == 2:
-            done = 6
-            tokens = collect(0, beside[2], beside[3], stores[:done], None)
-            (ahead, behind), (tokens,) = tie((ahead, behind), (tokens,))
-        ahead, behind = plan.turned(ahead, 1), plan.turned(behind, -1)
-        stores += [ahead, plan.swapped(ahead), behind, plan.swapped(behind)]
-    folded, single, source, block, keep = beside
-    late = []
-    if plan.opposite:
-        ahead, behind = plan.turned(ahead, 1, (0,)), plan.turned(behind, -1, (1,))
-        late = [ahead, plan.swapped(ahead, (0,)), behind, plan.swapped(behind, (1,))]
-    tokens = collect(done, source, block, stores[done:], tokens)
-    return attend(len(stores), source, block, keep, folded, single, tokens, w_value, late)
+    slots = range(plan.slots)
+    folded, single = fold(queries, w_key)
+    own = plan.swapped(neighbours)
+    waves = {(slot, way): neighbours[slot : slot + 1] for slot in slots for way in (1, -1)}
+    stores, swaps, waves_in, marks = [neighbours], [own], [], []
+    tokens, done = None, 0
+    for step in range(plan.reach + plan.opposite):
+        marks.append(len(stores))
+        for slot in slots:
+            ways = plan.ways(step, slot)
+            sent = [waves[slot, way] for way in ways]
+            if step == 0 and slot == 1:
+                sent = after(sent, [own])
+            if len(waves_in) > plan.slots:
+                sent = after(sent, waves_in[-plan.slots - 1])
+            if step == 1 and slot == plan.slots - 1:
+                sent = after(sent, [folded, source, block, keep])
+            arrived = [plan.turned(value, way) for value, way in zip(sent, ways)]
+            for way, value in zip(ways, arrived):
+                waves[slot, way] = value
+            stores += arrived
+            if waves_in:
+                swaps += [plan.swapped(value) for value in after(waves_in[-1], arrived[:1])]
+            waves_in.append(arrived)
+    swaps += [plan.swapped(value) for value in waves_in[-1]]
+    stores = [value for pair in zip(stores, swaps) for value in pair]
+    early = CORES * (marks[-1] if plan.opposite else len(stores) // CORES)
+    tokens = collect(0, source, block, stores[:early], None)
+    return attend(early, source, block, keep, folded, single, tokens, w_value, stores[early:])
 
 
 def solution(mesh):

time: 71.5 us -> 74.1 us (1.036)
  starting transfers between devices: 17.5 us -> 22.6 us
  waiting for transfers between devices: 27.7 us -> 24.5 us
  other arithmetic: 2.25 us -> 3.57 us
  Pallas kernels: 22.5 us -> 21.4 us
  local copies, waits for them, and re-layouts: 0.38 us -> 1.46 us
    ppermute x8 -> x14, starting transfers between devices: 11.3 us -> 16.3 us  [turned(): return lax.ppermute(value, 'seq', pairs)]
    ppermute x8 -> x14, waiting for transfers between devices: 27.7 us -> 23.6 us  [turned(): return lax.ppermute(value, 'seq', pairs)]
    slice x0 -> x1, local copies, waits for them, and re-layouts: none -> 1.09 us  [body(): neighbours[slot:slot + 1]]
    pallas_call x2 -> x1, Pallas kernels: 6.1 us -> 5.02 us  [collect(): pl.pallas_call(functools.partial(collect_kernel, first), out_shape=jax.Sh...]
    ppermute x9 -> x15, waiting for transfers between devices: 0.02 us -> 0.93 us  [swapped(): lax.ppermute(value, 'seq', [(i, i ^ 1) for i in range(CORES * self.size)])]
    ppermute x9 -> x15, starting transfers between devices: 3.75 us -> 4.29 us  [swapped(): lax.ppermute(value, 'seq', [(i, i ^ 1) for i in range(CORES * self.size)])]
  transfers between devices with their start and end apart: 18 -> 30, of which waited for: 6 -> 12; matrix products, arithmetic and copies ran while one was open for 4% -> 7% of each run, Pallas kernels for 16% -> 14%
where the time goes in v7:
time: 74.1 us; the launch traced here: 73.9 us
  waiting for transfers between devices  24.5 us (33%)
  starting transfers between devices  22.6 us (30%)
  Pallas kernels  21.4 us (29%)
  other arithmetic  3.57 us (5%)
  local copies, waits for them, and re-layouts  1.46 us (2%)
    ppermute x14, waiting for transfers between devices, turned(): return lax.ppermute(value, 'seq', pairs)  23.6 us
    ppermute x14, starting transfers between devices, turned(): return lax.ppermute(value, 'seq', pairs)  16.3 us
    pallas_call x1, Pallas kernels, attend(): pl.pallas_call(functools.partial(attend_kernel, early), out_shape=jax.Sha...  11.3 us
    pallas_call x1, Pallas kernels, fold(): pl.pallas_call(fold_kernel, out_shape=(pltpu.HBM(shape, jnp.bfloat16), ja...  5.06 us
    pallas_call x1, Pallas kernels, collect(): pl.pallas_call(functools.partial(collect_kernel, first), out_shape=jax.Sh...  5.02 us
    ppermute x15, starting transfers between devices, swapped(): lax.ppermute(value, 'seq', [(i, i ^ 1) for i in range(CORES * self.size)])  4.29 us
    ppermute x1, starting transfers between devices, body(): lax.ppermute(owner_slot[:, -1:], 'seq', [(i, i + 1) for i in range(device...  2.04 us
  transfers between devices with their start and end apart: 30, of which 12 were waited for; matrix products, arithmetic and copies ran while one was open for 7% of the time, Pallas kernels for 14%

profile of v7, /device:TPU:0, one launch (start us, length us, event | category | flops | bytes accessed | tf_op | source)
XLA Modules:
  0.0 73.9 jit_solution(11087323834653361288)
XLA Ops:
  0.0 0.5 collective-permute-start.1
  0.5 1.1 %fusion.9 = (bf16[1,128,896]{2,1,0:T(8,128)(2,1)S(1)}, bf16[1,128,896]{2,1,0:T(8,128)(2,1)S(1)}) fusion(bf16[2,128,896]{2,1,0:T(8,128)(2,1)} %rest_0_.1), kind=kLoop, calls=%fused_computation.29 | loop fusion | bytes 917504 | tf_op jit(solution)/shard_map/slice | solution.py:360
  1.6 2.7 %collective-permute-start.2 = (bf16[1,128,896]{2,1,0:T(8,128)(2,1)S(1)}, bf16[1,128,896]{2,1,0:T(8,128)(2,1)S(1)}, u32[]{:S(2)}, u32[]{:S(2)}) collective-permute-start(bf16[1,128,896]{2,1,0:T(8,128)(2,1)S(1)} %get-tuple-element.62), channel_id=1, source_target_pairs={{0,4},{1,5},{4,8},{5,9},{8,12},{9,13},{12,14},{13,15},{14,10},{15,... | collective-permute-start | bytes 688136 | tf_op jit(solution)/shard_map/ppermute | solution.py:315
  4.4 0.8 %pad_add_fusion = s32[2,1,2]{1,2,0:T(2,128)S(1)} fusion(s32[1,4,2]{1,2,0:T(2,128)} %bitcast.2, s32[1,4,2]{1,2,0:T(2,128)} %bitcast.4), kind=kLoop, calls=%fused_computation.6 | loop fusion | flops 4 | bytes 80 | tf_op jit(solution)/shard_map/stack | solution.py:350
  5.1 2.0 %collective-permute-start = (s32[2,1,2]{1,2,0:T(2,128)S(1)}, s32[2,1,2]{1,2,0:T(2,128)S(1)}, u32[]{:S(2)}, u32[]{:S(2)}) collective-permute-start(s32[2,1,2]{1,2,0:T(2,128)S(1)} %pad_add_fusion), channel_id=1, source_target_pairs={{0,1},{1,2},{2,3},{3,4},{4,5},{5,6},{6,7},{7,8},{8,9},{9,10},{10,1... | collective-permute-start | bytes 56 | tf_op jit(solution)/shard_map/ppermute | solution.py:351
  7.2 1.3 %fusion.2 = s32[]{:T(128)} fusion(s32[8]{0:T(128)} %constant.71.clone, s32[]{:T(128)S(6)} %select_n.52), kind=kLoop, calls=%fused_computation.22 | loop fusion | flops 23 | bytes 40 | tf_op jit(solution)/shard_map/reduce_sum | solution.py:330
  8.5 0.7 and_convert_fusion.keep_ref
  9.2 5.1 %fold_queries.1 = (bf16[16,256,896]{2,1,0:T(8,128)(2,1)}, f32[16,896]{1,0:T(8,128)S(1)}) custom-call(bf16[256,2048]{1,0:T(8,128)(2,1)} %query_hbm.1, bf16[896,2048]{1,0:T(8,128)(2,1)} %key_hbm.1), custom_call_target="tpu_custom_call" | custom-call | flops 939524096 | bytes 12582912 | tf_op jit(solution)/shard_map/fold_queries/pallas_call | solution.py:72
  14.3 0.1 add_add_fusion
  14.3 0.1 copy.14
  14.4 0.1 unstack.15
  14.5 0.1 copy.13
  14.6 0.1 unstack.13
  14.7 0.1 select_reduce_fusion
  14.8 1.9 %collective-permute-start.4 = (bf16[1,128,896]{2,1,0:T(8,128)(2,1)S(1)}, bf16[1,128,896]{2,1,0:T(8,128)(2,1)S(1)}, u32[]{:S(2)}, u32[]{:S(2)}) collective-permute-start(bf16[1,128,896]{2,1,0:T(8,128)(2,1)S(1)} %get-tuple-element.37), channel_id=1, source_target_pairs={{0,4},{1,5},{4,8},{5,9},{8,12},{9,13},{12,14},{13,15},{14,10},{15,... | collective-permute-start | bytes 688136 | tf_op jit(solution)/shard_map/ppermute | solution.py:315
  16.7 0.1 collective-permute-start.7
  16.9 0.7 compare_select_fusion.8
  17.6 1.9 %collective-permute-start.8 = (bf16[1,128,896]{2,1,0:T(8,128)(2,1)S(1)}, bf16[1,128,896]{2,1,0:T(8,128)(2,1)S(1)}, u32[]{:S(2)}, u32[]{:S(2)}) collective-permute-start(bf16[1,128,896]{2,1,0:T(8,128)(2,1)S(1)} %collective-permute-done.2.rest_2_), channel_id=1, source_target_pairs={{0,4},{1,5},{4,8},{5,9},{8,12},{9,13},{12,14},{13,15},{14,10},{15,... | collective-permute-start | bytes 688136 | tf_op jit(solution)/shard_map/ppermute | solution.py:315
  19.5 0.1 collective-permute-start.11
  19.7 2.7 %collective-permute-done.4.rest_6_ = bf16[1,128,896]{2,1,0:T(8,128)(2,1)S(1)} collective-permute-done((bf16[1,128,896]{2,1,0:T(8,128)(2,1)S(1)}, bf16[1,128,896]{2,1,0:T(8,128)(2,1)S(1)}, u32[]{:S(2)}, u32[]{:S(2)}) %collective-permute-start.4) | collective-permute-done | bytes 229408 | tf_op jit(solution)/shard_map/ppermute | solution.py:315
  22.4 2.5 %collective-permute-done.7.rest_8_ = bf16[1,128,896]{2,1,0:T(8,128)(2,1)S(1)} collective-permute-done((bf16[1,128,896]{2,1,0:T(8,128)(2,1)S(1)}, bf16[1,128,896]{2,1,0:T(8,128)(2,1)S(1)}, u32[]{:S(2)}, u32[]{:S(2)}) %collective-permute-start.7) | collective-permute-done | bytes 229408 | tf_op jit(solution)/shard_map/ppermute | solution.py:315
  24.9 1.6 %collective-permute-start.12 = (bf16[1,128,896]{2,1,0:T(8,128)(2,1)S(1)}, bf16[1,128,896]{2,1,0:T(8,128)(2,1)S(1)}, u32[]{:S(2)}, u32[]{:S(2)}) collective-permute-start(bf16[1,128,896]{2,1,0:T(8,128)(2,1)S(1)} %collective-permute-done.4.rest_6_), channel_id=1, source_target_pairs={{0,4},{1,5},{4,8},{5,9},{8,12},{9,13},{12,14},{13,15},{14,10},{15,... | collective-permute-start | bytes 688136 | tf_op jit(solution)/shard_map/ppermute | solution.py:315
  26.5 0.4 collective-permute-start.15
  27.0 0.1 collective-permute-start.5
  27.1 0.2 collective-permute-done.8.rest_10_
  27.3 1.1 %collective-permute-start.6 = (bf16[1,128,896]{2,1,0:T(8,128)(2,1)S(1)}, bf16[1,128,896]{2,1,0:T(8,128)(2,1)S(1)}, u32[]{:S(2)}, u32[]{:S(2)}) collective-permute-start(bf16[1,128,896]{2,1,0:T(8,128)(2,1)S(1)} %collective-permute-done.3.rest_4_), channel_id=1, source_target_pairs={{0,1},{1,0},{2,3},{3,2},{4,5},{5,4},{6,7},{7,6},{8,9},{9,8},{10,11... | collective-permute-start | bytes 688136 | tf_op jit(solution)/shard_map/ppermute | solution.py:318
  28.4 1.5 %collective-permute-done.11.rest_12_ = bf16[1,128,896]{2,1,0:T(8,128)(2,1)S(1)} collective-permute-done((bf16[1,128,896]{2,1,0:T(8,128)(2,1)S(1)}, bf16[1,128,896]{2,1,0:T(8,128)(2,1)S(1)}, u32[]{:S(2)}, u32[]{:S(2)}) %collective-permute-start.11) | collective-permute-done | bytes 229408 | tf_op jit(solution)/shard_map/ppermute | solution.py:315
  29.8 1.6 %collective-permute-start.16 = (bf16[1,128,896]{2,1,0:T(8,128)(2,1)S(1)}, bf16[1,128,896]{2,1,0:T(8,128)(2,1)S(1)}, u32[]{:S(2)}, u32[]{:S(2)}) collective-permute-start(bf16[1,128,896]{2,1,0:T(8,128)(2,1)S(1)} %collective-permute-done.8.rest_10_), channel_id=1, source_target_pairs={{0,4},{1,5},{4,8},{5,9},{8,12},{9,13},{12,14},{13,15},{14,10},{15,... | collective-permute-start | bytes 688136 | tf_op jit(solution)/shard_map/ppermute | solution.py:315
  31.4 2.0 %collective-permute-done.12.rest_14_ = bf16[1,128,896]{2,1,0:T(8,128)(2,1)S(1)} collective-permute-done((bf16[1,128,896]{2,1,0:T(8,128)(2,1)S(1)}, bf16[1,128,896]{2,1,0:T(8,128)(2,1)S(1)}, u32[]{:S(2)}, u32[]{:S(2)}) %collective-permute-start.12) | collective-permute-done | bytes 229408 | tf_op jit(solution)/shard_map/ppermute | solution.py:315
  33.4 1.0 %collective-permute-start.19 = (bf16[1,128,896]{2,1,0:T(8,128)(2,1)S(1)}, bf16[1,128,896]{2,1,0:T(8,128)(2,1)S(1)}, u32[]{:S(2)}, u32[]{:S(2)}) collective-permute-start(bf16[1,128,896]{2,1,0:T(8,128)(2,1)S(1)} %collective-permute-done.11.rest_12_), channel_id=1, source_target_pairs={{0,2},{1,3},{4,0},{5,1},{8,4},{9,5},{12,8},{13,9},{14,12},{15,13},... | collective-permute-start | bytes 688136 | tf_op jit(solution)/shard_map/ppermute | solution.py:315
  34.4 0.7 collective-permute-done.15.rest_16_
  35.0 0.9 %collective-permute-start.23 = (bf16[1,128,896]{2,1,0:T(8,128)(2,1)S(1)}, bf16[1,128,896]{2,1,0:T(8,128)(2,1)S(1)}, u32[]{:S(2)}, u32[]{:S(2)}) collective-permute-start(bf16[1,128,896]{2,1,0:T(8,128)(2,1)S(1)} %collective-permute-done.15.rest_16_), channel_id=1, source_target_pairs={{0,2},{1,3},{4,0},{5,1},{8,4},{9,5},{12,8},{13,9},{14,12},{15,13},... | collective-permute-start | bytes 688136 | tf_op jit(solution)/shard_map/ppermute | solution.py:315
  36.0 0.8 %collective-permute-start.9 = (bf16[1,128,896]{2,1,0:T(8,128)(2,1)S(1)}, bf16[1,128,896]{2,1,0:T(8,128)(2,1)S(1)}, u32[]{:S(2)}, u32[]{:S(2)}) collective-permute-start(bf16[1,128,896]{2,1,0:T(8,128)(2,1)S(1)} %collective-permute-done.4.rest_6_), channel_id=1, source_target_pairs={{0,1},{1,0},{2,3},{3,2},{4,5},{5,4},{6,7},{7,6},{8,9},{9,8},{10,11... | collective-permute-start | bytes 688136 | tf_op jit(solution)/shard_map/ppermute | solution.py:318
  36.7 0.1 collective-permute-start.10
  36.8 1.3 %collective-permute-done.16.rest_18_ = bf16[1,128,896]{2,1,0:T(8,128)(2,1)S(1)} collective-permute-done((bf16[1,128,896]{2,1,0:T(8,128)(2,1)S(1)}, bf16[1,128,896]{2,1,0:T(8,128)(2,1)S(1)}, u32[]{:S(2)}, u32[]{:S(2)}) %collective-permute-start.16) | collective-permute-done | bytes 229408 | tf_op jit(solution)/shard_map/ppermute | solution.py:315
  38.1 1.9 %collective-permute-start.20 = (bf16[1,128,896]{2,1,0:T(8,128)(2,1)S(1)}, bf16[1,128,896]{2,1,0:T(8,128)(2,1)S(1)}, u32[]{:S(2)}, u32[]{:S(2)}) collective-permute-start(bf16[1,128,896]{2,1,0:T(8,128)(2,1)S(1)} %collective-permute-done.12.rest_14_), channel_id=1, source_target_pairs={{0,4},{1,5},{4,8},{5,9},{8,12},{9,13},{12,14},{13,15},{14,10},{15,... | collective-permute-start | bytes 688136 | tf_op jit(solution)/shard_map/ppermute | solution.py:315
  40.0 1.9 %collective-permute-done.19.rest_20_ = bf16[1,128,896]{2,1,0:T(8,128)(2,1)S(1)} collective-permute-done((bf16[1,128,896]{2,1,0:T(8,128)(2,1)S(1)}, bf16[1,128,896]{2,1,0:T(8,128)(2,1)S(1)}, u32[]{:S(2)}, u32[]{:S(2)}) %collective-permute-start.19) | collective-permute-done | bytes 229408 | tf_op jit(solution)/shard_map/ppermute | solution.py:315
  41.9 4.0 %collective-permute-done.23.rest_24_ = bf16[1,128,896]{2,1,0:T(8,128)(2,1)S(1)} collective-permute-done((bf16[1,128,896]{2,1,0:T(8,128)(2,1)S(1)}, bf16[1,128,896]{2,1,0:T(8,128)(2,1)S(1)}, u32[]{:S(2)}, u32[]{:S(2)}) %collective-permute-start.23) | collective-permute-done | bytes 229408 | tf_op jit(solution)/shard_map/ppermute | solution.py:315
  45.8 1.7 %collective-permute-start.24 = (bf16[1,128,896]{2,1,0:T(8,128)(2,1)S(1)}, bf16[1,128,896]{2,1,0:T(8,128)(2,1)S(1)}, u32[]{:S(2)}, u32[]{:S(2)}) collective-permute-start(bf16[1,128,896]{2,1,0:T(8,128)(2,1)S(1)} %collective-permute-done.16.rest_18_), channel_id=1, source_target_pairs={{0,4},{1,5},{4,8},{5,9},{8,12},{9,13},{12,14},{13,15},{14,10},{15,... | collective-permute-start | bytes 688136 | tf_op jit(solution)/shard_map/ppermute | solution.py:315
  47.6 0.5 collective-permute-start.17
  48.1 0.3 collective-permute-start.27
  48.4 5.0 %collective-permute-done.24.rest_0_ = bf16[1,128,896]{2,1,0:T(8,128)(2,1)S(1)} collective-permute-done((bf16[1,128,896]{2,1,0:T(8,128)(2,1)S(1)}, bf16[1,128,896]{2,1,0:T(8,128)(2,1)S(1)}, u32[]{:S(2)}, u32[]{:S(2)}) %collective-permute-start.24) | collective-permute-done | bytes 229408 | tf_op jit(solution)/shard_map/ppermute | solution.py:315
  53.4 0.5 collective-permute-start.22
  54.0 1.8 %collective-permute-done.27.rest_2_ = bf16[1,128,896]{2,1,0:T(8,128)(2,1)S(1)} collective-permute-done((bf16[1,128,896]{2,1,0:T(8,128)(2,1)S(1)}, bf16[1,128,896]{2,1,0:T(8,128)(2,1)S(1)}, u32[]{:S(2)}, u32[]{:S(2)}) %collective-permute-start.27) | collective-permute-done | bytes 229408 | tf_op jit(solution)/shard_map/ppermute | solution.py:315
  55.9 0.5 collective-permute-start.28
  56.4 0.9 %collective-permute-done.26.rest_25_ = bf16[1,128,896]{2,1,0:T(8,128)(2,1)S(1)} collective-permute-done((bf16[1,128,896]{2,1,0:T(8,128)(2,1)S(1)}, bf16[1,128,896]{2,1,0:T(8,128)(2,1)S(1)}, u32[]{:S(2)}, u32[]{:S(2)}) %collective-permute-start.26) | collective-permute-done | bytes 229408 | tf_op jit(solution)/shard_map/ppermute | solution.py:318
  57.3 5.0 %collect_blocks.1.tokens_in = bf16[10,128,896]{2,1,0:T(8,128)(2,1)S(1)} custom-call(s32[10]{0:T(128)S(1)} %fusion.1.source_ref, s32[10]{0:T(128)S(1)} %get-tuple-element.59.block_ref, bf16[2,128,896]{2,1,0:T(8,128)(2,1)S(1)} %copy-done, bf16[2,128,896]{2,1,0:T(8,128)(2,1)S(1)} %collective-permute-done.1.rest_1_, ...), custom_call_target="tpu_custom_call" | custom-call | flops 4194304 | bytes 8388608 | tf_op jit(solution)/shard_map/collect_blocks/pallas_call | solution.py:148
  62.4 11.3 %attend_windows.1 = bf16[256,2048]{1,0:T(8,128)(2,1)} custom-call(s32[10]{0:T(128)S(1)} %fusion.1.source_ref, s32[10]{0:T(128)S(1)} %get-tuple-element.59.block_ref, s32[4]{0:T(128)S(1)} %and_convert_fusion.keep_ref, bf16[16,256,896]{2,1,0:T(8,128)(2,1)} %get-tuple-element.32.folded_hbm, f32[16,896]{1,0:T(8,128)S(1)} %get-tuple-element.33.single_ref, ...), custom_call_target="tpu_custom_call" | custom-call | flops 4697620480 | bytes 16777216 | tf_op jit(solution)/shard_map/attend_windows/pallas_call | solution.py:263
  (39 shorter events, 0.3 us)
Async XLA Ops:
  0.0 14.7 %copy-start.4 = (s32[8]{0:T(128)S(1)}, s32[8]{0:T(128)}, u32[]{:S(2)}) copy-start(s32[8]{0:T(128)} %constant.71.clone) | copy-start | bytes 100
  0.0 57.3 %copy-start = (bf16[2,128,896]{2,1,0:T(8,128)(2,1)S(1)}, bf16[2,128,896]{2,1,0:T(8,128)(2,1)}, u32[]{:S(2)}) copy-start(bf16[2,128,896]{2,1,0:T(8,128)(2,1)} %rest_0_.1) | copy-start | bytes 1376260
  0.0 14.2 %copy-start.2 = (s32[4,2]{0,1:T(2,128)S(1)}, s32[4,2]{0,1:T(2,128)}, u32[]{:S(2)}) copy-start(s32[4,2]{0,1:T(2,128)} %param.13) | copy-start | bytes 100
  0.0 14.2 %copy-start.3 = (s32[4,2]{0,1:T(2,128)S(1)}, s32[4,2]{0,1:T(2,128)}, u32[]{:S(2)}) copy-start(s32[4,2]{0,1:T(2,128)} %param.12) | copy-start | bytes 100
  0.0 14.8 %collective-permute-start.1 = (bf16[2,128,896]{2,1,0:T(8,128)(2,1)}, bf16[2,128,896]{2,1,0:T(8,128)(2,1)S(1)}, u32[]{:S(2)}, u32[]{:S(2)}) collective-permute-start(bf16[2,128,896]{2,1,0:T(8,128)(2,1)} %rest_0_.1), channel_id=1, source_target_pairs={{0,1},{1,0},{2,3},{3,2},{4,5},{5,4},{6,7},{7,6},{8,9},{9,8},{10,11... | collective-permute-start | bytes 1376264 | tf_op jit(solution)/shard_map/ppermute | solution.py:318
  1.6 15.9 %collective-permute-start.2 = (bf16[1,128,896]{2,1,0:T(8,128)(2,1)S(1)}, bf16[1,128,896]{2,1,0:T(8,128)(2,1)S(1)}, u32[]{:S(2)}, u32[]{:S(2)}) collective-permute-start(bf16[1,128,896]{2,1,0:T(8,128)(2,1)S(1)} %get-tuple-element.62), channel_id=1, source_target_pairs={{0,4},{1,5},{4,8},{5,9},{8,12},{9,13},{12,14},{13,15},{14,10},{15,... | collective-permute-start | bytes 688136 | tf_op jit(solution)/shard_map/ppermute | solution.py:315
  4.4 15.2 %collective-permute-start.3 = (bf16[1,128,896]{2,1,0:T(8,128)(2,1)S(1)}, bf16[1,128,896]{2,1,0:T(8,128)(2,1)S(1)}, u32[]{:S(2)}, u32[]{:S(2)}) collective-permute-start(bf16[1,128,896]{2,1,0:T(8,128)(2,1)S(1)} %get-tuple-element.62), channel_id=1, source_target_pairs={{0,2},{1,3},{4,0},{5,1},{8,4},{9,5},{12,8},{13,9},{14,12},{15,13},... | collective-permute-start | bytes 688136 | tf_op jit(solution)/shard_map/ppermute | solution.py:315
  5.1 9.1 %collective-permute-start = (s32[2,1,2]{1,2,0:T(2,128)S(1)}, s32[2,1,2]{1,2,0:T(2,128)S(1)}, u32[]{:S(2)}, u32[]{:S(2)}) collective-permute-start(s32[2,1,2]{1,2,0:T(2,128)S(1)} %pad_add_fusion), channel_id=1, source_target_pairs={{0,1},{1,2},{2,3},{3,4},{4,5},{5,6},{6,7},{7,8},{8,9},{9,10},{10,1... | collective-permute-start | bytes 56 | tf_op jit(solution)/shard_map/ppermute | solution.py:351
  14.8 7.6 %collective-permute-start.4 = (bf16[1,128,896]{2,1,0:T(8,128)(2,1)S(1)}, bf16[1,128,896]{2,1,0:T(8,128)(2,1)S(1)}, u32[]{:S(2)}, u32[]{:S(2)}) collective-permute-start(bf16[1,128,896]{2,1,0:T(8,128)(2,1)S(1)} %get-tuple-element.37), channel_id=1, source_target_pairs={{0,4},{1,5},{4,8},{5,9},{8,12},{9,13},{12,14},{13,15},{14,10},{15,... | collective-permute-start | bytes 688136 | tf_op jit(solution)/shard_map/ppermute | solution.py:315
  16.7 8.2 %collective-permute-start.7 = (bf16[1,128,896]{2,1,0:T(8,128)(2,1)S(1)}, bf16[1,128,896]{2,1,0:T(8,128)(2,1)S(1)}, u32[]{:S(2)}, u32[]{:S(2)}) collective-permute-start(bf16[1,128,896]{2,1,0:T(8,128)(2,1)S(1)} %get-tuple-element.37), channel_id=1, source_target_pairs={{0,2},{1,3},{4,0},{5,1},{8,4},{9,5},{12,8},{13,9},{14,12},{15,13},... | collective-permute-start | bytes 688136 | tf_op jit(solution)/shard_map/ppermute | solution.py:315
  17.6 9.7 %collective-permute-start.8 = (bf16[1,128,896]{2,1,0:T(8,128)(2,1)S(1)}, bf16[1,128,896]{2,1,0:T(8,128)(2,1)S(1)}, u32[]{:S(2)}, u32[]{:S(2)}) collective-permute-start(bf16[1,128,896]{2,1,0:T(8,128)(2,1)S(1)} %collective-permute-done.2.rest_2_), channel_id=1, source_target_pairs={{0,4},{1,5},{4,8},{5,9},{8,12},{9,13},{12,14},{13,15},{14,10},{15,... | collective-permute-start | bytes 688136 | tf_op jit(solution)/shard_map/ppermute | solution.py:315
  19.5 10.3 %collective-permute-start.11 = (bf16[1,128,896]{2,1,0:T(8,128)(2,1)S(1)}, bf16[1,128,896]{2,1,0:T(8,128)(2,1)S(1)}, u32[]{:S(2)}, u32[]{:S(2)}) collective-permute-start(bf16[1,128,896]{2,1,0:T(8,128)(2,1)S(1)} %collective-permute-done.3.rest_4_), channel_id=1, source_target_pairs={{0,2},{1,3},{4,0},{5,1},{8,4},{9,5},{12,8},{13,9},{14,12},{15,13},... | collective-permute-start | bytes 688136 | tf_op jit(solution)/shard_map/ppermute | solution.py:315
  24.9 37.5 %copy-start.1 = (bf16[896,2048]{1,0:T(8,128)(2,1)S(1)}, bf16[896,2048]{1,0:T(8,128)(2,1)}, u32[]{:S(2)}) copy-start(bf16[896,2048]{1,0:T(8,128)(2,1)} %value_ref.1) | copy-start | bytes 11010052
  24.9 8.5 %collective-permute-start.12 = (bf16[1,128,896]{2,1,0:T(8,128)(2,1)S(1)}, bf16[1,128,896]{2,1,0:T(8,128)(2,1)S(1)}, u32[]{:S(2)}, u32[]{:S(2)}) collective-permute-start(bf16[1,128,896]{2,1,0:T(8,128)(2,1)S(1)} %collective-permute-done.4.rest_6_), channel_id=1, source_target_pairs={{0,4},{1,5},{4,8},{5,9},{8,12},{9,13},{12,14},{13,15},{14,10},{15,... | collective-permute-start | bytes 688136 | tf_op jit(solution)/shard_map/ppermute | solution.py:315
  26.5 8.5 %collective-permute-start.15 = (bf16[1,128,896]{2,1,0:T(8,128)(2,1)S(1)}, bf16[1,128,896]{2,1,0:T(8,128)(2,1)S(1)}, u32[]{:S(2)}, u32[]{:S(2)}) collective-permute-start(bf16[1,128,896]{2,1,0:T(8,128)(2,1)S(1)} %collective-permute-done.7.rest_8_), channel_id=1, source_target_pairs={{0,2},{1,3},{4,0},{5,1},{8,4},{9,5},{12,8},{13,9},{14,12},{15,13},... | collective-permute-start | bytes 688136 | tf_op jit(solution)/shard_map/ppermute | solution.py:315
  27.0 9.0 %collective-permute-start.5 = (bf16[1,128,896]{2,1,0:T(8,128)(2,1)S(1)}, bf16[1,128,896]{2,1,0:T(8,128)(2,1)S(1)}, u32[]{:S(2)}, u32[]{:S(2)}) collective-permute-start(bf16[1,128,896]{2,1,0:T(8,128)(2,1)S(1)} %collective-permute-done.2.rest_2_), channel_id=1, source_target_pairs={{0,1},{1,0},{2,3},{3,2},{4,5},{5,4},{6,7},{7,6},{8,9},{9,8},{10,11... | collective-permute-start | bytes 688136 | tf_op jit(solution)/shard_map/ppermute | solution.py:318
  27.3 9.4 %collective-permute-start.6 = (bf16[1,128,896]{2,1,0:T(8,128)(2,1)S(1)}, bf16[1,128,896]{2,1,0:T(8,128)(2,1)S(1)}, u32[]{:S(2)}, u32[]{:S(2)}) collective-permute-start(bf16[1,128,896]{2,1,0:T(8,128)(2,1)S(1)} %collective-permute-done.3.rest_4_), channel_id=1, source_target_pairs={{0,1},{1,0},{2,3},{3,2},{4,5},{5,4},{6,7},{7,6},{8,9},{9,8},{10,11... | collective-permute-start | bytes 688136 | tf_op jit(solution)/shard_map/ppermute | solution.py:318
  29.8 8.2 %collective-permute-start.16 = (bf16[1,128,896]{2,1,0:T(8,128)(2,1)S(1)}, bf16[1,128,896]{2,1,0:T(8,128)(2,1)S(1)}, u32[]{:S(2)}, u32[]{:S(2)}) collective-permute-start(bf16[1,128,896]{2,1,0:T(8,128)(2,1)S(1)} %collective-permute-done.8.rest_10_), channel_id=1, source_target_pairs={{0,4},{1,5},{4,8},{5,9},{8,12},{9,13},{12,14},{13,15},{14,10},{15,... | collective-permute-start | bytes 688136 | tf_op jit(solution)/shard_map/ppermute | solution.py:315
  33.4 8.5 %collective-permute-start.19 = (bf16[1,128,896]{2,1,0:T(8,128)(2,1)S(1)}, bf16[1,128,896]{2,1,0:T(8,128)(2,1)S(1)}, u32[]{:S(2)}, u32[]{:S(2)}) collective-permute-start(bf16[1,128,896]{2,1,0:T(8,128)(2,1)S(1)} %collective-permute-done.11.rest_12_), channel_id=1, source_target_pairs={{0,2},{1,3},{4,0},{5,1},{8,4},{9,5},{12,8},{13,9},{14,12},{15,13},... | collective-permute-start | bytes 688136 | tf_op jit(solution)/shard_map/ppermute | solution.py:315
  35.0 10.8 %collective-permute-start.23 = (bf16[1,128,896]{2,1,0:T(8,128)(2,1)S(1)}, bf16[1,128,896]{2,1,0:T(8,128)(2,1)S(1)}, u32[]{:S(2)}, u32[]{:S(2)}) collective-permute-start(bf16[1,128,896]{2,1,0:T(8,128)(2,1)S(1)} %collective-permute-done.15.rest_16_), channel_id=1, source_target_pairs={{0,2},{1,3},{4,0},{5,1},{8,4},{9,5},{12,8},{13,9},{14,12},{15,13},... | collective-permute-start | bytes 688136 | tf_op jit(solution)/shard_map/ppermute | solution.py:315
  36.0 11.6 %collective-permute-start.9 = (bf16[1,128,896]{2,1,0:T(8,128)(2,1)S(1)}, bf16[1,128,896]{2,1,0:T(8,128)(2,1)S(1)}, u32[]{:S(2)}, u32[]{:S(2)}) collective-permute-start(bf16[1,128,896]{2,1,0:T(8,128)(2,1)S(1)} %collective-permute-done.4.rest_6_), channel_id=1, source_target_pairs={{0,1},{1,0},{2,3},{3,2},{4,5},{5,4},{6,7},{7,6},{8,9},{9,8},{10,11... | collective-permute-start | bytes 688136 | tf_op jit(solution)/shard_map/ppermute | solution.py:318
  36.7 10.9 %collective-permute-start.10 = (bf16[1,128,896]{2,1,0:T(8,128)(2,1)S(1)}, bf16[1,128,896]{2,1,0:T(8,128)(2,1)S(1)}, u32[]{:S(2)}, u32[]{:S(2)}) collective-permute-start(bf16[1,128,896]{2,1,0:T(8,128)(2,1)S(1)} %collective-permute-done.7.rest_8_), channel_id=1, source_target_pairs={{0,1},{1,0},{2,3},{3,2},{4,5},{5,4},{6,7},{7,6},{8,9},{9,8},{10,11... | collective-permute-start | bytes 688136 | tf_op jit(solution)/shard_map/ppermute | solution.py:318
  38.1 10.0 %collective-permute-start.20 = (bf16[1,128,896]{2,1,0:T(8,128)(2,1)S(1)}, bf16[1,128,896]{2,1,0:T(8,128)(2,1)S(1)}, u32[]{:S(2)}, u32[]{:S(2)}) collective-permute-start(bf16[1,128,896]{2,1,0:T(8,128)(2,1)S(1)} %collective-permute-done.12.rest_14_), channel_id=1, source_target_pairs={{0,4},{1,5},{4,8},{5,9},{8,12},{9,13},{12,14},{13,15},{14,10},{15,... | collective-permute-start | bytes 688136 | tf_op jit(solution)/shard_map/ppermute | solution.py:315
  41.9 6.5 %collective-permute-start.13 = (bf16[1,128,896]{2,1,0:T(8,128)(2,1)S(1)}, bf16[1,128,896]{2,1,0:T(8,128)(2,1)S(1)}, u32[]{:S(2)}, u32[]{:S(2)}) collective-permute-start(bf16[1,128,896]{2,1,0:T(8,128)(2,1)S(1)} %collective-permute-done.8.rest_10_), channel_id=1, source_target_pairs={{0,1},{1,0},{2,3},{3,2},{4,5},{5,4},{6,7},{7,6},{8,9},{9,8},{10,11... | collective-permute-start | bytes 688136 | tf_op jit(solution)/shard_map/ppermute | solution.py:318
  45.8 7.6 %collective-permute-start.24 = (bf16[1,128,896]{2,1,0:T(8,128)(2,1)S(1)}, bf16[1,128,896]{2,1,0:T(8,128)(2,1)S(1)}, u32[]{:S(2)}, u32[]{:S(2)}) collective-permute-start(bf16[1,128,896]{2,1,0:T(8,128)(2,1)S(1)} %collective-permute-done.16.rest_18_), channel_id=1, source_target_pairs={{0,4},{1,5},{4,8},{5,9},{8,12},{9,13},{12,14},{13,15},{14,10},{15,... | collective-permute-start | bytes 688136 | tf_op jit(solution)/shard_map/ppermute | solution.py:315
  47.6 5.8 %collective-permute-start.14 = (bf16[1,128,896]{2,1,0:T(8,128)(2,1)S(1)}, bf16[1,128,896]{2,1,0:T(8,128)(2,1)S(1)}, u32[]{:S(2)}, u32[]{:S(2)}) collective-permute-start(bf16[1,128,896]{2,1,0:T(8,128)(2,1)S(1)} %collective-permute-done.11.rest_12_), channel_id=1, source_target_pairs={{0,1},{1,0},{2,3},{3,2},{4,5},{5,4},{6,7},{7,6},{8,9},{9,8},{10,11... | collective-permute-start | bytes 688136 | tf_op jit(solution)/shard_map/ppermute | solution.py:318
  47.6 6.3 %collective-permute-start.17 = (bf16[1,128,896]{2,1,0:T(8,128)(2,1)S(1)}, bf16[1,128,896]{2,1,0:T(8,128)(2,1)S(1)}, u32[]{:S(2)}, u32[]{:S(2)}) collective-permute-start(bf16[1,128,896]{2,1,0:T(8,128)(2,1)S(1)} %collective-permute-done.12.rest_14_), channel_id=1, source_target_pairs={{0,1},{1,0},{2,3},{3,2},{4,5},{5,4},{6,7},{7,6},{8,9},{9,8},{10,11... | collective-permute-start | bytes 688136 | tf_op jit(solution)/shard_map/ppermute | solution.py:318
  48.1 7.7 %collective-permute-start.27 = (bf16[1,128,896]{2,1,0:T(8,128)(2,1)S(1)}, bf16[1,128,896]{2,1,0:T(8,128)(2,1)S(1)}, u32[]{:S(2)}, u32[]{:S(2)}) collective-permute-start(bf16[1,128,896]{2,1,0:T(8,128)(2,1)S(1)} %collective-permute-done.23.rest_24_), channel_id=1, source_target_pairs={{0,2},{1,3},{4,0},{5,1},{8,4},{9,5},{12,8},{13,9},{14,12},{15,13},... | collective-permute-start | bytes 688136 | tf_op jit(solution)/shard_map/ppermute | solution.py:315
  48.4 7.5 %collective-permute-start.18 = (bf16[1,128,896]{2,1,0:T(8,128)(2,1)S(1)}, bf16[1,128,896]{2,1,0:T(8,128)(2,1)S(1)}, u32[]{:S(2)}, u32[]{:S(2)}) collective-permute-start(bf16[1,128,896]{2,1,0:T(8,128)(2,1)S(1)} %collective-permute-done.15.rest_16_), channel_id=1, source_target_pairs={{0,1},{1,0},{2,3},{3,2},{4,5},{5,4},{6,7},{7,6},{8,9},{9,8},{10,11... | collective-permute-start | bytes 688136 | tf_op jit(solution)/shard_map/ppermute | solution.py:318
  53.4 3.0 %collective-permute-start.21 = (bf16[1,128,896]{2,1,0:T(8,128)(2,1)S(1)}, bf16[1,128,896]{2,1,0:T(8,128)(2,1)S(1)}, u32[]{:S(2)}, u32[]{:S(2)}) collective-permute-start(bf16[1,128,896]{2,1,0:T(8,128)(2,1)S(1)} %collective-permute-done.16.rest_18_), channel_id=1, source_target_pairs={{0,1},{1,0},{2,3},{3,2},{4,5},{5,4},{6,7},{7,6},{8,9},{9,8},{10,11... | collective-permute-start | bytes 688136 | tf_op jit(solution)/shard_map/ppermute | solution.py:318
  53.4 3.0 %collective-permute-start.22 = (bf16[1,128,896]{2,1,0:T(8,128)(2,1)S(1)}, bf16[1,128,896]{2,1,0:T(8,128)(2,1)S(1)}, u32[]{:S(2)}, u32[]{:S(2)}) collective-permute-start(bf16[1,128,896]{2,1,0:T(8,128)(2,1)S(1)} %collective-permute-done.19.rest_20_), channel_id=1, source_target_pairs={{0,1},{1,0},{2,3},{3,2},{4,5},{5,4},{6,7},{7,6},{8,9},{9,8},{10,11... | collective-permute-start | bytes 688136 | tf_op jit(solution)/shard_map/ppermute | solution.py:318
  53.9 2.5 %collective-permute-start.25 = (bf16[1,128,896]{2,1,0:T(8,128)(2,1)S(1)}, bf16[1,128,896]{2,1,0:T(8,128)(2,1)S(1)}, u32[]{:S(2)}, u32[]{:S(2)}) collective-permute-start(bf16[1,128,896]{2,1,0:T(8,128)(2,1)S(1)} %collective-permute-done.20.rest_22_), channel_id=1, source_target_pairs={{0,1},{1,0},{2,3},{3,2},{4,5},{5,4},{6,7},{7,6},{8,9},{9,8},{10,11... | collective-permute-start | bytes 688136 | tf_op jit(solution)/shard_map/ppermute | solution.py:318
  55.8 1.5 %collective-permute-start.26 = (bf16[1,128,896]{2,1,0:T(8,128)(2,1)S(1)}, bf16[1,128,896]{2,1,0:T(8,128)(2,1)S(1)}, u32[]{:S(2)}, u32[]{:S(2)}) collective-permute-start(bf16[1,128,896]{2,1,0:T(8,128)(2,1)S(1)} %collective-permute-done.23.rest_24_), channel_id=1, source_target_pairs={{0,1},{1,0},{2,3},{3,2},{4,5},{5,4},{6,7},{7,6},{8,9},{9,8},{10,11... | collective-permute-start | bytes 688136 | tf_op jit(solution)/shard_map/ppermute | solution.py:318
  55.9 6.5 %collective-permute-start.28 = (bf16[1,128,896]{2,1,0:T(8,128)(2,1)S(1)}, bf16[1,128,896]{2,1,0:T(8,128)(2,1)S(1)}, u32[]{:S(2)}, u32[]{:S(2)}) collective-permute-start(bf16[1,128,896]{2,1,0:T(8,128)(2,1)S(1)} %collective-permute-done.24.rest_0_), channel_id=1, source_target_pairs={{0,1},{1,0},{2,3},{3,2},{4,5},{5,4},{6,7},{7,6},{8,9},{9,8},{10,11... | collective-permute-start | bytes 688136 | tf_op jit(solution)/shard_map/ppermute | solution.py:318
  56.4 6.0 %collective-permute-start.29 = (bf16[1,128,896]{2,1,0:T(8,128)(2,1)S(1)}, bf16[1,128,896]{2,1,0:T(8,128)(2,1)S(1)}, u32[]{:S(2)}, u32[]{:S(2)}) collective-permute-start(bf16[1,128,896]{2,1,0:T(8,128)(2,1)S(1)} %collective-permute-done.27.rest_2_), channel_id=1, source_target_pairs={{0,1},{1,0},{2,3},{3,2},{4,5},{5,4},{6,7},{7,6},{8,9},{9,8},{10,11... | collective-permute-start | bytes 688136 | tf_op jit(solution)/shard_map/ppermute | solution.py:318

commit v8 on v6

v8 whole, which is shorter than its diff:
```python
import functools
import math

import jax
import jax.numpy as jnp
from jax import lax
from jax.experimental import pallas as pl
from jax.experimental.pallas import tpu as pltpu
from jax.sharding import PartitionSpec as P

SPAN = 64
HEADS = 16
HEAD_DIM = 128
EPS = 1e-6
SCALE = math.log2(math.e) / math.sqrt(HEAD_DIM)
CORES = 2
GROUP = 4
MIB = 2**20


SMEM_SPEC = pl.BlockSpec(memory_space=pltpu.SMEM)
VMEM_SPEC = pl.BlockSpec(memory_space=pltpu.VMEM)
HBM_SPEC = pl.BlockSpec(memory_space=pltpu.HBM)


def contract(left, right, dims):
    return lax.dot_general(left, right, (dims, ((), ())), preferred_element_type=jnp.float32)


def in_hbm(value):
    return pltpu.with_memory_space_constraint(value, pltpu.HBM)


def head_columns(head):
    return slice(head * HEAD_DIM, (head + 1) * HEAD_DIM)


def fold_kernel(query_hbm, key_hbm, folded_hbm, single_ref, query, key, folded, in_sems, out_sems):
    groups = HEADS // GROUP

    def fetch(group):
        columns = slice(group * GROUP * HEAD_DIM, (group + 1) * GROUP * HEAD_DIM)
        return (
            pltpu.make_async_copy(query_hbm.at[:, columns], query.at[:, columns], in_sems.at[group, 0]),
            pltpu.make_async_copy(key_hbm.at[:, columns], key.at[:, columns], in_sems.at[group, 1]),
        )

    def put(head):
        return pltpu.make_async_copy(folded.at[head], folded_hbm.at[head], out_sems.at[head])

    for group in range(groups):
        for copy in fetch(group):
            copy.start()
    for head in range(HEADS):
        if head % GROUP == 0:
            for copy in fetch(head // GROUP):
                copy.wait()
        columns = head_columns(head)
        queries = pltpu.roll(query[:, columns].astype(jnp.float32), 1, 0).astype(jnp.bfloat16)
        rows = contract(queries, key[:, columns], ((1,), (1,))) * SCALE
        single_ref[head : head + 1, :] = rows[:1]
        folded[head] = rows.astype(jnp.bfloat16)
        put(head).start()
    for head in range(HEADS):
        put(head).wait()


def fold(queries, w_key):
    count, width = queries.shape[0], w_key.shape[0]
    shape = (HEADS, count, width)
    return pl.pallas_call(
        fold_kernel,
        out_shape=(
            pltpu.HBM(shape, jnp.bfloat16),
            jax.ShapeDtypeStruct((HEADS, width), jnp.float32),
        ),
        in_specs=[HBM_SPEC] * 2,
        out_specs=(HBM_SPEC, VMEM_SPEC),
        scratch_shapes=[
            pltpu.VMEM(queries.shape, jnp.bfloat16),
            pltpu.VMEM(w_key.shape, jnp.bfloat16),
            pltpu.VMEM(shape, jnp.bfloat16),
            pltpu.SemaphoreType.DMA((HEADS // GROUP, 2)),
            pltpu.SemaphoreType.DMA((HEADS,)),
        ],
        compiler_params=pltpu.CompilerParams(vmem_limit_bytes=28 * MIB),
        cost_estimate=pl.CostEstimate(
            flops=2 * queries.size * width, bytes_accessed=12 * MIB, transcendentals=0
        ),
        name="fold_queries",
    )(in_hbm(queries), in_hbm(w_key))


def prepare_kernel(raw_ref, *slot_refs):
    for slot, slot_ref in enumerate(slot_refs):
        widened = raw_ref[slot].astype(jnp.float32)
        factor = lax.rsqrt(jnp.mean(widened * widened, axis=-1, keepdims=True) + EPS)
        slot_ref[0] = (widened * factor).astype(jnp.bfloat16)


def prepare(neighbours):
    slots, length, width = neighbours.shape
    return pl.pallas_call(
        prepare_kernel,
        out_shape=(jax.ShapeDtypeStruct((1, length, width), jnp.bfloat16),) * slots,
        in_specs=[VMEM_SPEC],
        out_specs=(VMEM_SPEC,) * slots,
        compiler_params=pltpu.CompilerParams(vmem_limit_bytes=8 * MIB),
        cost_estimate=pl.CostEstimate(flops=4 * neighbours.size, bytes_accessed=MIB, transcendentals=0),
        name="normalise_own",
    )(neighbours)


def among(stores, first, source, act):
    if len(stores) == 1:
        pl.when(source == first)(lambda: act(stores[0]))
        return
    half = len(stores) // 2
    pl.when(source < first + half)(lambda: among(stores[:half], first, source, act))
    pl.when(source >= first + half)(lambda: among(stores[half:], first + half, source, act))


def weigh(scores):
    powers = jnp.exp2(scores - jnp.max(scores, axis=-1, keepdims=True))
    totals = jnp.sum(powers, axis=-1, keepdims=True)
    return (powers * (1.0 / totals)).astype(jnp.bfloat16)


def attend_kernel(source_ref, block_ref, keep_ref, folded_hbm, single_ref, value_ref, *rest):
    *stores, out_ref, tokens, folded, scores, weights, mixed, sems, folded_sems = rest
    requests, length, width = tokens.shape
    blocks = requests // 2 - 1
    count = blocks * SPAN
    rows_at_once = GROUP * SPAN

    def fetch_folded(group):
        heads = pl.ds(group * GROUP, GROUP)
        return pltpu.make_async_copy(folded_hbm.at[heads], folded.at[heads], folded_sems.at[group])

    def fetch(request, store):
        return pltpu.make_async_copy(store.at[block_ref[request]], tokens.at[request], sems.at[request])

    def arrive(window):
        for request in (2 * window, 2 * window + 1):
            fetch(request, stores[0]).wait()

    for request in [2 * blocks, 2 * blocks + 1, *range(2 * blocks)]:
        among(stores, 0, source_ref[request], lambda store: fetch(request, store).start())
        if request == 1:
            fetch_folded(0).start()
    for group in range(1, HEADS // GROUP):
        fetch_folded(group).start()

    def along(window):
        return tokens[2 * window : 2 * window + 2].reshape(2 * length, width)

    arrive(blocks)
    lone = weigh(contract(single_ref[...].astype(jnp.bfloat16), along(blocks), ((1,), (1,))))
    lone = contract(lone, along(blocks), ((1,), (0,)))

    place = lax.broadcasted_iota(jnp.int32, (count, HEAD_DIM), 0)
    kept = place % SPAN == 0
    for block in range(blocks):
        kept = kept | ((place // SPAN == block) & (keep_ref[block] > 0))

    units = [(group, window) for group in range(HEADS // GROUP) for window in range(blocks)]

    def score(unit):
        group, window = units[unit]
        heads, rows = slice(group * GROUP, (group + 1) * GROUP), slice(window * SPAN, (window + 1) * SPAN)
        if group == 0:
            arrive(window)
        if window == 0:
            fetch_folded(group).wait()
        taken = folded[heads, rows].reshape(rows_at_once, width)
        scores[unit] = contract(taken, along(window), ((1,), (1,)))

    def soften(unit):
        for part in range(GROUP):
            rows = slice(part * SPAN, (part + 1) * SPAN)
            weights[unit, rows] = weigh(scores[unit, rows])

    def combine(unit):
        group, window = units[unit]
        heads, rows = slice(group * GROUP, (group + 1) * GROUP), slice(window * SPAN, (window + 1) * SPAN)
        sums = contract(weights[unit], along(window), ((1,), (0,))).reshape(GROUP, SPAN, width)
        if window == 0:
            first = lax.broadcasted_iota(jnp.int32, sums.shape, 1) == 0
            sums = jnp.where(first, lone[heads][:, None, :], sums)
        mixed[heads, rows] = sums.astype(jnp.bfloat16)

    def project(group):
        for head in range(group * GROUP, (group + 1) * GROUP):
            columns = head_columns(head)
            sums = contract(mixed[head], value_ref[:, columns], ((1,), (0,)))
            sums = jnp.where(kept, sums, 0.0)
            out_ref[:, columns] = pltpu.roll(sums, count - 1, 0).astype(jnp.bfloat16)

    for step in range(len(units) + 2):
        if step < len(units):
            score(step)
        if step >= 2:
            combine(step - 2)
        if 1 <= step <= len(units):
            soften(step - 1)
        if step >= 2 and units[step - 2][1] == blocks - 1:
            project(units[step - 2][0])


def attend(source, block, keep, folded, single, w_value, stores):
    requests = source.shape[0]
    length, width = stores[0].shape[1:]
    count = folded.shape[1]
    units = HEADS // GROUP * (count // SPAN)
    return pl.pallas_call(
        attend_kernel,
        out_shape=jax.ShapeDtypeStruct((count, w_value.shape[1]), jnp.bfloat16),
        in_specs=[SMEM_SPEC] * 3 + [HBM_SPEC] + [VMEM_SPEC] * 2 + [HBM_SPEC] * len(stores),
        out_specs=VMEM_SPEC,
        scratch_shapes=[
            pltpu.VMEM((requests, length, width), jnp.bfloat16),
            pltpu.VMEM(folded.shape, jnp.bfloat16),
            pltpu.VMEM((units, GROUP * SPAN, 2 * length), jnp.float32),
            pltpu.VMEM((units, GROUP * SPAN, 2 * length), jnp.bfloat16),
            pltpu.VMEM(folded.shape, jnp.bfloat16),
            pltpu.SemaphoreType.DMA((requests,)),
            pltpu.SemaphoreType.DMA((HEADS // GROUP,)),
        ],
        compiler_params=pltpu.CompilerParams(vmem_limit_bytes=40 * MIB),
        cost_estimate=pl.CostEstimate(
            flops=2 * HEADS * count * width * (4 * length + HEAD_DIM),
            bytes_accessed=16 * MIB,
            transcendentals=HEADS * count * 2 * length,
        ),
        name="attend_windows",
    )(source, block, keep, in_hbm(folded), single, w_value, *map(in_hbm, stores))


def chip_ring(mesh):
    row = mesh.devices.reshape(-1, mesh.shape["seq"])[0]
    chips = list(range(len(row) // CORES))
    columns = [tuple(getattr(row[CORES * chip], "coords", (0, 0))[:2]) for chip in chips]
    if len(set(columns)) != 2:
        return chips
    up = [chip for chip in chips if columns[chip] == columns[0]]
    return up + [chip for chip in reversed(chips) if columns[chip] != columns[0]]


def body(ring, queries, neighbours, w_key, w_value, retrieval_owner, retrieval_slot, doc_starts):
    devices = lax.axis_size("seq")
    here = lax.axis_index("seq")
    along = [CORES * chip + core for chip in ring for core in range(CORES)]
    orders = [along[:: 1 if slot % 2 == 0 else -1] for slot in range(neighbours.shape[0])]
    stores = [
        lax.all_gather(rows, "seq", axis=0, tiled=True, axis_index_groups=[order])
        for rows, order in zip(prepare(neighbours), orders)
    ]
    owner_slot = jnp.stack([retrieval_owner, retrieval_slot])
    before = lax.ppermute(owner_slot[:, -1:], "seq", [(i, i + 1) for i in range(devices - 1)])
    owner, source = jnp.concatenate([before, owner_slot], 1).reshape(2, -1)
    block = jnp.zeros_like(owner)
    for slot, order in enumerate(orders):
        places = jnp.asarray([order.index(device) for device in range(devices)], jnp.int32)
        found = jnp.sum(jnp.where(owner[:, None] == jnp.arange(devices), places, 0), axis=-1)
        block = jnp.where(source == slot, found, block)
    blocks = doc_starts.shape[0]
    opening = (here == 0) & (jnp.arange(blocks) == 0)
    keep = ((doc_starts == 0) & jnp.logical_not(opening)).astype(jnp.int32)
    folded, single = fold(queries, w_key)
    return attend(source, block, keep, folded, single, w_value, stores)


def solution(mesh):
    return jax.shard_map(
        functools.partial(body, chip_ring(mesh)),
        mesh=mesh,
        in_specs=(
            P(("groups", "seq"), None),
            P(("groups", "seq"), None, None),
            P(),
            P(),
            P(("groups", "seq"), None),
            P(("groups", "seq"), None),
            P(("groups", "seq")),
        ),
        out_specs=P(("groups", "seq"), None),
        check_vma=False,
    )
```

time: 71.5 us -> 114 us (1.59)
  waiting for transfers between devices: 27.7 us -> 75.5 us
  starting transfers between devices: 17.5 us -> 2.39 us
  between operations: 0.4 us -> 13.5 us
  Pallas kernels: 22.5 us -> 18 us
  local copies, waits for them, and re-layouts: 0.38 us -> 3.44 us
  other arithmetic: 2.25 us -> 1.04 us
    all_gather x0 -> x2, waiting for transfers between devices: none -> 74.8 us  [body(): lax.all_gather(rows, 'seq', axis=0, tiled=True, axis_index_groups=[order])]
    ppermute x17 -> x0, waiting for transfers between devices: 27.7 us -> none  [the longest x8 27.7 us: turned(): return lax.ppermute(value, 'seq', pairs)]
    ppermute x17 -> x0, starting transfers between devices: 15.1 us -> none  [the longest x8 11.3 us: turned(): return lax.ppermute(value, 'seq', pairs)]
    pallas_call x3 -> x2, Pallas kernels: 17.4 us -> 13 us  [the longest x1 12.1 us: attend(): pl.pallas_call(attend_kernel, out_shape=jax.ShapeDtypeStruct((count, w_va...]
    unnamed x12 -> x14, local copies, waits for them, and re-layouts: 0.02 us -> 3.09 us
  transfers between devices with their start and end apart: 18 -> 3, of which waited for: 6 -> 2; matrix products, arithmetic and copies ran while one was open for 4% -> 1% of each run, Pallas kernels for 16% -> 4%
where the time goes in v8:
time: 114 us
  waiting for transfers between devices  75.5 us (66%)
  Pallas kernels  18 us (16%)
  between operations  13.5 us (12%)
  local copies, waits for them, and re-layouts  3.44 us (3%)
  starting transfers between devices  2.39 us (2%)
    all_gather x2, waiting for transfers between devices, body(): lax.all_gather(rows, 'seq', axis=0, tiled=True, axis_index_groups=[order])  74.8 us
    pallas_call x1, Pallas kernels, attend(): pl.pallas_call(attend_kernel, out_shape=jax.ShapeDtypeStruct((count, w_va...  12.1 us
    pallas_call x1, Pallas kernels, fold(): pl.pallas_call(fold_kernel, out_shape=(pltpu.HBM(shape, jnp.bfloat16), ja...  5.05 us
    unnamed x14, local copies, waits for them, and re-layouts  3.09 us
    ppermute x1, starting transfers between devices, body(): lax.ppermute(owner_slot[:, -1:], 'seq', [(i, i + 1) for i in range(device...  2.35 us
  transfers between devices with their start and end apart: 3, of which 2 were waited for; matrix products, arithmetic and copies ran while one was open for 1% of the time, Pallas kernels for 4%

profile of v8, /device:TPU:0, one launch (start us, length us, event | category | flops | bytes accessed | tf_op | source)
XLA Modules:
  0.0 113.9 jit_solution(16976397890575041831)
XLA Ops:
  6.5 0.0 copy-start.4
  6.5 0.0 all-gather.3.cloned.1.call-start
  6.5 0.0 copy-start.1
  6.5 1.0 copy-done.1
  7.6 0.0 copy-start.6
  7.6 0.0 copy-start.2
  7.6 0.0 copy-start.3
  7.6 0.0 copy-start.5
  7.6 0.9 normalise_own.1
  8.5 0.0 all-gather.3.cloned.1.call-update
  8.5 0.0 all-gather.5.cloned.1.call-start
  8.6 0.7 all-gather.5.cloned.1.call-update
  9.3 0.8 pad_add_fusion
  10.0 2.3 %collective-permute-start = (s32[2,1,2]{1,2,0:T(2,128)S(1)}, s32[2,1,2]{1,2,0:T(2,128)S(1)}, u32[]{:S(2)}, u32[]{:S(2)}) collective-permute-start(s32[2,1,2]{1,2,0:T(2,128)S(1)} %pad_add_fusion), channel_id=1, source_target_pairs={{0,1},{1,2},{2,3},{3,4},{4,5},{5,6},{6,7},{7,8},{8,9},{9,10},{10,1... | collective-permute-start | bytes 56 | tf_op jit(solution)/shard_map/ppermute | solution.py:259
  12.4 5.1 %fold_queries.1 = (bf16[16,256,896]{2,1,0:T(8,128)(2,1)}, f32[16,896]{1,0:T(8,128)S(1)}) custom-call(bf16[256,2048]{1,0:T(8,128)(2,1)} %query_hbm.1, bf16[896,2048]{1,0:T(8,128)(2,1)} %key_hbm.1), custom_call_target="tpu_custom_call" | custom-call | flops 939524096 | bytes 12582912 | tf_op jit(solution)/shard_map/fold_queries/pallas_call | solution.py:71
  17.5 0.0 copy-done.6
  17.5 0.0 collective-permute-done
  17.5 0.0 copy-done.2
  17.5 0.0 copy-done.3
  17.5 0.1 add_add_fusion
  17.6 0.1 copy.17
  17.7 0.1 eq.38
  17.8 0.1 copy.16
  17.9 0.1 unstack.10.source_ref
  18.0 0.0 copy-done.4
  18.0 0.0 copy-done.5
  18.0 0.2 select_reduce_fusion
  18.1 27.8 %all-gather.3.cloned.1.call-done.rest_0_ = bf16[16,128,896]{2,1,0:T(8,128)(2,1)} async-done(((bf16[1,128,896]{2,1,0:T(8,128)(2,1)}), bf16[16,128,896]{2,1,0:T(8,128)(2,1)}) %all-gather.3.cloned.1.call-update) | async-done | bytes 3670032 | tf_op jit(solution)/shard_map/all_gather | solution.py:255
  45.9 47.0 %all-gather.5.cloned.1.call-done.rest_1_ = bf16[16,128,896]{2,1,0:T(8,128)(2,1)} async-done(((bf16[1,128,896]{2,1,0:T(8,128)(2,1)}), bf16[16,128,896]{2,1,0:T(8,128)(2,1)}) %all-gather.5.cloned.1.call-update) | async-done | bytes 3670032 | tf_op jit(solution)/shard_map/all_gather | solution.py:255
  92.9 0.0 copy-start
  92.9 2.0 %copy-done = bf16[896,2048]{1,0:T(8,128)(2,1)S(1)} copy-done((bf16[896,2048]{1,0:T(8,128)(2,1)S(1)}, bf16[896,2048]{1,0:T(8,128)(2,1)}, u32[]{:S(2)}) %copy-start) | copy-done | bytes 3670040
  95.0 12.1 %attend_windows.1 = bf16[256,2048]{1,0:T(8,128)(2,1)} custom-call(s32[10]{0:T(128)S(1)} %unstack.10.source_ref, s32[10]{0:T(128)S(1)} %compare_select_fusion.1.block_ref, s32[4]{0:T(128)S(1)} %and_convert_fusion.keep_ref, bf16[16,256,896]{2,1,0:T(8,128)(2,1)} %get-tuple-element.9.folded_hbm, f32[16,896]{1,0:T(8,128)S(1)} %get-tuple-element.10.single_ref, ...), custom_call_target="tpu_custom_call" | custom-call | flops 4697620480 | bytes 16777216 | tf_op jit(solution)/shard_map/attend_windows/pallas_call | solution.py:215
  (3 shorter events, 0.0 us)
Async XLA Ops:
  6.5 11.4 %copy-start.4 = (s32[16]{0:T(128)S(1)}, s32[16]{0:T(128)}, u32[]{:S(2)}) copy-start(s32[16]{0:T(128)} %constant.4.clone) | copy-start | bytes 196
  6.5 39.4 %all-gather.3.cloned.1.call-start = ((), (), s32[]{:S(2)}) async-start(), calls=%async_computation | async-start | bytes 3899392 | tf_op jit(solution)/shard_map/all_gather | solution.py:255
  6.5 1.0 copy-start.1
  7.6 9.9 %copy-start.6 = (s32[4]{0:T(128)S(1)}, s32[4]{0:T(128)}, u32[]{:S(2)}) copy-start(s32[4]{0:T(128)} %param.15) | copy-start | bytes 52
  7.6 9.9 %copy-start.2 = (s32[4,2]{0,1:T(2,128)S(1)}, s32[4,2]{0,1:T(2,128)}, u32[]{:S(2)}) copy-start(s32[4,2]{0,1:T(2,128)} %param.14) | copy-start | bytes 100
  7.6 9.9 %copy-start.3 = (s32[4,2]{0,1:T(2,128)S(1)}, s32[4,2]{0,1:T(2,128)}, u32[]{:S(2)}) copy-start(s32[4,2]{0,1:T(2,128)} %param.13) | copy-start | bytes 100
  7.6 10.4 %copy-start.5 = (s32[16]{0:T(128)S(1)}, s32[16]{0:T(128)}, u32[]{:S(2)}) copy-start(s32[16]{0:T(128)} %constant.3.clone) | copy-start | bytes 196
  8.5 84.4 %all-gather.5.cloned.1.call-start = ((), (), s32[]{:S(2)}) async-start(), calls=%async_computation.1 | async-start | bytes 3899392 | tf_op jit(solution)/shard_map/all_gather | solution.py:255
  10.0 7.4 %collective-permute-start = (s32[2,1,2]{1,2,0:T(2,128)S(1)}, s32[2,1,2]{1,2,0:T(2,128)S(1)}, u32[]{:S(2)}, u32[]{:S(2)}) collective-permute-start(s32[2,1,2]{1,2,0:T(2,128)S(1)} %pad_add_fusion), channel_id=1, source_target_pairs={{0,1},{1,2},{2,3},{3,4},{4,5},{5,6},{6,7},{7,8},{8,9},{9,10},{10,1... | collective-permute-start | bytes 56 | tf_op jit(solution)/shard_map/ppermute | solution.py:259
  92.9 2.0 %copy-start = (bf16[896,2048]{1,0:T(8,128)(2,1)S(1)}, bf16[896,2048]{1,0:T(8,128)(2,1)}, u32[]{:S(2)}) copy-start(bf16[896,2048]{1,0:T(8,128)(2,1)} %value_ref.1) | copy-start | bytes 11010052
Sparse Core Ops, SparseCore 0:
  9.0 36.9 all-gather.2
  47.5 45.4 all-gather.4

commit v9 on v6

--- a/solution.py
+++ b/solution.py
@@ -107,25 +107,43 @@
     pl.when(source >= first + half)(lambda: among(stores[half:], first + half, source, act))
 
 
-def collect_kernel(first, source_ref, block_ref, *rest):
-    *stores, tokens_ref, raw, sems = rest
+def locate(request, plan_refs, size):
+    here_ref, place_ref, before_ref, owner_ref, slot_ref = plan_refs
+    window, part = request // 2, request % 2
+    own = jnp.maximum(window - 1, 0)
+    owner = jnp.where(window == 0, before_ref[0, part], owner_ref[own, part])
+    slot = jnp.where(window == 0, before_ref[1, part], slot_ref[own, part])
+    here = here_ref[0]
+    away = place_ref[here // CORES] - place_ref[owner // CORES]
+    away = jnp.where(away < 0, away + size, away)
+    reach = (size - 1) // 2
+    core, opposite = owner % CORES, size - reach - 1
+    holder = jnp.where((away == 0) | ((away > reach) & (away <= opposite)), core, jnp.where(away <= reach, 0, 1))
+    step = jnp.where(away <= opposite, away, size - away)
+    arrival = jnp.where(away == 0, 0, 2 * step - 1 + jnp.where(core == holder, 0, 1))
+    return CORES * arrival + jnp.where(holder == here % CORES, 0, 1), slot
+
+
+def collect_kernel(first, size, *refs):
+    plan_refs, (*stores, tokens_ref, raw, sems) = refs[:5], refs[5:]
     before_ref = stores.pop() if first else None
     requests = raw.shape[0]
 
-    def fetch(request, store):
-        return pltpu.make_async_copy(store.at[block_ref[request]], raw.at[request], sems.at[request])
+    def fetch(request, store, block):
+        return pltpu.make_async_copy(store.at[block], raw.at[request], sems.at[request])
 
     def begin(request, carry):
-        among(stores, first, source_ref[request], lambda store: fetch(request, store).start())
+        source, block = locate(request, plan_refs, size)
+        among(stores, first, source, lambda store: fetch(request, store, block).start())
         return carry
 
     def finish(request, carry):
-        source = source_ref[request]
+        source, block = locate(request, plan_refs, size)
         here = (source >= first) & (source < first + len(stores))
 
         @pl.when(here)
         def _():
-            fetch(request, stores[0]).wait()
+            fetch(request, stores[0], block).wait()
             normalise(raw[request], tokens_ref.at[request])
 
         if before_ref is not None:
@@ -140,21 +158,21 @@
     lax.fori_loop(0, requests, finish, 0)
 
 
-def collect(first, source, block, stores, before):
-    requests = source.shape[0]
+def collect(first, size, plan, stores, before):
+    requests = 2 * plan[3].shape[0] + 2
     length, width = stores[0].shape[1:]
     shape = (requests, length, width)
     before = [before] if first else []
     return pl.pallas_call(
-        functools.partial(collect_kernel, first),
+        functools.partial(collect_kernel, first, size),
         out_shape=jax.ShapeDtypeStruct(shape, jnp.bfloat16),
-        in_specs=[SMEM_SPEC] * 2 + [ANY_SPEC] * len(stores) + [VMEM_SPEC] * len(before),
+        in_specs=[SMEM_SPEC] * 5 + [ANY_SPEC] * len(stores) + [VMEM_SPEC] * len(before),
         out_specs=VMEM_SPEC,
         scratch_shapes=[pltpu.VMEM(shape, jnp.bfloat16), pltpu.SemaphoreType.DMA((requests,))],
         compiler_params=pltpu.CompilerParams(vmem_limit_bytes=16 * MIB),
         cost_estimate=pl.CostEstimate(flops=4 * MIB, bytes_accessed=8 * MIB, transcendentals=0),
         name="collect_blocks",
-    )(source, block, *stores, *before)
+    )(*plan, *stores, *before)
 
 
 def weigh(scores):
@@ -163,9 +181,8 @@
     return (powers * (1.0 / totals)).astype(jnp.bfloat16)
 
 
-def attend_kernel(
-    early, source_ref, block_ref, keep_ref, folded_hbm, single_ref, tokens_in, value_ref, *rest
-):
+def attend_kernel(early, size, *refs):
+    plan_refs, (starts_ref, folded_hbm, single_ref, tokens_in, value_ref, *rest) = refs[:5], refs[5:]
     *late, out_ref, tokens, raw, folded, scores, weights, mixed, sems, folded_sems = rest
     requests, length, width = raw.shape
     blocks = requests // 2 - 1
@@ -176,23 +193,26 @@
         heads = pl.ds(group * GROUP, GROUP)
         return pltpu.make_async_copy(folded_hbm.at[heads], folded.at[heads], folded_sems.at[group])
 
-    def fetch_late(request, store):
-        return pltpu.make_async_copy(store.at[block_ref[request]], raw.at[request], sems.at[request])
+    def fetch_late(request, store, block):
+        return pltpu.make_async_copy(store.at[block], raw.at[request], sems.at[request])
 
     def begin(request, carry):
-        among(late, early, source_ref[request], lambda store: fetch_late(request, store).start())
+        source, block = locate(request, plan_refs, size)
+        among(late, early, source, lambda store: fetch_late(request, store, block).start())
         return carry
 
     def finish(request, carry):
-        @pl.when(source_ref[request] < early)
+        source, block = locate(request, plan_refs, size)
+
+        @pl.when(source < early)
         def _():
             tokens[request] = tokens_in[request]
 
         if late:
 
-            @pl.when(source_ref[request] >= early)
+            @pl.when(source >= early)
             def _():
-                fetch_late(request, late[0]).wait()
+                fetch_late(request, late[0], block).wait()
                 normalise(raw[request], tokens.at[request])
 
         return carry
@@ -212,7 +232,10 @@
     place = lax.broadcasted_iota(jnp.int32, (count, HEAD_DIM), 0)
     kept = place % SPAN == 0
     for block in range(blocks):
-        kept = kept | ((place // SPAN == block) & (keep_ref[block] > 0))
+        fresh = starts_ref[block] == 0
+        if block == 0:
+            fresh = fresh & (plan_refs[0][0] > 0)
+        kept = kept | ((place // SPAN == block) & fresh)
 
     units = [(group, window) for group in range(HEADS // GROUP) for window in range(blocks)]
 
@@ -256,14 +279,14 @@
             project(units[step - 2][0])
 
 
-def attend(early, source, block, keep, folded, single, tokens, w_value, late):
+def attend(early, size, plan, doc_starts, folded, single, tokens, w_value, late):
     requests, length, width = tokens.shape
     count = folded.shape[1]
     units = HEADS // GROUP * (count // SPAN)
     return pl.pallas_call(
-        functools.partial(attend_kernel, early),
+        functools.partial(attend_kernel, early, size),
         out_shape=jax.ShapeDtypeStruct((count, w_value.shape[1]), jnp.bfloat16),
-        in_specs=[SMEM_SPEC] * 3
+        in_specs=[SMEM_SPEC] * 6
         + [HBM_SPEC]
         + [VMEM_SPEC] * 3
         + [ANY_SPEC] * len(late),
@@ -285,7 +308,7 @@
             transcendentals=HEADS * count * 2 * length,
         ),
         name="attend_windows",
-    )(source, block, keep, in_hbm(folded), single, tokens, w_value, *late)
+    )(*plan, doc_starts, in_hbm(folded), single, tokens, w_value, *late)
 
 
 def chip_ring(mesh):
@@ -298,75 +321,48 @@
     return up + [chip for chip in reversed(chips) if columns[chip] != columns[0]]
 
 
-class Ring:
-    def __init__(self, ring):
-        self.ring = ring
-        self.size = len(ring)
-        self.reach = (self.size - 1) // 2
-        self.opposite = self.size % 2 == 0
-
-    def turned(self, value, steps, cores=range(CORES)):
-        size = self.size
-        pairs = [
-            (CORES * self.ring[i] + core, CORES * self.ring[(i + steps) % size] + core)
-            for i in range(size)
-            for core in cores
-        ]
-        return lax.ppermute(value, "seq", pairs)
-
-    def swapped(self, value, cores=range(CORES)):
-        return lax.ppermute(value, "seq", [(CORES * i + core, CORES * i + 1 - core) for i in range(self.size) for core in cores])
-
-    def locate(self, owner, here):
-        order = jnp.asarray([self.ring.index(chip) for chip in range(self.size)], jnp.int32)
-
-        def place_of(device):
-            chips = jnp.arange(self.size)
-            return jnp.sum(jnp.where((device // CORES)[..., None] == chips, order, 0), axis=-1)
-
-        away = (place_of(here) - place_of(owner)) % self.size
-        back = away > self.reach
-        arrival = jnp.where(back, 2 * (self.size - away), jnp.maximum(2 * away - 1, 0))
-        if self.opposite:
-            arrival = jnp.where(away == self.size // 2, 2 * self.reach + 1 + owner % CORES, arrival)
-        return CORES * arrival + (owner % CORES != here % CORES)
-
-
-def tie(values, others):
-    values, others = lax.optimization_barrier((tuple(values), tuple(others)))
-    return list(values), list(others)
+def after(values, others):
+    return list(lax.optimization_barrier((tuple(values), tuple(others)))[0])
 
 
 def body(ring, queries, neighbours, w_key, w_value, retrieval_owner, retrieval_slot, doc_starts):
     devices = lax.axis_size("seq")
-    here = lax.axis_index("seq")
-    plan = Ring(ring)
-    owner_slot = jnp.stack([retrieval_owner, retrieval_slot])
-    before = lax.ppermute(owner_slot[:, -1:], "seq", [(i, i + 1) for i in range(devices - 1)])
-    owner, slot = jnp.concatenate([before, owner_slot], 1).reshape(2, -1)
-    source, block = plan.locate(owner, here), slot
-    blocks = doc_starts.shape[0]
-    opening = (here == 0) & (jnp.arange(blocks) == 0)
-    keep = ((doc_starts == 0) & jnp.logical_not(opening)).astype(jnp.int32)
-    beside = [*fold(queries, w_key), source, block, keep]
-    ahead = behind = neighbours
-    stores, tokens, done = [neighbours, plan.swapped(neighbours)], None, 0
-    for step in range(plan.reach):
-        if step == 1:
-            (ahead, behind), beside = tie((ahead, behind), beside)
-        if step == 2:
-            done = 6
-            tokens = collect(0, beside[2], beside[3], stores[:done], None)
-            (ahead, behind), (tokens,) = tie((ahead, behind), (tokens,))
-        ahead, behind = plan.turned(ahead, 1), plan.turned(behind, -1)
-        stores += [ahead, plan.swapped(ahead), behind, plan.swapped(behind)]
-    folded, single, source, block, keep = beside
+    size = len(ring)
+    reach = (size - 1) // 2
+
+    ways = [
+        (CORES * ring[i] + core, CORES * ring[(i + way) % size] + core)
+        for i in range(size)
+        for core, way in enumerate((1, -1))
+    ]
+    onwards = functools.partial(lax.ppermute, axis_name="seq", perm=ways)
+    swapped = functools.partial(lax.ppermute, axis_name="seq", perm=[(i, i ^ 1) for i in range(devices)])
+
+    folded, single = fold(queries, w_key)
+    owner_slot = jnp.stack([retrieval_owner[-1], retrieval_slot[-1]])
+    before = lax.ppermute(owner_slot, "seq", [(i, i + 1) for i in range(devices - 1)])
+    places = jnp.asarray([ring.index(chip) for chip in range(size)], jnp.int32)
+    plan = [lax.axis_index("seq").reshape(1), places, before, retrieval_owner, retrieval_slot]
+
+    chains = [neighbours, swapped(neighbours)]
+    stores, tokens, done = list(chains), None, 0
+    for step in range(reach):
+        for chain in range(2):
+            sent = [chains[chain]]
+            if step == 1 and chain == 0:
+                sent = after(sent, [folded, single])
+            if step == reach - 1 and chain == 1 and reach > 1:
+                done = CORES * (2 * reach - 3)
+                tokens = collect(0, size, plan, stores[:done], None)
+                sent = after(sent, [tokens])
+            chains[chain] = onwards(sent[0])
+            stores += [chains[chain], swapped(chains[chain])]
+    tokens = collect(done, size, plan, stores[done:], tokens)
     late = []
-    if plan.opposite:
-        ahead, behind = plan.turned(ahead, 1, (0,)), plan.turned(behind, -1, (1,))
-        late = [ahead, plan.swapped(ahead, (0,)), behind, plan.swapped(behind, (1,))]
-    tokens = collect(done, source, block, stores[done:], tokens)
-    return attend(len(stores), source, block, keep, folded, single, tokens, w_value, late)
+    if size % 2 == 0:
+        last = onwards(chains[0])
+        late = [last, swapped(after([last], [tokens])[0])]
+    return attend(len(stores), size, plan, doc_starts, folded, single, tokens, w_value, late)
 
 
 def solution(mesh):

time: 71.5 us -> 59 us (0.83)
  waiting for transfers between devices: 27.7 us -> 13.3 us
  starting transfers between devices: 17.5 us -> 20.5 us
  other arithmetic: 2.25 us -> 0.01 us
  Pallas kernels: 22.5 us -> 24 us
    ppermute x18 -> x16, waiting for transfers between devices: 27.7 us -> 13.3 us  [the longest x6 8.86 us: body(): chains[chain] = onwards(sent[0])]
    ppermute x18 -> x16, starting transfers between devices: 17.5 us -> 20.5 us  [the longest x6 14.8 us: body(): chains[chain] = onwards(sent[0])]
    pallas_call x3, Pallas kernels: 17.4 us -> 18.9 us  [the longest x1 11.2 us: attend(): pl.pallas_call(functools.partial(attend_kernel, early, size), out_shape=j...]
    another operation x1, other arithmetic: 0.78 us -> 0.01 us  [body(): owner_slot = jnp.stack([retrieval_owner[-1], retrieval_slot[-1]])]
    reduce_sum x2 -> x0, other arithmetic: 0.72 us -> none  [place_of(): jnp.sum(jnp.where((device // CORES)[..., None] == chips, order, 0), axis=-1)]
  transfers between devices with their start and end apart: 18 -> 16, of which waited for: 6 -> 5; matrix products, arithmetic and copies ran while one was open for 4% -> 0% of each run, Pallas kernels for 16% -> 22%
where the time goes in v9:
time: 59 us; the launch traced here: 58.3 us
  Pallas kernels  24 us (41%)
  starting transfers between devices  20.5 us (35%)
  waiting for transfers between devices  13.3 us (23%)
    ppermute x6, starting transfers between devices, body(): chains[chain] = onwards(sent[0])  14.8 us
    pallas_call x1, Pallas kernels, attend(): pl.pallas_call(functools.partial(attend_kernel, early, size), out_shape=j...  11.2 us
    ppermute x6, waiting for transfers between devices, body(): chains[chain] = onwards(sent[0])  8.86 us
    pallas_call x2, Pallas kernels, collect(): pl.pallas_call(functools.partial(collect_kernel, first, size), out_shape=...  7.7 us
    pallas_call x1, Pallas kernels, fold(): pl.pallas_call(fold_kernel, out_shape=(pltpu.HBM(shape, jnp.bfloat16), ja...  5.07 us
    ppermute x1, waiting for transfers between devices, body(): last = onwards(chains[0])  2.71 us
    ppermute x1, starting transfers between devices, body(): last = onwards(chains[0])  2.48 us
    ppermute x1, starting transfers between devices, body(): lax.ppermute(owner_slot, 'seq', [(i, i + 1) for i in range(devices - 1)])  2.07 us
  transfers between devices with their start and end apart: 16, of which 5 were waited for; matrix products, arithmetic and copies ran while one was open for 0% of the time, Pallas kernels for 22%

profile of v9, /device:TPU:0, one launch (start us, length us, event | category | flops | bytes accessed | tf_op | source)
XLA Modules:
  0.0 58.3 jit_solution(5404323341954462395)
XLA Ops:
  0.0 0.0 copy-start.1
  0.0 0.0 copy-start
  0.0 0.5 collective-permute-start.4
  0.5 2.6 %collective-permute-start.1 = (bf16[2,128,896]{2,1,0:T(8,128)(2,1)}, bf16[2,128,896]{2,1,0:T(8,128)(2,1)S(1)}, u32[]{:S(2)}, u32[]{:S(2)}) collective-permute-start(bf16[2,128,896]{2,1,0:T(8,128)(2,1)} %refs_5_.2), channel_id=1, source_target_pairs={{0,4},{1,3},{4,8},{5,1},{8,12},{9,5},{12,14},{13,9},{14,10},{15,13... | collective-permute-start | bytes 1376264 | tf_op jit(solution)/shard_map/ppermute | solution.py:358
  3.2 0.0 collective-permute-done.4.refs_6_
  3.2 2.0 %collective-permute-start.5 = (bf16[2,128,896]{2,1,0:T(8,128)(2,1)S(1)}, bf16[2,128,896]{2,1,0:T(8,128)(2,1)S(1)}, u32[]{:S(2)}, u32[]{:S(2)}) collective-permute-start(bf16[2,128,896]{2,1,0:T(8,128)(2,1)S(1)} %collective-permute-done.4.refs_6_), channel_id=1, source_target_pairs={{0,4},{1,3},{4,8},{5,1},{8,12},{9,5},{12,14},{13,9},{14,10},{15,13... | collective-permute-start | bytes 1376264 | tf_op jit(solution)/shard_map/ppermute | solution.py:358
  5.1 5.1 %fold_queries.1 = (bf16[16,256,896]{2,1,0:T(8,128)(2,1)}, f32[16,896]{1,0:T(8,128)S(1)}) custom-call(bf16[256,2048]{1,0:T(8,128)(2,1)} %query_hbm.1, bf16[896,2048]{1,0:T(8,128)(2,1)} %key_hbm.1), custom_call_target="tpu_custom_call" | custom-call | flops 939524096 | bytes 12582912 | tf_op jit(solution)/shard_map/fold_queries/pallas_call | solution.py:72
  10.2 0.0 collective-permute-done.1.refs_7_
  10.2 1.6 %collective-permute-start.2 = (bf16[2,128,896]{2,1,0:T(8,128)(2,1)S(1)}, bf16[2,128,896]{2,1,0:T(8,128)(2,1)S(1)}, u32[]{:S(2)}, u32[]{:S(2)}) collective-permute-start(bf16[2,128,896]{2,1,0:T(8,128)(2,1)S(1)} %collective-permute-done.1.refs_7_), channel_id=1, source_target_pairs={{0,4},{1,3},{4,8},{5,1},{8,12},{9,5},{12,14},{13,9},{14,10},{15,13... | collective-permute-start | bytes 1376264 | tf_op jit(solution)/shard_map/ppermute | solution.py:358
  11.9 0.0 collective-permute-start.10
  11.9 2.8 %collective-permute-done.5.refs_9_ = bf16[2,128,896]{2,1,0:T(8,128)(2,1)S(1)} collective-permute-done((bf16[2,128,896]{2,1,0:T(8,128)(2,1)S(1)}, bf16[2,128,896]{2,1,0:T(8,128)(2,1)S(1)}, u32[]{:S(2)}, u32[]{:S(2)}) %collective-permute-start.5) | collective-permute-done | bytes 458784 | tf_op jit(solution)/shard_map/ppermute | solution.py:358
  14.7 0.0 collective-permute-start.11
  14.7 2.1 %collective-permute-start.6 = (bf16[2,128,896]{2,1,0:T(8,128)(2,1)S(1)}, bf16[2,128,896]{2,1,0:T(8,128)(2,1)S(1)}, u32[]{:S(2)}, u32[]{:S(2)}) collective-permute-start(bf16[2,128,896]{2,1,0:T(8,128)(2,1)S(1)} %collective-permute-done.5.refs_9_), channel_id=1, source_target_pairs={{0,4},{1,3},{4,8},{5,1},{8,12},{9,5},{12,14},{13,9},{14,10},{15,13... | collective-permute-start | bytes 1376264 | tf_op jit(solution)/shard_map/ppermute | solution.py:358
  16.8 0.0 copy-done.4
  16.8 0.1 copy.9.refs_3_
  16.9 0.0 copy-done.5
  16.9 0.1 copy.10.refs_4_
  17.0 2.1 %collective-permute-start = (s32[2,2]{1,0:T(2,128)S(1)}, s32[2,2]{1,0:T(2,128)S(1)}, u32[]{:S(2)}, u32[]{:S(2)}) collective-permute-start(s32[2,2]{1,0:T(2,128)S(1)} %pad_add_fusion), channel_id=1, source_target_pairs={{0,1},{1,2},{2,3},{3,4},{4,5},{5,6},{6,7},{7,8},{8,9},{9,10},{10,1... | collective-permute-start | bytes 56 | tf_op jit(solution)/shard_map/ppermute | solution.py:343
  19.1 0.5 collective-permute-done.2.refs_5_
  19.6 2.1 %collective-permute-start.8 = (bf16[2,128,896]{2,1,0:T(8,128)(2,1)S(1)}, bf16[2,128,896]{2,1,0:T(8,128)(2,1)S(1)}, u32[]{:S(2)}, u32[]{:S(2)}) collective-permute-start(bf16[2,128,896]{2,1,0:T(8,128)(2,1)S(1)} %collective-permute-done.2.refs_5_), channel_id=1, source_target_pairs={{0,4},{1,3},{4,8},{5,1},{8,12},{9,5},{12,14},{13,9},{14,10},{15,13... | collective-permute-start | bytes 1376264 | tf_op jit(solution)/shard_map/ppermute | solution.py:358
  21.7 0.0 collective-permute-done.refs_2_
  21.7 0.0 collective-permute-done.10.refs_8_
  21.7 0.0 collective-permute-done.11.refs_10_
  21.7 0.0 copy-done.1
  21.7 0.0 copy-done
  21.7 4.4 %collect_blocks.2.refs_13_ = bf16[10,128,896]{2,1,0:T(8,128)(2,1)S(1)} custom-call(s32[1]{0:T(128)} %bitcast.refs_0_, s32[8]{0:T(128)S(1)} %copy-done.1, s32[2,2]{1,0:T(2,128)S(1)} %collective-permute-done.refs_2_, s32[4,2]{1,0:T(4,128)S(1)} %copy.9.refs_3_, s32[4,2]{1,0:T(4,128)S(1)} %copy.10.refs_4_, bf16[2,128,896]{2,1,0:T(8,128)(2,1)S(1)} %copy-done, ...), custom_call_target="tpu_custom_call" | custom-call | flops 4194304 | bytes 8388608 | tf_op jit(solution)/shard_map/collect_blocks/pallas_call | solution.py:166
  26.2 0.0 copy-start.2
  26.2 0.0 copy-start.3
  26.2 0.0 collective-permute-done.6.refs_7_
  26.2 4.4 %collective-permute-start.12 = (bf16[2,128,896]{2,1,0:T(8,128)(2,1)S(1)}, bf16[2,128,896]{2,1,0:T(8,128)(2,1)S(1)}, u32[]{:S(2)}, u32[]{:S(2)}) collective-permute-start(bf16[2,128,896]{2,1,0:T(8,128)(2,1)S(1)} %collective-permute-done.6.refs_7_), channel_id=1, source_target_pairs={{0,4},{1,3},{4,8},{5,1},{8,12},{9,5},{12,14},{13,9},{14,10},{15,13... | collective-permute-start | bytes 1376264 | tf_op jit(solution)/shard_map/ppermute | solution.py:358
  30.6 0.0 collective-permute-start.3
  30.6 0.5 collective-permute-start.7
  31.1 0.0 collective-permute-done.8.refs_9_
  31.2 0.0 collective-permute-start.9
  31.2 5.5 %collective-permute-done.12.refs_11_ = bf16[2,128,896]{2,1,0:T(8,128)(2,1)S(1)} collective-permute-done((bf16[2,128,896]{2,1,0:T(8,128)(2,1)S(1)}, bf16[2,128,896]{2,1,0:T(8,128)(2,1)S(1)}, u32[]{:S(2)}, u32[]{:S(2)}) %collective-permute-start.12) | collective-permute-done | bytes 458784 | tf_op jit(solution)/shard_map/ppermute | solution.py:358
  36.6 0.0 collective-permute-start.13
  36.6 2.5 %collective-permute-start.14 = (bf16[2,128,896]{2,1,0:T(8,128)(2,1)S(1)}, bf16[2,128,896]{2,1,0:T(8,128)(2,1)S(1)}, u32[]{:S(2)}, u32[]{:S(2)}) collective-permute-start(bf16[2,128,896]{2,1,0:T(8,128)(2,1)S(1)} %collective-permute-done.8.refs_9_), channel_id=1, source_target_pairs={{0,4},{1,3},{4,8},{5,1},{8,12},{9,5},{12,14},{13,9},{14,10},{15,13... | collective-permute-start | bytes 1376264 | tf_op jit(solution)/shard_map/ppermute | solution.py:363
  39.1 0.0 collective-permute-done.3.refs_6_
  39.1 0.0 collective-permute-done.9.refs_10_
  39.1 0.0 collective-permute-done.7.refs_8_
  39.1 0.0 collective-permute-done.13.refs_12_
  39.1 3.3 %collect_blocks.3.refs_8_ = bf16[10,128,896]{2,1,0:T(8,128)(2,1)S(1)} custom-call(s32[1]{0:T(128)} %bitcast.refs_0_, s32[8]{0:T(128)S(1)} %copy-done.1, s32[2,2]{1,0:T(2,128)S(1)} %collective-permute-done.refs_2_, s32[4,2]{1,0:T(4,128)S(1)} %copy.9.refs_3_, s32[4,2]{1,0:T(4,128)S(1)} %copy.10.refs_4_, ...), custom_call_target="tpu_custom_call" | custom-call | flops 4194304 | bytes 8388608 | tf_op jit(solution)/shard_map/collect_blocks/pallas_call | solution.py:166
  42.4 2.7 %collective-permute-done.14.refs_10_ = bf16[2,128,896]{2,1,0:T(8,128)(2,1)S(1)} collective-permute-done((bf16[2,128,896]{2,1,0:T(8,128)(2,1)S(1)}, bf16[2,128,896]{2,1,0:T(8,128)(2,1)S(1)}, u32[]{:S(2)}, u32[]{:S(2)}) %collective-permute-start.14) | collective-permute-done | bytes 458784 | tf_op jit(solution)/shard_map/ppermute | solution.py:363
  45.1 0.1 collective-permute-start.15
  45.2 1.7 %collective-permute-done.15.refs_11_ = bf16[2,128,896]{2,1,0:T(8,128)(2,1)S(1)} collective-permute-done((bf16[2,128,896]{2,1,0:T(8,128)(2,1)S(1)}, bf16[2,128,896]{2,1,0:T(8,128)(2,1)S(1)}, u32[]{:S(2)}, u32[]{:S(2)}) %collective-permute-start.15) | collective-permute-done | bytes 458784 | tf_op jit(solution)/shard_map/ppermute | solution.py:364
  46.9 0.0 copy-done.2
  46.9 0.0 copy-done.3
  46.9 11.2 %attend_windows.1 = bf16[256,2048]{1,0:T(8,128)(2,1)} custom-call(s32[1]{0:T(128)} %bitcast.refs_0_, s32[8]{0:T(128)S(1)} %copy-done.1, s32[2,2]{1,0:T(2,128)S(1)} %collective-permute-done.refs_2_, s32[4,2]{1,0:T(4,128)S(1)} %copy.9.refs_3_, s32[4,2]{1,0:T(4,128)S(1)} %copy.10.refs_4_, s32[4]{0:T(128)S(1)} %copy-done.3, ...), custom_call_target="tpu_custom_call" | custom-call | flops 4697620480 | bytes 16777216 | tf_op jit(solution)/shard_map/attend_windows/pallas_call | solution.py:286
  (5 shorter events, 0.0 us)
Async XLA Ops:
  0.0 21.7 %copy-start.1 = (s32[8]{0:T(128)S(1)}, s32[8]{0:T(128)}, u32[]{:S(2)}) copy-start(s32[8]{0:T(128)} %constant.6.clone.refs_1_) | copy-start | bytes 100
  0.0 21.7 %copy-start = (bf16[2,128,896]{2,1,0:T(8,128)(2,1)S(1)}, bf16[2,128,896]{2,1,0:T(8,128)(2,1)}, u32[]{:S(2)}) copy-start(bf16[2,128,896]{2,1,0:T(8,128)(2,1)} %refs_5_.2) | copy-start | bytes 1376260
  0.0 16.8 %copy-start.4 = (s32[4,2]{0,1:T(2,128)S(1)}, s32[4,2]{0,1:T(2,128)}, u32[]{:S(2)}) copy-start(s32[4,2]{0,1:T(2,128)} %param.12) | copy-start | bytes 100
  0.0 16.9 %copy-start.5 = (s32[4,2]{0,1:T(2,128)S(1)}, s32[4,2]{0,1:T(2,128)}, u32[]{:S(2)}) copy-start(s32[4,2]{0,1:T(2,128)} %param.13) | copy-start | bytes 100
  0.0 3.2 %collective-permute-start.4 = (bf16[2,128,896]{2,1,0:T(8,128)(2,1)}, bf16[2,128,896]{2,1,0:T(8,128)(2,1)S(1)}, u32[]{:S(2)}, u32[]{:S(2)}) collective-permute-start(bf16[2,128,896]{2,1,0:T(8,128)(2,1)} %refs_5_.2), channel_id=1, source_target_pairs={{0,1},{1,0},{2,3},{3,2},{4,5},{5,4},{6,7},{7,6},{8,9},{9,8},{10,11... | collective-permute-start | bytes 1376264 | tf_op jit(solution)/shard_map/ppermute | solution.py:347
  0.5 9.7 %collective-permute-start.1 = (bf16[2,128,896]{2,1,0:T(8,128)(2,1)}, bf16[2,128,896]{2,1,0:T(8,128)(2,1)S(1)}, u32[]{:S(2)}, u32[]{:S(2)}) collective-permute-start(bf16[2,128,896]{2,1,0:T(8,128)(2,1)} %refs_5_.2), channel_id=1, source_target_pairs={{0,4},{1,3},{4,8},{5,1},{8,12},{9,5},{12,14},{13,9},{14,10},{15,13... | collective-permute-start | bytes 1376264 | tf_op jit(solution)/shard_map/ppermute | solution.py:358
  3.2 11.5 %collective-permute-start.5 = (bf16[2,128,896]{2,1,0:T(8,128)(2,1)S(1)}, bf16[2,128,896]{2,1,0:T(8,128)(2,1)S(1)}, u32[]{:S(2)}, u32[]{:S(2)}) collective-permute-start(bf16[2,128,896]{2,1,0:T(8,128)(2,1)S(1)} %collective-permute-done.4.refs_6_), channel_id=1, source_target_pairs={{0,4},{1,3},{4,8},{5,1},{8,12},{9,5},{12,14},{13,9},{14,10},{15,13... | collective-permute-start | bytes 1376264 | tf_op jit(solution)/shard_map/ppermute | solution.py:358
  10.2 9.4 %collective-permute-start.2 = (bf16[2,128,896]{2,1,0:T(8,128)(2,1)S(1)}, bf16[2,128,896]{2,1,0:T(8,128)(2,1)S(1)}, u32[]{:S(2)}, u32[]{:S(2)}) collective-permute-start(bf16[2,128,896]{2,1,0:T(8,128)(2,1)S(1)} %collective-permute-done.1.refs_7_), channel_id=1, source_target_pairs={{0,4},{1,3},{4,8},{5,1},{8,12},{9,5},{12,14},{13,9},{14,10},{15,13... | collective-permute-start | bytes 1376264 | tf_op jit(solution)/shard_map/ppermute | solution.py:358
  11.9 9.8 %collective-permute-start.10 = (bf16[2,128,896]{2,1,0:T(8,128)(2,1)S(1)}, bf16[2,128,896]{2,1,0:T(8,128)(2,1)S(1)}, u32[]{:S(2)}, u32[]{:S(2)}) collective-permute-start(bf16[2,128,896]{2,1,0:T(8,128)(2,1)S(1)} %collective-permute-done.1.refs_7_), channel_id=1, source_target_pairs={{0,1},{1,0},{2,3},{3,2},{4,5},{5,4},{6,7},{7,6},{8,9},{9,8},{10,11... | collective-permute-start | bytes 1376264 | tf_op jit(solution)/shard_map/ppermute | solution.py:359
  14.7 7.0 %collective-permute-start.11 = (bf16[2,128,896]{2,1,0:T(8,128)(2,1)S(1)}, bf16[2,128,896]{2,1,0:T(8,128)(2,1)}, u32[]{:S(2)}, u32[]{:S(2)}) collective-permute-start(bf16[2,128,896]{2,1,0:T(8,128)(2,1)S(1)} %collective-permute-done.5.refs_9_), channel_id=1, source_target_pairs={{0,1},{1,0},{2,3},{3,2},{4,5},{5,4},{6,7},{7,6},{8,9},{9,8},{10,11... | collective-permute-start | bytes 1376264 | tf_op jit(solution)/shard_map/ppermute | solution.py:359
  14.7 11.5 %collective-permute-start.6 = (bf16[2,128,896]{2,1,0:T(8,128)(2,1)S(1)}, bf16[2,128,896]{2,1,0:T(8,128)(2,1)S(1)}, u32[]{:S(2)}, u32[]{:S(2)}) collective-permute-start(bf16[2,128,896]{2,1,0:T(8,128)(2,1)S(1)} %collective-permute-done.5.refs_9_), channel_id=1, source_target_pairs={{0,4},{1,3},{4,8},{5,1},{8,12},{9,5},{12,14},{13,9},{14,10},{15,13... | collective-permute-start | bytes 1376264 | tf_op jit(solution)/shard_map/ppermute | solution.py:358
  17.0 4.7 %collective-permute-start = (s32[2,2]{1,0:T(2,128)S(1)}, s32[2,2]{1,0:T(2,128)S(1)}, u32[]{:S(2)}, u32[]{:S(2)}) collective-permute-start(s32[2,2]{1,0:T(2,128)S(1)} %pad_add_fusion), channel_id=1, source_target_pairs={{0,1},{1,2},{2,3},{3,4},{4,5},{5,6},{6,7},{7,8},{8,9},{9,10},{10,1... | collective-permute-start | bytes 56 | tf_op jit(solution)/shard_map/ppermute | solution.py:343
  19.6 11.5 %collective-permute-start.8 = (bf16[2,128,896]{2,1,0:T(8,128)(2,1)S(1)}, bf16[2,128,896]{2,1,0:T(8,128)(2,1)S(1)}, u32[]{:S(2)}, u32[]{:S(2)}) collective-permute-start(bf16[2,128,896]{2,1,0:T(8,128)(2,1)S(1)} %collective-permute-done.2.refs_5_), channel_id=1, source_target_pairs={{0,4},{1,3},{4,8},{5,1},{8,12},{9,5},{12,14},{13,9},{14,10},{15,13... | collective-permute-start | bytes 1376264 | tf_op jit(solution)/shard_map/ppermute | solution.py:358
  26.2 20.8 %copy-start.2 = (bf16[896,2048]{1,0:T(8,128)(2,1)S(1)}, bf16[896,2048]{1,0:T(8,128)(2,1)}, u32[]{:S(2)}) copy-start(bf16[896,2048]{1,0:T(8,128)(2,1)} %refs_9_.1) | copy-start | bytes 11010052
  26.2 20.7 %copy-start.3 = (s32[4]{0:T(128)S(1)}, s32[4]{0:T(128)}, u32[]{:S(2)}) copy-start(s32[4]{0:T(128)} %refs_5_.3) | copy-start | bytes 52
  26.2 10.4 %collective-permute-start.12 = (bf16[2,128,896]{2,1,0:T(8,128)(2,1)S(1)}, bf16[2,128,896]{2,1,0:T(8,128)(2,1)S(1)}, u32[]{:S(2)}, u32[]{:S(2)}) collective-permute-start(bf16[2,128,896]{2,1,0:T(8,128)(2,1)S(1)} %collective-permute-done.6.refs_7_), channel_id=1, source_target_pairs={{0,4},{1,3},{4,8},{5,1},{8,12},{9,5},{12,14},{13,9},{14,10},{15,13... | collective-permute-start | bytes 1376264 | tf_op jit(solution)/shard_map/ppermute | solution.py:358
  30.6 8.5 %collective-permute-start.3 = (bf16[2,128,896]{2,1,0:T(8,128)(2,1)S(1)}, bf16[2,128,896]{2,1,0:T(8,128)(2,1)S(1)}, u32[]{:S(2)}, u32[]{:S(2)}) collective-permute-start(bf16[2,128,896]{2,1,0:T(8,128)(2,1)S(1)} %collective-permute-done.2.refs_5_), channel_id=1, source_target_pairs={{0,1},{1,0},{2,3},{3,2},{4,5},{5,4},{6,7},{7,6},{8,9},{9,8},{10,11... | collective-permute-start | bytes 1376264 | tf_op jit(solution)/shard_map/ppermute | solution.py:359
  30.6 8.5 %collective-permute-start.7 = (bf16[2,128,896]{2,1,0:T(8,128)(2,1)S(1)}, bf16[2,128,896]{2,1,0:T(8,128)(2,1)S(1)}, u32[]{:S(2)}, u32[]{:S(2)}) collective-permute-start(bf16[2,128,896]{2,1,0:T(8,128)(2,1)S(1)} %collective-permute-done.6.refs_7_), channel_id=1, source_target_pairs={{0,1},{1,0},{2,3},{3,2},{4,5},{5,4},{6,7},{7,6},{8,9},{9,8},{10,11... | collective-permute-start | bytes 1376264 | tf_op jit(solution)/shard_map/ppermute | solution.py:359
  31.2 8.0 %collective-permute-start.9 = (bf16[2,128,896]{2,1,0:T(8,128)(2,1)S(1)}, bf16[2,128,896]{2,1,0:T(8,128)(2,1)S(1)}, u32[]{:S(2)}, u32[]{:S(2)}) collective-permute-start(bf16[2,128,896]{2,1,0:T(8,128)(2,1)S(1)} %collective-permute-done.8.refs_9_), channel_id=1, source_target_pairs={{0,1},{1,0},{2,3},{3,2},{4,5},{5,4},{6,7},{7,6},{8,9},{9,8},{10,11... | collective-permute-start | bytes 1376264 | tf_op jit(solution)/shard_map/ppermute | solution.py:359
  36.6 2.5 %collective-permute-start.13 = (bf16[2,128,896]{2,1,0:T(8,128)(2,1)S(1)}, bf16[2,128,896]{2,1,0:T(8,128)(2,1)S(1)}, u32[]{:S(2)}, u32[]{:S(2)}) collective-permute-start(bf16[2,128,896]{2,1,0:T(8,128)(2,1)S(1)} %collective-permute-done.12.refs_11_), channel_id=1, source_target_pairs={{0,1},{1,0},{2,3},{3,2},{4,5},{5,4},{6,7},{7,6},{8,9},{9,8},{10,11... | collective-permute-start | bytes 1376264 | tf_op jit(solution)/shard_map/ppermute | solution.py:359
  36.6 8.5 %collective-permute-start.14 = (bf16[2,128,896]{2,1,0:T(8,128)(2,1)S(1)}, bf16[2,128,896]{2,1,0:T(8,128)(2,1)S(1)}, u32[]{:S(2)}, u32[]{:S(2)}) collective-permute-start(bf16[2,128,896]{2,1,0:T(8,128)(2,1)S(1)} %collective-permute-done.8.refs_9_), channel_id=1, source_target_pairs={{0,4},{1,3},{4,8},{5,1},{8,12},{9,5},{12,14},{13,9},{14,10},{15,13... | collective-permute-start | bytes 1376264 | tf_op jit(solution)/shard_map/ppermute | solution.py:363
  45.1 1.8 %collective-permute-start.15 = (bf16[2,128,896]{2,1,0:T(8,128)(2,1)S(1)}, bf16[2,128,896]{2,1,0:T(8,128)(2,1)S(1)}, u32[]{:S(2)}, u32[]{:S(2)}) collective-permute-start(bf16[2,128,896]{2,1,0:T(8,128)(2,1)S(1)} %collective-permute-done.14.refs_10_), channel_id=1, source_target_pairs={{0,1},{1,0},{2,3},{3,2},{4,5},{5,4},{6,7},{7,6},{8,9},{9,8},{10,11... | collective-permute-start | bytes 1376264 | tf_op jit(solution)/shard_map/ppermute | solution.py:364

commit v10 on v8

v10 whole, which is shorter than its diff:
```python
import functools
import math

import jax
import jax.numpy as jnp
from jax import lax
from jax.experimental import pallas as pl
from jax.experimental.pallas import tpu as pltpu
from jax.sharding import PartitionSpec as P

SPAN = 64
HEADS = 16
HEAD_DIM = 128
EPS = 1e-6
SCALE = math.log2(math.e) / math.sqrt(HEAD_DIM)
CORES = 2
GROUP = 4
MIB = 2**20


SMEM_SPEC = pl.BlockSpec(memory_space=pltpu.SMEM)
VMEM_SPEC = pl.BlockSpec(memory_space=pltpu.VMEM)
ANY_SPEC = pl.BlockSpec(memory_space=pl.ANY)
HBM_SPEC = pl.BlockSpec(memory_space=pltpu.HBM)


def contract(left, right, dims):
    return lax.dot_general(left, right, (dims, ((), ())), preferred_element_type=jnp.float32)


def in_hbm(value):
    return pltpu.with_memory_space_constraint(value, pltpu.HBM)


def head_columns(head):
    return slice(head * HEAD_DIM, (head + 1) * HEAD_DIM)


def fold_kernel(query_hbm, key_hbm, folded_hbm, single_ref, query, key, folded, in_sems, out_sems):
    groups = HEADS // GROUP

    def fetch(group):
        columns = slice(group * GROUP * HEAD_DIM, (group + 1) * GROUP * HEAD_DIM)
        return (
            pltpu.make_async_copy(query_hbm.at[:, columns], query.at[:, columns], in_sems.at[group, 0]),
            pltpu.make_async_copy(key_hbm.at[:, columns], key.at[:, columns], in_sems.at[group, 1]),
        )

    def put(head):
        return pltpu.make_async_copy(folded.at[head], folded_hbm.at[head], out_sems.at[head])

    for group in range(groups):
        for copy in fetch(group):
            copy.start()
    for head in range(HEADS):
        if head % GROUP == 0:
            for copy in fetch(head // GROUP):
                copy.wait()
        columns = head_columns(head)
        queries = pltpu.roll(query[:, columns].astype(jnp.float32), 1, 0).astype(jnp.bfloat16)
        rows = contract(queries, key[:, columns], ((1,), (1,))) * SCALE
        single_ref[head : head + 1, :] = rows[:1]
        folded[head] = rows.astype(jnp.bfloat16)
        put(head).start()
    for head in range(HEADS):
        put(head).wait()


def fold(queries, w_key):
    count, width = queries.shape[0], w_key.shape[0]
    shape = (HEADS, count, width)
    return pl.pallas_call(
        fold_kernel,
        out_shape=(
            pltpu.HBM(shape, jnp.bfloat16),
            jax.ShapeDtypeStruct((HEADS, width), jnp.float32),
        ),
        in_specs=[HBM_SPEC] * 2,
        out_specs=(HBM_SPEC, VMEM_SPEC),
        scratch_shapes=[
            pltpu.VMEM(queries.shape, jnp.bfloat16),
            pltpu.VMEM(w_key.shape, jnp.bfloat16),
            pltpu.VMEM(shape, jnp.bfloat16),
            pltpu.SemaphoreType.DMA((HEADS // GROUP, 2)),
            pltpu.SemaphoreType.DMA((HEADS,)),
        ],
        compiler_params=pltpu.CompilerParams(vmem_limit_bytes=28 * MIB),
        cost_estimate=pl.CostEstimate(
            flops=2 * queries.size * width, bytes_accessed=12 * MIB, transcendentals=0
        ),
        name="fold_queries",
    )(in_hbm(queries), in_hbm(w_key))


def normalise(raw, tokens_ref):
    widened = raw.astype(jnp.float32)
    factor = lax.rsqrt(jnp.mean(widened * widened, axis=-1, keepdims=True) + EPS)
    tokens_ref[...] = (widened * factor).astype(jnp.bfloat16)


def among(stores, first, source, act):
    if len(stores) == 1:
        pl.when(source == first)(lambda: act(stores[0]))
        return
    half = len(stores) // 2
    pl.when(source < first + half)(lambda: among(stores[:half], first, source, act))
    pl.when(source >= first + half)(lambda: among(stores[half:], first + half, source, act))


def plan_kernel(size, here_ref, place_ref, before_ref, owner_ref, slot_ref, source_ref, block_ref):
    reach = (size - 1) // 2
    opposite = size - reach - 1
    here = here_ref[0]

    def place(request, carry):
        window, part = request // 2, request % 2
        own = jnp.maximum(window - 1, 0)
        owner = jnp.where(window == 0, before_ref[0, part], owner_ref[own, part])
        away = place_ref[here // CORES] - place_ref[owner // CORES]
        away = jnp.where(away < 0, away + size, away)
        core = owner % CORES
        holder = jnp.where((away == 0) | ((away > reach) & (away <= opposite)), core, jnp.where(away <= reach, 0, 1))
        step = jnp.where(away <= opposite, away, size - away)
        arrival = jnp.where(away == 0, 0, 2 * step - 1 + jnp.where(core == holder, 0, 1))
        source_ref[request] = CORES * arrival + jnp.where(holder == here % CORES, 0, 1)
        block_ref[request] = jnp.where(window == 0, before_ref[1, part], slot_ref[own, part])
        return carry

    lax.fori_loop(0, source_ref.shape[0], place, 0)


def plan_requests(size, here, places, before, owner, slot):
    requests = 2 * owner.shape[0] + 2
    return pl.pallas_call(
        functools.partial(plan_kernel, size),
        out_shape=(jax.ShapeDtypeStruct((requests,), jnp.int32),) * 2,
        in_specs=[SMEM_SPEC] * 5,
        out_specs=(SMEM_SPEC,) * 2,
        name="plan_requests",
    )(here, places, before, owner, slot)


def weigh(scores):
    powers = jnp.exp2(scores - jnp.max(scores, axis=-1, keepdims=True))
    totals = jnp.sum(powers, axis=-1, keepdims=True)
    return (powers * (1.0 / totals)).astype(jnp.bfloat16)


def attend_kernel(
    source_ref, block_ref, here_ref, starts_ref, folded_hbm, single_ref, value_ref, *rest
):
    *stores, out_hbm, tokens, raw, folded, scores, weights, mixed, out, sems, folded_sems, out_sems = rest
    requests, length, width = raw.shape
    blocks = requests // 2 - 1
    count = blocks * SPAN
    rows_at_once = GROUP * SPAN
    groups = HEADS // GROUP
    lone_window = blocks
    order = [*range(1, blocks), lone_window, 0]

    def fetch(request, store):
        return pltpu.make_async_copy(store.at[block_ref[request]], raw.at[request], sems.at[request])

    def fetch_folded(group):
        heads = pl.ds(group * GROUP, GROUP)
        return pltpu.make_async_copy(folded_hbm.at[heads], folded.at[heads], folded_sems.at[group])

    def put(group):
        columns = pl.ds(group * GROUP * HEAD_DIM, GROUP * HEAD_DIM)
        return pltpu.make_async_copy(out.at[:, columns], out_hbm.at[:, columns], out_sems.at[group])

    for window in order:
        for request in (2 * window, 2 * window + 1):
            among(stores, 0, source_ref[request], lambda store: fetch(request, store).start())
        if window == order[0]:
            fetch_folded(0).start()
    for group in range(1, groups):
        fetch_folded(group).start()

    place = lax.broadcasted_iota(jnp.int32, (count, HEAD_DIM), 0)
    kept = place % SPAN == 0
    for block in range(blocks):
        fresh = starts_ref[block] == 0
        if block == 0:
            fresh = fresh & (here_ref[0] > 0)
        kept = kept | ((place // SPAN == block) & fresh)

    def ready(window):
        for request in (2 * window, 2 * window + 1):
            fetch(request, stores[0]).wait()
        for request in (2 * window, 2 * window + 1):
            normalise(raw[request], tokens.at[request])

    def along(window):
        return tokens[2 * window : 2 * window + 2].reshape(2 * length, width)

    units = [(group, window) for group in range(groups) for window in order if group == 0 or window != lone_window]
    lone = {}

    def place_of(unit):
        group, window = units[unit]
        slot = group * blocks + window
        return slot, slice(group * GROUP, (group + 1) * GROUP), slice(window * SPAN, (window + 1) * SPAN)

    def score(unit):
        window = units[unit][1]
        if window == lone_window:
            lone["scores"] = contract(single_ref[...].astype(jnp.bfloat16), along(window), ((1,), (1,)))
            return
        slot, heads, rows = place_of(unit)
        taken = folded[heads, rows].reshape(rows_at_once, width)
        scores[slot] = contract(taken, along(window), ((1,), (1,)))

    def soften(unit):
        if units[unit][1] == lone_window:
            lone["weights"] = weigh(lone["scores"])
            return
        slot, _, _ = place_of(unit)
        for part in range(GROUP):
            rows = slice(part * SPAN, (part + 1) * SPAN)
            weights[slot, rows] = weigh(scores[slot, rows])

    def combine(unit):
        window = units[unit][1]
        if window == lone_window:
            lone["sums"] = contract(lone["weights"], along(window), ((1,), (0,)))
            return
        slot, heads, rows = place_of(unit)
        sums = contract(weights[slot], along(window), ((1,), (0,))).reshape(GROUP, SPAN, width)
        if window == 0:
            first = lax.broadcasted_iota(jnp.int32, sums.shape, 1) == 0
            sums = jnp.where(first, lone["sums"][heads][:, None, :], sums)
        mixed[heads, rows] = sums.astype(jnp.bfloat16)

    def project(group):
        for head in range(group * GROUP, (group + 1) * GROUP):
            columns = head_columns(head)
            sums = contract(mixed[head], value_ref[:, columns], ((1,), (0,)))
            sums = jnp.where(kept, sums, 0.0)
            out[:, columns] = pltpu.roll(sums, count - 1, 0).astype(jnp.bfloat16)
        put(group).start()

    ready(order[0])
    for step in range(len(units) + 2):
        if step == 0:
            fetch_folded(0).wait()
        if step == len(order):
            for group in range(1, groups):
                fetch_folded(group).wait()
        if step + 1 < len(order):
            ready(order[step + 1])
        if step < len(units):
            score(step)
        if step >= 2:
            combine(step - 2)
        if 1 <= step <= len(units):
            soften(step - 1)
        if step >= 2 and units[step - 2][1] == order[-1]:
            project(units[step - 2][0])
    for group in range(groups):
        put(group).wait()


def attend(source, block, here, doc_starts, folded, single, w_value, stores):
    requests = source.shape[0]
    length, width = stores[0].shape[1:]
    count = folded.shape[1]
    groups = HEADS // GROUP
    units = groups * (count // SPAN)
    model_width = w_value.shape[1]
    return pl.pallas_call(
        attend_kernel,
        out_shape=jax.ShapeDtypeStruct((count, model_width), jnp.bfloat16),
        in_specs=[SMEM_SPEC] * 4 + [HBM_SPEC] + [VMEM_SPEC] * 2 + [ANY_SPEC] * len(stores),
        out_specs=HBM_SPEC,
        scratch_shapes=[
            pltpu.VMEM((requests, length, width), jnp.bfloat16),
            pltpu.VMEM((requests, length, width), jnp.bfloat16),
            pltpu.VMEM(folded.shape, jnp.bfloat16),
            pltpu.VMEM((units, GROUP * SPAN, 2 * length), jnp.float32),
            pltpu.VMEM((units, GROUP * SPAN, 2 * length), jnp.bfloat16),
            pltpu.VMEM(folded.shape, jnp.bfloat16),
            pltpu.VMEM((count, model_width), jnp.bfloat16),
            pltpu.SemaphoreType.DMA((requests,)),
            pltpu.SemaphoreType.DMA((groups,)),
            pltpu.SemaphoreType.DMA((groups,)),
        ],
        compiler_params=pltpu.CompilerParams(vmem_limit_bytes=40 * MIB),
        cost_estimate=pl.CostEstimate(
            flops=2 * HEADS * count * width * (4 * length + HEAD_DIM),
            bytes_accessed=16 * MIB,
            transcendentals=HEADS * count * 2 * length,
        ),
        name="attend_windows",
    )(source, block, here, doc_starts, in_hbm(folded), single, w_value, *stores)


def chip_ring(mesh):
    row = mesh.devices.reshape(-1, mesh.shape["seq"])[0]
    chips = list(range(len(row) // CORES))
    columns = [tuple(getattr(row[CORES * chip], "coords", (0, 0))[:2]) for chip in chips]
    if len(set(columns)) != 2:
        return chips
    up = [chip for chip in chips if columns[chip] == columns[0]]
    return up + [chip for chip in reversed(chips) if columns[chip] != columns[0]]


def after(values, others):
    return list(lax.optimization_barrier((tuple(values), tuple(others)))[0])


def body(ring, queries, neighbours, w_key, w_value, retrieval_owner, retrieval_slot, doc_starts):
    devices = lax.axis_size("seq")
    size = len(ring)
    reach = (size - 1) // 2

    ways = [
        (CORES * ring[i] + core, CORES * ring[(i + way) % size] + core)
        for i in range(size)
        for core, way in enumerate((1, -1))
    ]
    onwards = functools.partial(lax.ppermute, axis_name="seq", perm=ways)
    swapped = functools.partial(lax.ppermute, axis_name="seq", perm=[(i, i ^ 1) for i in range(devices)])

    chains = [neighbours, swapped(neighbours)]
    stores = list(chains)
    folded, single = fold(*after([queries], [chains[1]]), w_key)

    owner_slot = jnp.stack([retrieval_owner[-1], retrieval_slot[-1]])
    before = lax.ppermute(*after([owner_slot], [single]), "seq", [(i, i + 1) for i in range(devices - 1)])
    places = jnp.asarray([ring.index(chip) for chip in range(size)], jnp.int32)
    here = lax.axis_index("seq").reshape(1)
    source, block = plan_requests(size, here, places, before, retrieval_owner, retrieval_slot)

    beside = {(1, 0): [folded, single], (1, 1): [before]}
    for step in range(reach):
        for chain in range(2):
            others = beside.get((step, chain), []) + (stores[2 * chain + 4 * step - 5 :][:1] if step > 1 else [])
            sent = after([chains[chain]], others) if others else [chains[chain]]
            chains[chain] = onwards(sent[0])
            stores += [chains[chain], swapped(chains[chain])]
    if size % 2 == 0:
        sent = after([chains[0]], stores[-7:-4:2]) if reach > 1 else [chains[0]]
        last = onwards(sent[0])
        if reach:
            stores[-1] = swapped(after([chains[1]], [last, stores[-3], source, block])[0])
        stores += [last, swapped(last)]
    return attend(source, block, here, doc_starts, folded, single, w_value, stores)


def solution(mesh):
    return jax.shard_map(
        functools.partial(body, chip_ring(mesh)),
        mesh=mesh,
        in_specs=(
            P(("groups", "seq"), None),
            P(("groups", "seq"), None, None),
            P(),
            P(),
            P(("groups", "seq"), None),
            P(("groups", "seq"), None),
            P(("groups", "seq")),
        ),
        out_specs=P(("groups", "seq"), None),
        check_vma=False,
    )
```

time: 114 us -> 65.8 us (0.58)
  waiting for transfers between devices: 75.5 us -> 19.8 us
  starting transfers between devices: 2.39 us -> 15.8 us
  between operations: 13.5 us -> 0.23 us
  local copies, waits for them, and re-layouts: 3.44 us -> 10.2 us
    all_gather x2 -> x0, waiting for transfers between devices: 74.8 us -> none  [body(): lax.all_gather(rows, 'seq', axis=0, tiled=True, axis_index_groups=[order])]
    ppermute x1 -> x16, waiting for transfers between devices: 0.01 us -> 19.8 us  [the longest x6 12.2 us: body(): chains[chain] = onwards(sent[0])]
    ppermute x1 -> x16, starting transfers between devices: 2.35 us -> 15.8 us  [the longest x6 11.7 us: body(): chains[chain] = onwards(sent[0])]
    unnamed x14 -> x30, local copies, waits for them, and re-layouts: 3.09 us -> 10.2 us
  transfers between devices with their start and end apart: 3 -> 16, of which waited for: 2 -> 7; matrix products, arithmetic and copies ran while one was open for 1% -> 2% of each run, Pallas kernels for 4% -> 10%
where the time goes in v10:
time: 65.8 us; the launch traced here: 65.1 us
  waiting for transfers between devices  19.8 us (30%)
  Pallas kernels  19.1 us (29%)
  starting transfers between devices  15.8 us (24%)
  local copies, waits for them, and re-layouts  10.2 us (16%)
    pallas_call x1, Pallas kernels, attend(): pl.pallas_call(attend_kernel, out_shape=jax.ShapeDtypeStruct((count, mode...  12.4 us
    ppermute x6, waiting for transfers between devices, body(): chains[chain] = onwards(sent[0])  12.2 us
    ppermute x6, starting transfers between devices, body(): chains[chain] = onwards(sent[0])  11.7 us
    unnamed x30, local copies, waits for them, and re-layouts  10.2 us
    ppermute x1, waiting for transfers between devices, body(): last = onwards(sent[0])  5.44 us
    pallas_call x1, Pallas kernels, fold(): pl.pallas_call(fold_kernel, out_shape=(pltpu.HBM(shape, jnp.bfloat16), ja...  5.05 us
    ppermute x1, starting transfers between devices, body(): lax.ppermute(*after([owner_slot], [single]), 'seq', [(i, i + 1) for i in...  1.71 us
    pallas_call x1, Pallas kernels, plan_requests(): pl.pallas_call(functools.partial(plan_kernel, size), out_shape=(jax.Shape...  1.64 us
  transfers between devices with their start and end apart: 16, of which 7 were waited for; matrix products, arithmetic and copies ran while one was open for 2% of the time, Pallas kernels for 10%

profile of v10, /device:TPU:0, one launch (start us, length us, event | category | flops | bytes accessed | tf_op | source)
XLA Modules:
  0.0 65.1 jit_solution(7851156943636983962)
XLA Ops:
  0.0 0.5 collective-permute-start
  0.5 2.6 %collective-permute-start.2 = (bf16[2,128,896]{2,1,0:T(8,128)(2,1)}, bf16[2,128,896]{2,1,0:T(8,128)(2,1)S(1)}, u32[]{:S(2)}, u32[]{:S(2)}) collective-permute-start(bf16[2,128,896]{2,1,0:T(8,128)(2,1)} %rest_0_.1), channel_id=1, source_target_pairs={{0,4},{1,3},{4,8},{5,1},{8,12},{9,5},{12,14},{13,9},{14,10},{15,13... | collective-permute-start | bytes 1376264 | tf_op jit(solution)/shard_map/ppermute | solution.py:340
  3.1 0.0 collective-permute-done.rest_1_
  3.1 2.0 %collective-permute-start.4 = (bf16[2,128,896]{2,1,0:T(8,128)(2,1)S(1)}, bf16[2,128,896]{2,1,0:T(8,128)(2,1)S(1)}, u32[]{:S(2)}, u32[]{:S(2)}) collective-permute-start(bf16[2,128,896]{2,1,0:T(8,128)(2,1)S(1)} %collective-permute-done.rest_1_), channel_id=1, source_target_pairs={{0,4},{1,3},{4,8},{5,1},{8,12},{9,5},{12,14},{13,9},{14,10},{15,13... | collective-permute-start | bytes 1376264 | tf_op jit(solution)/shard_map/ppermute | solution.py:340
  5.1 0.8 %copy.9.owner_ref = s32[4,2]{1,0:T(4,128)S(1)} copy(s32[4,2]{0,1:T(2,128)} %param.12) | data formatting | bytes 64 | tf_op args[4]
  5.8 0.8 %copy.10.slot_ref = s32[4,2]{1,0:T(4,128)S(1)} copy(s32[4,2]{0,1:T(2,128)} %param.13) | data formatting | bytes 64 | tf_op args[5]
  6.6 5.1 %fold_queries.1 = (bf16[16,256,896]{2,1,0:T(8,128)(2,1)}, f32[16,896]{1,0:T(8,128)S(1)}) custom-call(bf16[256,2048]{1,0:T(8,128)(2,1)} %query_hbm, bf16[896,2048]{1,0:T(8,128)(2,1)} %key_hbm.1), custom_call_target="tpu_custom_call" | custom-call | flops 939524096 | bytes 12582912 | tf_op jit(solution)/shard_map/fold_queries/pallas_call | solution.py:72
  11.7 0.0 collective-permute-done.2.rest_2_
  11.7 1.7 %collective-permute-start.1 = (s32[2,2]{1,0:T(2,128)S(1)}, s32[2,2]{1,0:T(2,128)S(1)}, u32[]{:S(2)}, u32[]{:S(2)}) collective-permute-start(s32[2,2]{1,0:T(2,128)S(1)} %pad_add_fusion), channel_id=1, source_target_pairs={{0,1},{1,2},{2,3},{3,4},{4,5},{5,6},{6,7},{7,8},{8,9},{9,10},{10,1... | collective-permute-start | bytes 56 | tf_op jit(solution)/shard_map/ppermute | solution.py:330
  13.4 0.4 collective-permute-start.3
  13.8 1.9 %collective-permute-start.6 = (bf16[2,128,896]{2,1,0:T(8,128)(2,1)S(1)}, bf16[2,128,896]{2,1,0:T(8,128)(2,1)S(1)}, u32[]{:S(2)}, u32[]{:S(2)}) collective-permute-start(bf16[2,128,896]{2,1,0:T(8,128)(2,1)S(1)} %collective-permute-done.2.rest_2_), channel_id=1, source_target_pairs={{0,4},{1,3},{4,8},{5,1},{8,12},{9,5},{12,14},{13,9},{14,10},{15,13... | collective-permute-start | bytes 1376264 | tf_op jit(solution)/shard_map/ppermute | solution.py:340
  15.7 0.0 collective-permute-done.1.before_ref
  15.8 0.0 collective-permute-done.4.rest_4_
  15.8 3.3 %collective-permute-start.8 = (bf16[2,128,896]{2,1,0:T(8,128)(2,1)S(1)}, bf16[2,128,896]{2,1,0:T(8,128)(2,1)S(1)}, u32[]{:S(2)}, u32[]{:S(2)}) collective-permute-start(bf16[2,128,896]{2,1,0:T(8,128)(2,1)S(1)} %collective-permute-done.4.rest_4_), channel_id=1, source_target_pairs={{0,4},{1,3},{4,8},{5,1},{8,12},{9,5},{12,14},{13,9},{14,10},{15,13... | collective-permute-start | bytes 1376264 | tf_op jit(solution)/shard_map/ppermute | solution.py:340
  19.1 0.0 collective-permute-start.5
  19.1 0.0 collective-permute-done.3.rest_3_
  19.1 4.2 %collective-permute-done.6.rest_6_ = bf16[2,128,896]{2,1,0:T(8,128)(2,1)S(1)} collective-permute-done((bf16[2,128,896]{2,1,0:T(8,128)(2,1)S(1)}, bf16[2,128,896]{2,1,0:T(8,128)(2,1)S(1)}, u32[]{:S(2)}, u32[]{:S(2)}) %collective-permute-start.6) | collective-permute-done | bytes 458784 | tf_op jit(solution)/shard_map/ppermute | solution.py:340
  23.3 1.0 %collective-permute-start.10 = (bf16[2,128,896]{2,1,0:T(8,128)(2,1)S(1)}, bf16[2,128,896]{2,1,0:T(8,128)(2,1)}, u32[]{:S(2)}, u32[]{:S(2)}) collective-permute-start(bf16[2,128,896]{2,1,0:T(8,128)(2,1)S(1)} %collective-permute-done.6.rest_6_), channel_id=1, source_target_pairs={{0,4},{1,3},{4,8},{5,1},{8,12},{9,5},{12,14},{13,9},{14,10},{15,13... | collective-permute-start | bytes 1376264 | tf_op jit(solution)/shard_map/ppermute | solution.py:340
  24.2 0.0 collective-permute-start.7
  24.2 4.0 %collective-permute-done.8.rest_8_ = bf16[2,128,896]{2,1,0:T(8,128)(2,1)S(1)} collective-permute-done((bf16[2,128,896]{2,1,0:T(8,128)(2,1)S(1)}, bf16[2,128,896]{2,1,0:T(8,128)(2,1)S(1)}, u32[]{:S(2)}, u32[]{:S(2)}) %collective-permute-start.8) | collective-permute-done | bytes 458784 | tf_op jit(solution)/shard_map/ppermute | solution.py:340
  28.2 0.0 collective-permute-start.9
  28.2 0.0 collective-permute-done.5.rest_5_
  28.2 0.8 %copy-done.2 = bf16[2,128,896]{2,1,0:T(8,128)(2,1)} copy-done((bf16[2,128,896]{2,1,0:T(8,128)(2,1)}, bf16[2,128,896]{2,1,0:T(8,128)(2,1)S(1)}, u32[]{:S(2)}) %copy-start.2) | copy-done | bytes 458776
  29.0 1.0 %collective-permute-start.12 = (bf16[2,128,896]{2,1,0:T(8,128)(2,1)S(1)}, bf16[2,128,896]{2,1,0:T(8,128)(2,1)}, u32[]{:S(2)}, u32[]{:S(2)}) collective-permute-start(bf16[2,128,896]{2,1,0:T(8,128)(2,1)S(1)} %collective-permute-done.8.rest_8_), channel_id=1, source_target_pairs={{0,4},{1,3},{4,8},{5,1},{8,12},{9,5},{12,14},{13,9},{14,10},{15,13... | collective-permute-start | bytes 1376264 | tf_op jit(solution)/shard_map/ppermute | solution.py:340
  29.9 3.3 %collective-permute-done.10.rest_10_ = bf16[2,128,896]{2,1,0:T(8,128)(2,1)} collective-permute-done((bf16[2,128,896]{2,1,0:T(8,128)(2,1)S(1)}, bf16[2,128,896]{2,1,0:T(8,128)(2,1)}, u32[]{:S(2)}, u32[]{:S(2)}) %collective-permute-start.10) | collective-permute-done | bytes 458784 | tf_op jit(solution)/shard_map/ppermute | solution.py:340
  33.2 0.0 collective-permute-start.11
  33.2 0.0 collective-permute-done.7.rest_7_
  33.2 0.8 %copy-done.4 = bf16[2,128,896]{2,1,0:T(8,128)(2,1)} copy-done((bf16[2,128,896]{2,1,0:T(8,128)(2,1)}, bf16[2,128,896]{2,1,0:T(8,128)(2,1)S(1)}, u32[]{:S(2)}) %copy-start.4) | copy-done | bytes 458776
  34.0 0.0 collective-permute-done.9.rest_9_
  34.0 0.8 %copy-done.6 = bf16[2,128,896]{2,1,0:T(8,128)(2,1)} copy-done((bf16[2,128,896]{2,1,0:T(8,128)(2,1)}, bf16[2,128,896]{2,1,0:T(8,128)(2,1)S(1)}, u32[]{:S(2)}) %copy-start.6) | copy-done | bytes 458776
  34.8 1.0 %collective-permute-start.13 = (bf16[2,128,896]{2,1,0:T(8,128)(2,1)}, bf16[2,128,896]{2,1,0:T(8,128)(2,1)}, u32[]{:S(2)}, u32[]{:S(2)}) collective-permute-start(bf16[2,128,896]{2,1,0:T(8,128)(2,1)} %collective-permute-done.10.rest_10_), channel_id=1, source_target_pairs={{0,4},{1,3},{4,8},{5,1},{8,12},{9,5},{12,14},{13,9},{14,10},{15,13... | collective-permute-start | bytes 1376264 | tf_op jit(solution)/shard_map/ppermute | solution.py:344
  35.7 0.0 copy-done.11
  35.7 0.0 copy-done.12
  35.7 1.6 %plan_requests.1 = (s32[10]{0:T(128)}, s32[10]{0:T(128)}) custom-call(s32[1]{0:T(128)} %bitcast.here_ref, s32[8]{0:T(128)} %constant.6.clone.place_ref, s32[2,2]{1,0:T(2,128)} %copy-done.13, s32[4,2]{1,0:T(4,128)} %copy-done.11, s32[4,2]{1,0:T(4,128)} %copy-done.12), custom_call_target="tpu_custom_call" | custom-call | tf_op jit(solution)/shard_map/plan_requests/pallas_call | solution.py:134
  37.4 0.7 %collective-permute-done.12.rest_12_ = bf16[2,128,896]{2,1,0:T(8,128)(2,1)} collective-permute-done((bf16[2,128,896]{2,1,0:T(8,128)(2,1)S(1)}, bf16[2,128,896]{2,1,0:T(8,128)(2,1)}, u32[]{:S(2)}, u32[]{:S(2)}) %collective-permute-start.12) | collective-permute-done | bytes 458784 | tf_op jit(solution)/shard_map/ppermute | solution.py:340
  38.1 0.0 collective-permute-done.11.rest_11_
  38.1 5.4 %collective-permute-done.13.rest_14_ = bf16[2,128,896]{2,1,0:T(8,128)(2,1)} collective-permute-done((bf16[2,128,896]{2,1,0:T(8,128)(2,1)}, bf16[2,128,896]{2,1,0:T(8,128)(2,1)}, u32[]{:S(2)}, u32[]{:S(2)}) %collective-permute-start.13) | collective-permute-done | bytes 458784 | tf_op jit(solution)/shard_map/ppermute | solution.py:344
  43.6 0.0 collective-permute-start.14
  43.6 0.5 collective-permute-start.15
  44.1 1.5 %collective-permute-done.14.rest_13_ = bf16[2,128,896]{2,1,0:T(8,128)(2,1)S(1)} collective-permute-done((bf16[2,128,896]{2,1,0:T(8,128)(2,1)}, bf16[2,128,896]{2,1,0:T(8,128)(2,1)S(1)}, u32[]{:S(2)}, u32[]{:S(2)}) %collective-permute-start.14) | collective-permute-done | bytes 458784 | tf_op jit(solution)/shard_map/ppermute | solution.py:346
  45.6 0.7 %collective-permute-done.15.rest_15_ = bf16[2,128,896]{2,1,0:T(8,128)(2,1)S(1)} collective-permute-done((bf16[2,128,896]{2,1,0:T(8,128)(2,1)}, bf16[2,128,896]{2,1,0:T(8,128)(2,1)S(1)}, u32[]{:S(2)}, u32[]{:S(2)}) %collective-permute-start.15) | collective-permute-done | bytes 458784 | tf_op jit(solution)/shard_map/ppermute | solution.py:347
  46.3 2.0 %copy-done = bf16[896,2048]{1,0:T(8,128)(2,1)S(1)} copy-done((bf16[896,2048]{1,0:T(8,128)(2,1)S(1)}, bf16[896,2048]{1,0:T(8,128)(2,1)}, u32[]{:S(2)}) %copy-start) | copy-done | bytes 3670040
  48.3 1.0 %copy-done.3 = bf16[2,128,896]{2,1,0:T(8,128)(2,1)S(1)} copy-done((bf16[2,128,896]{2,1,0:T(8,128)(2,1)S(1)}, bf16[2,128,896]{2,1,0:T(8,128)(2,1)}, u32[]{:S(2)}) %copy-start.3) | copy-done | bytes 458776
  49.3 1.0 %copy-done.5 = bf16[2,128,896]{2,1,0:T(8,128)(2,1)S(1)} copy-done((bf16[2,128,896]{2,1,0:T(8,128)(2,1)S(1)}, bf16[2,128,896]{2,1,0:T(8,128)(2,1)}, u32[]{:S(2)}) %copy-start.5) | copy-done | bytes 458776
  50.3 1.0 %copy-done.7 = bf16[2,128,896]{2,1,0:T(8,128)(2,1)S(1)} copy-done((bf16[2,128,896]{2,1,0:T(8,128)(2,1)S(1)}, bf16[2,128,896]{2,1,0:T(8,128)(2,1)}, u32[]{:S(2)}) %copy-start.7) | copy-done | bytes 458776
  51.4 0.6 copy-done.9
  51.9 0.6 copy-done.10
  52.6 12.4 %attend_windows.1 = bf16[256,2048]{1,0:T(8,128)(2,1)} custom-call(s32[10]{0:T(128)S(1)} %copy-done.9, s32[10]{0:T(128)S(1)} %copy-done.10, s32[1]{0:T(128)} %bitcast.here_ref, s32[4]{0:T(128)S(1)} %copy-done.8, bf16[16,256,896]{2,1,0:T(8,128)(2,1)} %get-tuple-element.22.folded_hbm, f32[16,896]{1,0:T(8,128)S(1)} %get-tuple-element.18.single_ref, ...), custom_call_target="tpu_custom_call" | custom-call | flops 4697620480 | bytes 16777216 | tf_op jit(solution)/shard_map/attend_windows/pallas_call | solution.py:271
  (20 shorter events, 0.0 us)
Async XLA Ops:
  0.0 46.3 %copy-start.1 = (bf16[2,128,896]{2,1,0:T(8,128)(2,1)S(1)}, bf16[2,128,896]{2,1,0:T(8,128)(2,1)}, u32[]{:S(2)}) copy-start(bf16[2,128,896]{2,1,0:T(8,128)(2,1)} %rest_0_.1) | copy-start | bytes 1376260
  0.0 46.3 %copy-start.8 = (s32[4]{0:T(128)S(1)}, s32[4]{0:T(128)}, u32[]{:S(2)}) copy-start(s32[4]{0:T(128)} %starts_ref.1) | copy-start | bytes 52
  0.0 3.1 %collective-permute-start = (bf16[2,128,896]{2,1,0:T(8,128)(2,1)}, bf16[2,128,896]{2,1,0:T(8,128)(2,1)S(1)}, u32[]{:S(2)}, u32[]{:S(2)}) collective-permute-start(bf16[2,128,896]{2,1,0:T(8,128)(2,1)} %rest_0_.1), channel_id=1, source_target_pairs={{0,1},{1,0},{2,3},{3,2},{4,5},{5,4},{6,7},{7,6},{8,9},{9,8},{10,11... | collective-permute-start | bytes 1376264 | tf_op jit(solution)/shard_map/ppermute | solution.py:325
  0.5 11.2 %collective-permute-start.2 = (bf16[2,128,896]{2,1,0:T(8,128)(2,1)}, bf16[2,128,896]{2,1,0:T(8,128)(2,1)S(1)}, u32[]{:S(2)}, u32[]{:S(2)}) collective-permute-start(bf16[2,128,896]{2,1,0:T(8,128)(2,1)} %rest_0_.1), channel_id=1, source_target_pairs={{0,4},{1,3},{4,8},{5,1},{8,12},{9,5},{12,14},{13,9},{14,10},{15,13... | collective-permute-start | bytes 1376264 | tf_op jit(solution)/shard_map/ppermute | solution.py:340
  3.1 12.7 %collective-permute-start.4 = (bf16[2,128,896]{2,1,0:T(8,128)(2,1)S(1)}, bf16[2,128,896]{2,1,0:T(8,128)(2,1)S(1)}, u32[]{:S(2)}, u32[]{:S(2)}) collective-permute-start(bf16[2,128,896]{2,1,0:T(8,128)(2,1)S(1)} %collective-permute-done.rest_1_), channel_id=1, source_target_pairs={{0,4},{1,3},{4,8},{5,1},{8,12},{9,5},{12,14},{13,9},{14,10},{15,13... | collective-permute-start | bytes 1376264 | tf_op jit(solution)/shard_map/ppermute | solution.py:340
  5.8 29.9 %copy-start.11 = (s32[4,2]{1,0:T(4,128)}, s32[4,2]{1,0:T(4,128)S(1)}, u32[]{:S(2)}) copy-start(s32[4,2]{1,0:T(4,128)S(1)} %copy.9.owner_ref) | copy-start | bytes 100
  6.6 29.1 %copy-start.12 = (s32[4,2]{1,0:T(4,128)}, s32[4,2]{1,0:T(4,128)S(1)}, u32[]{:S(2)}) copy-start(s32[4,2]{1,0:T(4,128)S(1)} %copy.10.slot_ref) | copy-start | bytes 100
  11.7 4.1 %collective-permute-start.1 = (s32[2,2]{1,0:T(2,128)S(1)}, s32[2,2]{1,0:T(2,128)S(1)}, u32[]{:S(2)}, u32[]{:S(2)}) collective-permute-start(s32[2,2]{1,0:T(2,128)S(1)} %pad_add_fusion), channel_id=1, source_target_pairs={{0,1},{1,2},{2,3},{3,4},{4,5},{5,6},{6,7},{7,8},{8,9},{9,10},{10,1... | collective-permute-start | bytes 56 | tf_op jit(solution)/shard_map/ppermute | solution.py:330
  13.4 5.7 %collective-permute-start.3 = (bf16[2,128,896]{2,1,0:T(8,128)(2,1)S(1)}, bf16[2,128,896]{2,1,0:T(8,128)(2,1)S(1)}, u32[]{:S(2)}, u32[]{:S(2)}) collective-permute-start(bf16[2,128,896]{2,1,0:T(8,128)(2,1)S(1)} %collective-permute-done.2.rest_2_), channel_id=1, source_target_pairs={{0,1},{1,0},{2,3},{3,2},{4,5},{5,4},{6,7},{7,6},{8,9},{9,8},{10,11... | collective-permute-start | bytes 1376264 | tf_op jit(solution)/shard_map/ppermute | solution.py:341
  13.8 9.4 %collective-permute-start.6 = (bf16[2,128,896]{2,1,0:T(8,128)(2,1)S(1)}, bf16[2,128,896]{2,1,0:T(8,128)(2,1)S(1)}, u32[]{:S(2)}, u32[]{:S(2)}) collective-permute-start(bf16[2,128,896]{2,1,0:T(8,128)(2,1)S(1)} %collective-permute-done.2.rest_2_), channel_id=1, source_target_pairs={{0,4},{1,3},{4,8},{5,1},{8,12},{9,5},{12,14},{13,9},{14,10},{15,13... | collective-permute-start | bytes 1376264 | tf_op jit(solution)/shard_map/ppermute | solution.py:340
  15.8 20.0 %copy-start.13 = (s32[2,2]{1,0:T(2,128)}, s32[2,2]{1,0:T(2,128)S(1)}, u32[]{:S(2)}) copy-start(s32[2,2]{1,0:T(2,128)S(1)} %collective-permute-done.1.before_ref) | copy-start | bytes 52
  15.8 12.4 %collective-permute-start.8 = (bf16[2,128,896]{2,1,0:T(8,128)(2,1)S(1)}, bf16[2,128,896]{2,1,0:T(8,128)(2,1)S(1)}, u32[]{:S(2)}, u32[]{:S(2)}) collective-permute-start(bf16[2,128,896]{2,1,0:T(8,128)(2,1)S(1)} %collective-permute-done.4.rest_4_), channel_id=1, source_target_pairs={{0,4},{1,3},{4,8},{5,1},{8,12},{9,5},{12,14},{13,9},{14,10},{15,13... | collective-permute-start | bytes 1376264 | tf_op jit(solution)/shard_map/ppermute | solution.py:340
  19.1 9.1 %collective-permute-start.5 = (bf16[2,128,896]{2,1,0:T(8,128)(2,1)S(1)}, bf16[2,128,896]{2,1,0:T(8,128)(2,1)S(1)}, u32[]{:S(2)}, u32[]{:S(2)}) collective-permute-start(bf16[2,128,896]{2,1,0:T(8,128)(2,1)S(1)} %collective-permute-done.4.rest_4_), channel_id=1, source_target_pairs={{0,1},{1,0},{2,3},{3,2},{4,5},{5,4},{6,7},{7,6},{8,9},{9,8},{10,11... | collective-permute-start | bytes 1376264 | tf_op jit(solution)/shard_map/ppermute | solution.py:341
  23.3 9.9 %collective-permute-start.10 = (bf16[2,128,896]{2,1,0:T(8,128)(2,1)S(1)}, bf16[2,128,896]{2,1,0:T(8,128)(2,1)}, u32[]{:S(2)}, u32[]{:S(2)}) collective-permute-start(bf16[2,128,896]{2,1,0:T(8,128)(2,1)S(1)} %collective-permute-done.6.rest_6_), channel_id=1, source_target_pairs={{0,4},{1,3},{4,8},{5,1},{8,12},{9,5},{12,14},{13,9},{14,10},{15,13... | collective-permute-start | bytes 1376264 | tf_op jit(solution)/shard_map/ppermute | solution.py:340
  24.2 9.0 %collective-permute-start.7 = (bf16[2,128,896]{2,1,0:T(8,128)(2,1)S(1)}, bf16[2,128,896]{2,1,0:T(8,128)(2,1)S(1)}, u32[]{:S(2)}, u32[]{:S(2)}) collective-permute-start(bf16[2,128,896]{2,1,0:T(8,128)(2,1)S(1)} %collective-permute-done.6.rest_6_), channel_id=1, source_target_pairs={{0,1},{1,0},{2,3},{3,2},{4,5},{5,4},{6,7},{7,6},{8,9},{9,8},{10,11... | collective-permute-start | bytes 1376264 | tf_op jit(solution)/shard_map/ppermute | solution.py:341
  28.2 5.8 %collective-permute-start.9 = (bf16[2,128,896]{2,1,0:T(8,128)(2,1)S(1)}, bf16[2,128,896]{2,1,0:T(8,128)(2,1)S(1)}, u32[]{:S(2)}, u32[]{:S(2)}) collective-permute-start(bf16[2,128,896]{2,1,0:T(8,128)(2,1)S(1)} %collective-permute-done.8.rest_8_), channel_id=1, source_target_pairs={{0,1},{1,0},{2,3},{3,2},{4,5},{5,4},{6,7},{7,6},{8,9},{9,8},{10,11... | collective-permute-start | bytes 1376264 | tf_op jit(solution)/shard_map/ppermute | solution.py:341
  28.2 0.8 %copy-start.2 = (bf16[2,128,896]{2,1,0:T(8,128)(2,1)}, bf16[2,128,896]{2,1,0:T(8,128)(2,1)S(1)}, u32[]{:S(2)}) copy-start(bf16[2,128,896]{2,1,0:T(8,128)(2,1)S(1)} %collective-permute-done.5.rest_5_) | copy-start | bytes 1376260
  29.0 9.2 %collective-permute-start.12 = (bf16[2,128,896]{2,1,0:T(8,128)(2,1)S(1)}, bf16[2,128,896]{2,1,0:T(8,128)(2,1)}, u32[]{:S(2)}, u32[]{:S(2)}) collective-permute-start(bf16[2,128,896]{2,1,0:T(8,128)(2,1)S(1)} %collective-permute-done.8.rest_8_), channel_id=1, source_target_pairs={{0,4},{1,3},{4,8},{5,1},{8,12},{9,5},{12,14},{13,9},{14,10},{15,13... | collective-permute-start | bytes 1376264 | tf_op jit(solution)/shard_map/ppermute | solution.py:340
  33.2 4.9 %collective-permute-start.11 = (bf16[2,128,896]{2,1,0:T(8,128)(2,1)}, bf16[2,128,896]{2,1,0:T(8,128)(2,1)}, u32[]{:S(2)}, u32[]{:S(2)}) collective-permute-start(bf16[2,128,896]{2,1,0:T(8,128)(2,1)} %collective-permute-done.10.rest_10_), channel_id=1, source_target_pairs={{0,1},{1,0},{2,3},{3,2},{4,5},{5,4},{6,7},{7,6},{8,9},{9,8},{10,11... | collective-permute-start | bytes 1376264 | tf_op jit(solution)/shard_map/ppermute | solution.py:341
  33.2 0.8 %copy-start.4 = (bf16[2,128,896]{2,1,0:T(8,128)(2,1)}, bf16[2,128,896]{2,1,0:T(8,128)(2,1)S(1)}, u32[]{:S(2)}) copy-start(bf16[2,128,896]{2,1,0:T(8,128)(2,1)S(1)} %collective-permute-done.7.rest_7_) | copy-start | bytes 1376260
  34.0 0.8 %copy-start.6 = (bf16[2,128,896]{2,1,0:T(8,128)(2,1)}, bf16[2,128,896]{2,1,0:T(8,128)(2,1)S(1)}, u32[]{:S(2)}) copy-start(bf16[2,128,896]{2,1,0:T(8,128)(2,1)S(1)} %collective-permute-done.9.rest_9_) | copy-start | bytes 1376260
  34.8 8.8 %collective-permute-start.13 = (bf16[2,128,896]{2,1,0:T(8,128)(2,1)}, bf16[2,128,896]{2,1,0:T(8,128)(2,1)}, u32[]{:S(2)}, u32[]{:S(2)}) collective-permute-start(bf16[2,128,896]{2,1,0:T(8,128)(2,1)} %collective-permute-done.10.rest_10_), channel_id=1, source_target_pairs={{0,4},{1,3},{4,8},{5,1},{8,12},{9,5},{12,14},{13,9},{14,10},{15,13... | collective-permute-start | bytes 1376264 | tf_op jit(solution)/shard_map/ppermute | solution.py:344
  43.6 2.0 %collective-permute-start.14 = (bf16[2,128,896]{2,1,0:T(8,128)(2,1)}, bf16[2,128,896]{2,1,0:T(8,128)(2,1)S(1)}, u32[]{:S(2)}, u32[]{:S(2)}) collective-permute-start(bf16[2,128,896]{2,1,0:T(8,128)(2,1)} %collective-permute-done.12.rest_12_), channel_id=1, source_target_pairs={{0,1},{1,0},{2,3},{3,2},{4,5},{5,4},{6,7},{7,6},{8,9},{9,8},{10,11... | collective-permute-start | bytes 1376264 | tf_op jit(solution)/shard_map/ppermute | solution.py:346
  43.6 2.7 %collective-permute-start.15 = (bf16[2,128,896]{2,1,0:T(8,128)(2,1)}, bf16[2,128,896]{2,1,0:T(8,128)(2,1)S(1)}, u32[]{:S(2)}, u32[]{:S(2)}) collective-permute-start(bf16[2,128,896]{2,1,0:T(8,128)(2,1)} %collective-permute-done.13.rest_14_), channel_id=1, source_target_pairs={{0,1},{1,0},{2,3},{3,2},{4,5},{5,4},{6,7},{7,6},{8,9},{9,8},{10,11... | collective-permute-start | bytes 1376264 | tf_op jit(solution)/shard_map/ppermute | solution.py:347
  46.3 2.0 %copy-start = (bf16[896,2048]{1,0:T(8,128)(2,1)S(1)}, bf16[896,2048]{1,0:T(8,128)(2,1)}, u32[]{:S(2)}) copy-start(bf16[896,2048]{1,0:T(8,128)(2,1)} %value_ref.1) | copy-start | bytes 11010052
  48.3 1.0 %copy-start.3 = (bf16[2,128,896]{2,1,0:T(8,128)(2,1)S(1)}, bf16[2,128,896]{2,1,0:T(8,128)(2,1)}, u32[]{:S(2)}) copy-start(bf16[2,128,896]{2,1,0:T(8,128)(2,1)} %copy-done.2) | copy-start | bytes 1376260
  49.3 1.0 %copy-start.5 = (bf16[2,128,896]{2,1,0:T(8,128)(2,1)S(1)}, bf16[2,128,896]{2,1,0:T(8,128)(2,1)}, u32[]{:S(2)}) copy-start(bf16[2,128,896]{2,1,0:T(8,128)(2,1)} %copy-done.4) | copy-start | bytes 1376260
  50.3 1.0 %copy-start.7 = (bf16[2,128,896]{2,1,0:T(8,128)(2,1)S(1)}, bf16[2,128,896]{2,1,0:T(8,128)(2,1)}, u32[]{:S(2)}) copy-start(bf16[2,128,896]{2,1,0:T(8,128)(2,1)} %copy-done.6) | copy-start | bytes 1376260
  51.4 0.6 copy-start.9
  51.9 0.6 copy-start.10

commit v11 on v10

--- a/solution.py
+++ b/solution.py
@@ -107,37 +107,21 @@
     pl.when(source >= first + half)(lambda: among(stores[half:], first + half, source, act))
 
 
-def plan_kernel(size, here_ref, place_ref, before_ref, owner_ref, slot_ref, source_ref, block_ref):
+def locate(request, plan_refs, size):
+    here_ref, place_ref, before_ref, owner_ref, slot_ref = plan_refs
+    window, part = divmod(request, 2)
+    owner = before_ref[0, part] if window == 0 else owner_ref[window - 1, part]
+    slot = before_ref[1, part] if window == 0 else slot_ref[window - 1, part]
     reach = (size - 1) // 2
     opposite = size - reach - 1
     here = here_ref[0]
-
-    def place(request, carry):
-        window, part = request // 2, request % 2
-        own = jnp.maximum(window - 1, 0)
-        owner = jnp.where(window == 0, before_ref[0, part], owner_ref[own, part])
-        away = place_ref[here // CORES] - place_ref[owner // CORES]
-        away = jnp.where(away < 0, away + size, away)
-        core = owner % CORES
-        holder = jnp.where((away == 0) | ((away > reach) & (away <= opposite)), core, jnp.where(away <= reach, 0, 1))
-        step = jnp.where(away <= opposite, away, size - away)
-        arrival = jnp.where(away == 0, 0, 2 * step - 1 + jnp.where(core == holder, 0, 1))
-        source_ref[request] = CORES * arrival + jnp.where(holder == here % CORES, 0, 1)
-        block_ref[request] = jnp.where(window == 0, before_ref[1, part], slot_ref[own, part])
-        return carry
-
-    lax.fori_loop(0, source_ref.shape[0], place, 0)
-
-
-def plan_requests(size, here, places, before, owner, slot):
-    requests = 2 * owner.shape[0] + 2
-    return pl.pallas_call(
-        functools.partial(plan_kernel, size),
-        out_shape=(jax.ShapeDtypeStruct((requests,), jnp.int32),) * 2,
-        in_specs=[SMEM_SPEC] * 5,
-        out_specs=(SMEM_SPEC,) * 2,
-        name="plan_requests",
-    )(here, places, before, owner, slot)
+    away = place_ref[here // CORES] - place_ref[owner // CORES]
+    away = jnp.where(away < 0, away + size, away)
+    core = owner % CORES
+    holder = jnp.where((away == 0) | ((away > reach) & (away <= opposite)), core, jnp.where(away <= reach, 0, 1))
+    step = jnp.where(away <= opposite, away, size - away)
+    arrival = jnp.where(away == 0, 0, 2 * step - 1 + jnp.where(core == holder, 0, 1))
+    return CORES * arrival + jnp.where(holder == here % CORES, 0, 1), slot
 
 
 def weigh(scores):
@@ -146,9 +130,8 @@
     return (powers * (1.0 / totals)).astype(jnp.bfloat16)
 
 
-def attend_kernel(
-    source_ref, block_ref, here_ref, starts_ref, folded_hbm, single_ref, value_ref, *rest
-):
+def attend_kernel(size, *refs):
+    plan_refs, (starts_ref, folded_hbm, single_ref, value_ref, *rest) = refs[:5], refs[5:]
     *stores, out_hbm, tokens, raw, folded, scores, weights, mixed, out, sems, folded_sems, out_sems = rest
     requests, length, width = raw.shape
     blocks = requests // 2 - 1
@@ -158,8 +141,8 @@
     lone_window = blocks
     order = [*range(1, blocks), lone_window, 0]
 
-    def fetch(request, store):
-        return pltpu.make_async_copy(store.at[block_ref[request]], raw.at[request], sems.at[request])
+    def fetch(request, store, block):
+        return pltpu.make_async_copy(store.at[block], raw.at[request], sems.at[request])
 
     def fetch_folded(group):
         heads = pl.ds(group * GROUP, GROUP)
@@ -171,7 +154,8 @@
 
     for window in order:
         for request in (2 * window, 2 * window + 1):
-            among(stores, 0, source_ref[request], lambda store: fetch(request, store).start())
+            source, block = locate(request, plan_refs, size)
+            among(stores, 0, source, lambda store: fetch(request, store, block).start())
         if window == order[0]:
             fetch_folded(0).start()
     for group in range(1, groups):
@@ -182,12 +166,12 @@
     for block in range(blocks):
         fresh = starts_ref[block] == 0
         if block == 0:
-            fresh = fresh & (here_ref[0] > 0)
+            fresh = fresh & (plan_refs[0][0] > 0)
         kept = kept | ((place // SPAN == block) & fresh)
 
     def ready(window):
         for request in (2 * window, 2 * window + 1):
-            fetch(request, stores[0]).wait()
+            fetch(request, stores[0], 0).wait()
         for request in (2 * window, 2 * window + 1):
             normalise(raw[request], tokens.at[request])
 
@@ -199,8 +183,8 @@
 
     def place_of(unit):
         group, window = units[unit]
-        slot = group * blocks + window
-        return slot, slice(group * GROUP, (group + 1) * GROUP), slice(window * SPAN, (window + 1) * SPAN)
+        heads, rows = slice(group * GROUP, (group + 1) * GROUP), slice(window * SPAN, (window + 1) * SPAN)
+        return unit % len(scores), heads, rows
 
     def score(unit):
         window = units[unit][1]
@@ -230,12 +214,12 @@
         if window == 0:
             first = lax.broadcasted_iota(jnp.int32, sums.shape, 1) == 0
             sums = jnp.where(first, lone["sums"][heads][:, None, :], sums)
-        mixed[heads, rows] = sums.astype(jnp.bfloat16)
+        mixed[units[unit][0] % 2, :, rows] = sums.astype(jnp.bfloat16)
 
     def project(group):
         for head in range(group * GROUP, (group + 1) * GROUP):
             columns = head_columns(head)
-            sums = contract(mixed[head], value_ref[:, columns], ((1,), (0,)))
+            sums = contract(mixed[group % 2, head % GROUP], value_ref[:, columns], ((1,), (0,)))
             sums = jnp.where(kept, sums, 0.0)
             out[:, columns] = pltpu.roll(sums, count - 1, 0).astype(jnp.bfloat16)
         put(group).start()
@@ -261,38 +245,37 @@
         put(group).wait()
 
 
-def attend(source, block, here, doc_starts, folded, single, w_value, stores):
-    requests = source.shape[0]
+def attend(size, plan, doc_starts, folded, single, w_value, stores):
+    requests = 2 * plan[3].shape[0] + 2
     length, width = stores[0].shape[1:]
     count = folded.shape[1]
     groups = HEADS // GROUP
-    units = groups * (count // SPAN)
     model_width = w_value.shape[1]
     return pl.pallas_call(
-        attend_kernel,
+        functools.partial(attend_kernel, size),
         out_shape=jax.ShapeDtypeStruct((count, model_width), jnp.bfloat16),
-        in_specs=[SMEM_SPEC] * 4 + [HBM_SPEC] + [VMEM_SPEC] * 2 + [ANY_SPEC] * len(stores),
+        in_specs=[SMEM_SPEC] * 6 + [HBM_SPEC] + [VMEM_SPEC] * 2 + [ANY_SPEC] * len(stores),
         out_specs=HBM_SPEC,
         scratch_shapes=[
             pltpu.VMEM((requests, length, width), jnp.bfloat16),
             pltpu.VMEM((requests, length, width), jnp.bfloat16),
             pltpu.VMEM(folded.shape, jnp.bfloat16),
-            pltpu.VMEM((units, GROUP * SPAN, 2 * length), jnp.float32),
-            pltpu.VMEM((units, GROUP * SPAN, 2 * length), jnp.bfloat16),
-            pltpu.VMEM(folded.shape, jnp.bfloat16),
+            pltpu.VMEM((5, GROUP * SPAN, 2 * length), jnp.float32),
+            pltpu.VMEM((5, GROUP * SPAN, 2 * length), jnp.bfloat16),
+            pltpu.VMEM((2, GROUP, count, width), jnp.bfloat16),
             pltpu.VMEM((count, model_width), jnp.bfloat16),
             pltpu.SemaphoreType.DMA((requests,)),
             pltpu.SemaphoreType.DMA((groups,)),
             pltpu.SemaphoreType.DMA((groups,)),
         ],
-        compiler_params=pltpu.CompilerParams(vmem_limit_bytes=40 * MIB),
+        compiler_params=pltpu.CompilerParams(vmem_limit_bytes=24 * MIB),
         cost_estimate=pl.CostEstimate(
             flops=2 * HEADS * count * width * (4 * length + HEAD_DIM),
             bytes_accessed=16 * MIB,
             transcendentals=HEADS * count * 2 * length,
         ),
         name="attend_windows",
-    )(source, block, here, doc_starts, in_hbm(folded), single, w_value, *stores)
+    )(*plan, doc_starts, in_hbm(folded), single, w_value, *stores)
 
 
 def chip_ring(mesh):
@@ -326,26 +309,27 @@
     stores = list(chains)
     folded, single = fold(*after([queries], [chains[1]]), w_key)
 
-    owner_slot = jnp.stack([retrieval_owner[-1], retrieval_slot[-1]])
-    before = lax.ppermute(*after([owner_slot], [single]), "seq", [(i, i + 1) for i in range(devices - 1)])
-    places = jnp.asarray([ring.index(chip) for chip in range(size)], jnp.int32)
-    here = lax.axis_index("seq").reshape(1)
-    source, block = plan_requests(size, here, places, before, retrieval_owner, retrieval_slot)
-
-    beside = {(1, 0): [folded, single], (1, 1): [before]}
+    beside = {(1, 0): [folded, single]}
     for step in range(reach):
         for chain in range(2):
             others = beside.get((step, chain), []) + (stores[2 * chain + 4 * step - 5 :][:1] if step > 1 else [])
             sent = after([chains[chain]], others) if others else [chains[chain]]
             chains[chain] = onwards(sent[0])
             stores += [chains[chain], swapped(chains[chain])]
+            if (step, chain) == (0, 1):
+                owner, slot = after([retrieval_owner, retrieval_slot], [chains[1]])
+                asked = jnp.stack([owner[-1], slot[-1]])
+                before = lax.ppermute(asked, "seq", [(i, i + 1) for i in range(devices - 1)])
+                beside[reach - 1, 1] = [before]
+    places = jnp.asarray([ring.index(chip) for chip in range(size)], jnp.int32)
+    plan = [lax.axis_index("seq").reshape(1), places, before, owner, slot]
     if size % 2 == 0:
         sent = after([chains[0]], stores[-7:-4:2]) if reach > 1 else [chains[0]]
         last = onwards(sent[0])
         if reach:
-            stores[-1] = swapped(after([chains[1]], [last, stores[-3], source, block])[0])
+            stores[-1] = swapped(after([chains[1]], [last, stores[-3]])[0])
         stores += [last, swapped(last)]
-    return attend(source, block, here, doc_starts, folded, single, w_value, stores)
+    return attend(size, plan, doc_starts, folded, single, w_value, stores)
 
 
 def solution(mesh):

time: 65.8 us -> 62.4 us (0.948)
  local copies, waits for them, and re-layouts: 10.2 us -> 4.04 us
  starting transfers between devices: 15.8 us -> 20.2 us
  Pallas kernels: 19.1 us -> 17.4 us
    unnamed x30 -> x16, local copies, waits for them, and re-layouts: 10.2 us -> 3.84 us
    ppermute x6, starting transfers between devices: 11.7 us -> 15 us  [body(): chains[chain] = onwards(sent[0])]
    pallas_call x2 -> x1, Pallas kernels: 14.1 us -> 12.4 us  [attend(): pl.pallas_call(functools.partial(attend_kernel, size), out_shape=jax.Shap...]
    ppermute x1, waiting for transfers between devices: 5.44 us -> 4.25 us  [body(): last = onwards(sent[0])]
    ppermute x2, waiting for transfers between devices: 1.52 us -> 2.45 us  [the longest x1 1.65 us: body(): stores[-1] = swapped(after([chains[1]], [last, stores[-3]])[0])]
    ppermute x2, starting transfers between devices: 1.71 us -> 2.41 us  [the longest x1 2.41 us: body(): lax.ppermute(asked, 'seq', [(i, i + 1) for i in range(devices - 1)])]
    ppermute x1, starting transfers between devices: 0.95 us -> 1.63 us  [body(): last = onwards(sent[0])]
  transfers between devices with their start and end apart: 16 -> 16, of which waited for: 7 -> 8; matrix products, arithmetic and copies ran while one was open for 2% -> 0% of each run, Pallas kernels for 10% -> 8%
where the time goes in v11:
time: 62.4 us; the launch traced here: 62.1 us
  starting transfers between devices  20.2 us (32%)
  waiting for transfers between devices  20.2 us (32%)
  Pallas kernels  17.4 us (28%)
  local copies, waits for them, and re-layouts  4.04 us (6%)
    ppermute x6, starting transfers between devices, body(): chains[chain] = onwards(sent[0])  15 us
    ppermute x6, waiting for transfers between devices, body(): chains[chain] = onwards(sent[0])  12.8 us
    pallas_call x1, Pallas kernels, attend(): pl.pallas_call(functools.partial(attend_kernel, size), out_shape=jax.Shap...  12.4 us
    pallas_call x1, Pallas kernels, fold(): pl.pallas_call(fold_kernel, out_shape=(pltpu.HBM(shape, jnp.bfloat16), ja...  5.07 us
    ppermute x1, waiting for transfers between devices, body(): last = onwards(sent[0])  4.25 us
    unnamed x16, local copies, waits for them, and re-layouts  3.84 us
    ppermute x1, starting transfers between devices, body(): lax.ppermute(asked, 'seq', [(i, i + 1) for i in range(devices - 1)])  2.41 us
    ppermute x1, waiting for transfers between devices, body(): stores[-1] = swapped(after([chains[1]], [last, stores[-3]])[0])  1.65 us
  transfers between devices with their start and end apart: 16, of which 8 were waited for; matrix products, arithmetic and copies ran while one was open for 0% of the time, Pallas kernels for 8%

profile of v11, /device:TPU:0, one launch (start us, length us, event | category | flops | bytes accessed | tf_op | source)
XLA Modules:
  0.0 62.1 jit_solution(18420688602097447641)
XLA Ops:
  0.0 0.0 copy-start.5
  0.0 0.0 copy-start.1
  0.0 0.0 copy-start.7
  0.0 0.5 collective-permute-start
  0.5 2.6 %collective-permute-start.3 = (bf16[2,128,896]{2,1,0:T(8,128)(2,1)}, bf16[2,128,896]{2,1,0:T(8,128)(2,1)S(1)}, u32[]{:S(2)}, u32[]{:S(2)}) collective-permute-start(bf16[2,128,896]{2,1,0:T(8,128)(2,1)} %refs_9_.1), channel_id=1, source_target_pairs={{0,4},{1,3},{4,8},{5,1},{8,12},{9,5},{12,14},{13,9},{14,10},{15,13... | collective-permute-start | bytes 1376264 | tf_op jit(solution)/shard_map/ppermute | solution.py:317
  3.2 0.0 collective-permute-done.refs_10_
  3.2 2.0 %collective-permute-start.1 = (bf16[2,128,896]{2,1,0:T(8,128)(2,1)S(1)}, bf16[2,128,896]{2,1,0:T(8,128)(2,1)S(1)}, u32[]{:S(2)}, u32[]{:S(2)}) collective-permute-start(bf16[2,128,896]{2,1,0:T(8,128)(2,1)S(1)} %collective-permute-done.refs_10_), channel_id=1, source_target_pairs={{0,4},{1,3},{4,8},{5,1},{8,12},{9,5},{12,14},{13,9},{14,10},{15,13... | collective-permute-start | bytes 1376264 | tf_op jit(solution)/shard_map/ppermute | solution.py:317
  5.1 5.1 %fold_queries.1 = (bf16[16,256,896]{2,1,0:T(8,128)(2,1)}, f32[16,896]{1,0:T(8,128)S(1)}) custom-call(bf16[256,2048]{1,0:T(8,128)(2,1)} %query_hbm, bf16[896,2048]{1,0:T(8,128)(2,1)} %key_hbm.1), custom_call_target="tpu_custom_call" | custom-call | flops 939524096 | bytes 12582912 | tf_op jit(solution)/shard_map/fold_queries/pallas_call | solution.py:72
  10.2 0.0 collective-permute-done.3.refs_11_
  10.2 0.1 collective-permute-start.4
  10.3 1.6 %collective-permute-start.6 = (bf16[2,128,896]{2,1,0:T(8,128)(2,1)S(1)}, bf16[2,128,896]{2,1,0:T(8,128)(2,1)S(1)}, u32[]{:S(2)}, u32[]{:S(2)}) collective-permute-start(bf16[2,128,896]{2,1,0:T(8,128)(2,1)S(1)} %collective-permute-done.3.refs_11_), channel_id=1, source_target_pairs={{0,4},{1,3},{4,8},{5,1},{8,12},{9,5},{12,14},{13,9},{14,10},{15,13... | collective-permute-start | bytes 1376264 | tf_op jit(solution)/shard_map/ppermute | solution.py:317
  11.9 2.8 %collective-permute-done.1.refs_13_ = bf16[2,128,896]{2,1,0:T(8,128)(2,1)S(1)} collective-permute-done((bf16[2,128,896]{2,1,0:T(8,128)(2,1)S(1)}, bf16[2,128,896]{2,1,0:T(8,128)(2,1)S(1)}, u32[]{:S(2)}, u32[]{:S(2)}) %collective-permute-start.1) | collective-permute-done | bytes 458784 | tf_op jit(solution)/shard_map/ppermute | solution.py:317
  14.7 2.1 %collective-permute-start.8 = (bf16[2,128,896]{2,1,0:T(8,128)(2,1)S(1)}, bf16[2,128,896]{2,1,0:T(8,128)(2,1)S(1)}, u32[]{:S(2)}, u32[]{:S(2)}) collective-permute-start(bf16[2,128,896]{2,1,0:T(8,128)(2,1)S(1)} %collective-permute-done.1.refs_13_), channel_id=1, source_target_pairs={{0,4},{1,3},{4,8},{5,1},{8,12},{9,5},{12,14},{13,9},{14,10},{15,13... | collective-permute-start | bytes 1376264 | tf_op jit(solution)/shard_map/ppermute | solution.py:317
  16.8 0.0 collective-permute-start.5
  16.8 0.0 collective-permute-done.4.refs_12_
  16.8 2.8 %collective-permute-done.6.refs_15_ = bf16[2,128,896]{2,1,0:T(8,128)(2,1)S(1)} collective-permute-done((bf16[2,128,896]{2,1,0:T(8,128)(2,1)S(1)}, bf16[2,128,896]{2,1,0:T(8,128)(2,1)S(1)}, u32[]{:S(2)}, u32[]{:S(2)}) %collective-permute-start.6) | collective-permute-done | bytes 458784 | tf_op jit(solution)/shard_map/ppermute | solution.py:317
  19.6 2.1 %collective-permute-start.10 = (bf16[2,128,896]{2,1,0:T(8,128)(2,1)S(1)}, bf16[2,128,896]{2,1,0:T(8,128)(2,1)}, u32[]{:S(2)}, u32[]{:S(2)}) collective-permute-start(bf16[2,128,896]{2,1,0:T(8,128)(2,1)S(1)} %collective-permute-done.6.refs_15_), channel_id=1, source_target_pairs={{0,4},{1,3},{4,8},{5,1},{8,12},{9,5},{12,14},{13,9},{14,10},{15,13... | collective-permute-start | bytes 1376264 | tf_op jit(solution)/shard_map/ppermute | solution.py:317
  21.7 0.0 collective-permute-start.7
  21.7 2.8 %collective-permute-done.8.refs_17_ = bf16[2,128,896]{2,1,0:T(8,128)(2,1)S(1)} collective-permute-done((bf16[2,128,896]{2,1,0:T(8,128)(2,1)S(1)}, bf16[2,128,896]{2,1,0:T(8,128)(2,1)S(1)}, u32[]{:S(2)}, u32[]{:S(2)}) %collective-permute-start.8) | collective-permute-done | bytes 458784 | tf_op jit(solution)/shard_map/ppermute | solution.py:317
  24.5 0.0 collective-permute-start.9
  24.5 0.0 copy-done.6
  24.5 0.1 copy.9.refs_3_
  24.6 0.0 copy-done.7
  24.7 0.1 copy.10.refs_4_
  24.8 2.4 %collective-permute-start.2 = (s32[2,2]{1,0:T(2,128)S(1)}, s32[2,2]{1,0:T(2,128)S(1)}, u32[]{:S(2)}, u32[]{:S(2)}) collective-permute-start(s32[2,2]{1,0:T(2,128)S(1)} %pad_add_fusion), channel_id=1, source_target_pairs={{0,1},{1,2},{2,3},{3,4},{4,5},{5,6},{6,7},{7,8},{8,9},{9,10},{10,1... | collective-permute-start | bytes 56 | tf_op jit(solution)/shard_map/ppermute | solution.py:322
  27.2 0.8 %collective-permute-done.2.refs_2_ = s32[2,2]{1,0:T(2,128)S(1)} collective-permute-done((s32[2,2]{1,0:T(2,128)S(1)}, s32[2,2]{1,0:T(2,128)S(1)}, u32[]{:S(2)}, u32[]{:S(2)}) %collective-permute-start.2) | collective-permute-done | bytes 48 | tf_op jit(solution)/shard_map/ppermute | solution.py:322
  28.0 0.0 collective-permute-done.5.refs_14_
  28.0 4.6 %collective-permute-start.12 = (bf16[2,128,896]{2,1,0:T(8,128)(2,1)S(1)}, bf16[2,128,896]{2,1,0:T(8,128)(2,1)}, u32[]{:S(2)}, u32[]{:S(2)}) collective-permute-start(bf16[2,128,896]{2,1,0:T(8,128)(2,1)S(1)} %collective-permute-done.8.refs_17_), channel_id=1, source_target_pairs={{0,4},{1,3},{4,8},{5,1},{8,12},{9,5},{12,14},{13,9},{14,10},{15,13... | collective-permute-start | bytes 1376264 | tf_op jit(solution)/shard_map/ppermute | solution.py:317
  32.6 0.0 collective-permute-done.10.refs_19_
  32.6 0.0 collective-permute-start.11
  32.6 0.0 collective-permute-done.7.refs_16_
  32.6 0.0 collective-permute-done.9.refs_18_
  32.7 1.6 %collective-permute-start.13 = (bf16[2,128,896]{2,1,0:T(8,128)(2,1)}, bf16[2,128,896]{2,1,0:T(8,128)(2,1)}, u32[]{:S(2)}, u32[]{:S(2)}) collective-permute-start(bf16[2,128,896]{2,1,0:T(8,128)(2,1)} %collective-permute-done.10.refs_19_), channel_id=1, source_target_pairs={{0,4},{1,3},{4,8},{5,1},{8,12},{9,5},{12,14},{13,9},{14,10},{15,13... | collective-permute-start | bytes 1376264 | tf_op jit(solution)/shard_map/ppermute | solution.py:328
  34.3 4.3 %collective-permute-done.12.refs_21_ = bf16[2,128,896]{2,1,0:T(8,128)(2,1)} collective-permute-done((bf16[2,128,896]{2,1,0:T(8,128)(2,1)S(1)}, bf16[2,128,896]{2,1,0:T(8,128)(2,1)}, u32[]{:S(2)}, u32[]{:S(2)}) %collective-permute-start.12) | collective-permute-done | bytes 458784 | tf_op jit(solution)/shard_map/ppermute | solution.py:317
  38.6 0.0 collective-permute-done.11.refs_20_
  38.6 0.8 %copy-done.2 = bf16[2,128,896]{2,1,0:T(8,128)(2,1)} copy-done((bf16[2,128,896]{2,1,0:T(8,128)(2,1)}, bf16[2,128,896]{2,1,0:T(8,128)(2,1)S(1)}, u32[]{:S(2)}) %copy-start.2) | copy-done | bytes 458776
  39.4 4.2 %collective-permute-done.13.refs_23_ = bf16[2,128,896]{2,1,0:T(8,128)(2,1)} collective-permute-done((bf16[2,128,896]{2,1,0:T(8,128)(2,1)}, bf16[2,128,896]{2,1,0:T(8,128)(2,1)}, u32[]{:S(2)}, u32[]{:S(2)}) %collective-permute-start.13) | collective-permute-done | bytes 458784 | tf_op jit(solution)/shard_map/ppermute | solution.py:328
  43.6 0.0 collective-permute-start.14
  43.6 0.5 collective-permute-start.15
  44.2 1.6 %collective-permute-done.14.refs_22_ = bf16[2,128,896]{2,1,0:T(8,128)(2,1)} collective-permute-done((bf16[2,128,896]{2,1,0:T(8,128)(2,1)}, bf16[2,128,896]{2,1,0:T(8,128)(2,1)}, u32[]{:S(2)}, u32[]{:S(2)}) %collective-permute-start.14) | collective-permute-done | bytes 458784 | tf_op jit(solution)/shard_map/ppermute | solution.py:330
  45.8 0.7 %collective-permute-done.15.refs_24_ = bf16[2,128,896]{2,1,0:T(8,128)(2,1)} collective-permute-done((bf16[2,128,896]{2,1,0:T(8,128)(2,1)}, bf16[2,128,896]{2,1,0:T(8,128)(2,1)}, u32[]{:S(2)}, u32[]{:S(2)}) %collective-permute-start.15) | collective-permute-done | bytes 458784 | tf_op jit(solution)/shard_map/ppermute | solution.py:331
  46.5 0.0 copy-done.5
  46.5 0.0 copy-done.1
  46.5 0.0 copy-done.4
  46.5 0.0 copy-start
  46.5 2.0 %copy-done = bf16[896,2048]{1,0:T(8,128)(2,1)S(1)} copy-done((bf16[896,2048]{1,0:T(8,128)(2,1)S(1)}, bf16[896,2048]{1,0:T(8,128)(2,1)}, u32[]{:S(2)}) %copy-start) | copy-done | bytes 3670040
  48.5 1.0 %copy-done.3 = bf16[2,128,896]{2,1,0:T(8,128)(2,1)S(1)} copy-done((bf16[2,128,896]{2,1,0:T(8,128)(2,1)S(1)}, bf16[2,128,896]{2,1,0:T(8,128)(2,1)}, u32[]{:S(2)}) %copy-start.3) | copy-done | bytes 458776
  49.5 12.4 %attend_windows.1 = bf16[256,2048]{1,0:T(8,128)(2,1)} custom-call(s32[1]{0:T(128)} %bitcast.refs_0_, s32[8]{0:T(128)S(1)} %copy-done.5, s32[2,2]{1,0:T(2,128)S(1)} %collective-permute-done.2.refs_2_, s32[4,2]{1,0:T(4,128)S(1)} %copy.9.refs_3_, s32[4,2]{1,0:T(4,128)S(1)} %copy.10.refs_4_, s32[4]{0:T(128)S(1)} %copy-done.4, ...), custom_call_target="tpu_custom_call" | custom-call | flops 4697620480 | bytes 16777216 | tf_op jit(solution)/shard_map/attend_windows/pallas_call | solution.py:254
  (7 shorter events, 0.0 us)
Async XLA Ops:
  0.0 46.5 %copy-start.5 = (s32[8]{0:T(128)S(1)}, s32[8]{0:T(128)}, u32[]{:S(2)}) copy-start(s32[8]{0:T(128)} %constant.6.clone.refs_1_) | copy-start | bytes 100
  0.0 46.5 %copy-start.1 = (bf16[2,128,896]{2,1,0:T(8,128)(2,1)S(1)}, bf16[2,128,896]{2,1,0:T(8,128)(2,1)}, u32[]{:S(2)}) copy-start(bf16[2,128,896]{2,1,0:T(8,128)(2,1)} %refs_9_.1) | copy-start | bytes 1376260
  0.0 24.6 %copy-start.7 = (s32[4,2]{0,1:T(2,128)S(1)}, s32[4,2]{0,1:T(2,128)}, u32[]{:S(2)}) copy-start(s32[4,2]{0,1:T(2,128)} %param.13) | copy-start | bytes 100
  0.0 24.5 %copy-start.6 = (s32[4,2]{0,1:T(2,128)S(1)}, s32[4,2]{0,1:T(2,128)}, u32[]{:S(2)}) copy-start(s32[4,2]{0,1:T(2,128)} %param.12) | copy-start | bytes 100
  0.0 46.5 %copy-start.4 = (s32[4]{0:T(128)S(1)}, s32[4]{0:T(128)}, u32[]{:S(2)}) copy-start(s32[4]{0:T(128)} %refs_5_.1) | copy-start | bytes 52
  0.0 3.2 %collective-permute-start = (bf16[2,128,896]{2,1,0:T(8,128)(2,1)}, bf16[2,128,896]{2,1,0:T(8,128)(2,1)S(1)}, u32[]{:S(2)}, u32[]{:S(2)}) collective-permute-start(bf16[2,128,896]{2,1,0:T(8,128)(2,1)} %refs_9_.1), channel_id=1, source_target_pairs={{0,1},{1,0},{2,3},{3,2},{4,5},{5,4},{6,7},{7,6},{8,9},{9,8},{10,11... | collective-permute-start | bytes 1376264 | tf_op jit(solution)/shard_map/ppermute | solution.py:308
  0.5 9.7 %collective-permute-start.3 = (bf16[2,128,896]{2,1,0:T(8,128)(2,1)}, bf16[2,128,896]{2,1,0:T(8,128)(2,1)S(1)}, u32[]{:S(2)}, u32[]{:S(2)}) collective-permute-start(bf16[2,128,896]{2,1,0:T(8,128)(2,1)} %refs_9_.1), channel_id=1, source_target_pairs={{0,4},{1,3},{4,8},{5,1},{8,12},{9,5},{12,14},{13,9},{14,10},{15,13... | collective-permute-start | bytes 1376264 | tf_op jit(solution)/shard_map/ppermute | solution.py:317
  3.2 11.5 %collective-permute-start.1 = (bf16[2,128,896]{2,1,0:T(8,128)(2,1)S(1)}, bf16[2,128,896]{2,1,0:T(8,128)(2,1)S(1)}, u32[]{:S(2)}, u32[]{:S(2)}) collective-permute-start(bf16[2,128,896]{2,1,0:T(8,128)(2,1)S(1)} %collective-permute-done.refs_10_), channel_id=1, source_target_pairs={{0,4},{1,3},{4,8},{5,1},{8,12},{9,5},{12,14},{13,9},{14,10},{15,13... | collective-permute-start | bytes 1376264 | tf_op jit(solution)/shard_map/ppermute | solution.py:317
  10.2 6.6 %collective-permute-start.4 = (bf16[2,128,896]{2,1,0:T(8,128)(2,1)S(1)}, bf16[2,128,896]{2,1,0:T(8,128)(2,1)S(1)}, u32[]{:S(2)}, u32[]{:S(2)}) collective-permute-start(bf16[2,128,896]{2,1,0:T(8,128)(2,1)S(1)} %collective-permute-done.3.refs_11_), channel_id=1, source_target_pairs={{0,1},{1,0},{2,3},{3,2},{4,5},{5,4},{6,7},{7,6},{8,9},{9,8},{10,11... | collective-permute-start | bytes 1376264 | tf_op jit(solution)/shard_map/ppermute | solution.py:318
  10.3 9.3 %collective-permute-start.6 = (bf16[2,128,896]{2,1,0:T(8,128)(2,1)S(1)}, bf16[2,128,896]{2,1,0:T(8,128)(2,1)S(1)}, u32[]{:S(2)}, u32[]{:S(2)}) collective-permute-start(bf16[2,128,896]{2,1,0:T(8,128)(2,1)S(1)} %collective-permute-done.3.refs_11_), channel_id=1, source_target_pairs={{0,4},{1,3},{4,8},{5,1},{8,12},{9,5},{12,14},{13,9},{14,10},{15,13... | collective-permute-start | bytes 1376264 | tf_op jit(solution)/shard_map/ppermute | solution.py:317
  14.7 9.8 %collective-permute-start.8 = (bf16[2,128,896]{2,1,0:T(8,128)(2,1)S(1)}, bf16[2,128,896]{2,1,0:T(8,128)(2,1)S(1)}, u32[]{:S(2)}, u32[]{:S(2)}) collective-permute-start(bf16[2,128,896]{2,1,0:T(8,128)(2,1)S(1)} %collective-permute-done.1.refs_13_), channel_id=1, source_target_pairs={{0,4},{1,3},{4,8},{5,1},{8,12},{9,5},{12,14},{13,9},{14,10},{15,13... | collective-permute-start | bytes 1376264 | tf_op jit(solution)/shard_map/ppermute | solution.py:317
  16.8 11.2 %collective-permute-start.5 = (bf16[2,128,896]{2,1,0:T(8,128)(2,1)S(1)}, bf16[2,128,896]{2,1,0:T(8,128)(2,1)}, u32[]{:S(2)}, u32[]{:S(2)}) collective-permute-start(bf16[2,128,896]{2,1,0:T(8,128)(2,1)S(1)} %collective-permute-done.1.refs_13_), channel_id=1, source_target_pairs={{0,1},{1,0},{2,3},{3,2},{4,5},{5,4},{6,7},{7,6},{8,9},{9,8},{10,11... | collective-permute-start | bytes 1376264 | tf_op jit(solution)/shard_map/ppermute | solution.py:318
  19.6 13.0 %collective-permute-start.10 = (bf16[2,128,896]{2,1,0:T(8,128)(2,1)S(1)}, bf16[2,128,896]{2,1,0:T(8,128)(2,1)}, u32[]{:S(2)}, u32[]{:S(2)}) collective-permute-start(bf16[2,128,896]{2,1,0:T(8,128)(2,1)S(1)} %collective-permute-done.6.refs_15_), channel_id=1, source_target_pairs={{0,4},{1,3},{4,8},{5,1},{8,12},{9,5},{12,14},{13,9},{14,10},{15,13... | collective-permute-start | bytes 1376264 | tf_op jit(solution)/shard_map/ppermute | solution.py:317
  21.7 10.9 %collective-permute-start.7 = (bf16[2,128,896]{2,1,0:T(8,128)(2,1)S(1)}, bf16[2,128,896]{2,1,0:T(8,128)(2,1)}, u32[]{:S(2)}, u32[]{:S(2)}) collective-permute-start(bf16[2,128,896]{2,1,0:T(8,128)(2,1)S(1)} %collective-permute-done.6.refs_15_), channel_id=1, source_target_pairs={{0,1},{1,0},{2,3},{3,2},{4,5},{5,4},{6,7},{7,6},{8,9},{9,8},{10,11... | collective-permute-start | bytes 1376264 | tf_op jit(solution)/shard_map/ppermute | solution.py:318
  24.5 8.1 %collective-permute-start.9 = (bf16[2,128,896]{2,1,0:T(8,128)(2,1)S(1)}, bf16[2,128,896]{2,1,0:T(8,128)(2,1)}, u32[]{:S(2)}, u32[]{:S(2)}) collective-permute-start(bf16[2,128,896]{2,1,0:T(8,128)(2,1)S(1)} %collective-permute-done.8.refs_17_), channel_id=1, source_target_pairs={{0,1},{1,0},{2,3},{3,2},{4,5},{5,4},{6,7},{7,6},{8,9},{9,8},{10,11... | collective-permute-start | bytes 1376264 | tf_op jit(solution)/shard_map/ppermute | solution.py:318
  24.8 3.2 %collective-permute-start.2 = (s32[2,2]{1,0:T(2,128)S(1)}, s32[2,2]{1,0:T(2,128)S(1)}, u32[]{:S(2)}, u32[]{:S(2)}) collective-permute-start(s32[2,2]{1,0:T(2,128)S(1)} %pad_add_fusion), channel_id=1, source_target_pairs={{0,1},{1,2},{2,3},{3,4},{4,5},{5,6},{6,7},{7,8},{8,9},{9,10},{10,1... | collective-permute-start | bytes 56 | tf_op jit(solution)/shard_map/ppermute | solution.py:322
  28.0 10.6 %collective-permute-start.12 = (bf16[2,128,896]{2,1,0:T(8,128)(2,1)S(1)}, bf16[2,128,896]{2,1,0:T(8,128)(2,1)}, u32[]{:S(2)}, u32[]{:S(2)}) collective-permute-start(bf16[2,128,896]{2,1,0:T(8,128)(2,1)S(1)} %collective-permute-done.8.refs_17_), channel_id=1, source_target_pairs={{0,4},{1,3},{4,8},{5,1},{8,12},{9,5},{12,14},{13,9},{14,10},{15,13... | collective-permute-start | bytes 1376264 | tf_op jit(solution)/shard_map/ppermute | solution.py:317
  32.6 6.0 %collective-permute-start.11 = (bf16[2,128,896]{2,1,0:T(8,128)(2,1)}, bf16[2,128,896]{2,1,0:T(8,128)(2,1)S(1)}, u32[]{:S(2)}, u32[]{:S(2)}) collective-permute-start(bf16[2,128,896]{2,1,0:T(8,128)(2,1)} %collective-permute-done.10.refs_19_), channel_id=1, source_target_pairs={{0,1},{1,0},{2,3},{3,2},{4,5},{5,4},{6,7},{7,6},{8,9},{9,8},{10,11... | collective-permute-start | bytes 1376264 | tf_op jit(solution)/shard_map/ppermute | solution.py:318
  32.7 11.0 %collective-permute-start.13 = (bf16[2,128,896]{2,1,0:T(8,128)(2,1)}, bf16[2,128,896]{2,1,0:T(8,128)(2,1)}, u32[]{:S(2)}, u32[]{:S(2)}) collective-permute-start(bf16[2,128,896]{2,1,0:T(8,128)(2,1)} %collective-permute-done.10.refs_19_), channel_id=1, source_target_pairs={{0,4},{1,3},{4,8},{5,1},{8,12},{9,5},{12,14},{13,9},{14,10},{15,13... | collective-permute-start | bytes 1376264 | tf_op jit(solution)/shard_map/ppermute | solution.py:328
  38.6 0.8 %copy-start.2 = (bf16[2,128,896]{2,1,0:T(8,128)(2,1)}, bf16[2,128,896]{2,1,0:T(8,128)(2,1)S(1)}, u32[]{:S(2)}) copy-start(bf16[2,128,896]{2,1,0:T(8,128)(2,1)S(1)} %collective-permute-done.11.refs_20_) | copy-start | bytes 1376260
  43.6 2.2 %collective-permute-start.14 = (bf16[2,128,896]{2,1,0:T(8,128)(2,1)}, bf16[2,128,896]{2,1,0:T(8,128)(2,1)}, u32[]{:S(2)}, u32[]{:S(2)}) collective-permute-start(bf16[2,128,896]{2,1,0:T(8,128)(2,1)} %collective-permute-done.12.refs_21_), channel_id=1, source_target_pairs={{0,1},{1,0},{2,3},{3,2},{4,5},{5,4},{6,7},{7,6},{8,9},{9,8},{10,11... | collective-permute-start | bytes 1376264 | tf_op jit(solution)/shard_map/ppermute | solution.py:330
  43.6 2.8 %collective-permute-start.15 = (bf16[2,128,896]{2,1,0:T(8,128)(2,1)}, bf16[2,128,896]{2,1,0:T(8,128)(2,1)}, u32[]{:S(2)}, u32[]{:S(2)}) collective-permute-start(bf16[2,128,896]{2,1,0:T(8,128)(2,1)} %collective-permute-done.13.refs_23_), channel_id=1, source_target_pairs={{0,1},{1,0},{2,3},{3,2},{4,5},{5,4},{6,7},{7,6},{8,9},{9,8},{10,11... | collective-permute-start | bytes 1376264 | tf_op jit(solution)/shard_map/ppermute | solution.py:331
  46.5 2.0 %copy-start = (bf16[896,2048]{1,0:T(8,128)(2,1)S(1)}, bf16[896,2048]{1,0:T(8,128)(2,1)}, u32[]{:S(2)}) copy-start(bf16[896,2048]{1,0:T(8,128)(2,1)} %refs_8_.1) | copy-start | bytes 11010052
  48.5 1.0 %copy-start.3 = (bf16[2,128,896]{2,1,0:T(8,128)(2,1)S(1)}, bf16[2,128,896]{2,1,0:T(8,128)(2,1)}, u32[]{:S(2)}) copy-start(bf16[2,128,896]{2,1,0:T(8,128)(2,1)} %copy-done.2) | copy-start | bytes 1376260

commit v12 on v11

--- a/solution.py
+++ b/solution.py
@@ -36,11 +36,19 @@
     return slice(head * HEAD_DIM, (head + 1) * HEAD_DIM)
 
 
+def group_heads(group):
+    return pl.ds(group * GROUP, GROUP)
+
+
+def group_columns(group):
+    return pl.ds(group * GROUP * HEAD_DIM, GROUP * HEAD_DIM)
+
+
 def fold_kernel(query_hbm, key_hbm, folded_hbm, single_ref, query, key, folded, in_sems, out_sems):
     groups = HEADS // GROUP
 
     def fetch(group):
-        columns = slice(group * GROUP * HEAD_DIM, (group + 1) * GROUP * HEAD_DIM)
+        columns = group_columns(group)
         return (
             pltpu.make_async_copy(query_hbm.at[:, columns], query.at[:, columns], in_sems.at[group, 0]),
             pltpu.make_async_copy(key_hbm.at[:, columns], key.at[:, columns], in_sems.at[group, 1]),
@@ -108,10 +116,13 @@
 
 
 def locate(request, plan_refs, size):
-    here_ref, place_ref, before_ref, owner_ref, slot_ref = plan_refs
+    here_ref, place_ref, owner_before_ref, slot_before_ref, owner_ref, slot_ref = plan_refs
     window, part = divmod(request, 2)
-    owner = before_ref[0, part] if window == 0 else owner_ref[window - 1, part]
-    slot = before_ref[1, part] if window == 0 else slot_ref[window - 1, part]
+    if window == 0:
+        last = owner_before_ref.shape[1] - 1
+        owner, slot = owner_before_ref[part, last], slot_before_ref[part, last]
+    else:
+        owner, slot = owner_ref[part, window - 1], slot_ref[part, window - 1]
     reach = (size - 1) // 2
     opposite = size - reach - 1
     here = here_ref[0]
@@ -131,8 +142,8 @@
 
 
 def attend_kernel(size, *refs):
-    plan_refs, (starts_ref, folded_hbm, single_ref, value_ref, *rest) = refs[:5], refs[5:]
-    *stores, out_hbm, tokens, raw, folded, scores, weights, mixed, out, sems, folded_sems, out_sems = rest
+    plan_refs, (starts_ref, folded_hbm, single_ref, value_hbm, *rest) = refs[:6], refs[6:]
+    *stores, out_hbm, tokens, raw, folded, value, scores, weights, mixed, out, sems, group_sems = rest
     requests, length, width = raw.shape
     blocks = requests // 2 - 1
     count = blocks * SPAN
@@ -144,22 +155,27 @@
     def fetch(request, store, block):
         return pltpu.make_async_copy(store.at[block], raw.at[request], sems.at[request])
 
-    def fetch_folded(group):
-        heads = pl.ds(group * GROUP, GROUP)
-        return pltpu.make_async_copy(folded_hbm.at[heads], folded.at[heads], folded_sems.at[group])
+    def fetch_group(group):
+        heads, columns = group_heads(group), group_columns(group)
+        return (
+            pltpu.make_async_copy(folded_hbm.at[heads], folded.at[heads], group_sems.at[group, 0]),
+            pltpu.make_async_copy(value_hbm.at[:, columns], value.at[:, columns], group_sems.at[group, 1]),
+        )
 
     def put(group):
-        columns = pl.ds(group * GROUP * HEAD_DIM, GROUP * HEAD_DIM)
-        return pltpu.make_async_copy(out.at[:, columns], out_hbm.at[:, columns], out_sems.at[group])
+        columns = group_columns(group)
+        return pltpu.make_async_copy(out.at[:, columns], out_hbm.at[:, columns], group_sems.at[group, 2])
 
     for window in order:
         for request in (2 * window, 2 * window + 1):
             source, block = locate(request, plan_refs, size)
             among(stores, 0, source, lambda store: fetch(request, store, block).start())
         if window == order[0]:
-            fetch_folded(0).start()
+            fetch_group(0)[0].start()
+    fetch_group(0)[1].start()
     for group in range(1, groups):
-        fetch_folded(group).start()
+        for copy in fetch_group(group):
+            copy.start()
 
     place = lax.broadcasted_iota(jnp.int32, (count, HEAD_DIM), 0)
     kept = place % SPAN == 0
@@ -219,7 +235,7 @@
     def project(group):
         for head in range(group * GROUP, (group + 1) * GROUP):
             columns = head_columns(head)
-            sums = contract(mixed[group % 2, head % GROUP], value_ref[:, columns], ((1,), (0,)))
+            sums = contract(mixed[group % 2, head % GROUP], value[:, columns], ((1,), (0,)))
             sums = jnp.where(kept, sums, 0.0)
             out[:, columns] = pltpu.roll(sums, count - 1, 0).astype(jnp.bfloat16)
         put(group).start()
@@ -227,10 +243,12 @@
     ready(order[0])
     for step in range(len(units) + 2):
         if step == 0:
-            fetch_folded(0).wait()
+            fetch_group(0)[0].wait()
         if step == len(order):
+            fetch_group(0)[1].wait()
             for group in range(1, groups):
-                fetch_folded(group).wait()
+                for copy in fetch_group(group):
+                    copy.wait()
         if step + 1 < len(order):
             ready(order[step + 1])
         if step < len(units):
@@ -246,7 +264,7 @@
 
 
 def attend(size, plan, doc_starts, folded, single, w_value, stores):
-    requests = 2 * plan[3].shape[0] + 2
+    requests = plan[-1].size + 2
     length, width = stores[0].shape[1:]
     count = folded.shape[1]
     groups = HEADS // GROUP
@@ -254,28 +272,28 @@
     return pl.pallas_call(
         functools.partial(attend_kernel, size),
         out_shape=jax.ShapeDtypeStruct((count, model_width), jnp.bfloat16),
-        in_specs=[SMEM_SPEC] * 6 + [HBM_SPEC] + [VMEM_SPEC] * 2 + [ANY_SPEC] * len(stores),
+        in_specs=[SMEM_SPEC] * 7 + [HBM_SPEC, VMEM_SPEC, HBM_SPEC] + [ANY_SPEC] * len(stores),
         out_specs=HBM_SPEC,
         scratch_shapes=[
             pltpu.VMEM((requests, length, width), jnp.bfloat16),
             pltpu.VMEM((requests, length, width), jnp.bfloat16),
             pltpu.VMEM(folded.shape, jnp.bfloat16),
+            pltpu.VMEM(w_value.shape, jnp.bfloat16),
             pltpu.VMEM((5, GROUP * SPAN, 2 * length), jnp.float32),
             pltpu.VMEM((5, GROUP * SPAN, 2 * length), jnp.bfloat16),
             pltpu.VMEM((2, GROUP, count, width), jnp.bfloat16),
             pltpu.VMEM((count, model_width), jnp.bfloat16),
             pltpu.SemaphoreType.DMA((requests,)),
-            pltpu.SemaphoreType.DMA((groups,)),
-            pltpu.SemaphoreType.DMA((groups,)),
+            pltpu.SemaphoreType.DMA((groups, 3)),
         ],
-        compiler_params=pltpu.CompilerParams(vmem_limit_bytes=24 * MIB),
+        compiler_params=pltpu.CompilerParams(vmem_limit_bytes=28 * MIB),
         cost_estimate=pl.CostEstimate(
             flops=2 * HEADS * count * width * (4 * length + HEAD_DIM),
             bytes_accessed=16 * MIB,
             transcendentals=HEADS * count * 2 * length,
         ),
         name="attend_windows",
-    )(*plan, doc_starts, in_hbm(folded), single, w_value, *stores)
+    )(*plan, doc_starts, in_hbm(folded), single, in_hbm(w_value), *stores)
 
 
 def chip_ring(mesh):
@@ -305,8 +323,11 @@
     onwards = functools.partial(lax.ppermute, axis_name="seq", perm=ways)
     swapped = functools.partial(lax.ppermute, axis_name="seq", perm=[(i, i ^ 1) for i in range(devices)])
 
+    wanted = [retrieval_owner.T, retrieval_slot.T]
+    before = [lax.ppermute(rows, "seq", [(i, i + 1) for i in range(devices - 1)]) for rows in wanted]
+    neighbours, *before = lax.optimization_barrier((neighbours, *before))
     chains = [neighbours, swapped(neighbours)]
-    stores = list(chains)
+    stores = [neighbours, in_hbm(chains[1])]
     folded, single = fold(*after([queries], [chains[1]]), w_key)
 
     beside = {(1, 0): [folded, single]}
@@ -315,14 +336,10 @@
             others = beside.get((step, chain), []) + (stores[2 * chain + 4 * step - 5 :][:1] if step > 1 else [])
             sent = after([chains[chain]], others) if others else [chains[chain]]
             chains[chain] = onwards(sent[0])
-            stores += [chains[chain], swapped(chains[chain])]
-            if (step, chain) == (0, 1):
-                owner, slot = after([retrieval_owner, retrieval_slot], [chains[1]])
-                asked = jnp.stack([owner[-1], slot[-1]])
-                before = lax.ppermute(asked, "seq", [(i, i + 1) for i in range(devices - 1)])
-                beside[reach - 1, 1] = [before]
+            other = swapped(chains[chain])
+            stores += [chains[chain], in_hbm(other) if step + 1 < reach else other]
     places = jnp.asarray([ring.index(chip) for chip in range(size)], jnp.int32)
-    plan = [lax.axis_index("seq").reshape(1), places, before, owner, slot]
+    plan = [lax.axis_index("seq").reshape(1), places, *before, *wanted]
     if size % 2 == 0:
         sent = after([chains[0]], stores[-7:-4:2]) if reach > 1 else [chains[0]]
         last = onwards(sent[0])

time: 62.4 us -> 64.7 us (1.037)
  starting transfers between devices: 20.2 us -> 24.3 us
  waiting for transfers between devices: 20.2 us -> 18.6 us
  local copies, waits for them, and re-layouts: 4.04 us -> 2.62 us
  Pallas kernels: 17.4 us -> 18.8 us
    ppermute x6 -> x7, starting transfers between devices: 2.49 us -> 7.9 us  [the longest x2 7.04 us: body(): lax.ppermute(rows, 'seq', [(i, i + 1) for i in range(devices - 1)])]
    ppermute x6, waiting for transfers between devices: 12.8 us -> 11.1 us  [body(): chains[chain] = onwards(sent[0])]
    ppermute x6, starting transfers between devices: 15 us -> 13.4 us  [body(): chains[chain] = onwards(sent[0])]
    pallas_call x1, Pallas kernels: 12.4 us -> 13.7 us  [attend(): pl.pallas_call(functools.partial(attend_kernel, size), out_shape=jax.Shap...]
    unnamed x16 -> x22, local copies, waits for them, and re-layouts: 3.84 us -> 2.62 us
  transfers between devices with their start and end apart: 16 -> 17, of which waited for: 8 -> 9; matrix products, arithmetic and copies ran while one was open for 0% -> 0% of each run, Pallas kernels for 8% -> 8%
where the time goes in v12:
time: 64.7 us; the launch traced here: 64.6 us
  starting transfers between devices  24.3 us (38%)
  Pallas kernels  18.8 us (29%)
  waiting for transfers between devices  18.6 us (29%)
  local copies, waits for them, and re-layouts  2.62 us (4%)
    pallas_call x1, Pallas kernels, attend(): pl.pallas_call(functools.partial(attend_kernel, size), out_shape=jax.Shap...  13.7 us
    ppermute x6, starting transfers between devices, body(): chains[chain] = onwards(sent[0])  13.4 us
    ppermute x6, waiting for transfers between devices, body(): chains[chain] = onwards(sent[0])  11.1 us
    ppermute x2, starting transfers between devices, body(): lax.ppermute(rows, 'seq', [(i, i + 1) for i in range(devices - 1)])  7.04 us
    pallas_call x1, Pallas kernels, fold(): pl.pallas_call(fold_kernel, out_shape=(pltpu.HBM(shape, jnp.bfloat16), ja...  5.06 us
    ppermute x1, waiting for transfers between devices, body(): last = onwards(sent[0])  4.14 us
    unnamed x22, local copies, waits for them, and re-layouts  2.62 us
    ppermute x1, starting transfers between devices, body(): last = onwards(sent[0])  2.15 us
  transfers between devices with their start and end apart: 17, of which 9 were waited for; matrix products, arithmetic and copies ran while one was open for 0% of the time, Pallas kernels for 8%

profile of v12, /device:TPU:0, one launch (start us, length us, event | category | flops | bytes accessed | tf_op | source)
XLA Modules:
  0.0 64.6 jit_solution(3908334001295853795)
XLA Ops:
  0.0 2.5 %collective-permute-start = (s32[2,4]{1,0:T(2,128)}, s32[2,4]{1,0:T(2,128)S(1)}, u32[]{:S(2)}, u32[]{:S(2)}) collective-permute-start(s32[2,4]{1,0:T(2,128)} %bitcast.3), channel_id=1, source_target_pairs={{0,1},{1,2},{2,3},{3,4},{4,5},{5,6},{6,7},{7,8},{8,9},{9,10},{10,1... | collective-permute-start | bytes 104 | tf_op jit(solution)/shard_map/ppermute | solution.py:327
  2.5 4.5 %collective-permute-start.1 = (s32[2,4]{1,0:T(2,128)}, s32[2,4]{1,0:T(2,128)S(1)}, u32[]{:S(2)}, u32[]{:S(2)}) collective-permute-start(s32[2,4]{1,0:T(2,128)} %bitcast.5), channel_id=1, source_target_pairs={{0,1},{1,2},{2,3},{3,4},{4,5},{5,6},{6,7},{7,8},{8,9},{9,10},{10,1... | collective-permute-start | bytes 104 | tf_op jit(solution)/shard_map/ppermute | solution.py:327
  7.1 0.0 collective-permute-done.refs_2_
  7.1 1.0 %collective-permute-done.1.refs_3_ = s32[2,4]{1,0:T(2,128)S(1)} collective-permute-done((s32[2,4]{1,0:T(2,128)}, s32[2,4]{1,0:T(2,128)S(1)}, u32[]{:S(2)}, u32[]{:S(2)}) %collective-permute-start.1) | collective-permute-done | bytes 64 | tf_op jit(solution)/shard_map/ppermute | solution.py:327
  8.1 0.3 collective-permute-start.2
  8.4 2.7 %collective-permute-start.3 = (bf16[2,128,896]{2,1,0:T(8,128)(2,1)}, bf16[2,128,896]{2,1,0:T(8,128)(2,1)S(1)}, u32[]{:S(2)}, u32[]{:S(2)}) collective-permute-start(bf16[2,128,896]{2,1,0:T(8,128)(2,1)} %refs_10_), channel_id=1, source_target_pairs={{0,4},{1,3},{4,8},{5,1},{8,12},{9,5},{12,14},{13,9},{14,10},{15,13... | collective-permute-start | bytes 1376264 | tf_op jit(solution)/shard_map/ppermute | solution.py:338
  11.1 0.0 collective-permute-done.2.refs_11_
  11.1 2.0 %collective-permute-start.5 = (bf16[2,128,896]{2,1,0:T(8,128)(2,1)S(1)}, bf16[2,128,896]{2,1,0:T(8,128)(2,1)S(1)}, u32[]{:S(2)}, u32[]{:S(2)}) collective-permute-start(bf16[2,128,896]{2,1,0:T(8,128)(2,1)S(1)} %collective-permute-done.2.refs_11_), channel_id=1, source_target_pairs={{0,4},{1,3},{4,8},{5,1},{8,12},{9,5},{12,14},{13,9},{14,10},{15,13... | collective-permute-start | bytes 1376264 | tf_op jit(solution)/shard_map/ppermute | solution.py:338
  13.1 5.1 %fold_queries.1 = (bf16[16,256,896]{2,1,0:T(8,128)(2,1)}, f32[16,896]{1,0:T(8,128)S(1)}) custom-call(bf16[256,2048]{1,0:T(8,128)(2,1)} %query_hbm, bf16[896,2048]{1,0:T(8,128)(2,1)} %key_hbm.1), custom_call_target="tpu_custom_call" | custom-call | flops 939524096 | bytes 12582912 | tf_op jit(solution)/shard_map/fold_queries/pallas_call | solution.py:80
  18.2 0.0 collective-permute-done.3.refs_12_
  18.2 0.1 collective-permute-start.4
  18.3 1.6 %collective-permute-start.7 = (bf16[2,128,896]{2,1,0:T(8,128)(2,1)S(1)}, bf16[2,128,896]{2,1,0:T(8,128)(2,1)S(1)}, u32[]{:S(2)}, u32[]{:S(2)}) collective-permute-start(bf16[2,128,896]{2,1,0:T(8,128)(2,1)S(1)} %collective-permute-done.3.refs_12_), channel_id=1, source_target_pairs={{0,4},{1,3},{4,8},{5,1},{8,12},{9,5},{12,14},{13,9},{14,10},{15,13... | collective-permute-start | bytes 1376264 | tf_op jit(solution)/shard_map/ppermute | solution.py:338
  19.9 0.0 copy-done.7
  19.9 2.3 %collective-permute-done.5.refs_14_ = bf16[2,128,896]{2,1,0:T(8,128)(2,1)S(1)} collective-permute-done((bf16[2,128,896]{2,1,0:T(8,128)(2,1)S(1)}, bf16[2,128,896]{2,1,0:T(8,128)(2,1)S(1)}, u32[]{:S(2)}, u32[]{:S(2)}) %collective-permute-start.5) | collective-permute-done | bytes 458784 | tf_op jit(solution)/shard_map/ppermute | solution.py:338
  22.2 2.5 %collective-permute-start.9 = (bf16[2,128,896]{2,1,0:T(8,128)(2,1)S(1)}, bf16[2,128,896]{2,1,0:T(8,128)(2,1)S(1)}, u32[]{:S(2)}, u32[]{:S(2)}) collective-permute-start(bf16[2,128,896]{2,1,0:T(8,128)(2,1)S(1)} %collective-permute-done.5.refs_14_), channel_id=1, source_target_pairs={{0,4},{1,3},{4,8},{5,1},{8,12},{9,5},{12,14},{13,9},{14,10},{15,13... | collective-permute-start | bytes 1376264 | tf_op jit(solution)/shard_map/ppermute | solution.py:338
  24.7 0.0 collective-permute-start.6
  24.7 0.0 collective-permute-done.4.refs_13_
  24.7 0.8 %copy-done.8 = bf16[2,128,896]{2,1,0:T(8,128)(2,1)} copy-done((bf16[2,128,896]{2,1,0:T(8,128)(2,1)}, bf16[2,128,896]{2,1,0:T(8,128)(2,1)S(1)}, u32[]{:S(2)}) %copy-start.8) | copy-done | bytes 458776
  25.5 1.6 %collective-permute-done.7.refs_16_ = bf16[2,128,896]{2,1,0:T(8,128)(2,1)S(1)} collective-permute-done((bf16[2,128,896]{2,1,0:T(8,128)(2,1)S(1)}, bf16[2,128,896]{2,1,0:T(8,128)(2,1)S(1)}, u32[]{:S(2)}, u32[]{:S(2)}) %collective-permute-start.7) | collective-permute-done | bytes 458784 | tf_op jit(solution)/shard_map/ppermute | solution.py:338
  27.2 2.5 %collective-permute-start.11 = (bf16[2,128,896]{2,1,0:T(8,128)(2,1)S(1)}, bf16[2,128,896]{2,1,0:T(8,128)(2,1)S(1)}, u32[]{:S(2)}, u32[]{:S(2)}) collective-permute-start(bf16[2,128,896]{2,1,0:T(8,128)(2,1)S(1)} %collective-permute-done.7.refs_16_), channel_id=1, source_target_pairs={{0,4},{1,3},{4,8},{5,1},{8,12},{9,5},{12,14},{13,9},{14,10},{15,13... | collective-permute-start | bytes 1376264 | tf_op jit(solution)/shard_map/ppermute | solution.py:338
  29.6 0.0 collective-permute-start.8
  29.6 2.4 %collective-permute-done.9.refs_18_ = bf16[2,128,896]{2,1,0:T(8,128)(2,1)S(1)} collective-permute-done((bf16[2,128,896]{2,1,0:T(8,128)(2,1)S(1)}, bf16[2,128,896]{2,1,0:T(8,128)(2,1)S(1)}, u32[]{:S(2)}, u32[]{:S(2)}) %collective-permute-start.9) | collective-permute-done | bytes 458784 | tf_op jit(solution)/shard_map/ppermute | solution.py:338
  32.1 0.4 collective-permute-start.10
  32.5 0.0 collective-permute-done.6.refs_15_
  32.5 2.1 %collective-permute-start.13 = (bf16[2,128,896]{2,1,0:T(8,128)(2,1)S(1)}, bf16[2,128,896]{2,1,0:T(8,128)(2,1)S(1)}, u32[]{:S(2)}, u32[]{:S(2)}) collective-permute-start(bf16[2,128,896]{2,1,0:T(8,128)(2,1)S(1)} %collective-permute-done.9.refs_18_), channel_id=1, source_target_pairs={{0,4},{1,3},{4,8},{5,1},{8,12},{9,5},{12,14},{13,9},{14,10},{15,13... | collective-permute-start | bytes 1376264 | tf_op jit(solution)/shard_map/ppermute | solution.py:338
  34.6 2.4 %collective-permute-done.11.refs_20_ = bf16[2,128,896]{2,1,0:T(8,128)(2,1)S(1)} collective-permute-done((bf16[2,128,896]{2,1,0:T(8,128)(2,1)S(1)}, bf16[2,128,896]{2,1,0:T(8,128)(2,1)S(1)}, u32[]{:S(2)}, u32[]{:S(2)}) %collective-permute-start.11) | collective-permute-done | bytes 458784 | tf_op jit(solution)/shard_map/ppermute | solution.py:338
  37.0 0.4 collective-permute-start.12
  37.4 0.0 collective-permute-done.8.refs_17_
  37.4 0.0 collective-permute-done.10.refs_19_
  37.4 0.0 copy-start.10
  37.4 2.2 %collective-permute-start.14 = (bf16[2,128,896]{2,1,0:T(8,128)(2,1)S(1)}, bf16[2,128,896]{2,1,0:T(8,128)(2,1)}, u32[]{:S(2)}, u32[]{:S(2)}) collective-permute-start(bf16[2,128,896]{2,1,0:T(8,128)(2,1)S(1)} %collective-permute-done.11.refs_20_), channel_id=1, source_target_pairs={{0,4},{1,3},{4,8},{5,1},{8,12},{9,5},{12,14},{13,9},{14,10},{15,13... | collective-permute-start | bytes 1376264 | tf_op jit(solution)/shard_map/ppermute | solution.py:345
  39.5 2.3 %collective-permute-done.13.refs_22_ = bf16[2,128,896]{2,1,0:T(8,128)(2,1)S(1)} collective-permute-done((bf16[2,128,896]{2,1,0:T(8,128)(2,1)S(1)}, bf16[2,128,896]{2,1,0:T(8,128)(2,1)S(1)}, u32[]{:S(2)}, u32[]{:S(2)}) %collective-permute-start.13) | collective-permute-done | bytes 458784 | tf_op jit(solution)/shard_map/ppermute | solution.py:338
  41.9 0.0 collective-permute-done.12.refs_21_
  41.9 0.8 %copy-done.1 = bf16[2,128,896]{2,1,0:T(8,128)(2,1)} copy-done((bf16[2,128,896]{2,1,0:T(8,128)(2,1)}, bf16[2,128,896]{2,1,0:T(8,128)(2,1)S(1)}, u32[]{:S(2)}) %copy-start.1) | copy-done | bytes 458776
  42.7 4.1 %collective-permute-done.14.refs_24_ = bf16[2,128,896]{2,1,0:T(8,128)(2,1)} collective-permute-done((bf16[2,128,896]{2,1,0:T(8,128)(2,1)S(1)}, bf16[2,128,896]{2,1,0:T(8,128)(2,1)}, u32[]{:S(2)}, u32[]{:S(2)}) %collective-permute-start.14) | collective-permute-done | bytes 458784 | tf_op jit(solution)/shard_map/ppermute | solution.py:345
  46.8 0.0 copy-done.9
  46.8 0.2 collective-permute-start.15
  47.0 0.0 copy-done.10
  47.0 0.3 collective-permute-start.16
  47.3 1.4 %collective-permute-done.15.refs_23_ = bf16[2,128,896]{2,1,0:T(8,128)(2,1)} collective-permute-done((bf16[2,128,896]{2,1,0:T(8,128)(2,1)S(1)}, bf16[2,128,896]{2,1,0:T(8,128)(2,1)}, u32[]{:S(2)}, u32[]{:S(2)}) %collective-permute-start.15) | collective-permute-done | bytes 458784 | tf_op jit(solution)/shard_map/ppermute | solution.py:347
  48.8 0.9 %collective-permute-done.16.refs_25_ = bf16[2,128,896]{2,1,0:T(8,128)(2,1)} collective-permute-done((bf16[2,128,896]{2,1,0:T(8,128)(2,1)}, bf16[2,128,896]{2,1,0:T(8,128)(2,1)}, u32[]{:S(2)}, u32[]{:S(2)}) %collective-permute-start.16) | collective-permute-done | bytes 458784 | tf_op jit(solution)/shard_map/ppermute | solution.py:348
  49.6 0.0 copy-done.6
  49.6 0.0 copy-done.4
  49.6 0.0 copy-done
  49.7 0.0 copy-done.5
  49.7 0.0 copy-start.2
  49.7 1.0 %copy-done.2 = bf16[2,128,896]{2,1,0:T(8,128)(2,1)S(1)} copy-done((bf16[2,128,896]{2,1,0:T(8,128)(2,1)S(1)}, bf16[2,128,896]{2,1,0:T(8,128)(2,1)}, u32[]{:S(2)}) %copy-start.2) | copy-done | bytes 458776
  50.7 13.7 %attend_windows.1 = bf16[256,2048]{1,0:T(8,128)(2,1)} custom-call(s32[1]{0:T(128)} %bitcast.refs_0_, s32[8]{0:T(128)S(1)} %copy-done.6, s32[2,4]{1,0:T(2,128)S(1)} %collective-permute-done.refs_2_, s32[2,4]{1,0:T(2,128)S(1)} %collective-permute-done.1.refs_3_, s32[2,4]{1,0:T(2,128)S(1)} %bitcast.4, s32[2,4]{1,0:T(2,128)S(1)} %bitcast.6, s32[4]{0:T(128)S(1)} %copy-done.5, ...), custom_call_target="tpu_custom_call" | custom-call | flops 4697620480 | bytes 16777216 | tf_op jit(solution)/shard_map/attend_windows/pallas_call | solution.py:272
  (10 shorter events, 0.0 us)
Async XLA Ops:
  0.0 49.6 %copy-start.6 = (s32[8]{0:T(128)S(1)}, s32[8]{0:T(128)}, u32[]{:S(2)}) copy-start(s32[8]{0:T(128)} %constant.6.clone.refs_1_) | copy-start | bytes 100
  0.0 49.6 %copy-start.3 = (s32[4,2]{0,1:T(2,128)S(1)}, s32[4,2]{0,1:T(2,128)}, u32[]{:S(2)}) copy-start(s32[4,2]{0,1:T(2,128)} %param.12) | copy-start | bytes 100
  0.0 49.6 %copy-start.4 = (s32[4,2]{0,1:T(2,128)S(1)}, s32[4,2]{0,1:T(2,128)}, u32[]{:S(2)}) copy-start(s32[4,2]{0,1:T(2,128)} %param.13) | copy-start | bytes 100
  0.0 49.6 %copy-start = (bf16[2,128,896]{2,1,0:T(8,128)(2,1)S(1)}, bf16[2,128,896]{2,1,0:T(8,128)(2,1)}, u32[]{:S(2)}) copy-start(bf16[2,128,896]{2,1,0:T(8,128)(2,1)} %refs_10_) | copy-start | bytes 1376260
  0.0 49.6 %copy-start.5 = (s32[4]{0:T(128)S(1)}, s32[4]{0:T(128)}, u32[]{:S(2)}) copy-start(s32[4]{0:T(128)} %refs_6_.1) | copy-start | bytes 52
  0.0 7.1 %collective-permute-start = (s32[2,4]{1,0:T(2,128)}, s32[2,4]{1,0:T(2,128)S(1)}, u32[]{:S(2)}, u32[]{:S(2)}) collective-permute-start(s32[2,4]{1,0:T(2,128)} %bitcast.3), channel_id=1, source_target_pairs={{0,1},{1,2},{2,3},{3,4},{4,5},{5,6},{6,7},{7,8},{8,9},{9,10},{10,1... | collective-permute-start | bytes 104 | tf_op jit(solution)/shard_map/ppermute | solution.py:327
  2.5 5.6 %collective-permute-start.1 = (s32[2,4]{1,0:T(2,128)}, s32[2,4]{1,0:T(2,128)S(1)}, u32[]{:S(2)}, u32[]{:S(2)}) collective-permute-start(s32[2,4]{1,0:T(2,128)} %bitcast.5), channel_id=1, source_target_pairs={{0,1},{1,2},{2,3},{3,4},{4,5},{5,6},{6,7},{7,8},{8,9},{9,10},{10,1... | collective-permute-start | bytes 104 | tf_op jit(solution)/shard_map/ppermute | solution.py:327
  8.1 3.0 %collective-permute-start.2 = (bf16[2,128,896]{2,1,0:T(8,128)(2,1)}, bf16[2,128,896]{2,1,0:T(8,128)(2,1)S(1)}, u32[]{:S(2)}, u32[]{:S(2)}) collective-permute-start(bf16[2,128,896]{2,1,0:T(8,128)(2,1)} %refs_10_), channel_id=1, source_target_pairs={{0,1},{1,0},{2,3},{3,2},{4,5},{5,4},{6,7},{7,6},{8,9},{9,8},{10,11... | collective-permute-start | bytes 1376264 | tf_op jit(solution)/shard_map/ppermute | solution.py:329
  8.4 9.8 %collective-permute-start.3 = (bf16[2,128,896]{2,1,0:T(8,128)(2,1)}, bf16[2,128,896]{2,1,0:T(8,128)(2,1)S(1)}, u32[]{:S(2)}, u32[]{:S(2)}) collective-permute-start(bf16[2,128,896]{2,1,0:T(8,128)(2,1)} %refs_10_), channel_id=1, source_target_pairs={{0,4},{1,3},{4,8},{5,1},{8,12},{9,5},{12,14},{13,9},{14,10},{15,13... | collective-permute-start | bytes 1376264 | tf_op jit(solution)/shard_map/ppermute | solution.py:338
  11.1 8.8 %copy-start.7 = (bf16[2,128,896]{2,1,0:T(8,128)(2,1)}, bf16[2,128,896]{2,1,0:T(8,128)(2,1)S(1)}, u32[]{:S(2)}) copy-start(bf16[2,128,896]{2,1,0:T(8,128)(2,1)S(1)} %collective-permute-done.2.refs_11_) | copy-start | bytes 1376260
  11.1 11.1 %collective-permute-start.5 = (bf16[2,128,896]{2,1,0:T(8,128)(2,1)S(1)}, bf16[2,128,896]{2,1,0:T(8,128)(2,1)S(1)}, u32[]{:S(2)}, u32[]{:S(2)}) collective-permute-start(bf16[2,128,896]{2,1,0:T(8,128)(2,1)S(1)} %collective-permute-done.2.refs_11_), channel_id=1, source_target_pairs={{0,4},{1,3},{4,8},{5,1},{8,12},{9,5},{12,14},{13,9},{14,10},{15,13... | collective-permute-start | bytes 1376264 | tf_op jit(solution)/shard_map/ppermute | solution.py:338
  18.2 6.5 %collective-permute-start.4 = (bf16[2,128,896]{2,1,0:T(8,128)(2,1)S(1)}, bf16[2,128,896]{2,1,0:T(8,128)(2,1)S(1)}, u32[]{:S(2)}, u32[]{:S(2)}) collective-permute-start(bf16[2,128,896]{2,1,0:T(8,128)(2,1)S(1)} %collective-permute-done.3.refs_12_), channel_id=1, source_target_pairs={{0,1},{1,0},{2,3},{3,2},{4,5},{5,4},{6,7},{7,6},{8,9},{9,8},{10,11... | collective-permute-start | bytes 1376264 | tf_op jit(solution)/shard_map/ppermute | solution.py:339
  18.3 8.9 %collective-permute-start.7 = (bf16[2,128,896]{2,1,0:T(8,128)(2,1)S(1)}, bf16[2,128,896]{2,1,0:T(8,128)(2,1)S(1)}, u32[]{:S(2)}, u32[]{:S(2)}) collective-permute-start(bf16[2,128,896]{2,1,0:T(8,128)(2,1)S(1)} %collective-permute-done.3.refs_12_), channel_id=1, source_target_pairs={{0,4},{1,3},{4,8},{5,1},{8,12},{9,5},{12,14},{13,9},{14,10},{15,13... | collective-permute-start | bytes 1376264 | tf_op jit(solution)/shard_map/ppermute | solution.py:338
  22.2 9.8 %collective-permute-start.9 = (bf16[2,128,896]{2,1,0:T(8,128)(2,1)S(1)}, bf16[2,128,896]{2,1,0:T(8,128)(2,1)S(1)}, u32[]{:S(2)}, u32[]{:S(2)}) collective-permute-start(bf16[2,128,896]{2,1,0:T(8,128)(2,1)S(1)} %collective-permute-done.5.refs_14_), channel_id=1, source_target_pairs={{0,4},{1,3},{4,8},{5,1},{8,12},{9,5},{12,14},{13,9},{14,10},{15,13... | collective-permute-start | bytes 1376264 | tf_op jit(solution)/shard_map/ppermute | solution.py:338
  24.7 7.7 %collective-permute-start.6 = (bf16[2,128,896]{2,1,0:T(8,128)(2,1)S(1)}, bf16[2,128,896]{2,1,0:T(8,128)(2,1)}, u32[]{:S(2)}, u32[]{:S(2)}) collective-permute-start(bf16[2,128,896]{2,1,0:T(8,128)(2,1)S(1)} %collective-permute-done.5.refs_14_), channel_id=1, source_target_pairs={{0,1},{1,0},{2,3},{3,2},{4,5},{5,4},{6,7},{7,6},{8,9},{9,8},{10,11... | collective-permute-start | bytes 1376264 | tf_op jit(solution)/shard_map/ppermute | solution.py:339
  24.7 0.8 %copy-start.8 = (bf16[2,128,896]{2,1,0:T(8,128)(2,1)}, bf16[2,128,896]{2,1,0:T(8,128)(2,1)S(1)}, u32[]{:S(2)}) copy-start(bf16[2,128,896]{2,1,0:T(8,128)(2,1)S(1)} %collective-permute-done.4.refs_13_) | copy-start | bytes 1376260
  27.2 9.8 %collective-permute-start.11 = (bf16[2,128,896]{2,1,0:T(8,128)(2,1)S(1)}, bf16[2,128,896]{2,1,0:T(8,128)(2,1)S(1)}, u32[]{:S(2)}, u32[]{:S(2)}) collective-permute-start(bf16[2,128,896]{2,1,0:T(8,128)(2,1)S(1)} %collective-permute-done.7.refs_16_), channel_id=1, source_target_pairs={{0,4},{1,3},{4,8},{5,1},{8,12},{9,5},{12,14},{13,9},{14,10},{15,13... | collective-permute-start | bytes 1376264 | tf_op jit(solution)/shard_map/ppermute | solution.py:338
  29.6 7.7 %collective-permute-start.8 = (bf16[2,128,896]{2,1,0:T(8,128)(2,1)S(1)}, bf16[2,128,896]{2,1,0:T(8,128)(2,1)S(1)}, u32[]{:S(2)}, u32[]{:S(2)}) collective-permute-start(bf16[2,128,896]{2,1,0:T(8,128)(2,1)S(1)} %collective-permute-done.7.refs_16_), channel_id=1, source_target_pairs={{0,1},{1,0},{2,3},{3,2},{4,5},{5,4},{6,7},{7,6},{8,9},{9,8},{10,11... | collective-permute-start | bytes 1376264 | tf_op jit(solution)/shard_map/ppermute | solution.py:339
  32.1 5.3 %collective-permute-start.10 = (bf16[2,128,896]{2,1,0:T(8,128)(2,1)S(1)}, bf16[2,128,896]{2,1,0:T(8,128)(2,1)S(1)}, u32[]{:S(2)}, u32[]{:S(2)}) collective-permute-start(bf16[2,128,896]{2,1,0:T(8,128)(2,1)S(1)} %collective-permute-done.9.refs_18_), channel_id=1, source_target_pairs={{0,1},{1,0},{2,3},{3,2},{4,5},{5,4},{6,7},{7,6},{8,9},{9,8},{10,11... | collective-permute-start | bytes 1376264 | tf_op jit(solution)/shard_map/ppermute | solution.py:339
  32.5 9.4 %collective-permute-start.13 = (bf16[2,128,896]{2,1,0:T(8,128)(2,1)S(1)}, bf16[2,128,896]{2,1,0:T(8,128)(2,1)S(1)}, u32[]{:S(2)}, u32[]{:S(2)}) collective-permute-start(bf16[2,128,896]{2,1,0:T(8,128)(2,1)S(1)} %collective-permute-done.9.refs_18_), channel_id=1, source_target_pairs={{0,4},{1,3},{4,8},{5,1},{8,12},{9,5},{12,14},{13,9},{14,10},{15,13... | collective-permute-start | bytes 1376264 | tf_op jit(solution)/shard_map/ppermute | solution.py:338
  37.0 4.9 %collective-permute-start.12 = (bf16[2,128,896]{2,1,0:T(8,128)(2,1)S(1)}, bf16[2,128,896]{2,1,0:T(8,128)(2,1)S(1)}, u32[]{:S(2)}, u32[]{:S(2)}) collective-permute-start(bf16[2,128,896]{2,1,0:T(8,128)(2,1)S(1)} %collective-permute-done.11.refs_20_), channel_id=1, source_target_pairs={{0,1},{1,0},{2,3},{3,2},{4,5},{5,4},{6,7},{7,6},{8,9},{9,8},{10,11... | collective-permute-start | bytes 1376264 | tf_op jit(solution)/shard_map/ppermute | solution.py:339
  37.4 9.4 %copy-start.9 = (bf16[2,128,896]{2,1,0:T(8,128)(2,1)}, bf16[2,128,896]{2,1,0:T(8,128)(2,1)S(1)}, u32[]{:S(2)}) copy-start(bf16[2,128,896]{2,1,0:T(8,128)(2,1)S(1)} %collective-permute-done.8.refs_17_) | copy-start | bytes 1376260
  37.4 9.6 %copy-start.10 = (bf16[2,128,896]{2,1,0:T(8,128)(2,1)}, bf16[2,128,896]{2,1,0:T(8,128)(2,1)S(1)}, u32[]{:S(2)}) copy-start(bf16[2,128,896]{2,1,0:T(8,128)(2,1)S(1)} %collective-permute-done.10.refs_19_) | copy-start | bytes 1376260
  37.4 9.4 %collective-permute-start.14 = (bf16[2,128,896]{2,1,0:T(8,128)(2,1)S(1)}, bf16[2,128,896]{2,1,0:T(8,128)(2,1)}, u32[]{:S(2)}, u32[]{:S(2)}) collective-permute-start(bf16[2,128,896]{2,1,0:T(8,128)(2,1)S(1)} %collective-permute-done.11.refs_20_), channel_id=1, source_target_pairs={{0,4},{1,3},{4,8},{5,1},{8,12},{9,5},{12,14},{13,9},{14,10},{15,13... | collective-permute-start | bytes 1376264 | tf_op jit(solution)/shard_map/ppermute | solution.py:345
  41.9 0.8 %copy-start.1 = (bf16[2,128,896]{2,1,0:T(8,128)(2,1)}, bf16[2,128,896]{2,1,0:T(8,128)(2,1)S(1)}, u32[]{:S(2)}) copy-start(bf16[2,128,896]{2,1,0:T(8,128)(2,1)S(1)} %collective-permute-done.12.refs_21_) | copy-start | bytes 1376260
  46.8 1.9 %collective-permute-start.15 = (bf16[2,128,896]{2,1,0:T(8,128)(2,1)S(1)}, bf16[2,128,896]{2,1,0:T(8,128)(2,1)}, u32[]{:S(2)}, u32[]{:S(2)}) collective-permute-start(bf16[2,128,896]{2,1,0:T(8,128)(2,1)S(1)} %collective-permute-done.13.refs_22_), channel_id=1, source_target_pairs={{0,1},{1,0},{2,3},{3,2},{4,5},{5,4},{6,7},{7,6},{8,9},{9,8},{10,11... | collective-permute-start | bytes 1376264 | tf_op jit(solution)/shard_map/ppermute | solution.py:347
  47.0 2.6 %collective-permute-start.16 = (bf16[2,128,896]{2,1,0:T(8,128)(2,1)}, bf16[2,128,896]{2,1,0:T(8,128)(2,1)}, u32[]{:S(2)}, u32[]{:S(2)}) collective-permute-start(bf16[2,128,896]{2,1,0:T(8,128)(2,1)} %collective-permute-done.14.refs_24_), channel_id=1, source_target_pairs={{0,1},{1,0},{2,3},{3,2},{4,5},{5,4},{6,7},{7,6},{8,9},{9,8},{10,11... | collective-permute-start | bytes 1376264 | tf_op jit(solution)/shard_map/ppermute | solution.py:348
  49.7 1.0 %copy-start.2 = (bf16[2,128,896]{2,1,0:T(8,128)(2,1)S(1)}, bf16[2,128,896]{2,1,0:T(8,128)(2,1)}, u32[]{:S(2)}) copy-start(bf16[2,128,896]{2,1,0:T(8,128)(2,1)} %copy-done.1) | copy-start | bytes 1376260

commit v13 on v12

--- a/solution.py
+++ b/solution.py
@@ -115,14 +115,11 @@
     pl.when(source >= first + half)(lambda: among(stores[half:], first + half, source, act))
 
 
-def locate(request, plan_refs, size):
-    here_ref, place_ref, owner_before_ref, slot_before_ref, owner_ref, slot_ref = plan_refs
+def locate(request, plan_refs, size, stored):
+    here_ref, place_ref, before_ref, wanted_ref = plan_refs
     window, part = divmod(request, 2)
-    if window == 0:
-        last = owner_before_ref.shape[1] - 1
-        owner, slot = owner_before_ref[part, last], slot_before_ref[part, last]
-    else:
-        owner, slot = owner_ref[part, window - 1], slot_ref[part, window - 1]
+    wanted = before_ref[part, before_ref.shape[1] - 1] if window == 0 else wanted_ref[part, window - 1]
+    owner, slot = wanted // stored, wanted % stored
     reach = (size - 1) // 2
     opposite = size - reach - 1
     here = here_ref[0]
@@ -142,7 +139,7 @@
 
 
 def attend_kernel(size, *refs):
-    plan_refs, (starts_ref, folded_hbm, single_ref, value_hbm, *rest) = refs[:6], refs[6:]
+    plan_refs, (starts_ref, folded_hbm, single_ref, value_hbm, *rest) = refs[:4], refs[4:]
     *stores, out_hbm, tokens, raw, folded, value, scores, weights, mixed, out, sems, group_sems = rest
     requests, length, width = raw.shape
     blocks = requests // 2 - 1
@@ -168,7 +165,7 @@
 
     for window in order:
         for request in (2 * window, 2 * window + 1):
-            source, block = locate(request, plan_refs, size)
+            source, block = locate(request, plan_refs, size, stores[0].shape[0])
             among(stores, 0, source, lambda store: fetch(request, store, block).start())
         if window == order[0]:
             fetch_group(0)[0].start()
@@ -272,7 +269,7 @@
     return pl.pallas_call(
         functools.partial(attend_kernel, size),
         out_shape=jax.ShapeDtypeStruct((count, model_width), jnp.bfloat16),
-        in_specs=[SMEM_SPEC] * 7 + [HBM_SPEC, VMEM_SPEC, HBM_SPEC] + [ANY_SPEC] * len(stores),
+        in_specs=[SMEM_SPEC] * 5 + [HBM_SPEC, VMEM_SPEC, HBM_SPEC] + [ANY_SPEC] * len(stores),
         out_specs=HBM_SPEC,
         scratch_shapes=[
             pltpu.VMEM((requests, length, width), jnp.bfloat16),
@@ -323,9 +320,8 @@
     onwards = functools.partial(lax.ppermute, axis_name="seq", perm=ways)
     swapped = functools.partial(lax.ppermute, axis_name="seq", perm=[(i, i ^ 1) for i in range(devices)])
 
-    wanted = [retrieval_owner.T, retrieval_slot.T]
-    before = [lax.ppermute(rows, "seq", [(i, i + 1) for i in range(devices - 1)]) for rows in wanted]
-    neighbours, *before = lax.optimization_barrier((neighbours, *before))
+    stored = neighbours.shape[0]
+    wanted = (retrieval_owner * stored + retrieval_slot).T
     chains = [neighbours, swapped(neighbours)]
     stores = [neighbours, in_hbm(chains[1])]
     folded, single = fold(*after([queries], [chains[1]]), w_key)
@@ -336,10 +332,13 @@
             others = beside.get((step, chain), []) + (stores[2 * chain + 4 * step - 5 :][:1] if step > 1 else [])
             sent = after([chains[chain]], others) if others else [chains[chain]]
             chains[chain] = onwards(sent[0])
-            other = swapped(chains[chain])
-            stores += [chains[chain], in_hbm(other) if step + 1 < reach else other]
+            stores += [chains[chain], in_hbm(swapped(chains[chain]))]
+            if (step, chain) == (0, 1):
+                asked = after([wanted], [chains[1]])[0]
+                before = lax.ppermute(asked, "seq", [(i, i + 1) for i in range(devices - 1)])
+                beside[2, 0] = [before]
     places = jnp.asarray([ring.index(chip) for chip in range(size)], jnp.int32)
-    plan = [lax.axis_index("seq").reshape(1), places, *before, *wanted]
+    plan = [lax.axis_index("seq").reshape(1), places, before, wanted]
     if size % 2 == 0:
         sent = after([chains[0]], stores[-7:-4:2]) if reach > 1 else [chains[0]]
         last = onwards(sent[0])

time: 64.7 us -> 59.5 us (0.920)
  local copies, waits for them, and re-layouts: 2.62 us -> 0.09 us
  waiting for transfers between devices: 18.6 us -> 17 us
  starting transfers between devices: 24.3 us -> 23.5 us
    ppermute x7 -> x6, starting transfers between devices: 7.9 us -> 2.63 us  [the longest x5 1.34 us: body(): stores += [chains[chain], in_hbm(swapped(chains[chain]))]]
    ppermute x6, starting transfers between devices: 13.4 us -> 17.3 us  [body(): chains[chain] = onwards(sent[0])]
    unnamed x22 -> x20, local copies, waits for them, and re-layouts: 2.62 us -> 0.09 us
    ppermute x6, waiting for transfers between devices: 11.1 us -> 9.8 us  [body(): chains[chain] = onwards(sent[0])]
    ppermute x7 -> x6, waiting for transfers between devices: 1.02 us -> 0.02 us  [the longest x5 0.01 us: body(): stores += [chains[chain], in_hbm(swapped(chains[chain]))]]
    ppermute x1, waiting for transfers between devices: 4.14 us -> 4.91 us  [body(): last = onwards(sent[0])]
  transfers between devices with their start and end apart: 17 -> 16, of which waited for: 9 -> 7; matrix products, arithmetic and copies ran while one was open for 0% -> 0% of each run, Pallas kernels for 8% -> 9%
where the time goes in v13:
time: 59.5 us; the launch traced here: 59 us
  starting transfers between devices  23.5 us (39%)
  Pallas kernels  18.2 us (31%)
  waiting for transfers between devices  17 us (29%)
    ppermute x6, starting transfers between devices, body(): chains[chain] = onwards(sent[0])  17.3 us
    pallas_call x1, Pallas kernels, attend(): pl.pallas_call(functools.partial(attend_kernel, size), out_shape=jax.Shap...  13.2 us
    ppermute x6, waiting for transfers between devices, body(): chains[chain] = onwards(sent[0])  9.8 us
    pallas_call x1, Pallas kernels, fold(): pl.pallas_call(fold_kernel, out_shape=(pltpu.HBM(shape, jnp.bfloat16), ja...  5.05 us
    ppermute x1, waiting for transfers between devices, body(): last = onwards(sent[0])  4.91 us
    ppermute x1, starting transfers between devices, body(): last = onwards(sent[0])  2.54 us
    ppermute x1, waiting for transfers between devices, body(): stores[-1] = swapped(after([chains[1]], [last, stores[-3]])[0])  1.43 us
    ppermute x5, starting transfers between devices, body(): stores += [chains[chain], in_hbm(swapped(chains[chain]))]  1.34 us
  transfers between devices with their start and end apart: 16, of which 7 were waited for; matrix products, arithmetic and copies ran while one was open for 0% of the time, Pallas kernels for 9%

profile of v13, /device:TPU:0, one launch (start us, length us, event | category | flops | bytes accessed | tf_op | source)
XLA Modules:
  0.0 59.0 jit_solution(12092309706683409077)
XLA Ops:
  0.0 0.0 copy-start
  0.0 0.0 copy-start.8
  0.0 0.0 copy-start.9
  0.0 0.5 collective-permute-start
  0.5 2.6 %collective-permute-start.3 = (bf16[2,128,896]{2,1,0:T(8,128)(2,1)}, bf16[2,128,896]{2,1,0:T(8,128)(2,1)S(1)}, u32[]{:S(2)}, u32[]{:S(2)}) collective-permute-start(bf16[2,128,896]{2,1,0:T(8,128)(2,1)} %refs_8_.1), channel_id=1, source_target_pairs={{0,4},{1,3},{4,8},{5,1},{8,12},{9,5},{12,14},{13,9},{14,10},{15,13... | collective-permute-start | bytes 1376264 | tf_op jit(solution)/shard_map/ppermute | solution.py:334
  3.2 0.0 collective-permute-done.refs_9_
  3.2 2.0 %collective-permute-start.1 = (bf16[2,128,896]{2,1,0:T(8,128)(2,1)S(1)}, bf16[2,128,896]{2,1,0:T(8,128)(2,1)S(1)}, u32[]{:S(2)}, u32[]{:S(2)}) collective-permute-start(bf16[2,128,896]{2,1,0:T(8,128)(2,1)S(1)} %collective-permute-done.refs_9_), channel_id=1, source_target_pairs={{0,4},{1,3},{4,8},{5,1},{8,12},{9,5},{12,14},{13,9},{14,10},{15,13... | collective-permute-start | bytes 1376264 | tf_op jit(solution)/shard_map/ppermute | solution.py:334
  5.1 5.1 %fold_queries.1 = (bf16[16,256,896]{2,1,0:T(8,128)(2,1)}, f32[16,896]{1,0:T(8,128)S(1)}) custom-call(bf16[256,2048]{1,0:T(8,128)(2,1)} %query_hbm, bf16[896,2048]{1,0:T(8,128)(2,1)} %key_hbm.1), custom_call_target="tpu_custom_call" | custom-call | flops 939524096 | bytes 12582912 | tf_op jit(solution)/shard_map/fold_queries/pallas_call | solution.py:80
  10.2 0.0 collective-permute-done.3.refs_10_
  10.2 0.1 collective-permute-start.4
  10.3 1.6 %collective-permute-start.6 = (bf16[2,128,896]{2,1,0:T(8,128)(2,1)S(1)}, bf16[2,128,896]{2,1,0:T(8,128)(2,1)S(1)}, u32[]{:S(2)}, u32[]{:S(2)}) collective-permute-start(bf16[2,128,896]{2,1,0:T(8,128)(2,1)S(1)} %collective-permute-done.3.refs_10_), channel_id=1, source_target_pairs={{0,4},{1,3},{4,8},{5,1},{8,12},{9,5},{12,14},{13,9},{14,10},{15,13... | collective-permute-start | bytes 1376264 | tf_op jit(solution)/shard_map/ppermute | solution.py:334
  11.9 0.0 copy-done.3
  11.9 2.8 %collective-permute-done.1.refs_12_ = bf16[2,128,896]{2,1,0:T(8,128)(2,1)S(1)} collective-permute-done((bf16[2,128,896]{2,1,0:T(8,128)(2,1)S(1)}, bf16[2,128,896]{2,1,0:T(8,128)(2,1)S(1)}, u32[]{:S(2)}, u32[]{:S(2)}) %collective-permute-start.1) | collective-permute-done | bytes 458784 | tf_op jit(solution)/shard_map/ppermute | solution.py:334
  14.7 2.1 %collective-permute-start.8 = (bf16[2,128,896]{2,1,0:T(8,128)(2,1)S(1)}, bf16[2,128,896]{2,1,0:T(8,128)(2,1)S(1)}, u32[]{:S(2)}, u32[]{:S(2)}) collective-permute-start(bf16[2,128,896]{2,1,0:T(8,128)(2,1)S(1)} %collective-permute-done.1.refs_12_), channel_id=1, source_target_pairs={{0,4},{1,3},{4,8},{5,1},{8,12},{9,5},{12,14},{13,9},{14,10},{15,13... | collective-permute-start | bytes 1376264 | tf_op jit(solution)/shard_map/ppermute | solution.py:334
  16.8 0.0 copy-done.8
  16.8 0.0 copy-done.9
  16.8 1.3 %collective-permute-start.2 = (s32[2,4]{1,0:T(2,128)S(1)}, s32[2,4]{1,0:T(2,128)S(1)}, u32[]{:S(2)}, u32[]{:S(2)}) collective-permute-start(s32[2,4]{1,0:T(2,128)S(1)} %add_bitcast_fusion.refs_3_), channel_id=1, source_target_pairs={{0,1},{1,2},{2,3},{3,4},{4,5},{5,6},{6,7},{7,8},{8,9},{9,10},{10,1... | collective-permute-start | bytes 104 | tf_op jit(solution)/shard_map/ppermute | solution.py:338
  18.1 0.8 %collective-permute-start.5 = (bf16[2,128,896]{2,1,0:T(8,128)(2,1)S(1)}, bf16[2,128,896]{2,1,0:T(8,128)(2,1)}, u32[]{:S(2)}, u32[]{:S(2)}) collective-permute-start(bf16[2,128,896]{2,1,0:T(8,128)(2,1)S(1)} %collective-permute-done.1.refs_12_), channel_id=1, source_target_pairs={{0,1},{1,0},{2,3},{3,2},{4,5},{5,4},{6,7},{7,6},{8,9},{9,8},{10,11... | collective-permute-start | bytes 1376264 | tf_op jit(solution)/shard_map/ppermute | solution.py:335
  18.9 0.0 collective-permute-done.4.refs_11_
  18.9 0.8 %collective-permute-done.6.refs_14_ = bf16[2,128,896]{2,1,0:T(8,128)(2,1)S(1)} collective-permute-done((bf16[2,128,896]{2,1,0:T(8,128)(2,1)S(1)}, bf16[2,128,896]{2,1,0:T(8,128)(2,1)S(1)}, u32[]{:S(2)}, u32[]{:S(2)}) %collective-permute-start.6) | collective-permute-done | bytes 458784 | tf_op jit(solution)/shard_map/ppermute | solution.py:334
  19.6 0.1 copy-done.4
  19.7 0.0 collective-permute-done.2.refs_2_
  19.7 7.4 %collective-permute-start.10 = (bf16[2,128,896]{2,1,0:T(8,128)(2,1)S(1)}, bf16[2,128,896]{2,1,0:T(8,128)(2,1)S(1)}, u32[]{:S(2)}, u32[]{:S(2)}) collective-permute-start(bf16[2,128,896]{2,1,0:T(8,128)(2,1)S(1)} %collective-permute-done.6.refs_14_), channel_id=1, source_target_pairs={{0,4},{1,3},{4,8},{5,1},{8,12},{9,5},{12,14},{13,9},{14,10},{15,13... | collective-permute-start | bytes 1376264 | tf_op jit(solution)/shard_map/ppermute | solution.py:334
  27.1 0.0 collective-permute-start.7
  27.1 0.0 collective-permute-done.8.refs_16_
  27.1 0.5 collective-permute-start.9
  27.6 0.0 collective-permute-done.5.refs_13_
  27.6 1.6 %collective-permute-start.12 = (bf16[2,128,896]{2,1,0:T(8,128)(2,1)S(1)}, bf16[2,128,896]{2,1,0:T(8,128)(2,1)S(1)}, u32[]{:S(2)}, u32[]{:S(2)}) collective-permute-start(bf16[2,128,896]{2,1,0:T(8,128)(2,1)S(1)} %collective-permute-done.8.refs_16_), channel_id=1, source_target_pairs={{0,4},{1,3},{4,8},{5,1},{8,12},{9,5},{12,14},{13,9},{14,10},{15,13... | collective-permute-start | bytes 1376264 | tf_op jit(solution)/shard_map/ppermute | solution.py:334
  29.2 3.9 %collective-permute-done.10.refs_18_ = bf16[2,128,896]{2,1,0:T(8,128)(2,1)S(1)} collective-permute-done((bf16[2,128,896]{2,1,0:T(8,128)(2,1)S(1)}, bf16[2,128,896]{2,1,0:T(8,128)(2,1)S(1)}, u32[]{:S(2)}, u32[]{:S(2)}) %collective-permute-start.10) | collective-permute-done | bytes 458784 | tf_op jit(solution)/shard_map/ppermute | solution.py:334
  33.1 0.0 collective-permute-start.11
  33.1 0.0 collective-permute-done.7.refs_15_
  33.1 0.0 collective-permute-done.9.refs_17_
  33.1 0.0 copy-start.6
  33.1 2.5 %collective-permute-start.13 = (bf16[2,128,896]{2,1,0:T(8,128)(2,1)S(1)}, bf16[2,128,896]{2,1,0:T(8,128)(2,1)}, u32[]{:S(2)}, u32[]{:S(2)}) collective-permute-start(bf16[2,128,896]{2,1,0:T(8,128)(2,1)S(1)} %collective-permute-done.10.refs_18_), channel_id=1, source_target_pairs={{0,4},{1,3},{4,8},{5,1},{8,12},{9,5},{12,14},{13,9},{14,10},{15,13... | collective-permute-start | bytes 1376264 | tf_op jit(solution)/shard_map/ppermute | solution.py:344
  35.6 2.3 %collective-permute-done.12.refs_20_ = bf16[2,128,896]{2,1,0:T(8,128)(2,1)S(1)} collective-permute-done((bf16[2,128,896]{2,1,0:T(8,128)(2,1)S(1)}, bf16[2,128,896]{2,1,0:T(8,128)(2,1)S(1)}, u32[]{:S(2)}, u32[]{:S(2)}) %collective-permute-start.12) | collective-permute-done | bytes 458784 | tf_op jit(solution)/shard_map/ppermute | solution.py:334
  38.0 0.0 collective-permute-done.11.refs_19_
  38.0 4.9 %collective-permute-done.13.refs_22_ = bf16[2,128,896]{2,1,0:T(8,128)(2,1)} collective-permute-done((bf16[2,128,896]{2,1,0:T(8,128)(2,1)S(1)}, bf16[2,128,896]{2,1,0:T(8,128)(2,1)}, u32[]{:S(2)}, u32[]{:S(2)}) %collective-permute-start.13) | collective-permute-done | bytes 458784 | tf_op jit(solution)/shard_map/ppermute | solution.py:344
  42.9 0.0 copy-done.5
  42.9 0.0 collective-permute-start.14
  42.9 0.0 copy-done.6
  42.9 0.5 collective-permute-start.15
  43.4 0.0 copy-done.7
  43.4 1.4 %collective-permute-done.14.refs_21_ = bf16[2,128,896]{2,1,0:T(8,128)(2,1)} collective-permute-done((bf16[2,128,896]{2,1,0:T(8,128)(2,1)S(1)}, bf16[2,128,896]{2,1,0:T(8,128)(2,1)}, u32[]{:S(2)}, u32[]{:S(2)}) %collective-permute-start.14) | collective-permute-done | bytes 458784 | tf_op jit(solution)/shard_map/ppermute | solution.py:346
  44.8 0.9 %collective-permute-done.15.refs_23_ = bf16[2,128,896]{2,1,0:T(8,128)(2,1)} collective-permute-done((bf16[2,128,896]{2,1,0:T(8,128)(2,1)}, bf16[2,128,896]{2,1,0:T(8,128)(2,1)}, u32[]{:S(2)}, u32[]{:S(2)}) %collective-permute-start.15) | collective-permute-done | bytes 458784 | tf_op jit(solution)/shard_map/ppermute | solution.py:347
  45.7 0.0 copy-done.2
  45.7 0.0 copy-done
  45.7 0.0 copy-done.1
  45.7 13.2 %attend_windows.1 = bf16[256,2048]{1,0:T(8,128)(2,1)} custom-call(s32[1]{0:T(128)} %bitcast.refs_0_, s32[8]{0:T(128)S(1)} %copy-done.2, s32[2,4]{1,0:T(2,128)S(1)} %collective-permute-done.2.refs_2_, s32[2,4]{1,0:T(2,128)S(1)} %add_bitcast_fusion.refs_3_, s32[4]{0:T(128)S(1)} %copy-done.1, bf16[16,256,896]{2,1,0:T(8,128)(2,1)} %get-tuple-element.16.refs_5_, ...), custom_call_target="tpu_custom_call" | custom-call | flops 4697620480 | bytes 16777216 | tf_op jit(solution)/shard_map/attend_windows/pallas_call | solution.py:269
  (7 shorter events, 0.0 us)
Async XLA Ops:
  0.0 45.7 %copy-start.2 = (s32[8]{0:T(128)S(1)}, s32[8]{0:T(128)}, u32[]{:S(2)}) copy-start(s32[8]{0:T(128)} %constant.8.clone.refs_1_) | copy-start | bytes 100
  0.0 45.7 %copy-start = (bf16[2,128,896]{2,1,0:T(8,128)(2,1)S(1)}, bf16[2,128,896]{2,1,0:T(8,128)(2,1)}, u32[]{:S(2)}) copy-start(bf16[2,128,896]{2,1,0:T(8,128)(2,1)} %refs_8_.1) | copy-start | bytes 1376260
  0.0 16.8 %copy-start.8 = (s32[4,2]{0,1:T(2,128)S(1)}, s32[4,2]{0,1:T(2,128)}, u32[]{:S(2)}) copy-start(s32[4,2]{0,1:T(2,128)} %param.13) | copy-start | bytes 100
  0.0 16.8 %copy-start.9 = (s32[4,2]{0,1:T(2,128)S(1)}, s32[4,2]{0,1:T(2,128)}, u32[]{:S(2)}) copy-start(s32[4,2]{0,1:T(2,128)} %param.12) | copy-start | bytes 100
  0.0 45.7 %copy-start.1 = (s32[4]{0:T(128)S(1)}, s32[4]{0:T(128)}, u32[]{:S(2)}) copy-start(s32[4]{0:T(128)} %refs_4_.1) | copy-start | bytes 52
  0.0 3.2 %collective-permute-start = (bf16[2,128,896]{2,1,0:T(8,128)(2,1)}, bf16[2,128,896]{2,1,0:T(8,128)(2,1)S(1)}, u32[]{:S(2)}, u32[]{:S(2)}) collective-permute-start(bf16[2,128,896]{2,1,0:T(8,128)(2,1)} %refs_8_.1), channel_id=1, source_target_pairs={{0,1},{1,0},{2,3},{3,2},{4,5},{5,4},{6,7},{7,6},{8,9},{9,8},{10,11... | collective-permute-start | bytes 1376264 | tf_op jit(solution)/shard_map/ppermute | solution.py:325
  0.5 9.7 %collective-permute-start.3 = (bf16[2,128,896]{2,1,0:T(8,128)(2,1)}, bf16[2,128,896]{2,1,0:T(8,128)(2,1)S(1)}, u32[]{:S(2)}, u32[]{:S(2)}) collective-permute-start(bf16[2,128,896]{2,1,0:T(8,128)(2,1)} %refs_8_.1), channel_id=1, source_target_pairs={{0,4},{1,3},{4,8},{5,1},{8,12},{9,5},{12,14},{13,9},{14,10},{15,13... | collective-permute-start | bytes 1376264 | tf_op jit(solution)/shard_map/ppermute | solution.py:334
  3.2 8.7 %copy-start.3 = (bf16[2,128,896]{2,1,0:T(8,128)(2,1)}, bf16[2,128,896]{2,1,0:T(8,128)(2,1)S(1)}, u32[]{:S(2)}) copy-start(bf16[2,128,896]{2,1,0:T(8,128)(2,1)S(1)} %collective-permute-done.refs_9_) | copy-start | bytes 1376260
  3.2 11.5 %collective-permute-start.1 = (bf16[2,128,896]{2,1,0:T(8,128)(2,1)S(1)}, bf16[2,128,896]{2,1,0:T(8,128)(2,1)S(1)}, u32[]{:S(2)}, u32[]{:S(2)}) collective-permute-start(bf16[2,128,896]{2,1,0:T(8,128)(2,1)S(1)} %collective-permute-done.refs_9_), channel_id=1, source_target_pairs={{0,4},{1,3},{4,8},{5,1},{8,12},{9,5},{12,14},{13,9},{14,10},{15,13... | collective-permute-start | bytes 1376264 | tf_op jit(solution)/shard_map/ppermute | solution.py:334
  10.2 8.6 %collective-permute-start.4 = (bf16[2,128,896]{2,1,0:T(8,128)(2,1)S(1)}, bf16[2,128,896]{2,1,0:T(8,128)(2,1)S(1)}, u32[]{:S(2)}, u32[]{:S(2)}) collective-permute-start(bf16[2,128,896]{2,1,0:T(8,128)(2,1)S(1)} %collective-permute-done.3.refs_10_), channel_id=1, source_target_pairs={{0,1},{1,0},{2,3},{3,2},{4,5},{5,4},{6,7},{7,6},{8,9},{9,8},{10,11... | collective-permute-start | bytes 1376264 | tf_op jit(solution)/shard_map/ppermute | solution.py:335
  10.3 9.3 %collective-permute-start.6 = (bf16[2,128,896]{2,1,0:T(8,128)(2,1)S(1)}, bf16[2,128,896]{2,1,0:T(8,128)(2,1)S(1)}, u32[]{:S(2)}, u32[]{:S(2)}) collective-permute-start(bf16[2,128,896]{2,1,0:T(8,128)(2,1)S(1)} %collective-permute-done.3.refs_10_), channel_id=1, source_target_pairs={{0,4},{1,3},{4,8},{5,1},{8,12},{9,5},{12,14},{13,9},{14,10},{15,13... | collective-permute-start | bytes 1376264 | tf_op jit(solution)/shard_map/ppermute | solution.py:334
  14.7 12.4 %collective-permute-start.8 = (bf16[2,128,896]{2,1,0:T(8,128)(2,1)S(1)}, bf16[2,128,896]{2,1,0:T(8,128)(2,1)S(1)}, u32[]{:S(2)}, u32[]{:S(2)}) collective-permute-start(bf16[2,128,896]{2,1,0:T(8,128)(2,1)S(1)} %collective-permute-done.1.refs_12_), channel_id=1, source_target_pairs={{0,4},{1,3},{4,8},{5,1},{8,12},{9,5},{12,14},{13,9},{14,10},{15,13... | collective-permute-start | bytes 1376264 | tf_op jit(solution)/shard_map/ppermute | solution.py:334
  16.8 2.9 %collective-permute-start.2 = (s32[2,4]{1,0:T(2,128)S(1)}, s32[2,4]{1,0:T(2,128)S(1)}, u32[]{:S(2)}, u32[]{:S(2)}) collective-permute-start(s32[2,4]{1,0:T(2,128)S(1)} %add_bitcast_fusion.refs_3_), channel_id=1, source_target_pairs={{0,1},{1,2},{2,3},{3,4},{4,5},{5,6},{6,7},{7,8},{8,9},{9,10},{10,1... | collective-permute-start | bytes 104 | tf_op jit(solution)/shard_map/ppermute | solution.py:338
  18.1 9.5 %collective-permute-start.5 = (bf16[2,128,896]{2,1,0:T(8,128)(2,1)S(1)}, bf16[2,128,896]{2,1,0:T(8,128)(2,1)}, u32[]{:S(2)}, u32[]{:S(2)}) collective-permute-start(bf16[2,128,896]{2,1,0:T(8,128)(2,1)S(1)} %collective-permute-done.1.refs_12_), channel_id=1, source_target_pairs={{0,1},{1,0},{2,3},{3,2},{4,5},{5,4},{6,7},{7,6},{8,9},{9,8},{10,11... | collective-permute-start | bytes 1376264 | tf_op jit(solution)/shard_map/ppermute | solution.py:335
  18.9 0.8 %copy-start.4 = (bf16[2,128,896]{2,1,0:T(8,128)(2,1)}, bf16[2,128,896]{2,1,0:T(8,128)(2,1)S(1)}, u32[]{:S(2)}) copy-start(bf16[2,128,896]{2,1,0:T(8,128)(2,1)S(1)} %collective-permute-done.4.refs_11_) | copy-start | bytes 1376260
  19.7 13.4 %collective-permute-start.10 = (bf16[2,128,896]{2,1,0:T(8,128)(2,1)S(1)}, bf16[2,128,896]{2,1,0:T(8,128)(2,1)S(1)}, u32[]{:S(2)}, u32[]{:S(2)}) collective-permute-start(bf16[2,128,896]{2,1,0:T(8,128)(2,1)S(1)} %collective-permute-done.6.refs_14_), channel_id=1, source_target_pairs={{0,4},{1,3},{4,8},{5,1},{8,12},{9,5},{12,14},{13,9},{14,10},{15,13... | collective-permute-start | bytes 1376264 | tf_op jit(solution)/shard_map/ppermute | solution.py:334
  27.1 6.0 %collective-permute-start.7 = (bf16[2,128,896]{2,1,0:T(8,128)(2,1)S(1)}, bf16[2,128,896]{2,1,0:T(8,128)(2,1)S(1)}, u32[]{:S(2)}, u32[]{:S(2)}) collective-permute-start(bf16[2,128,896]{2,1,0:T(8,128)(2,1)S(1)} %collective-permute-done.6.refs_14_), channel_id=1, source_target_pairs={{0,1},{1,0},{2,3},{3,2},{4,5},{5,4},{6,7},{7,6},{8,9},{9,8},{10,11... | collective-permute-start | bytes 1376264 | tf_op jit(solution)/shard_map/ppermute | solution.py:335
  27.1 6.0 %collective-permute-start.9 = (bf16[2,128,896]{2,1,0:T(8,128)(2,1)S(1)}, bf16[2,128,896]{2,1,0:T(8,128)(2,1)S(1)}, u32[]{:S(2)}, u32[]{:S(2)}) collective-permute-start(bf16[2,128,896]{2,1,0:T(8,128)(2,1)S(1)} %collective-permute-done.8.refs_16_), channel_id=1, source_target_pairs={{0,1},{1,0},{2,3},{3,2},{4,5},{5,4},{6,7},{7,6},{8,9},{9,8},{10,11... | collective-permute-start | bytes 1376264 | tf_op jit(solution)/shard_map/ppermute | solution.py:335
  27.6 10.4 %collective-permute-start.12 = (bf16[2,128,896]{2,1,0:T(8,128)(2,1)S(1)}, bf16[2,128,896]{2,1,0:T(8,128)(2,1)S(1)}, u32[]{:S(2)}, u32[]{:S(2)}) collective-permute-start(bf16[2,128,896]{2,1,0:T(8,128)(2,1)S(1)} %collective-permute-done.8.refs_16_), channel_id=1, source_target_pairs={{0,4},{1,3},{4,8},{5,1},{8,12},{9,5},{12,14},{13,9},{14,10},{15,13... | collective-permute-start | bytes 1376264 | tf_op jit(solution)/shard_map/ppermute | solution.py:334
  33.1 4.9 %collective-permute-start.11 = (bf16[2,128,896]{2,1,0:T(8,128)(2,1)S(1)}, bf16[2,128,896]{2,1,0:T(8,128)(2,1)S(1)}, u32[]{:S(2)}, u32[]{:S(2)}) collective-permute-start(bf16[2,128,896]{2,1,0:T(8,128)(2,1)S(1)} %collective-permute-done.10.refs_18_), channel_id=1, source_target_pairs={{0,1},{1,0},{2,3},{3,2},{4,5},{5,4},{6,7},{7,6},{8,9},{9,8},{10,11... | collective-permute-start | bytes 1376264 | tf_op jit(solution)/shard_map/ppermute | solution.py:335
  33.1 9.8 %copy-start.5 = (bf16[2,128,896]{2,1,0:T(8,128)(2,1)}, bf16[2,128,896]{2,1,0:T(8,128)(2,1)S(1)}, u32[]{:S(2)}) copy-start(bf16[2,128,896]{2,1,0:T(8,128)(2,1)S(1)} %collective-permute-done.7.refs_15_) | copy-start | bytes 1376260
  33.1 9.8 %copy-start.6 = (bf16[2,128,896]{2,1,0:T(8,128)(2,1)}, bf16[2,128,896]{2,1,0:T(8,128)(2,1)S(1)}, u32[]{:S(2)}) copy-start(bf16[2,128,896]{2,1,0:T(8,128)(2,1)S(1)} %collective-permute-done.9.refs_17_) | copy-start | bytes 1376260
  33.1 9.8 %collective-permute-start.13 = (bf16[2,128,896]{2,1,0:T(8,128)(2,1)S(1)}, bf16[2,128,896]{2,1,0:T(8,128)(2,1)}, u32[]{:S(2)}, u32[]{:S(2)}) collective-permute-start(bf16[2,128,896]{2,1,0:T(8,128)(2,1)S(1)} %collective-permute-done.10.refs_18_), channel_id=1, source_target_pairs={{0,4},{1,3},{4,8},{5,1},{8,12},{9,5},{12,14},{13,9},{14,10},{15,13... | collective-permute-start | bytes 1376264 | tf_op jit(solution)/shard_map/ppermute | solution.py:344
  38.0 5.4 %copy-start.7 = (bf16[2,128,896]{2,1,0:T(8,128)(2,1)}, bf16[2,128,896]{2,1,0:T(8,128)(2,1)S(1)}, u32[]{:S(2)}) copy-start(bf16[2,128,896]{2,1,0:T(8,128)(2,1)S(1)} %collective-permute-done.11.refs_19_) | copy-start | bytes 1376260
  42.9 1.9 %collective-permute-start.14 = (bf16[2,128,896]{2,1,0:T(8,128)(2,1)S(1)}, bf16[2,128,896]{2,1,0:T(8,128)(2,1)}, u32[]{:S(2)}, u32[]{:S(2)}) collective-permute-start(bf16[2,128,896]{2,1,0:T(8,128)(2,1)S(1)} %collective-permute-done.12.refs_20_), channel_id=1, source_target_pairs={{0,1},{1,0},{2,3},{3,2},{4,5},{5,4},{6,7},{7,6},{8,9},{9,8},{10,11... | collective-permute-start | bytes 1376264 | tf_op jit(solution)/shard_map/ppermute | solution.py:346
  42.9 2.8 %collective-permute-start.15 = (bf16[2,128,896]{2,1,0:T(8,128)(2,1)}, bf16[2,128,896]{2,1,0:T(8,128)(2,1)}, u32[]{:S(2)}, u32[]{:S(2)}) collective-permute-start(bf16[2,128,896]{2,1,0:T(8,128)(2,1)} %collective-permute-done.13.refs_22_), channel_id=1, source_target_pairs={{0,1},{1,0},{2,3},{3,2},{4,5},{5,4},{6,7},{7,6},{8,9},{9,8},{10,11... | collective-permute-start | bytes 1376264 | tf_op jit(solution)/shard_map/ppermute | solution.py:347

commit v14 on v13

--- a/solution.py
+++ b/solution.py
@@ -140,7 +140,7 @@
 
 def attend_kernel(size, *refs):
     plan_refs, (starts_ref, folded_hbm, single_ref, value_hbm, *rest) = refs[:4], refs[4:]
-    *stores, out_hbm, tokens, raw, folded, value, scores, weights, mixed, out, sems, group_sems = rest
+    *stores, out_hbm, tokens, turned, raw, folded, value, scores, weights, mixed, out, sems, group_sems = rest
     requests, length, width = raw.shape
     blocks = requests // 2 - 1
     count = blocks * SPAN
@@ -187,6 +187,10 @@
             fetch(request, stores[0], 0).wait()
         for request in (2 * window, 2 * window + 1):
             normalise(raw[request], tokens.at[request])
+            turned[request] = tokens[request].T
+
+    def across(window):
+        return jnp.concatenate([turned[2 * window], turned[2 * window + 1]], axis=1)
 
     def along(window):
         return tokens[2 * window : 2 * window + 2].reshape(2 * length, width)
@@ -202,11 +206,11 @@
     def score(unit):
         window = units[unit][1]
         if window == lone_window:
-            lone["scores"] = contract(single_ref[...].astype(jnp.bfloat16), along(window), ((1,), (1,)))
+            lone["scores"] = contract(single_ref[...].astype(jnp.bfloat16), across(window), ((1,), (0,)))
             return
         slot, heads, rows = place_of(unit)
         taken = folded[heads, rows].reshape(rows_at_once, width)
-        scores[slot] = contract(taken, along(window), ((1,), (1,)))
+        scores[slot] = contract(taken, across(window), ((1,), (0,)))
 
     def soften(unit):
         if units[unit][1] == lone_window:
@@ -273,6 +277,7 @@
         out_specs=HBM_SPEC,
         scratch_shapes=[
             pltpu.VMEM((requests, length, width), jnp.bfloat16),
+            pltpu.VMEM((requests, width, length), jnp.bfloat16),
             pltpu.VMEM((requests, length, width), jnp.bfloat16),
             pltpu.VMEM(folded.shape, jnp.bfloat16),
             pltpu.VMEM(w_value.shape, jnp.bfloat16),
@@ -326,21 +331,19 @@
     stores = [neighbours, in_hbm(chains[1])]
     folded, single = fold(*after([queries], [chains[1]]), w_key)
 
-    beside = {(1, 0): [folded, single]}
+    asked = after([wanted], [single])[0]
+    before = lax.ppermute(asked, "seq", [(i, i + 1) for i in range(devices - 1)])
+    beside = {(1, 0): [folded, single], (1, 1): [before]}
     for step in range(reach):
         for chain in range(2):
             others = beside.get((step, chain), []) + (stores[2 * chain + 4 * step - 5 :][:1] if step > 1 else [])
             sent = after([chains[chain]], others) if others else [chains[chain]]
             chains[chain] = onwards(sent[0])
             stores += [chains[chain], in_hbm(swapped(chains[chain]))]
-            if (step, chain) == (0, 1):
-                asked = after([wanted], [chains[1]])[0]
-                before = lax.ppermute(asked, "seq", [(i, i + 1) for i in range(devices - 1)])
-                beside[2, 0] = [before]
     places = jnp.asarray([ring.index(chip) for chip in range(size)], jnp.int32)
     plan = [lax.axis_index("seq").reshape(1), places, before, wanted]
     if size % 2 == 0:
-        sent = after([chains[0]], stores[-7:-4:2]) if reach > 1 else [chains[0]]
+        sent = after([chains[0]], [before, *stores[-7:-4:2]]) if reach > 1 else [chains[0]]
         last = onwards(sent[0])
         if reach:
             stores[-1] = swapped(after([chains[1]], [last, stores[-3]])[0])

time: 59.5 us -> 58.7 us (0.987)
  starting transfers between devices: 23.5 us -> 17.3 us
  waiting for transfers between devices: 17 us -> 21.1 us
  local copies, waits for them, and re-layouts: 0.09 us -> 0.86 us
  other arithmetic: 0.01 us -> 0.7 us
    ppermute x6, starting transfers between devices: 17.3 us -> 11.9 us  [body(): chains[chain] = onwards(sent[0])]
    ppermute x6, waiting for transfers between devices: 9.8 us -> 13.7 us  [body(): chains[chain] = onwards(sent[0])]
    ppermute x1, starting transfers between devices: 2.54 us -> 1.49 us  [body(): last = onwards(sent[0])]
    unnamed x20 -> x16, local copies, waits for them, and re-layouts: 0.09 us -> 0.86 us
    transpose x1, other arithmetic: 0.01 us -> 0.7 us  [body(): wanted = (retrieval_owner * stored + retrieval_slot).T]
  transfers between devices with their start and end apart: 16 -> 16, of which waited for: 7 -> 7; matrix products, arithmetic and copies ran while one was open for 0% -> 1% of each run, Pallas kernels for 9% -> 9%
where the time goes in v14:
time: 58.7 us; the launch traced here: 58.4 us
  waiting for transfers between devices  21.1 us (36%)
  Pallas kernels  18.2 us (31%)
  starting transfers between devices  17.3 us (29%)
  local copies, waits for them, and re-layouts  0.86 us (1%)
  other arithmetic  0.7 us (1%)
    ppermute x6, waiting for transfers between devices, body(): chains[chain] = onwards(sent[0])  13.7 us
    pallas_call x1, Pallas kernels, attend(): pl.pallas_call(functools.partial(attend_kernel, size), out_shape=jax.Shap...  13.1 us
    ppermute x6, starting transfers between devices, body(): chains[chain] = onwards(sent[0])  11.9 us
    pallas_call x1, Pallas kernels, fold(): pl.pallas_call(fold_kernel, out_shape=(pltpu.HBM(shape, jnp.bfloat16), ja...  5.06 us
    ppermute x1, waiting for transfers between devices, body(): last = onwards(sent[0])  5.02 us
    ppermute x1, starting transfers between devices, body(): lax.ppermute(asked, 'seq', [(i, i + 1) for i in range(devices - 1)])  1.71 us
    ppermute x1, starting transfers between devices, body(): last = onwards(sent[0])  1.49 us
    ppermute x1, waiting for transfers between devices, body(): stores[-1] = swapped(after([chains[1]], [last, stores[-3]])[0])  1.43 us
  transfers between devices with their start and end apart: 16, of which 7 were waited for; matrix products, arithmetic and copies ran while one was open for 1% of the time, Pallas kernels for 9%

profile of v14, /device:TPU:0, one launch (start us, length us, event | category | flops | bytes accessed | tf_op | source)
XLA Modules:
  0.0 58.4 jit_solution(7252743608978468924)
XLA Ops:
  0.0 0.0 copy-start.2
  0.0 0.0 copy-start
  0.0 0.0 copy-start.1
  0.0 0.5 collective-permute-start
  0.5 2.6 %collective-permute-start.2 = (bf16[2,128,896]{2,1,0:T(8,128)(2,1)}, bf16[2,128,896]{2,1,0:T(8,128)(2,1)S(1)}, u32[]{:S(2)}, u32[]{:S(2)}) collective-permute-start(bf16[2,128,896]{2,1,0:T(8,128)(2,1)} %refs_8_.1), channel_id=1, source_target_pairs={{0,4},{1,3},{4,8},{5,1},{8,12},{9,5},{12,14},{13,9},{14,10},{15,13... | collective-permute-start | bytes 1376264 | tf_op jit(solution)/shard_map/ppermute | solution.py:341
  3.2 0.0 collective-permute-done.refs_9_
  3.2 0.0 copy-start.3
  3.2 2.0 %collective-permute-start.4 = (bf16[2,128,896]{2,1,0:T(8,128)(2,1)S(1)}, bf16[2,128,896]{2,1,0:T(8,128)(2,1)S(1)}, u32[]{:S(2)}, u32[]{:S(2)}) collective-permute-start(bf16[2,128,896]{2,1,0:T(8,128)(2,1)S(1)} %collective-permute-done.refs_9_), channel_id=1, source_target_pairs={{0,4},{1,3},{4,8},{5,1},{8,12},{9,5},{12,14},{13,9},{14,10},{15,13... | collective-permute-start | bytes 1376264 | tf_op jit(solution)/shard_map/ppermute | solution.py:341
  5.1 0.7 %add_bitcast_fusion.refs_3_ = s32[2,4]{1,0:T(2,128)S(1)} fusion(s32[4,2]{0,1:T(2,128)} %param.13, s32[4,2]{0,1:T(2,128)} %param.12), kind=kLoop, calls=%fused_computation | loop fusion | flops 16 | bytes 96 | tf_op jit(solution)/shard_map/transpose | solution.py:329
  5.8 5.1 %fold_queries.1 = (bf16[16,256,896]{2,1,0:T(8,128)(2,1)}, f32[16,896]{1,0:T(8,128)S(1)}) custom-call(bf16[256,2048]{1,0:T(8,128)(2,1)} %query_hbm, bf16[896,2048]{1,0:T(8,128)(2,1)} %key_hbm.1), custom_call_target="tpu_custom_call" | custom-call | flops 939524096 | bytes 12582912 | tf_op jit(solution)/shard_map/fold_queries/pallas_call | solution.py:80
  10.9 0.0 collective-permute-done.2.refs_10_
  10.9 1.7 %collective-permute-start.1 = (s32[2,4]{1,0:T(2,128)S(1)}, s32[2,4]{1,0:T(2,128)S(1)}, u32[]{:S(2)}, u32[]{:S(2)}) collective-permute-start(s32[2,4]{1,0:T(2,128)S(1)} %add_bitcast_fusion.refs_3_), channel_id=1, source_target_pairs={{0,1},{1,2},{2,3},{3,4},{4,5},{5,6},{6,7},{7,8},{8,9},{9,10},{10,1... | collective-permute-start | bytes 104 | tf_op jit(solution)/shard_map/ppermute | solution.py:335
  12.6 1.3 %collective-permute-start.3 = (bf16[2,128,896]{2,1,0:T(8,128)(2,1)S(1)}, bf16[2,128,896]{2,1,0:T(8,128)(2,1)S(1)}, u32[]{:S(2)}, u32[]{:S(2)}) collective-permute-start(bf16[2,128,896]{2,1,0:T(8,128)(2,1)S(1)} %collective-permute-done.2.refs_10_), channel_id=1, source_target_pairs={{0,1},{1,0},{2,3},{3,2},{4,5},{5,4},{6,7},{7,6},{8,9},{9,8},{10,11... | collective-permute-start | bytes 1376264 | tf_op jit(solution)/shard_map/ppermute | solution.py:342
  13.9 1.6 %collective-permute-start.6 = (bf16[2,128,896]{2,1,0:T(8,128)(2,1)S(1)}, bf16[2,128,896]{2,1,0:T(8,128)(2,1)S(1)}, u32[]{:S(2)}, u32[]{:S(2)}) collective-permute-start(bf16[2,128,896]{2,1,0:T(8,128)(2,1)S(1)} %collective-permute-done.2.refs_10_), channel_id=1, source_target_pairs={{0,4},{1,3},{4,8},{5,1},{8,12},{9,5},{12,14},{13,9},{14,10},{15,13... | collective-permute-start | bytes 1376264 | tf_op jit(solution)/shard_map/ppermute | solution.py:341
  15.5 0.0 collective-permute-done.1.refs_2_
  15.5 0.0 copy-done.3
  15.5 0.0 collective-permute-done.4.refs_12_
  15.5 2.8 %collective-permute-start.8 = (bf16[2,128,896]{2,1,0:T(8,128)(2,1)S(1)}, bf16[2,128,896]{2,1,0:T(8,128)(2,1)S(1)}, u32[]{:S(2)}, u32[]{:S(2)}) collective-permute-start(bf16[2,128,896]{2,1,0:T(8,128)(2,1)S(1)} %collective-permute-done.4.refs_12_), channel_id=1, source_target_pairs={{0,4},{1,3},{4,8},{5,1},{8,12},{9,5},{12,14},{13,9},{14,10},{15,13... | collective-permute-start | bytes 1376264 | tf_op jit(solution)/shard_map/ppermute | solution.py:341
  18.3 0.0 collective-permute-start.5
  18.3 0.0 collective-permute-done.3.refs_11_
  18.3 0.8 %copy-done.4 = bf16[2,128,896]{2,1,0:T(8,128)(2,1)} copy-done((bf16[2,128,896]{2,1,0:T(8,128)(2,1)}, bf16[2,128,896]{2,1,0:T(8,128)(2,1)S(1)}, u32[]{:S(2)}) %copy-start.4) | copy-done | bytes 458776
  19.1 3.4 %collective-permute-done.6.refs_14_ = bf16[2,128,896]{2,1,0:T(8,128)(2,1)S(1)} collective-permute-done((bf16[2,128,896]{2,1,0:T(8,128)(2,1)S(1)}, bf16[2,128,896]{2,1,0:T(8,128)(2,1)S(1)}, u32[]{:S(2)}, u32[]{:S(2)}) %collective-permute-start.6) | collective-permute-done | bytes 458784 | tf_op jit(solution)/shard_map/ppermute | solution.py:341
  22.5 1.4 %collective-permute-start.10 = (bf16[2,128,896]{2,1,0:T(8,128)(2,1)S(1)}, bf16[2,128,896]{2,1,0:T(8,128)(2,1)S(1)}, u32[]{:S(2)}, u32[]{:S(2)}) collective-permute-start(bf16[2,128,896]{2,1,0:T(8,128)(2,1)S(1)} %collective-permute-done.6.refs_14_), channel_id=1, source_target_pairs={{0,4},{1,3},{4,8},{5,1},{8,12},{9,5},{12,14},{13,9},{14,10},{15,13... | collective-permute-start | bytes 1376264 | tf_op jit(solution)/shard_map/ppermute | solution.py:341
  23.9 0.0 collective-permute-start.7
  23.9 3.5 %collective-permute-done.8.refs_16_ = bf16[2,128,896]{2,1,0:T(8,128)(2,1)S(1)} collective-permute-done((bf16[2,128,896]{2,1,0:T(8,128)(2,1)S(1)}, bf16[2,128,896]{2,1,0:T(8,128)(2,1)S(1)}, u32[]{:S(2)}, u32[]{:S(2)}) %collective-permute-start.8) | collective-permute-done | bytes 458784 | tf_op jit(solution)/shard_map/ppermute | solution.py:341
  27.4 0.0 collective-permute-start.9
  27.4 0.0 collective-permute-done.5.refs_13_
  27.4 1.4 %collective-permute-start.12 = (bf16[2,128,896]{2,1,0:T(8,128)(2,1)S(1)}, bf16[2,128,896]{2,1,0:T(8,128)(2,1)S(1)}, u32[]{:S(2)}, u32[]{:S(2)}) collective-permute-start(bf16[2,128,896]{2,1,0:T(8,128)(2,1)S(1)} %collective-permute-done.8.refs_16_), channel_id=1, source_target_pairs={{0,4},{1,3},{4,8},{5,1},{8,12},{9,5},{12,14},{13,9},{14,10},{15,13... | collective-permute-start | bytes 1376264 | tf_op jit(solution)/shard_map/ppermute | solution.py:341
  28.9 3.5 %collective-permute-done.10.refs_18_ = bf16[2,128,896]{2,1,0:T(8,128)(2,1)S(1)} collective-permute-done((bf16[2,128,896]{2,1,0:T(8,128)(2,1)S(1)}, bf16[2,128,896]{2,1,0:T(8,128)(2,1)S(1)}, u32[]{:S(2)}, u32[]{:S(2)}) %collective-permute-start.10) | collective-permute-done | bytes 458784 | tf_op jit(solution)/shard_map/ppermute | solution.py:341
  32.3 0.0 collective-permute-start.11
  32.3 0.0 collective-permute-done.7.refs_15_
  32.3 0.0 collective-permute-done.9.refs_17_
  32.4 0.0 copy-start.6
  32.4 1.5 %collective-permute-start.13 = (bf16[2,128,896]{2,1,0:T(8,128)(2,1)S(1)}, bf16[2,128,896]{2,1,0:T(8,128)(2,1)}, u32[]{:S(2)}, u32[]{:S(2)}) collective-permute-start(bf16[2,128,896]{2,1,0:T(8,128)(2,1)S(1)} %collective-permute-done.10.refs_18_), channel_id=1, source_target_pairs={{0,4},{1,3},{4,8},{5,1},{8,12},{9,5},{12,14},{13,9},{14,10},{15,13... | collective-permute-start | bytes 1376264 | tf_op jit(solution)/shard_map/ppermute | solution.py:347
  33.9 3.4 %collective-permute-done.12.refs_20_ = bf16[2,128,896]{2,1,0:T(8,128)(2,1)S(1)} collective-permute-done((bf16[2,128,896]{2,1,0:T(8,128)(2,1)S(1)}, bf16[2,128,896]{2,1,0:T(8,128)(2,1)S(1)}, u32[]{:S(2)}, u32[]{:S(2)}) %collective-permute-start.12) | collective-permute-done | bytes 458784 | tf_op jit(solution)/shard_map/ppermute | solution.py:341
  37.3 0.0 collective-permute-done.11.refs_19_
  37.3 5.0 %collective-permute-done.13.refs_22_ = bf16[2,128,896]{2,1,0:T(8,128)(2,1)} collective-permute-done((bf16[2,128,896]{2,1,0:T(8,128)(2,1)S(1)}, bf16[2,128,896]{2,1,0:T(8,128)(2,1)}, u32[]{:S(2)}, u32[]{:S(2)}) %collective-permute-start.13) | collective-permute-done | bytes 458784 | tf_op jit(solution)/shard_map/ppermute | solution.py:347
  42.3 0.0 copy-done.5
  42.3 0.0 collective-permute-start.14
  42.3 0.0 copy-done.6
  42.3 0.5 collective-permute-start.15
  42.8 0.0 copy-done.7
  42.8 1.4 %collective-permute-done.14.refs_21_ = bf16[2,128,896]{2,1,0:T(8,128)(2,1)} collective-permute-done((bf16[2,128,896]{2,1,0:T(8,128)(2,1)S(1)}, bf16[2,128,896]{2,1,0:T(8,128)(2,1)}, u32[]{:S(2)}, u32[]{:S(2)}) %collective-permute-start.14) | collective-permute-done | bytes 458784 | tf_op jit(solution)/shard_map/ppermute | solution.py:349
  44.2 0.9 %collective-permute-done.15.refs_23_ = bf16[2,128,896]{2,1,0:T(8,128)(2,1)} collective-permute-done((bf16[2,128,896]{2,1,0:T(8,128)(2,1)}, bf16[2,128,896]{2,1,0:T(8,128)(2,1)}, u32[]{:S(2)}, u32[]{:S(2)}) %collective-permute-start.15) | collective-permute-done | bytes 458784 | tf_op jit(solution)/shard_map/ppermute | solution.py:350
  45.1 0.0 copy-done.2
  45.1 0.0 copy-done
  45.1 0.0 copy-done.1
  45.1 13.1 %attend_windows.1 = bf16[256,2048]{1,0:T(8,128)(2,1)} custom-call(s32[1]{0:T(128)} %bitcast.refs_0_, s32[8]{0:T(128)S(1)} %copy-done.2, s32[2,4]{1,0:T(2,128)S(1)} %collective-permute-done.1.refs_2_, s32[2,4]{1,0:T(2,128)S(1)} %add_bitcast_fusion.refs_3_, s32[4]{0:T(128)S(1)} %copy-done.1, bf16[16,256,896]{2,1,0:T(8,128)(2,1)} %get-tuple-element.18.refs_5_, ...), custom_call_target="tpu_custom_call" | custom-call | flops 4697620480 | bytes 16777216 | tf_op jit(solution)/shard_map/attend_windows/pallas_call | solution.py:273
  (3 shorter events, 0.0 us)
Async XLA Ops:
  0.0 45.1 %copy-start.2 = (s32[8]{0:T(128)S(1)}, s32[8]{0:T(128)}, u32[]{:S(2)}) copy-start(s32[8]{0:T(128)} %constant.8.clone.refs_1_) | copy-start | bytes 100
  0.0 45.1 %copy-start = (bf16[2,128,896]{2,1,0:T(8,128)(2,1)S(1)}, bf16[2,128,896]{2,1,0:T(8,128)(2,1)}, u32[]{:S(2)}) copy-start(bf16[2,128,896]{2,1,0:T(8,128)(2,1)} %refs_8_.1) | copy-start | bytes 1376260
  0.0 45.1 %copy-start.1 = (s32[4]{0:T(128)S(1)}, s32[4]{0:T(128)}, u32[]{:S(2)}) copy-start(s32[4]{0:T(128)} %refs_4_.1) | copy-start | bytes 52
  0.0 3.2 %collective-permute-start = (bf16[2,128,896]{2,1,0:T(8,128)(2,1)}, bf16[2,128,896]{2,1,0:T(8,128)(2,1)S(1)}, u32[]{:S(2)}, u32[]{:S(2)}) collective-permute-start(bf16[2,128,896]{2,1,0:T(8,128)(2,1)} %refs_8_.1), channel_id=1, source_target_pairs={{0,1},{1,0},{2,3},{3,2},{4,5},{5,4},{6,7},{7,6},{8,9},{9,8},{10,11... | collective-permute-start | bytes 1376264 | tf_op jit(solution)/shard_map/ppermute | solution.py:330
  0.5 10.4 %collective-permute-start.2 = (bf16[2,128,896]{2,1,0:T(8,128)(2,1)}, bf16[2,128,896]{2,1,0:T(8,128)(2,1)S(1)}, u32[]{:S(2)}, u32[]{:S(2)}) collective-permute-start(bf16[2,128,896]{2,1,0:T(8,128)(2,1)} %refs_8_.1), channel_id=1, source_target_pairs={{0,4},{1,3},{4,8},{5,1},{8,12},{9,5},{12,14},{13,9},{14,10},{15,13... | collective-permute-start | bytes 1376264 | tf_op jit(solution)/shard_map/ppermute | solution.py:341
  3.2 12.3 %copy-start.3 = (bf16[2,128,896]{2,1,0:T(8,128)(2,1)}, bf16[2,128,896]{2,1,0:T(8,128)(2,1)S(1)}, u32[]{:S(2)}) copy-start(bf16[2,128,896]{2,1,0:T(8,128)(2,1)S(1)} %collective-permute-done.refs_9_) | copy-start | bytes 1376260
  3.2 12.3 %collective-permute-start.4 = (bf16[2,128,896]{2,1,0:T(8,128)(2,1)S(1)}, bf16[2,128,896]{2,1,0:T(8,128)(2,1)S(1)}, u32[]{:S(2)}, u32[]{:S(2)}) collective-permute-start(bf16[2,128,896]{2,1,0:T(8,128)(2,1)S(1)} %collective-permute-done.refs_9_), channel_id=1, source_target_pairs={{0,4},{1,3},{4,8},{5,1},{8,12},{9,5},{12,14},{13,9},{14,10},{15,13... | collective-permute-start | bytes 1376264 | tf_op jit(solution)/shard_map/ppermute | solution.py:341
  10.9 4.6 %collective-permute-start.1 = (s32[2,4]{1,0:T(2,128)S(1)}, s32[2,4]{1,0:T(2,128)S(1)}, u32[]{:S(2)}, u32[]{:S(2)}) collective-permute-start(s32[2,4]{1,0:T(2,128)S(1)} %add_bitcast_fusion.refs_3_), channel_id=1, source_target_pairs={{0,1},{1,2},{2,3},{3,4},{4,5},{5,6},{6,7},{7,8},{8,9},{9,10},{10,1... | collective-permute-start | bytes 104 | tf_op jit(solution)/shard_map/ppermute | solution.py:335
  12.6 5.7 %collective-permute-start.3 = (bf16[2,128,896]{2,1,0:T(8,128)(2,1)S(1)}, bf16[2,128,896]{2,1,0:T(8,128)(2,1)S(1)}, u32[]{:S(2)}, u32[]{:S(2)}) collective-permute-start(bf16[2,128,896]{2,1,0:T(8,128)(2,1)S(1)} %collective-permute-done.2.refs_10_), channel_id=1, source_target_pairs={{0,1},{1,0},{2,3},{3,2},{4,5},{5,4},{6,7},{7,6},{8,9},{9,8},{10,11... | collective-permute-start | bytes 1376264 | tf_op jit(solution)/shard_map/ppermute | solution.py:342
  13.9 8.6 %collective-permute-start.6 = (bf16[2,128,896]{2,1,0:T(8,128)(2,1)S(1)}, bf16[2,128,896]{2,1,0:T(8,128)(2,1)S(1)}, u32[]{:S(2)}, u32[]{:S(2)}) collective-permute-start(bf16[2,128,896]{2,1,0:T(8,128)(2,1)S(1)} %collective-permute-done.2.refs_10_), channel_id=1, source_target_pairs={{0,4},{1,3},{4,8},{5,1},{8,12},{9,5},{12,14},{13,9},{14,10},{15,13... | collective-permute-start | bytes 1376264 | tf_op jit(solution)/shard_map/ppermute | solution.py:341
  15.5 11.9 %collective-permute-start.8 = (bf16[2,128,896]{2,1,0:T(8,128)(2,1)S(1)}, bf16[2,128,896]{2,1,0:T(8,128)(2,1)S(1)}, u32[]{:S(2)}, u32[]{:S(2)}) collective-permute-start(bf16[2,128,896]{2,1,0:T(8,128)(2,1)S(1)} %collective-permute-done.4.refs_12_), channel_id=1, source_target_pairs={{0,4},{1,3},{4,8},{5,1},{8,12},{9,5},{12,14},{13,9},{14,10},{15,13... | collective-permute-start | bytes 1376264 | tf_op jit(solution)/shard_map/ppermute | solution.py:341
  18.3 9.1 %collective-permute-start.5 = (bf16[2,128,896]{2,1,0:T(8,128)(2,1)S(1)}, bf16[2,128,896]{2,1,0:T(8,128)(2,1)}, u32[]{:S(2)}, u32[]{:S(2)}) collective-permute-start(bf16[2,128,896]{2,1,0:T(8,128)(2,1)S(1)} %collective-permute-done.4.refs_12_), channel_id=1, source_target_pairs={{0,1},{1,0},{2,3},{3,2},{4,5},{5,4},{6,7},{7,6},{8,9},{9,8},{10,11... | collective-permute-start | bytes 1376264 | tf_op jit(solution)/shard_map/ppermute | solution.py:342
  18.3 0.8 %copy-start.4 = (bf16[2,128,896]{2,1,0:T(8,128)(2,1)}, bf16[2,128,896]{2,1,0:T(8,128)(2,1)S(1)}, u32[]{:S(2)}) copy-start(bf16[2,128,896]{2,1,0:T(8,128)(2,1)S(1)} %collective-permute-done.3.refs_11_) | copy-start | bytes 1376260
  22.5 9.8 %collective-permute-start.10 = (bf16[2,128,896]{2,1,0:T(8,128)(2,1)S(1)}, bf16[2,128,896]{2,1,0:T(8,128)(2,1)S(1)}, u32[]{:S(2)}, u32[]{:S(2)}) collective-permute-start(bf16[2,128,896]{2,1,0:T(8,128)(2,1)S(1)} %collective-permute-done.6.refs_14_), channel_id=1, source_target_pairs={{0,4},{1,3},{4,8},{5,1},{8,12},{9,5},{12,14},{13,9},{14,10},{15,13... | collective-permute-start | bytes 1376264 | tf_op jit(solution)/shard_map/ppermute | solution.py:341
  23.9 8.4 %collective-permute-start.7 = (bf16[2,128,896]{2,1,0:T(8,128)(2,1)S(1)}, bf16[2,128,896]{2,1,0:T(8,128)(2,1)S(1)}, u32[]{:S(2)}, u32[]{:S(2)}) collective-permute-start(bf16[2,128,896]{2,1,0:T(8,128)(2,1)S(1)} %collective-permute-done.6.refs_14_), channel_id=1, source_target_pairs={{0,1},{1,0},{2,3},{3,2},{4,5},{5,4},{6,7},{7,6},{8,9},{9,8},{10,11... | collective-permute-start | bytes 1376264 | tf_op jit(solution)/shard_map/ppermute | solution.py:342
  27.4 4.9 %collective-permute-start.9 = (bf16[2,128,896]{2,1,0:T(8,128)(2,1)S(1)}, bf16[2,128,896]{2,1,0:T(8,128)(2,1)S(1)}, u32[]{:S(2)}, u32[]{:S(2)}) collective-permute-start(bf16[2,128,896]{2,1,0:T(8,128)(2,1)S(1)} %collective-permute-done.8.refs_16_), channel_id=1, source_target_pairs={{0,1},{1,0},{2,3},{3,2},{4,5},{5,4},{6,7},{7,6},{8,9},{9,8},{10,11... | collective-permute-start | bytes 1376264 | tf_op jit(solution)/shard_map/ppermute | solution.py:342
  27.4 9.8 %collective-permute-start.12 = (bf16[2,128,896]{2,1,0:T(8,128)(2,1)S(1)}, bf16[2,128,896]{2,1,0:T(8,128)(2,1)S(1)}, u32[]{:S(2)}, u32[]{:S(2)}) collective-permute-start(bf16[2,128,896]{2,1,0:T(8,128)(2,1)S(1)} %collective-permute-done.8.refs_16_), channel_id=1, source_target_pairs={{0,4},{1,3},{4,8},{5,1},{8,12},{9,5},{12,14},{13,9},{14,10},{15,13... | collective-permute-start | bytes 1376264 | tf_op jit(solution)/shard_map/ppermute | solution.py:341
  32.3 4.9 %collective-permute-start.11 = (bf16[2,128,896]{2,1,0:T(8,128)(2,1)S(1)}, bf16[2,128,896]{2,1,0:T(8,128)(2,1)S(1)}, u32[]{:S(2)}, u32[]{:S(2)}) collective-permute-start(bf16[2,128,896]{2,1,0:T(8,128)(2,1)S(1)} %collective-permute-done.10.refs_18_), channel_id=1, source_target_pairs={{0,1},{1,0},{2,3},{3,2},{4,5},{5,4},{6,7},{7,6},{8,9},{9,8},{10,11... | collective-permute-start | bytes 1376264 | tf_op jit(solution)/shard_map/ppermute | solution.py:342
  32.3 9.9 %copy-start.5 = (bf16[2,128,896]{2,1,0:T(8,128)(2,1)}, bf16[2,128,896]{2,1,0:T(8,128)(2,1)S(1)}, u32[]{:S(2)}) copy-start(bf16[2,128,896]{2,1,0:T(8,128)(2,1)S(1)} %collective-permute-done.7.refs_15_) | copy-start | bytes 1376260
  32.4 9.9 %copy-start.6 = (bf16[2,128,896]{2,1,0:T(8,128)(2,1)}, bf16[2,128,896]{2,1,0:T(8,128)(2,1)S(1)}, u32[]{:S(2)}) copy-start(bf16[2,128,896]{2,1,0:T(8,128)(2,1)S(1)} %collective-permute-done.9.refs_17_) | copy-start | bytes 1376260
  32.4 9.9 %collective-permute-start.13 = (bf16[2,128,896]{2,1,0:T(8,128)(2,1)S(1)}, bf16[2,128,896]{2,1,0:T(8,128)(2,1)}, u32[]{:S(2)}, u32[]{:S(2)}) collective-permute-start(bf16[2,128,896]{2,1,0:T(8,128)(2,1)S(1)} %collective-permute-done.10.refs_18_), channel_id=1, source_target_pairs={{0,4},{1,3},{4,8},{5,1},{8,12},{9,5},{12,14},{13,9},{14,10},{15,13... | collective-permute-start | bytes 1376264 | tf_op jit(solution)/shard_map/ppermute | solution.py:347
  37.3 5.5 %copy-start.7 = (bf16[2,128,896]{2,1,0:T(8,128)(2,1)}, bf16[2,128,896]{2,1,0:T(8,128)(2,1)S(1)}, u32[]{:S(2)}) copy-start(bf16[2,128,896]{2,1,0:T(8,128)(2,1)S(1)} %collective-permute-done.11.refs_19_) | copy-start | bytes 1376260
  42.3 1.9 %collective-permute-start.14 = (bf16[2,128,896]{2,1,0:T(8,128)(2,1)S(1)}, bf16[2,128,896]{2,1,0:T(8,128)(2,1)}, u32[]{:S(2)}, u32[]{:S(2)}) collective-permute-start(bf16[2,128,896]{2,1,0:T(8,128)(2,1)S(1)} %collective-permute-done.12.refs_20_), channel_id=1, source_target_pairs={{0,1},{1,0},{2,3},{3,2},{4,5},{5,4},{6,7},{7,6},{8,9},{9,8},{10,11... | collective-permute-start | bytes 1376264 | tf_op jit(solution)/shard_map/ppermute | solution.py:349
  42.3 2.8 %collective-permute-start.15 = (bf16[2,128,896]{2,1,0:T(8,128)(2,1)}, bf16[2,128,896]{2,1,0:T(8,128)(2,1)}, u32[]{:S(2)}, u32[]{:S(2)}) collective-permute-start(bf16[2,128,896]{2,1,0:T(8,128)(2,1)} %collective-permute-done.13.refs_22_), channel_id=1, source_target_pairs={{0,1},{1,0},{2,3},{3,2},{4,5},{5,4},{6,7},{7,6},{8,9},{9,8},{10,11... | collective-permute-start | bytes 1376264 | tf_op jit(solution)/shard_map/ppermute | solution.py:350

commit v15 on v13

--- a/solution.py
+++ b/solution.py
@@ -15,6 +15,7 @@
 SCALE = math.log2(math.e) / math.sqrt(HEAD_DIM)
 CORES = 2
 GROUP = 4
+FOLDS = 2
 MIB = 2**20
 
 
@@ -44,23 +45,23 @@
     return pl.ds(group * GROUP * HEAD_DIM, GROUP * HEAD_DIM)
 
 
-def fold_kernel(query_hbm, key_hbm, folded_hbm, single_ref, query, key, folded, in_sems, out_sems):
-    groups = HEADS // GROUP
+def fold_kernel(first, query_hbm, key_hbm, folded_hbm, single_ref, query, key, folded, in_sems, out_sems):
+    heads = folded.shape[0]
 
     def fetch(group):
-        columns = group_columns(group)
+        columns, held = group_columns(first // GROUP + group), group_columns(group)
         return (
-            pltpu.make_async_copy(query_hbm.at[:, columns], query.at[:, columns], in_sems.at[group, 0]),
-            pltpu.make_async_copy(key_hbm.at[:, columns], key.at[:, columns], in_sems.at[group, 1]),
+            pltpu.make_async_copy(query_hbm.at[:, columns], query.at[:, held], in_sems.at[group, 0]),
+            pltpu.make_async_copy(key_hbm.at[:, columns], key.at[:, held], in_sems.at[group, 1]),
         )
 
     def put(head):
         return pltpu.make_async_copy(folded.at[head], folded_hbm.at[head], out_sems.at[head])
 
-    for group in range(groups):
+    for group in range(heads // GROUP):
         for copy in fetch(group):
             copy.start()
-    for head in range(HEADS):
+    for head in range(heads):
         if head % GROUP == 0:
             for copy in fetch(head // GROUP):
                 copy.wait()
@@ -70,31 +71,31 @@
         single_ref[head : head + 1, :] = rows[:1]
         folded[head] = rows.astype(jnp.bfloat16)
         put(head).start()
-    for head in range(HEADS):
+    for head in range(heads):
         put(head).wait()
 
 
-def fold(queries, w_key):
+def fold(first, heads, queries, w_key):
     count, width = queries.shape[0], w_key.shape[0]
-    shape = (HEADS, count, width)
+    shape, columns = (heads, count, width), heads * HEAD_DIM
     return pl.pallas_call(
-        fold_kernel,
+        functools.partial(fold_kernel, first),
         out_shape=(
             pltpu.HBM(shape, jnp.bfloat16),
-            jax.ShapeDtypeStruct((HEADS, width), jnp.float32),
+            jax.ShapeDtypeStruct((heads, width), jnp.float32),
         ),
         in_specs=[HBM_SPEC] * 2,
         out_specs=(HBM_SPEC, VMEM_SPEC),
         scratch_shapes=[
-            pltpu.VMEM(queries.shape, jnp.bfloat16),
-            pltpu.VMEM(w_key.shape, jnp.bfloat16),
+            pltpu.VMEM((count, columns), jnp.bfloat16),
+            pltpu.VMEM((width, columns), jnp.bfloat16),
             pltpu.VMEM(shape, jnp.bfloat16),
-            pltpu.SemaphoreType.DMA((HEADS // GROUP, 2)),
-            pltpu.SemaphoreType.DMA((HEADS,)),
+            pltpu.SemaphoreType.DMA((heads // GROUP, 2)),
+            pltpu.SemaphoreType.DMA((heads,)),
         ],
-        compiler_params=pltpu.CompilerParams(vmem_limit_bytes=28 * MIB),
+        compiler_params=pltpu.CompilerParams(vmem_limit_bytes=16 * MIB),
         cost_estimate=pl.CostEstimate(
-            flops=2 * queries.size * width, bytes_accessed=12 * MIB, transcendentals=0
+            flops=2 * count * columns * width, bytes_accessed=6 * MIB, transcendentals=0
         ),
         name="fold_queries",
     )(in_hbm(queries), in_hbm(w_key))
@@ -139,7 +140,8 @@
 
 
 def attend_kernel(size, *refs):
-    plan_refs, (starts_ref, folded_hbm, single_ref, value_hbm, *rest) = refs[:4], refs[4:]
+    plan_refs, (starts_ref, *folds, value_hbm) = refs[:4], refs[4 : 6 + 2 * FOLDS]
+    rest = refs[6 + 2 * FOLDS :]
     *stores, out_hbm, tokens, raw, folded, value, scores, weights, mixed, out, sems, group_sems = rest
     requests, length, width = raw.shape
     blocks = requests // 2 - 1
@@ -153,9 +155,12 @@
         return pltpu.make_async_copy(store.at[block], raw.at[request], sems.at[request])
 
     def fetch_group(group):
-        heads, columns = group_heads(group), group_columns(group)
+        columns = group_columns(group)
+        piece, place = divmod(group, groups // FOLDS)
         return (
-            pltpu.make_async_copy(folded_hbm.at[heads], folded.at[heads], group_sems.at[group, 0]),
+            pltpu.make_async_copy(
+                folds[piece].at[group_heads(place)], folded.at[group_heads(group)], group_sems.at[group, 0]
+            ),
             pltpu.make_async_copy(value_hbm.at[:, columns], value.at[:, columns], group_sems.at[group, 1]),
         )
 
@@ -188,6 +193,9 @@
         for request in (2 * window, 2 * window + 1):
             normalise(raw[request], tokens.at[request])
 
+    def single_rows():
+        return jnp.concatenate([single_ref[...] for single_ref in folds[FOLDS:]], axis=0).astype(jnp.bfloat16)
+
     def along(window):
         return tokens[2 * window : 2 * window + 2].reshape(2 * length, width)
 
@@ -202,32 +210,37 @@
     def score(unit):
         window = units[unit][1]
         if window == lone_window:
-            lone["scores"] = contract(single_ref[...].astype(jnp.bfloat16), along(window), ((1,), (1,)))
+            lone["scores"] = contract(single_rows(), along(window), ((1,), (1,)))
             return
         slot, heads, rows = place_of(unit)
         taken = folded[heads, rows].reshape(rows_at_once, width)
         scores[slot] = contract(taken, along(window), ((1,), (1,)))
 
-    def soften(unit):
+    parts = GROUP
+    tile = -(-width // (parts * 128)) * 128
+
+    def soften(unit, part):
         if units[unit][1] == lone_window:
-            lone["weights"] = weigh(lone["scores"])
+            if part == 0:
+                lone["weights"] = weigh(lone["scores"])
             return
         slot, _, _ = place_of(unit)
-        for part in range(GROUP):
-            rows = slice(part * SPAN, (part + 1) * SPAN)
-            weights[slot, rows] = weigh(scores[slot, rows])
-
-    def combine(unit):
+        rows = slice(part * SPAN, (part + 1) * SPAN)
+        weights[slot, rows] = weigh(scores[slot, rows])
+
+    def combine(unit, part):
         window = units[unit][1]
+        columns = slice(part * tile, min(width, (part + 1) * tile))
+        keys = tokens[2 * window : 2 * window + 2, :, columns].reshape(2 * length, columns.stop - columns.start)
         if window == lone_window:
-            lone["sums"] = contract(lone["weights"], along(window), ((1,), (0,)))
+            lone["sums", part] = contract(lone["weights"], keys, ((1,), (0,)))
             return
         slot, heads, rows = place_of(unit)
-        sums = contract(weights[slot], along(window), ((1,), (0,))).reshape(GROUP, SPAN, width)
+        sums = contract(weights[slot], keys, ((1,), (0,))).reshape(GROUP, SPAN, columns.stop - columns.start)
         if window == 0:
             first = lax.broadcasted_iota(jnp.int32, sums.shape, 1) == 0
-            sums = jnp.where(first, lone["sums"][heads][:, None, :], sums)
-        mixed[units[unit][0] % 2, :, rows] = sums.astype(jnp.bfloat16)
+            sums = jnp.where(first, lone["sums", part][heads][:, None, :], sums)
+        mixed[units[unit][0] % 2, :, rows, columns] = sums.astype(jnp.bfloat16)
 
     def project(group):
         for head in range(group * GROUP, (group + 1) * GROUP):
@@ -250,31 +263,37 @@
             ready(order[step + 1])
         if step < len(units):
             score(step)
-        if step >= 2:
-            combine(step - 2)
-        if 1 <= step <= len(units):
-            soften(step - 1)
+        for part in range(parts):
+            if 1 <= step <= len(units):
+                soften(step - 1, part)
+            if step >= 2:
+                combine(step - 2, part)
         if step >= 2 and units[step - 2][1] == order[-1]:
             project(units[step - 2][0])
     for group in range(groups):
         put(group).wait()
 
 
-def attend(size, plan, doc_starts, folded, single, w_value, stores):
+def attend(size, plan, doc_starts, folds, w_value, stores):
+    folded, single = zip(*folds)
     requests = plan[-1].size + 2
     length, width = stores[0].shape[1:]
-    count = folded.shape[1]
+    count = folded[0].shape[1]
     groups = HEADS // GROUP
     model_width = w_value.shape[1]
     return pl.pallas_call(
         functools.partial(attend_kernel, size),
         out_shape=jax.ShapeDtypeStruct((count, model_width), jnp.bfloat16),
-        in_specs=[SMEM_SPEC] * 5 + [HBM_SPEC, VMEM_SPEC, HBM_SPEC] + [ANY_SPEC] * len(stores),
+        in_specs=[SMEM_SPEC] * 5
+        + [HBM_SPEC] * FOLDS
+        + [VMEM_SPEC] * FOLDS
+        + [HBM_SPEC]
+        + [ANY_SPEC] * len(stores),
         out_specs=HBM_SPEC,
         scratch_shapes=[
             pltpu.VMEM((requests, length, width), jnp.bfloat16),
             pltpu.VMEM((requests, length, width), jnp.bfloat16),
-            pltpu.VMEM(folded.shape, jnp.bfloat16),
+            pltpu.VMEM((HEADS, count, width), jnp.bfloat16),
             pltpu.VMEM(w_value.shape, jnp.bfloat16),
             pltpu.VMEM((5, GROUP * SPAN, 2 * length), jnp.float32),
             pltpu.VMEM((5, GROUP * SPAN, 2 * length), jnp.bfloat16),
@@ -290,7 +309,7 @@
             transcendentals=HEADS * count * 2 * length,
         ),
         name="attend_windows",
-    )(*plan, doc_starts, in_hbm(folded), single, in_hbm(w_value), *stores)
+    )(*plan, doc_starts, *map(in_hbm, folded), *single, in_hbm(w_value), *stores)
 
 
 def chip_ring(mesh):
@@ -324,28 +343,30 @@
     wanted = (retrieval_owner * stored + retrieval_slot).T
     chains = [neighbours, swapped(neighbours)]
     stores = [neighbours, in_hbm(chains[1])]
-    folded, single = fold(*after([queries], [chains[1]]), w_key)
-
-    beside = {(1, 0): [folded, single]}
+    half = HEADS // FOLDS
+    folds = [fold(0, half, *after([queries], [chains[1]]), w_key)]
+
+    asked = after([wanted], folds[0][1:])[0]
+    before = lax.ppermute(asked, "seq", [(i, i + 1) for i in range(devices - 1)])
+    beside = {(1, 0): folds[0], (1, 1): [before]}
     for step in range(reach):
         for chain in range(2):
-            others = beside.get((step, chain), []) + (stores[2 * chain + 4 * step - 5 :][:1] if step > 1 else [])
+            others = list(beside.get((step, chain), ())) + (stores[2 * chain + 4 * step - 5 :][:1] if step > 1 else [])
             sent = after([chains[chain]], others) if others else [chains[chain]]
             chains[chain] = onwards(sent[0])
             stores += [chains[chain], in_hbm(swapped(chains[chain]))]
             if (step, chain) == (0, 1):
-                asked = after([wanted], [chains[1]])[0]
-                before = lax.ppermute(asked, "seq", [(i, i + 1) for i in range(devices - 1)])
-                beside[2, 0] = [before]
+                folds += [fold(part * half, half, *after([queries], [chains[1]]), w_key) for part in range(1, FOLDS)]
+                beside[2, 0] = [value for part in folds[1:] for value in part]
     places = jnp.asarray([ring.index(chip) for chip in range(size)], jnp.int32)
     plan = [lax.axis_index("seq").reshape(1), places, before, wanted]
     if size % 2 == 0:
-        sent = after([chains[0]], stores[-7:-4:2]) if reach > 1 else [chains[0]]
+        sent = after([chains[0]], [before, *stores[-7:-4:2]]) if reach > 1 else [chains[0]]
         last = onwards(sent[0])
         if reach:
             stores[-1] = swapped(after([chains[1]], [last, stores[-3]])[0])
         stores += [last, swapped(last)]
-    return attend(size, plan, doc_starts, folded, single, w_value, stores)
+    return attend(size, plan, doc_starts, folds, w_value, stores)
 
 
 def solution(mesh):

time: 59.5 us -> 61.1 us (1.027)
  Pallas kernels: 18.2 us -> 20.1 us
  waiting for transfers between devices: 17 us -> 16.1 us
  local copies, waits for them, and re-layouts: 0.09 us -> 0.84 us
  starting transfers between devices: 23.5 us -> 22.8 us
  other arithmetic: 0.01 us -> 0.7 us
    pallas_call x1 -> x2, Pallas kernels: 5.05 us -> 7.23 us  [fold(): pl.pallas_call(functools.partial(fold_kernel, first), out_shape=(pltpu.HB...]
    ppermute x6, waiting for transfers between devices: 9.8 us -> 7.95 us  [body(): chains[chain] = onwards(sent[0])]
    ppermute x1, starting transfers between devices: 2.54 us -> 1.62 us  [body(): last = onwards(sent[0])]
    ppermute x5, starting transfers between devices: 1.34 us -> 0.52 us  [body(): stores += [chains[chain], in_hbm(swapped(chains[chain]))]]
    ppermute x1, waiting for transfers between devices: 0.01 us -> 0.8 us  [body(): lax.ppermute(asked, 'seq', [(i, i + 1) for i in range(devices - 1)])]
    ppermute x1, starting transfers between devices: 1.29 us -> 2.06 us  [body(): lax.ppermute(asked, 'seq', [(i, i + 1) for i in range(devices - 1)])]
    unnamed x20 -> x16, local copies, waits for them, and re-layouts: 0.09 us -> 0.84 us
    transpose x1, other arithmetic: 0.01 us -> 0.7 us  [body(): wanted = (retrieval_owner * stored + retrieval_slot).T]
  transfers between devices with their start and end apart: 16 -> 16, of which waited for: 7 -> 7; matrix products, arithmetic and copies ran while one was open for 0% -> 1% of each run, Pallas kernels for 9% -> 12%
where the time goes in v15:
time: 61.1 us; the launch traced here: 60.8 us
  starting transfers between devices  22.8 us (37%)
  Pallas kernels  20.1 us (33%)
  waiting for transfers between devices  16.1 us (26%)
  local copies, waits for them, and re-layouts  0.84 us (1%)
  other arithmetic  0.7 us (1%)
    ppermute x6, starting transfers between devices, body(): chains[chain] = onwards(sent[0])  17.6 us
    pallas_call x1, Pallas kernels, attend(): pl.pallas_call(functools.partial(attend_kernel, size), out_shape=jax.Shap...  12.9 us
    ppermute x6, waiting for transfers between devices, body(): chains[chain] = onwards(sent[0])  7.95 us
    pallas_call x2, Pallas kernels, fold(): pl.pallas_call(functools.partial(fold_kernel, first), out_shape=(pltpu.HB...  7.23 us
    ppermute x1, waiting for transfers between devices, body(): last = onwards(sent[0])  5.02 us
    ppermute x1, starting transfers between devices, body(): lax.ppermute(asked, 'seq', [(i, i + 1) for i in range(devices - 1)])  2.06 us
    ppermute x1, starting transfers between devices, body(): last = onwards(sent[0])  1.62 us
    ppermute x1, waiting for transfers between devices, body(): stores[-1] = swapped(after([chains[1]], [last, stores[-3]])[0])  1.43 us
  transfers between devices with their start and end apart: 16, of which 7 were waited for; matrix products, arithmetic and copies ran while one was open for 1% of the time, Pallas kernels for 12%

profile of v15, /device:TPU:0, one launch (start us, length us, event | category | flops | bytes accessed | tf_op | source)
XLA Modules:
  0.0 60.8 jit_solution(15062060551287359291)
XLA Ops:
  0.0 0.5 collective-permute-start
  0.5 2.6 %collective-permute-start.3 = (bf16[2,128,896]{2,1,0:T(8,128)(2,1)}, bf16[2,128,896]{2,1,0:T(8,128)(2,1)S(1)}, u32[]{:S(2)}, u32[]{:S(2)}) collective-permute-start(bf16[2,128,896]{2,1,0:T(8,128)(2,1)} %refs_10_.1), channel_id=1, source_target_pairs={{0,4},{1,3},{4,8},{5,1},{8,12},{9,5},{12,14},{13,9},{14,10},{15,13... | collective-permute-start | bytes 1376264 | tf_op jit(solution)/shard_map/ppermute | solution.py:356
  3.0 0.0 collective-permute-done.refs_11_
  3.0 0.0 copy-start.3
  3.0 2.0 %collective-permute-start.2 = (bf16[2,128,896]{2,1,0:T(8,128)(2,1)S(1)}, bf16[2,128,896]{2,1,0:T(8,128)(2,1)S(1)}, u32[]{:S(2)}, u32[]{:S(2)}) collective-permute-start(bf16[2,128,896]{2,1,0:T(8,128)(2,1)S(1)} %collective-permute-done.refs_11_), channel_id=1, source_target_pairs={{0,4},{1,3},{4,8},{5,1},{8,12},{9,5},{12,14},{13,9},{14,10},{15,13... | collective-permute-start | bytes 1376264 | tf_op jit(solution)/shard_map/ppermute | solution.py:356
  5.1 0.7 %add_bitcast_fusion.refs_3_ = s32[2,4]{1,0:T(2,128)S(1)} fusion(s32[4,2]{0,1:T(2,128)} %param.13, s32[4,2]{0,1:T(2,128)} %param.12), kind=kLoop, calls=%fused_computation | loop fusion | flops 16 | bytes 96 | tf_op jit(solution)/shard_map/transpose | solution.py:343
  5.8 0.0 copy-start
  5.8 3.6 %fold_queries.2 = (bf16[8,256,896]{2,1,0:T(8,128)(2,1)}, f32[8,896]{1,0:T(8,128)S(1)}) custom-call(bf16[256,2048]{1,0:T(8,128)(2,1)} %query_hbm.1, bf16[896,2048]{1,0:T(8,128)(2,1)} %key_hbm.3), custom_call_target="tpu_custom_call" | custom-call | flops 469762048 | bytes 6291456 | tf_op jit(solution)/shard_map/fold_queries/pallas_call | solution.py:81
  9.4 0.2 collective-permute-done.3.refs_12_
  9.6 0.0 collective-permute-start.4
  9.6 2.1 %collective-permute-start.6 = (bf16[2,128,896]{2,1,0:T(8,128)(2,1)S(1)}, bf16[2,128,896]{2,1,0:T(8,128)(2,1)S(1)}, u32[]{:S(2)}, u32[]{:S(2)}) collective-permute-start(bf16[2,128,896]{2,1,0:T(8,128)(2,1)S(1)} %collective-permute-done.3.refs_12_), channel_id=1, source_target_pairs={{0,4},{1,3},{4,8},{5,1},{8,12},{9,5},{12,14},{13,9},{14,10},{15,13... | collective-permute-start | bytes 1376264 | tf_op jit(solution)/shard_map/ppermute | solution.py:356
  11.7 2.1 %collective-permute-start.1 = (s32[2,4]{1,0:T(2,128)S(1)}, s32[2,4]{1,0:T(2,128)S(1)}, u32[]{:S(2)}, u32[]{:S(2)}) collective-permute-start(s32[2,4]{1,0:T(2,128)S(1)} %add_bitcast_fusion.refs_3_), channel_id=1, source_target_pairs={{0,1},{1,2},{2,3},{3,4},{4,5},{5,6},{6,7},{7,8},{8,9},{9,10},{10,1... | collective-permute-start | bytes 104 | tf_op jit(solution)/shard_map/ppermute | solution.py:350
  13.8 0.8 %collective-permute-done.1.refs_2_ = s32[2,4]{1,0:T(2,128)S(1)} collective-permute-done((s32[2,4]{1,0:T(2,128)S(1)}, s32[2,4]{1,0:T(2,128)S(1)}, u32[]{:S(2)}, u32[]{:S(2)}) %collective-permute-start.1) | collective-permute-done | bytes 64 | tf_op jit(solution)/shard_map/ppermute | solution.py:350
  14.6 0.0 copy-done.3
  14.6 0.0 collective-permute-done.2.refs_14_
  14.6 7.5 %collective-permute-start.8 = (bf16[2,128,896]{2,1,0:T(8,128)(2,1)S(1)}, bf16[2,128,896]{2,1,0:T(8,128)(2,1)S(1)}, u32[]{:S(2)}, u32[]{:S(2)}) collective-permute-start(bf16[2,128,896]{2,1,0:T(8,128)(2,1)S(1)} %collective-permute-done.2.refs_14_), channel_id=1, source_target_pairs={{0,4},{1,3},{4,8},{5,1},{8,12},{9,5},{12,14},{13,9},{14,10},{15,13... | collective-permute-start | bytes 1376264 | tf_op jit(solution)/shard_map/ppermute | solution.py:356
  22.1 0.0 collective-permute-start.5
  22.1 3.6 %fold_queries.3 = (bf16[8,256,896]{2,1,0:T(8,128)(2,1)}, f32[8,896]{1,0:T(8,128)S(1)}) custom-call(bf16[256,2048]{1,0:T(8,128)(2,1)} %query_hbm.1, bf16[896,2048]{1,0:T(8,128)(2,1)} %key_hbm.3), custom_call_target="tpu_custom_call" | custom-call | flops 469762048 | bytes 6291456 | tf_op jit(solution)/shard_map/fold_queries/pallas_call | solution.py:81
  25.7 0.0 collective-permute-done.4.refs_13_
  25.7 0.0 copy-start.4
  25.7 0.0 collective-permute-done.6.refs_16_
  25.7 0.8 %copy-done.4 = bf16[2,128,896]{2,1,0:T(8,128)(2,1)} copy-done((bf16[2,128,896]{2,1,0:T(8,128)(2,1)}, bf16[2,128,896]{2,1,0:T(8,128)(2,1)S(1)}, u32[]{:S(2)}) %copy-start.4) | copy-done | bytes 458776
  26.5 1.6 %collective-permute-start.10 = (bf16[2,128,896]{2,1,0:T(8,128)(2,1)S(1)}, bf16[2,128,896]{2,1,0:T(8,128)(2,1)S(1)}, u32[]{:S(2)}, u32[]{:S(2)}) collective-permute-start(bf16[2,128,896]{2,1,0:T(8,128)(2,1)S(1)} %collective-permute-done.6.refs_16_), channel_id=1, source_target_pairs={{0,4},{1,3},{4,8},{5,1},{8,12},{9,5},{12,14},{13,9},{14,10},{15,13... | collective-permute-start | bytes 1376264 | tf_op jit(solution)/shard_map/ppermute | solution.py:356
  28.1 0.0 collective-permute-start.7
  28.1 0.0 collective-permute-done.8.refs_18_
  28.1 0.5 collective-permute-start.9
  28.6 0.0 collective-permute-done.5.refs_15_
  28.6 1.9 %collective-permute-start.12 = (bf16[2,128,896]{2,1,0:T(8,128)(2,1)S(1)}, bf16[2,128,896]{2,1,0:T(8,128)(2,1)S(1)}, u32[]{:S(2)}, u32[]{:S(2)}) collective-permute-start(bf16[2,128,896]{2,1,0:T(8,128)(2,1)S(1)} %collective-permute-done.8.refs_18_), channel_id=1, source_target_pairs={{0,4},{1,3},{4,8},{5,1},{8,12},{9,5},{12,14},{13,9},{14,10},{15,13... | collective-permute-start | bytes 1376264 | tf_op jit(solution)/shard_map/ppermute | solution.py:356
  30.5 4.4 %collective-permute-done.10.refs_20_ = bf16[2,128,896]{2,1,0:T(8,128)(2,1)S(1)} collective-permute-done((bf16[2,128,896]{2,1,0:T(8,128)(2,1)S(1)}, bf16[2,128,896]{2,1,0:T(8,128)(2,1)S(1)}, u32[]{:S(2)}, u32[]{:S(2)}) %collective-permute-start.10) | collective-permute-done | bytes 458784 | tf_op jit(solution)/shard_map/ppermute | solution.py:356
  35.0 0.0 collective-permute-start.11
  35.0 0.0 collective-permute-done.7.refs_17_
  35.0 0.0 collective-permute-done.9.refs_19_
  35.0 0.0 copy-start.6
  35.0 1.6 %collective-permute-start.13 = (bf16[2,128,896]{2,1,0:T(8,128)(2,1)S(1)}, bf16[2,128,896]{2,1,0:T(8,128)(2,1)}, u32[]{:S(2)}, u32[]{:S(2)}) collective-permute-start(bf16[2,128,896]{2,1,0:T(8,128)(2,1)S(1)} %collective-permute-done.10.refs_20_), channel_id=1, source_target_pairs={{0,4},{1,3},{4,8},{5,1},{8,12},{9,5},{12,14},{13,9},{14,10},{15,13... | collective-permute-start | bytes 1376264 | tf_op jit(solution)/shard_map/ppermute | solution.py:365
  36.6 3.3 %collective-permute-done.12.refs_22_ = bf16[2,128,896]{2,1,0:T(8,128)(2,1)S(1)} collective-permute-done((bf16[2,128,896]{2,1,0:T(8,128)(2,1)S(1)}, bf16[2,128,896]{2,1,0:T(8,128)(2,1)S(1)}, u32[]{:S(2)}, u32[]{:S(2)}) %collective-permute-start.12) | collective-permute-done | bytes 458784 | tf_op jit(solution)/shard_map/ppermute | solution.py:356
  39.9 0.0 collective-permute-done.11.refs_21_
  39.9 5.0 %collective-permute-done.13.refs_24_ = bf16[2,128,896]{2,1,0:T(8,128)(2,1)} collective-permute-done((bf16[2,128,896]{2,1,0:T(8,128)(2,1)S(1)}, bf16[2,128,896]{2,1,0:T(8,128)(2,1)}, u32[]{:S(2)}, u32[]{:S(2)}) %collective-permute-start.13) | collective-permute-done | bytes 458784 | tf_op jit(solution)/shard_map/ppermute | solution.py:365
  44.9 0.0 copy-done.5
  44.9 0.0 collective-permute-start.14
  44.9 0.0 copy-done.6
  44.9 0.5 collective-permute-start.15
  45.4 0.0 copy-done.7
  45.4 1.4 %collective-permute-done.14.refs_23_ = bf16[2,128,896]{2,1,0:T(8,128)(2,1)} collective-permute-done((bf16[2,128,896]{2,1,0:T(8,128)(2,1)S(1)}, bf16[2,128,896]{2,1,0:T(8,128)(2,1)}, u32[]{:S(2)}, u32[]{:S(2)}) %collective-permute-start.14) | collective-permute-done | bytes 458784 | tf_op jit(solution)/shard_map/ppermute | solution.py:367
  46.9 0.9 %collective-permute-done.15.refs_25_ = bf16[2,128,896]{2,1,0:T(8,128)(2,1)} collective-permute-done((bf16[2,128,896]{2,1,0:T(8,128)(2,1)}, bf16[2,128,896]{2,1,0:T(8,128)(2,1)}, u32[]{:S(2)}, u32[]{:S(2)}) %collective-permute-start.15) | collective-permute-done | bytes 458784 | tf_op jit(solution)/shard_map/ppermute | solution.py:368
  47.7 0.0 copy-done
  47.8 0.0 copy-done.1
  47.8 0.0 copy-done.2
  47.8 12.9 %attend_windows.1 = bf16[256,2048]{1,0:T(8,128)(2,1)} custom-call(s32[1]{0:T(128)} %bitcast.refs_0_, s32[8]{0:T(128)S(1)} %copy-done.2, s32[2,4]{1,0:T(2,128)S(1)} %collective-permute-done.1.refs_2_, s32[2,4]{1,0:T(2,128)S(1)} %add_bitcast_fusion.refs_3_, s32[4]{0:T(128)S(1)} %copy-done.1, bf16[8,256,896]{2,1,0:T(8,128)(2,1)} %get-tuple-element.21.refs_5_, ...), custom_call_target="tpu_custom_call" | custom-call | flops 4697620480 | bytes 16777216 | tf_op jit(solution)/shard_map/attend_windows/pallas_call | solution.py:284
  (4 shorter events, 0.0 us)
Async XLA Ops:
  0.0 3.0 %collective-permute-start = (bf16[2,128,896]{2,1,0:T(8,128)(2,1)}, bf16[2,128,896]{2,1,0:T(8,128)(2,1)S(1)}, u32[]{:S(2)}, u32[]{:S(2)}) collective-permute-start(bf16[2,128,896]{2,1,0:T(8,128)(2,1)} %refs_10_.1), channel_id=1, source_target_pairs={{0,1},{1,0},{2,3},{3,2},{4,5},{5,4},{6,7},{7,6},{8,9},{9,8},{10,11... | collective-permute-start | bytes 1376264 | tf_op jit(solution)/shard_map/ppermute | solution.py:344
  0.5 9.2 %collective-permute-start.3 = (bf16[2,128,896]{2,1,0:T(8,128)(2,1)}, bf16[2,128,896]{2,1,0:T(8,128)(2,1)S(1)}, u32[]{:S(2)}, u32[]{:S(2)}) collective-permute-start(bf16[2,128,896]{2,1,0:T(8,128)(2,1)} %refs_10_.1), channel_id=1, source_target_pairs={{0,4},{1,3},{4,8},{5,1},{8,12},{9,5},{12,14},{13,9},{14,10},{15,13... | collective-permute-start | bytes 1376264 | tf_op jit(solution)/shard_map/ppermute | solution.py:356
  3.0 11.6 %copy-start.3 = (bf16[2,128,896]{2,1,0:T(8,128)(2,1)}, bf16[2,128,896]{2,1,0:T(8,128)(2,1)S(1)}, u32[]{:S(2)}) copy-start(bf16[2,128,896]{2,1,0:T(8,128)(2,1)S(1)} %collective-permute-done.refs_11_) | copy-start | bytes 1376260
  3.0 11.6 %collective-permute-start.2 = (bf16[2,128,896]{2,1,0:T(8,128)(2,1)S(1)}, bf16[2,128,896]{2,1,0:T(8,128)(2,1)S(1)}, u32[]{:S(2)}, u32[]{:S(2)}) collective-permute-start(bf16[2,128,896]{2,1,0:T(8,128)(2,1)S(1)} %collective-permute-done.refs_11_), channel_id=1, source_target_pairs={{0,4},{1,3},{4,8},{5,1},{8,12},{9,5},{12,14},{13,9},{14,10},{15,13... | collective-permute-start | bytes 1376264 | tf_op jit(solution)/shard_map/ppermute | solution.py:356
  5.8 42.0 %copy-start = (bf16[2,128,896]{2,1,0:T(8,128)(2,1)S(1)}, bf16[2,128,896]{2,1,0:T(8,128)(2,1)}, u32[]{:S(2)}) copy-start(bf16[2,128,896]{2,1,0:T(8,128)(2,1)} %refs_10_.1) | copy-start | bytes 1376260
  5.8 42.0 %copy-start.1 = (s32[4]{0:T(128)S(1)}, s32[4]{0:T(128)}, u32[]{:S(2)}) copy-start(s32[4]{0:T(128)} %refs_4_.1) | copy-start | bytes 52
  5.8 42.0 %copy-start.2 = (s32[8]{0:T(128)S(1)}, s32[8]{0:T(128)}, u32[]{:S(2)}) copy-start(s32[8]{0:T(128)} %constant.8.clone.refs_1_) | copy-start | bytes 100
  9.6 16.0 %collective-permute-start.4 = (bf16[2,128,896]{2,1,0:T(8,128)(2,1)S(1)}, bf16[2,128,896]{2,1,0:T(8,128)(2,1)S(1)}, u32[]{:S(2)}, u32[]{:S(2)}) collective-permute-start(bf16[2,128,896]{2,1,0:T(8,128)(2,1)S(1)} %collective-permute-done.3.refs_12_), channel_id=1, source_target_pairs={{0,1},{1,0},{2,3},{3,2},{4,5},{5,4},{6,7},{7,6},{8,9},{9,8},{10,11... | collective-permute-start | bytes 1376264 | tf_op jit(solution)/shard_map/ppermute | solution.py:357
  9.6 16.1 %collective-permute-start.6 = (bf16[2,128,896]{2,1,0:T(8,128)(2,1)S(1)}, bf16[2,128,896]{2,1,0:T(8,128)(2,1)S(1)}, u32[]{:S(2)}, u32[]{:S(2)}) collective-permute-start(bf16[2,128,896]{2,1,0:T(8,128)(2,1)S(1)} %collective-permute-done.3.refs_12_), channel_id=1, source_target_pairs={{0,4},{1,3},{4,8},{5,1},{8,12},{9,5},{12,14},{13,9},{14,10},{15,13... | collective-permute-start | bytes 1376264 | tf_op jit(solution)/shard_map/ppermute | solution.py:356
  11.7 2.9 %collective-permute-start.1 = (s32[2,4]{1,0:T(2,128)S(1)}, s32[2,4]{1,0:T(2,128)S(1)}, u32[]{:S(2)}, u32[]{:S(2)}) collective-permute-start(s32[2,4]{1,0:T(2,128)S(1)} %add_bitcast_fusion.refs_3_), channel_id=1, source_target_pairs={{0,1},{1,2},{2,3},{3,4},{4,5},{5,6},{6,7},{7,8},{8,9},{9,10},{10,1... | collective-permute-start | bytes 104 | tf_op jit(solution)/shard_map/ppermute | solution.py:350
  14.6 13.5 %collective-permute-start.8 = (bf16[2,128,896]{2,1,0:T(8,128)(2,1)S(1)}, bf16[2,128,896]{2,1,0:T(8,128)(2,1)S(1)}, u32[]{:S(2)}, u32[]{:S(2)}) collective-permute-start(bf16[2,128,896]{2,1,0:T(8,128)(2,1)S(1)} %collective-permute-done.2.refs_14_), channel_id=1, source_target_pairs={{0,4},{1,3},{4,8},{5,1},{8,12},{9,5},{12,14},{13,9},{14,10},{15,13... | collective-permute-start | bytes 1376264 | tf_op jit(solution)/shard_map/ppermute | solution.py:356
  22.1 6.5 %collective-permute-start.5 = (bf16[2,128,896]{2,1,0:T(8,128)(2,1)S(1)}, bf16[2,128,896]{2,1,0:T(8,128)(2,1)}, u32[]{:S(2)}, u32[]{:S(2)}) collective-permute-start(bf16[2,128,896]{2,1,0:T(8,128)(2,1)S(1)} %collective-permute-done.2.refs_14_), channel_id=1, source_target_pairs={{0,1},{1,0},{2,3},{3,2},{4,5},{5,4},{6,7},{7,6},{8,9},{9,8},{10,11... | collective-permute-start | bytes 1376264 | tf_op jit(solution)/shard_map/ppermute | solution.py:357
  25.7 0.8 %copy-start.4 = (bf16[2,128,896]{2,1,0:T(8,128)(2,1)}, bf16[2,128,896]{2,1,0:T(8,128)(2,1)S(1)}, u32[]{:S(2)}) copy-start(bf16[2,128,896]{2,1,0:T(8,128)(2,1)S(1)} %collective-permute-done.4.refs_13_) | copy-start | bytes 1376260
  26.5 8.5 %collective-permute-start.10 = (bf16[2,128,896]{2,1,0:T(8,128)(2,1)S(1)}, bf16[2,128,896]{2,1,0:T(8,128)(2,1)S(1)}, u32[]{:S(2)}, u32[]{:S(2)}) collective-permute-start(bf16[2,128,896]{2,1,0:T(8,128)(2,1)S(1)} %collective-permute-done.6.refs_16_), channel_id=1, source_target_pairs={{0,4},{1,3},{4,8},{5,1},{8,12},{9,5},{12,14},{13,9},{14,10},{15,13... | collective-permute-start | bytes 1376264 | tf_op jit(solution)/shard_map/ppermute | solution.py:356
  28.1 6.9 %collective-permute-start.7 = (bf16[2,128,896]{2,1,0:T(8,128)(2,1)S(1)}, bf16[2,128,896]{2,1,0:T(8,128)(2,1)S(1)}, u32[]{:S(2)}, u32[]{:S(2)}) collective-permute-start(bf16[2,128,896]{2,1,0:T(8,128)(2,1)S(1)} %collective-permute-done.6.refs_16_), channel_id=1, source_target_pairs={{0,1},{1,0},{2,3},{3,2},{4,5},{5,4},{6,7},{7,6},{8,9},{9,8},{10,11... | collective-permute-start | bytes 1376264 | tf_op jit(solution)/shard_map/ppermute | solution.py:357
  28.1 6.9 %collective-permute-start.9 = (bf16[2,128,896]{2,1,0:T(8,128)(2,1)S(1)}, bf16[2,128,896]{2,1,0:T(8,128)(2,1)S(1)}, u32[]{:S(2)}, u32[]{:S(2)}) collective-permute-start(bf16[2,128,896]{2,1,0:T(8,128)(2,1)S(1)} %collective-permute-done.8.refs_18_), channel_id=1, source_target_pairs={{0,1},{1,0},{2,3},{3,2},{4,5},{5,4},{6,7},{7,6},{8,9},{9,8},{10,11... | collective-permute-start | bytes 1376264 | tf_op jit(solution)/shard_map/ppermute | solution.py:357
  28.6 11.3 %collective-permute-start.12 = (bf16[2,128,896]{2,1,0:T(8,128)(2,1)S(1)}, bf16[2,128,896]{2,1,0:T(8,128)(2,1)S(1)}, u32[]{:S(2)}, u32[]{:S(2)}) collective-permute-start(bf16[2,128,896]{2,1,0:T(8,128)(2,1)S(1)} %collective-permute-done.8.refs_18_), channel_id=1, source_target_pairs={{0,4},{1,3},{4,8},{5,1},{8,12},{9,5},{12,14},{13,9},{14,10},{15,13... | collective-permute-start | bytes 1376264 | tf_op jit(solution)/shard_map/ppermute | solution.py:356
  35.0 4.9 %collective-permute-start.11 = (bf16[2,128,896]{2,1,0:T(8,128)(2,1)S(1)}, bf16[2,128,896]{2,1,0:T(8,128)(2,1)S(1)}, u32[]{:S(2)}, u32[]{:S(2)}) collective-permute-start(bf16[2,128,896]{2,1,0:T(8,128)(2,1)S(1)} %collective-permute-done.10.refs_20_), channel_id=1, source_target_pairs={{0,1},{1,0},{2,3},{3,2},{4,5},{5,4},{6,7},{7,6},{8,9},{9,8},{10,11... | collective-permute-start | bytes 1376264 | tf_op jit(solution)/shard_map/ppermute | solution.py:357
  35.0 9.9 %copy-start.5 = (bf16[2,128,896]{2,1,0:T(8,128)(2,1)}, bf16[2,128,896]{2,1,0:T(8,128)(2,1)S(1)}, u32[]{:S(2)}) copy-start(bf16[2,128,896]{2,1,0:T(8,128)(2,1)S(1)} %collective-permute-done.7.refs_17_) | copy-start | bytes 1376260
  35.0 9.9 %copy-start.6 = (bf16[2,128,896]{2,1,0:T(8,128)(2,1)}, bf16[2,128,896]{2,1,0:T(8,128)(2,1)S(1)}, u32[]{:S(2)}) copy-start(bf16[2,128,896]{2,1,0:T(8,128)(2,1)S(1)} %collective-permute-done.9.refs_19_) | copy-start | bytes 1376260
  35.0 9.9 %collective-permute-start.13 = (bf16[2,128,896]{2,1,0:T(8,128)(2,1)S(1)}, bf16[2,128,896]{2,1,0:T(8,128)(2,1)}, u32[]{:S(2)}, u32[]{:S(2)}) collective-permute-start(bf16[2,128,896]{2,1,0:T(8,128)(2,1)S(1)} %collective-permute-done.10.refs_20_), channel_id=1, source_target_pairs={{0,4},{1,3},{4,8},{5,1},{8,12},{9,5},{12,14},{13,9},{14,10},{15,13... | collective-permute-start | bytes 1376264 | tf_op jit(solution)/shard_map/ppermute | solution.py:365
  39.9 5.5 %copy-start.7 = (bf16[2,128,896]{2,1,0:T(8,128)(2,1)}, bf16[2,128,896]{2,1,0:T(8,128)(2,1)S(1)}, u32[]{:S(2)}) copy-start(bf16[2,128,896]{2,1,0:T(8,128)(2,1)S(1)} %collective-permute-done.11.refs_21_) | copy-start | bytes 1376260
  44.9 1.9 %collective-permute-start.14 = (bf16[2,128,896]{2,1,0:T(8,128)(2,1)S(1)}, bf16[2,128,896]{2,1,0:T(8,128)(2,1)}, u32[]{:S(2)}, u32[]{:S(2)}) collective-permute-start(bf16[2,128,896]{2,1,0:T(8,128)(2,1)S(1)} %collective-permute-done.12.refs_22_), channel_id=1, source_target_pairs={{0,1},{1,0},{2,3},{3,2},{4,5},{5,4},{6,7},{7,6},{8,9},{9,8},{10,11... | collective-permute-start | bytes 1376264 | tf_op jit(solution)/shard_map/ppermute | solution.py:367
  44.9 2.8 %collective-permute-start.15 = (bf16[2,128,896]{2,1,0:T(8,128)(2,1)}, bf16[2,128,896]{2,1,0:T(8,128)(2,1)}, u32[]{:S(2)}, u32[]{:S(2)}) collective-permute-start(bf16[2,128,896]{2,1,0:T(8,128)(2,1)} %collective-permute-done.13.refs_24_), channel_id=1, source_target_pairs={{0,1},{1,0},{2,3},{3,2},{4,5},{5,4},{6,7},{7,6},{8,9},{9,8},{10,11... | collective-permute-start | bytes 1376264 | tf_op jit(solution)/shard_map/ppermute | solution.py:368

commit v16 on v15

--- a/solution.py
+++ b/solution.py
@@ -355,16 +355,15 @@
             sent = after([chains[chain]], others) if others else [chains[chain]]
             chains[chain] = onwards(sent[0])
             stores += [chains[chain], in_hbm(swapped(chains[chain]))]
-            if (step, chain) == (0, 1):
-                folds += [fold(part * half, half, *after([queries], [chains[1]]), w_key) for part in range(1, FOLDS)]
-                beside[2, 0] = [value for part in folds[1:] for value in part]
     places = jnp.asarray([ring.index(chip) for chip in range(size)], jnp.int32)
     plan = [lax.axis_index("seq").reshape(1), places, before, wanted]
     if size % 2 == 0:
         sent = after([chains[0]], [before, *stores[-7:-4:2]]) if reach > 1 else [chains[0]]
         last = onwards(sent[0])
         if reach:
-            stores[-1] = swapped(after([chains[1]], [last, stores[-3]])[0])
+            folds += [fold(part * half, half, *after([queries], [chains[0]]), w_key) for part in range(1, FOLDS)]
+            others = [value for part in folds[1:] for value in part]
+            stores[-1] = swapped(after([chains[1]], [last, stores[-3], *others])[0])
         stores += [last, swapped(last)]
     return attend(size, plan, doc_starts, folds, w_value, stores)
 

time: 61.1 us -> 58.7 us (0.961)
  starting transfers between devices: 22.8 us -> 18.1 us
  local copies, waits for them, and re-layouts: 0.84 us -> 2.39 us
    ppermute x6, starting transfers between devices: 17.6 us -> 11.5 us  [body(): chains[chain] = onwards(sent[0])]
    ppermute x6, waiting for transfers between devices: 7.95 us -> 10.8 us  [body(): chains[chain] = onwards(sent[0])]
    ppermute x5, starting transfers between devices: 0.52 us -> 2.23 us  [body(): stores += [chains[chain], in_hbm(swapped(chains[chain]))]]
    ppermute x1, waiting for transfers between devices: 5.02 us -> 3.36 us  [body(): last = onwards(sent[0])]
    unnamed x16, local copies, waits for them, and re-layouts: 0.84 us -> 2.39 us
    ppermute x1, waiting for transfers between devices: 1.43 us -> 0.01 us  [body(): stores[-1] = swapped(after([chains[1]], [last, stores[-3], *others])[0])]
    ppermute x1, waiting for transfers between devices: 0.87 us -> 2.27 us  [body(): stores += [last, swapped(last)]]
    ppermute x1, waiting for transfers between devices: 0.8 us -> 0.01 us  [body(): lax.ppermute(asked, 'seq', [(i, i + 1) for i in range(devices - 1)])]
  transfers between devices with their start and end apart: 16 -> 16, of which waited for: 7 -> 6; matrix products, arithmetic and copies ran while one was open for 1% -> 1% of each run, Pallas kernels for 12% -> 12%
where the time goes in v16:
time: 58.7 us; the launch traced here: 58.1 us
  Pallas kernels  20.2 us (34%)
  starting transfers between devices  18.1 us (31%)
  waiting for transfers between devices  16.4 us (28%)
  local copies, waits for them, and re-layouts  2.39 us (4%)
  other arithmetic  0.7 us (1%)
    pallas_call x1, Pallas kernels, attend(): pl.pallas_call(functools.partial(attend_kernel, size), out_shape=jax.Shap...  12.9 us
    ppermute x6, starting transfers between devices, body(): chains[chain] = onwards(sent[0])  11.5 us
    ppermute x6, waiting for transfers between devices, body(): chains[chain] = onwards(sent[0])  10.8 us
    pallas_call x2, Pallas kernels, fold(): pl.pallas_call(functools.partial(fold_kernel, first), out_shape=(pltpu.HB...  7.24 us
    ppermute x1, waiting for transfers between devices, body(): last = onwards(sent[0])  3.36 us
    unnamed x16, local copies, waits for them, and re-layouts  2.39 us
    ppermute x1, waiting for transfers between devices, body(): stores += [last, swapped(last)]  2.27 us
    ppermute x5, starting transfers between devices, body(): stores += [chains[chain], in_hbm(swapped(chains[chain]))]  2.23 us
  transfers between devices with their start and end apart: 16, of which 6 were waited for; matrix products, arithmetic and copies ran while one was open for 1% of the time, Pallas kernels for 12%

profile of v16, /device:TPU:0, one launch (start us, length us, event | category | flops | bytes accessed | tf_op | source)
XLA Modules:
  0.0 58.1 jit_solution(11290272449921228412)
XLA Ops:
  0.0 0.5 collective-permute-start
  0.5 2.6 %collective-permute-start.2 = (bf16[2,128,896]{2,1,0:T(8,128)(2,1)}, bf16[2,128,896]{2,1,0:T(8,128)(2,1)S(1)}, u32[]{:S(2)}, u32[]{:S(2)}) collective-permute-start(bf16[2,128,896]{2,1,0:T(8,128)(2,1)} %refs_10_.1), channel_id=1, source_target_pairs={{0,4},{1,3},{4,8},{5,1},{8,12},{9,5},{12,14},{13,9},{14,10},{15,13... | collective-permute-start | bytes 1376264 | tf_op jit(solution)/shard_map/ppermute | solution.py:356
  3.0 0.0 collective-permute-done.refs_11_
  3.0 0.0 copy-start.3
  3.0 2.0 %collective-permute-start.6 = (bf16[2,128,896]{2,1,0:T(8,128)(2,1)S(1)}, bf16[2,128,896]{2,1,0:T(8,128)(2,1)S(1)}, u32[]{:S(2)}, u32[]{:S(2)}) collective-permute-start(bf16[2,128,896]{2,1,0:T(8,128)(2,1)S(1)} %collective-permute-done.refs_11_), channel_id=1, source_target_pairs={{0,4},{1,3},{4,8},{5,1},{8,12},{9,5},{12,14},{13,9},{14,10},{15,13... | collective-permute-start | bytes 1376264 | tf_op jit(solution)/shard_map/ppermute | solution.py:356
  5.1 0.7 %add_bitcast_fusion.refs_3_ = s32[2,4]{1,0:T(2,128)S(1)} fusion(s32[4,2]{0,1:T(2,128)} %param.13, s32[4,2]{0,1:T(2,128)} %param.12), kind=kLoop, calls=%fused_computation | loop fusion | flops 16 | bytes 96 | tf_op jit(solution)/shard_map/transpose | solution.py:343
  5.8 0.0 copy-start
  5.8 0.0 copy-start.1
  5.8 3.6 %fold_queries.2 = (bf16[8,256,896]{2,1,0:T(8,128)(2,1)}, f32[8,896]{1,0:T(8,128)S(1)}) custom-call(bf16[256,2048]{1,0:T(8,128)(2,1)} %query_hbm.1, bf16[896,2048]{1,0:T(8,128)(2,1)} %key_hbm.3), custom_call_target="tpu_custom_call" | custom-call | flops 469762048 | bytes 6291456 | tf_op jit(solution)/shard_map/fold_queries/pallas_call | solution.py:81
  9.4 0.2 collective-permute-done.2.refs_12_
  9.6 1.9 %collective-permute-start.1 = (s32[2,4]{1,0:T(2,128)S(1)}, s32[2,4]{1,0:T(2,128)S(1)}, u32[]{:S(2)}, u32[]{:S(2)}) collective-permute-start(s32[2,4]{1,0:T(2,128)S(1)} %add_bitcast_fusion.refs_3_), channel_id=1, source_target_pairs={{0,1},{1,2},{2,3},{3,4},{4,5},{5,6},{6,7},{7,8},{8,9},{9,10},{10,1... | collective-permute-start | bytes 104 | tf_op jit(solution)/shard_map/ppermute | solution.py:350
  11.5 2.2 %collective-permute-start.4 = (bf16[2,128,896]{2,1,0:T(8,128)(2,1)S(1)}, bf16[2,128,896]{2,1,0:T(8,128)(2,1)S(1)}, u32[]{:S(2)}, u32[]{:S(2)}) collective-permute-start(bf16[2,128,896]{2,1,0:T(8,128)(2,1)S(1)} %collective-permute-done.2.refs_12_), channel_id=1, source_target_pairs={{0,1},{1,0},{2,3},{3,2},{4,5},{5,4},{6,7},{7,6},{8,9},{9,8},{10,11... | collective-permute-start | bytes 1376264 | tf_op jit(solution)/shard_map/ppermute | solution.py:357
  13.7 1.6 %collective-permute-start.3 = (bf16[2,128,896]{2,1,0:T(8,128)(2,1)S(1)}, bf16[2,128,896]{2,1,0:T(8,128)(2,1)S(1)}, u32[]{:S(2)}, u32[]{:S(2)}) collective-permute-start(bf16[2,128,896]{2,1,0:T(8,128)(2,1)S(1)} %collective-permute-done.2.refs_12_), channel_id=1, source_target_pairs={{0,4},{1,3},{4,8},{5,1},{8,12},{9,5},{12,14},{13,9},{14,10},{15,13... | collective-permute-start | bytes 1376264 | tf_op jit(solution)/shard_map/ppermute | solution.py:356
  15.3 0.0 collective-permute-done.1.refs_2_
  15.3 0.0 copy-done.3
  15.3 0.0 collective-permute-done.6.refs_14_
  15.3 2.2 %collective-permute-start.9 = (bf16[2,128,896]{2,1,0:T(8,128)(2,1)S(1)}, bf16[2,128,896]{2,1,0:T(8,128)(2,1)S(1)}, u32[]{:S(2)}, u32[]{:S(2)}) collective-permute-start(bf16[2,128,896]{2,1,0:T(8,128)(2,1)S(1)} %collective-permute-done.6.refs_14_), channel_id=1, source_target_pairs={{0,4},{1,3},{4,8},{5,1},{8,12},{9,5},{12,14},{13,9},{14,10},{15,13... | collective-permute-start | bytes 1376264 | tf_op jit(solution)/shard_map/ppermute | solution.py:356
  17.5 0.0 collective-permute-start.7
  17.5 0.0 collective-permute-done.4.refs_13_
  17.5 0.8 %copy-done.4 = bf16[2,128,896]{2,1,0:T(8,128)(2,1)} copy-done((bf16[2,128,896]{2,1,0:T(8,128)(2,1)}, bf16[2,128,896]{2,1,0:T(8,128)(2,1)S(1)}, u32[]{:S(2)}) %copy-start.4) | copy-done | bytes 458776
  18.3 3.9 %collective-permute-done.3.refs_16_ = bf16[2,128,896]{2,1,0:T(8,128)(2,1)S(1)} collective-permute-done((bf16[2,128,896]{2,1,0:T(8,128)(2,1)S(1)}, bf16[2,128,896]{2,1,0:T(8,128)(2,1)S(1)}, u32[]{:S(2)}, u32[]{:S(2)}) %collective-permute-start.3) | collective-permute-done | bytes 458784 | tf_op jit(solution)/shard_map/ppermute | solution.py:356
  22.2 1.6 %collective-permute-start.5 = (bf16[2,128,896]{2,1,0:T(8,128)(2,1)S(1)}, bf16[2,128,896]{2,1,0:T(8,128)(2,1)S(1)}, u32[]{:S(2)}, u32[]{:S(2)}) collective-permute-start(bf16[2,128,896]{2,1,0:T(8,128)(2,1)S(1)} %collective-permute-done.3.refs_16_), channel_id=1, source_target_pairs={{0,4},{1,3},{4,8},{5,1},{8,12},{9,5},{12,14},{13,9},{14,10},{15,13... | collective-permute-start | bytes 1376264 | tf_op jit(solution)/shard_map/ppermute | solution.py:356
  23.8 0.0 collective-permute-start.8
  23.8 3.3 %collective-permute-done.9.refs_18_ = bf16[2,128,896]{2,1,0:T(8,128)(2,1)S(1)} collective-permute-done((bf16[2,128,896]{2,1,0:T(8,128)(2,1)S(1)}, bf16[2,128,896]{2,1,0:T(8,128)(2,1)S(1)}, u32[]{:S(2)}, u32[]{:S(2)}) %collective-permute-start.9) | collective-permute-done | bytes 458784 | tf_op jit(solution)/shard_map/ppermute | solution.py:356
  27.1 0.0 collective-permute-start.10
  27.1 0.0 collective-permute-done.7.refs_15_
  27.1 1.6 %collective-permute-start.12 = (bf16[2,128,896]{2,1,0:T(8,128)(2,1)S(1)}, bf16[2,128,896]{2,1,0:T(8,128)(2,1)S(1)}, u32[]{:S(2)}, u32[]{:S(2)}) collective-permute-start(bf16[2,128,896]{2,1,0:T(8,128)(2,1)S(1)} %collective-permute-done.9.refs_18_), channel_id=1, source_target_pairs={{0,4},{1,3},{4,8},{5,1},{8,12},{9,5},{12,14},{13,9},{14,10},{15,13... | collective-permute-start | bytes 1376264 | tf_op jit(solution)/shard_map/ppermute | solution.py:356
  28.7 3.3 %collective-permute-done.5.refs_20_ = bf16[2,128,896]{2,1,0:T(8,128)(2,1)S(1)} collective-permute-done((bf16[2,128,896]{2,1,0:T(8,128)(2,1)S(1)}, bf16[2,128,896]{2,1,0:T(8,128)(2,1)S(1)}, u32[]{:S(2)}, u32[]{:S(2)}) %collective-permute-start.5) | collective-permute-done | bytes 458784 | tf_op jit(solution)/shard_map/ppermute | solution.py:356
  32.1 0.0 collective-permute-start.11
  32.1 0.0 collective-permute-done.8.refs_17_
  32.1 0.0 collective-permute-done.10.refs_19_
  32.1 0.8 %copy-done.5 = bf16[2,128,896]{2,1,0:T(8,128)(2,1)} copy-done((bf16[2,128,896]{2,1,0:T(8,128)(2,1)}, bf16[2,128,896]{2,1,0:T(8,128)(2,1)S(1)}, u32[]{:S(2)}) %copy-start.5) | copy-done | bytes 458776
  32.9 0.8 %copy-done.6 = bf16[2,128,896]{2,1,0:T(8,128)(2,1)} copy-done((bf16[2,128,896]{2,1,0:T(8,128)(2,1)}, bf16[2,128,896]{2,1,0:T(8,128)(2,1)S(1)}, u32[]{:S(2)}) %copy-start.6) | copy-done | bytes 458776
  33.6 1.6 %collective-permute-start.13 = (bf16[2,128,896]{2,1,0:T(8,128)(2,1)S(1)}, bf16[2,128,896]{2,1,0:T(8,128)(2,1)}, u32[]{:S(2)}, u32[]{:S(2)}) collective-permute-start(bf16[2,128,896]{2,1,0:T(8,128)(2,1)S(1)} %collective-permute-done.5.refs_20_), channel_id=1, source_target_pairs={{0,4},{1,3},{4,8},{5,1},{8,12},{9,5},{12,14},{13,9},{14,10},{15,13... | collective-permute-start | bytes 1376264 | tf_op jit(solution)/shard_map/ppermute | solution.py:362
  35.2 3.6 %fold_queries.3 = (bf16[8,256,896]{2,1,0:T(8,128)(2,1)}, f32[8,896]{1,0:T(8,128)S(1)}) custom-call(bf16[256,2048]{1,0:T(8,128)(2,1)} %query_hbm.1, bf16[896,2048]{1,0:T(8,128)(2,1)} %key_hbm.3), custom_call_target="tpu_custom_call" | custom-call | flops 469762048 | bytes 6291456 | tf_op jit(solution)/shard_map/fold_queries/pallas_call | solution.py:81
  38.8 0.0 collective-permute-done.12.refs_22_
  38.8 0.0 collective-permute-done.11.refs_21_
  38.8 0.0 copy-start.7
  38.8 3.4 %collective-permute-done.13.refs_24_ = bf16[2,128,896]{2,1,0:T(8,128)(2,1)} collective-permute-done((bf16[2,128,896]{2,1,0:T(8,128)(2,1)S(1)}, bf16[2,128,896]{2,1,0:T(8,128)(2,1)}, u32[]{:S(2)}, u32[]{:S(2)}) %collective-permute-start.13) | collective-permute-done | bytes 458784 | tf_op jit(solution)/shard_map/ppermute | solution.py:362
  42.2 0.0 copy-done.7
  42.2 0.0 collective-permute-start.15
  42.2 0.5 collective-permute-start.14
  42.7 2.3 %collective-permute-done.15.refs_25_ = bf16[2,128,896]{2,1,0:T(8,128)(2,1)} collective-permute-done((bf16[2,128,896]{2,1,0:T(8,128)(2,1)}, bf16[2,128,896]{2,1,0:T(8,128)(2,1)}, u32[]{:S(2)}, u32[]{:S(2)}) %collective-permute-start.15) | collective-permute-done | bytes 458784 | tf_op jit(solution)/shard_map/ppermute | solution.py:367
  45.0 0.0 collective-permute-done.14.refs_23_
  45.0 0.0 copy-done
  45.0 0.0 copy-done.1
  45.0 0.0 copy-done.2
  45.0 12.9 %attend_windows.1 = bf16[256,2048]{1,0:T(8,128)(2,1)} custom-call(s32[1]{0:T(128)} %bitcast.refs_0_, s32[8]{0:T(128)S(1)} %copy-done.2, s32[2,4]{1,0:T(2,128)S(1)} %collective-permute-done.1.refs_2_, s32[2,4]{1,0:T(2,128)S(1)} %add_bitcast_fusion.refs_3_, s32[4]{0:T(128)S(1)} %copy-done.1, bf16[8,256,896]{2,1,0:T(8,128)(2,1)} %get-tuple-element.21.refs_5_, ...), custom_call_target="tpu_custom_call" | custom-call | flops 4697620480 | bytes 16777216 | tf_op jit(solution)/shard_map/attend_windows/pallas_call | solution.py:284
  (4 shorter events, 0.0 us)
Async XLA Ops:
  0.0 3.0 %collective-permute-start = (bf16[2,128,896]{2,1,0:T(8,128)(2,1)}, bf16[2,128,896]{2,1,0:T(8,128)(2,1)S(1)}, u32[]{:S(2)}, u32[]{:S(2)}) collective-permute-start(bf16[2,128,896]{2,1,0:T(8,128)(2,1)} %refs_10_.1), channel_id=1, source_target_pairs={{0,1},{1,0},{2,3},{3,2},{4,5},{5,4},{6,7},{7,6},{8,9},{9,8},{10,11... | collective-permute-start | bytes 1376264 | tf_op jit(solution)/shard_map/ppermute | solution.py:344
  0.5 9.2 %collective-permute-start.2 = (bf16[2,128,896]{2,1,0:T(8,128)(2,1)}, bf16[2,128,896]{2,1,0:T(8,128)(2,1)S(1)}, u32[]{:S(2)}, u32[]{:S(2)}) collective-permute-start(bf16[2,128,896]{2,1,0:T(8,128)(2,1)} %refs_10_.1), channel_id=1, source_target_pairs={{0,4},{1,3},{4,8},{5,1},{8,12},{9,5},{12,14},{13,9},{14,10},{15,13... | collective-permute-start | bytes 1376264 | tf_op jit(solution)/shard_map/ppermute | solution.py:356
  3.0 12.3 %copy-start.3 = (bf16[2,128,896]{2,1,0:T(8,128)(2,1)}, bf16[2,128,896]{2,1,0:T(8,128)(2,1)S(1)}, u32[]{:S(2)}) copy-start(bf16[2,128,896]{2,1,0:T(8,128)(2,1)S(1)} %collective-permute-done.refs_11_) | copy-start | bytes 1376260
  3.0 12.3 %collective-permute-start.6 = (bf16[2,128,896]{2,1,0:T(8,128)(2,1)S(1)}, bf16[2,128,896]{2,1,0:T(8,128)(2,1)S(1)}, u32[]{:S(2)}, u32[]{:S(2)}) collective-permute-start(bf16[2,128,896]{2,1,0:T(8,128)(2,1)S(1)} %collective-permute-done.refs_11_), channel_id=1, source_target_pairs={{0,4},{1,3},{4,8},{5,1},{8,12},{9,5},{12,14},{13,9},{14,10},{15,13... | collective-permute-start | bytes 1376264 | tf_op jit(solution)/shard_map/ppermute | solution.py:356
  5.8 39.2 %copy-start = (bf16[2,128,896]{2,1,0:T(8,128)(2,1)S(1)}, bf16[2,128,896]{2,1,0:T(8,128)(2,1)}, u32[]{:S(2)}) copy-start(bf16[2,128,896]{2,1,0:T(8,128)(2,1)} %refs_10_.1) | copy-start | bytes 1376260
  5.8 39.2 %copy-start.1 = (s32[4]{0:T(128)S(1)}, s32[4]{0:T(128)}, u32[]{:S(2)}) copy-start(s32[4]{0:T(128)} %refs_4_.1) | copy-start | bytes 52
  5.8 39.2 %copy-start.2 = (s32[8]{0:T(128)S(1)}, s32[8]{0:T(128)}, u32[]{:S(2)}) copy-start(s32[8]{0:T(128)} %constant.8.clone.refs_1_) | copy-start | bytes 100
  9.6 5.7 %collective-permute-start.1 = (s32[2,4]{1,0:T(2,128)S(1)}, s32[2,4]{1,0:T(2,128)S(1)}, u32[]{:S(2)}, u32[]{:S(2)}) collective-permute-start(s32[2,4]{1,0:T(2,128)S(1)} %add_bitcast_fusion.refs_3_), channel_id=1, source_target_pairs={{0,1},{1,2},{2,3},{3,4},{4,5},{5,6},{6,7},{7,8},{8,9},{9,10},{10,1... | collective-permute-start | bytes 104 | tf_op jit(solution)/shard_map/ppermute | solution.py:350
  11.5 6.0 %collective-permute-start.4 = (bf16[2,128,896]{2,1,0:T(8,128)(2,1)S(1)}, bf16[2,128,896]{2,1,0:T(8,128)(2,1)S(1)}, u32[]{:S(2)}, u32[]{:S(2)}) collective-permute-start(bf16[2,128,896]{2,1,0:T(8,128)(2,1)S(1)} %collective-permute-done.2.refs_12_), channel_id=1, source_target_pairs={{0,1},{1,0},{2,3},{3,2},{4,5},{5,4},{6,7},{7,6},{8,9},{9,8},{10,11... | collective-permute-start | bytes 1376264 | tf_op jit(solution)/shard_map/ppermute | solution.py:357
  13.7 8.5 %collective-permute-start.3 = (bf16[2,128,896]{2,1,0:T(8,128)(2,1)S(1)}, bf16[2,128,896]{2,1,0:T(8,128)(2,1)S(1)}, u32[]{:S(2)}, u32[]{:S(2)}) collective-permute-start(bf16[2,128,896]{2,1,0:T(8,128)(2,1)S(1)} %collective-permute-done.2.refs_12_), channel_id=1, source_target_pairs={{0,4},{1,3},{4,8},{5,1},{8,12},{9,5},{12,14},{13,9},{14,10},{15,13... | collective-permute-start | bytes 1376264 | tf_op jit(solution)/shard_map/ppermute | solution.py:356
  15.3 11.8 %collective-permute-start.9 = (bf16[2,128,896]{2,1,0:T(8,128)(2,1)S(1)}, bf16[2,128,896]{2,1,0:T(8,128)(2,1)S(1)}, u32[]{:S(2)}, u32[]{:S(2)}) collective-permute-start(bf16[2,128,896]{2,1,0:T(8,128)(2,1)S(1)} %collective-permute-done.6.refs_14_), channel_id=1, source_target_pairs={{0,4},{1,3},{4,8},{5,1},{8,12},{9,5},{12,14},{13,9},{14,10},{15,13... | collective-permute-start | bytes 1376264 | tf_op jit(solution)/shard_map/ppermute | solution.py:356
  17.5 9.6 %collective-permute-start.7 = (bf16[2,128,896]{2,1,0:T(8,128)(2,1)S(1)}, bf16[2,128,896]{2,1,0:T(8,128)(2,1)}, u32[]{:S(2)}, u32[]{:S(2)}) collective-permute-start(bf16[2,128,896]{2,1,0:T(8,128)(2,1)S(1)} %collective-permute-done.6.refs_14_), channel_id=1, source_target_pairs={{0,1},{1,0},{2,3},{3,2},{4,5},{5,4},{6,7},{7,6},{8,9},{9,8},{10,11... | collective-permute-start | bytes 1376264 | tf_op jit(solution)/shard_map/ppermute | solution.py:357
  17.5 0.8 %copy-start.4 = (bf16[2,128,896]{2,1,0:T(8,128)(2,1)}, bf16[2,128,896]{2,1,0:T(8,128)(2,1)S(1)}, u32[]{:S(2)}) copy-start(bf16[2,128,896]{2,1,0:T(8,128)(2,1)S(1)} %collective-permute-done.4.refs_13_) | copy-start | bytes 1376260
  22.2 9.8 %collective-permute-start.5 = (bf16[2,128,896]{2,1,0:T(8,128)(2,1)S(1)}, bf16[2,128,896]{2,1,0:T(8,128)(2,1)S(1)}, u32[]{:S(2)}, u32[]{:S(2)}) collective-permute-start(bf16[2,128,896]{2,1,0:T(8,128)(2,1)S(1)} %collective-permute-done.3.refs_16_), channel_id=1, source_target_pairs={{0,4},{1,3},{4,8},{5,1},{8,12},{9,5},{12,14},{13,9},{14,10},{15,13... | collective-permute-start | bytes 1376264 | tf_op jit(solution)/shard_map/ppermute | solution.py:356
  23.8 8.3 %collective-permute-start.8 = (bf16[2,128,896]{2,1,0:T(8,128)(2,1)S(1)}, bf16[2,128,896]{2,1,0:T(8,128)(2,1)S(1)}, u32[]{:S(2)}, u32[]{:S(2)}) collective-permute-start(bf16[2,128,896]{2,1,0:T(8,128)(2,1)S(1)} %collective-permute-done.3.refs_16_), channel_id=1, source_target_pairs={{0,1},{1,0},{2,3},{3,2},{4,5},{5,4},{6,7},{7,6},{8,9},{9,8},{10,11... | collective-permute-start | bytes 1376264 | tf_op jit(solution)/shard_map/ppermute | solution.py:357
  27.1 4.9 %collective-permute-start.10 = (bf16[2,128,896]{2,1,0:T(8,128)(2,1)S(1)}, bf16[2,128,896]{2,1,0:T(8,128)(2,1)S(1)}, u32[]{:S(2)}, u32[]{:S(2)}) collective-permute-start(bf16[2,128,896]{2,1,0:T(8,128)(2,1)S(1)} %collective-permute-done.9.refs_18_), channel_id=1, source_target_pairs={{0,1},{1,0},{2,3},{3,2},{4,5},{5,4},{6,7},{7,6},{8,9},{9,8},{10,11... | collective-permute-start | bytes 1376264 | tf_op jit(solution)/shard_map/ppermute | solution.py:357
  27.1 11.7 %collective-permute-start.12 = (bf16[2,128,896]{2,1,0:T(8,128)(2,1)S(1)}, bf16[2,128,896]{2,1,0:T(8,128)(2,1)S(1)}, u32[]{:S(2)}, u32[]{:S(2)}) collective-permute-start(bf16[2,128,896]{2,1,0:T(8,128)(2,1)S(1)} %collective-permute-done.9.refs_18_), channel_id=1, source_target_pairs={{0,4},{1,3},{4,8},{5,1},{8,12},{9,5},{12,14},{13,9},{14,10},{15,13... | collective-permute-start | bytes 1376264 | tf_op jit(solution)/shard_map/ppermute | solution.py:356
  32.1 6.8 %collective-permute-start.11 = (bf16[2,128,896]{2,1,0:T(8,128)(2,1)S(1)}, bf16[2,128,896]{2,1,0:T(8,128)(2,1)S(1)}, u32[]{:S(2)}, u32[]{:S(2)}) collective-permute-start(bf16[2,128,896]{2,1,0:T(8,128)(2,1)S(1)} %collective-permute-done.5.refs_20_), channel_id=1, source_target_pairs={{0,1},{1,0},{2,3},{3,2},{4,5},{5,4},{6,7},{7,6},{8,9},{9,8},{10,11... | collective-permute-start | bytes 1376264 | tf_op jit(solution)/shard_map/ppermute | solution.py:357
  32.1 0.8 %copy-start.5 = (bf16[2,128,896]{2,1,0:T(8,128)(2,1)}, bf16[2,128,896]{2,1,0:T(8,128)(2,1)S(1)}, u32[]{:S(2)}) copy-start(bf16[2,128,896]{2,1,0:T(8,128)(2,1)S(1)} %collective-permute-done.8.refs_17_) | copy-start | bytes 1376260
  32.9 0.8 %copy-start.6 = (bf16[2,128,896]{2,1,0:T(8,128)(2,1)}, bf16[2,128,896]{2,1,0:T(8,128)(2,1)S(1)}, u32[]{:S(2)}) copy-start(bf16[2,128,896]{2,1,0:T(8,128)(2,1)S(1)} %collective-permute-done.10.refs_19_) | copy-start | bytes 1376260
  33.6 8.6 %collective-permute-start.13 = (bf16[2,128,896]{2,1,0:T(8,128)(2,1)S(1)}, bf16[2,128,896]{2,1,0:T(8,128)(2,1)}, u32[]{:S(2)}, u32[]{:S(2)}) collective-permute-start(bf16[2,128,896]{2,1,0:T(8,128)(2,1)S(1)} %collective-permute-done.5.refs_20_), channel_id=1, source_target_pairs={{0,4},{1,3},{4,8},{5,1},{8,12},{9,5},{12,14},{13,9},{14,10},{15,13... | collective-permute-start | bytes 1376264 | tf_op jit(solution)/shard_map/ppermute | solution.py:362
  38.8 3.4 %copy-start.7 = (bf16[2,128,896]{2,1,0:T(8,128)(2,1)}, bf16[2,128,896]{2,1,0:T(8,128)(2,1)S(1)}, u32[]{:S(2)}) copy-start(bf16[2,128,896]{2,1,0:T(8,128)(2,1)S(1)} %collective-permute-done.11.refs_21_) | copy-start | bytes 1376260
  42.2 2.8 %collective-permute-start.15 = (bf16[2,128,896]{2,1,0:T(8,128)(2,1)}, bf16[2,128,896]{2,1,0:T(8,128)(2,1)}, u32[]{:S(2)}, u32[]{:S(2)}) collective-permute-start(bf16[2,128,896]{2,1,0:T(8,128)(2,1)} %collective-permute-done.13.refs_24_), channel_id=1, source_target_pairs={{0,1},{1,0},{2,3},{3,2},{4,5},{5,4},{6,7},{7,6},{8,9},{9,8},{10,11... | collective-permute-start | bytes 1376264 | tf_op jit(solution)/shard_map/ppermute | solution.py:367
  42.2 2.8 %collective-permute-start.14 = (bf16[2,128,896]{2,1,0:T(8,128)(2,1)S(1)}, bf16[2,128,896]{2,1,0:T(8,128)(2,1)}, u32[]{:S(2)}, u32[]{:S(2)}) collective-permute-start(bf16[2,128,896]{2,1,0:T(8,128)(2,1)S(1)} %collective-permute-done.12.refs_22_), channel_id=1, source_target_pairs={{0,1},{1,0},{2,3},{3,2},{4,5},{5,4},{6,7},{7,6},{8,9},{9,8},{10,11... | collective-permute-start | bytes 1376264 | tf_op jit(solution)/shard_map/ppermute | solution.py:366

commit v17 on v16

--- a/solution.py
+++ b/solution.py
@@ -346,24 +346,28 @@
     half = HEADS // FOLDS
     folds = [fold(0, half, *after([queries], [chains[1]]), w_key)]
 
-    asked = after([wanted], folds[0][1:])[0]
-    before = lax.ppermute(asked, "seq", [(i, i + 1) for i in range(devices - 1)])
-    beside = {(1, 0): folds[0], (1, 1): [before]}
+    beside = {(1, 0): folds[0]}
+    swaps = []
     for step in range(reach):
         for chain in range(2):
-            others = list(beside.get((step, chain), ())) + (stores[2 * chain + 4 * step - 5 :][:1] if step > 1 else [])
+            others = list(beside.get((step, chain), ()))
+            if step > 1:
+                others.append(swaps[2 * step - 4 + chain])
             sent = after([chains[chain]], others) if others else [chains[chain]]
             chains[chain] = onwards(sent[0])
-            stores += [chains[chain], in_hbm(swapped(chains[chain]))]
+            swaps.append(swapped(chains[chain]))
+            stores += [chains[chain], in_hbm(swaps[-1])]
+    asked = after([wanted], chains[1:])[0]
+    before = lax.ppermute(asked, "seq", [(i, i + 1) for i in range(devices - 1)])
     places = jnp.asarray([ring.index(chip) for chip in range(size)], jnp.int32)
     plan = [lax.axis_index("seq").reshape(1), places, before, wanted]
     if size % 2 == 0:
-        sent = after([chains[0]], [before, *stores[-7:-4:2]]) if reach > 1 else [chains[0]]
+        sent = after([chains[0]], swaps[-4:-2]) if reach > 1 else [chains[0]]
         last = onwards(sent[0])
         if reach:
             folds += [fold(part * half, half, *after([queries], [chains[0]]), w_key) for part in range(1, FOLDS)]
             others = [value for part in folds[1:] for value in part]
-            stores[-1] = swapped(after([chains[1]], [last, stores[-3], *others])[0])
+            stores[-1] = swapped(after([chains[1]], [last, swaps[-2], before, *others])[0])
         stores += [last, swapped(last)]
     return attend(size, plan, doc_starts, folds, w_value, stores)
 

time: 58.7 us -> 57.6 us (0.981)
  the two profiles are of different devices: /device:TPU:0 before, /device:TPU:18 now
where the time goes in v17:
time: 57.6 us; the launch traced here: 57.3 us
  Pallas kernels  20.6 us (36%)
  waiting for transfers between devices  20.4 us (35%)
  starting transfers between devices  13.6 us (24%)
  local copies, waits for them, and re-layouts  2.4 us (4%)
    ppermute x6, waiting for transfers between devices, body(): chains[chain] = onwards(sent[0])  14.1 us
    pallas_call x1, Pallas kernels, attend(): pl.pallas_call(functools.partial(attend_kernel, size), out_shape=jax.Shap...  13.4 us
    ppermute x6, starting transfers between devices, body(): chains[chain] = onwards(sent[0])  9.51 us
    pallas_call x2, Pallas kernels, fold(): pl.pallas_call(functools.partial(fold_kernel, first), out_shape=(pltpu.HB...  7.16 us
    ppermute x1, waiting for transfers between devices, body(): lax.ppermute(asked, 'seq', [(i, i + 1) for i in range(devices - 1)])  3.84 us
    unnamed x20, local copies, waits for them, and re-layouts  2.4 us
    ppermute x1, starting transfers between devices, body(): lax.ppermute(asked, 'seq', [(i, i + 1) for i in range(devices - 1)])  1.92 us
    ppermute x1, waiting for transfers between devices, body(): stores += [last, swapped(last)]  1.65 us
  transfers between devices with their start and end apart: 16, of which 9 were waited for; matrix products, arithmetic and copies ran while one was open for 0% of the time, Pallas kernels for 12%

profile of v17, /device:TPU:18, one launch (start us, length us, event | category | flops | bytes accessed | tf_op | source)
XLA Modules:
  0.0 57.3 jit_solution(3696247980254623866)
XLA Ops:
  0.0 0.0 copy-start.9
  0.0 0.0 copy-start.1
  0.0 0.1 collective-permute-start
  0.1 1.6 %collective-permute-start.6 = (bf16[2,128,896]{2,1,0:T(8,128)(2,1)}, bf16[2,128,896]{2,1,0:T(8,128)(2,1)S(1)}, u32[]{:S(2)}, u32[]{:S(2)}) collective-permute-start(bf16[2,128,896]{2,1,0:T(8,128)(2,1)} %refs_10_.1), channel_id=1, source_target_pairs={{0,4},{1,3},{4,8},{5,1},{8,12},{9,5},{12,14},{13,9},{14,10},{15,13... | collective-permute-start | bytes 1376264 | tf_op jit(solution)/shard_map/ppermute | solution.py:357
  1.7 0.4 collective-permute-done.refs_11_
  2.1 1.6 %collective-permute-start.1 = (bf16[2,128,896]{2,1,0:T(8,128)(2,1)S(1)}, bf16[2,128,896]{2,1,0:T(8,128)(2,1)S(1)}, u32[]{:S(2)}, u32[]{:S(2)}) collective-permute-start(bf16[2,128,896]{2,1,0:T(8,128)(2,1)S(1)} %collective-permute-done.refs_11_), channel_id=1, source_target_pairs={{0,4},{1,3},{4,8},{5,1},{8,12},{9,5},{12,14},{13,9},{14,10},{15,13... | collective-permute-start | bytes 1376264 | tf_op jit(solution)/shard_map/ppermute | solution.py:357
  3.7 3.6 %fold_queries.2 = (bf16[8,256,896]{2,1,0:T(8,128)(2,1)}, f32[8,896]{1,0:T(8,128)S(1)}) custom-call(bf16[256,2048]{1,0:T(8,128)(2,1)} %query_hbm.1, bf16[896,2048]{1,0:T(8,128)(2,1)} %key_hbm.3), custom_call_target="tpu_custom_call" | custom-call | flops 469762048 | bytes 6291456 | tf_op jit(solution)/shard_map/fold_queries/pallas_call | solution.py:81
  7.3 1.6 %collective-permute-done.6.refs_12_ = bf16[2,128,896]{2,1,0:T(8,128)(2,1)S(1)} collective-permute-done((bf16[2,128,896]{2,1,0:T(8,128)(2,1)}, bf16[2,128,896]{2,1,0:T(8,128)(2,1)S(1)}, u32[]{:S(2)}, u32[]{:S(2)}) %collective-permute-start.6) | collective-permute-done | bytes 458784 | tf_op jit(solution)/shard_map/ppermute | solution.py:357
  8.9 0.0 collective-permute-start.8
  8.9 1.6 %collective-permute-start.7 = (bf16[2,128,896]{2,1,0:T(8,128)(2,1)S(1)}, bf16[2,128,896]{2,1,0:T(8,128)(2,1)S(1)}, u32[]{:S(2)}, u32[]{:S(2)}) collective-permute-start(bf16[2,128,896]{2,1,0:T(8,128)(2,1)S(1)} %collective-permute-done.6.refs_12_), channel_id=1, source_target_pairs={{0,4},{1,3},{4,8},{5,1},{8,12},{9,5},{12,14},{13,9},{14,10},{15,13... | collective-permute-start | bytes 1376264 | tf_op jit(solution)/shard_map/ppermute | solution.py:357
  10.4 0.0 copy-done.3
  10.4 3.3 %collective-permute-done.1.refs_14_ = bf16[2,128,896]{2,1,0:T(8,128)(2,1)S(1)} collective-permute-done((bf16[2,128,896]{2,1,0:T(8,128)(2,1)S(1)}, bf16[2,128,896]{2,1,0:T(8,128)(2,1)S(1)}, u32[]{:S(2)}, u32[]{:S(2)}) %collective-permute-start.1) | collective-permute-done | bytes 458784 | tf_op jit(solution)/shard_map/ppermute | solution.py:357
  13.8 1.6 %collective-permute-start.2 = (bf16[2,128,896]{2,1,0:T(8,128)(2,1)S(1)}, bf16[2,128,896]{2,1,0:T(8,128)(2,1)S(1)}, u32[]{:S(2)}, u32[]{:S(2)}) collective-permute-start(bf16[2,128,896]{2,1,0:T(8,128)(2,1)S(1)} %collective-permute-done.1.refs_14_), channel_id=1, source_target_pairs={{0,4},{1,3},{4,8},{5,1},{8,12},{9,5},{12,14},{13,9},{14,10},{15,13... | collective-permute-start | bytes 1376264 | tf_op jit(solution)/shard_map/ppermute | solution.py:357
  15.3 0.0 collective-permute-start.3
  15.3 0.0 collective-permute-done.8.refs_13_
  15.4 0.8 %copy-done.4 = bf16[2,128,896]{2,1,0:T(8,128)(2,1)} copy-done((bf16[2,128,896]{2,1,0:T(8,128)(2,1)}, bf16[2,128,896]{2,1,0:T(8,128)(2,1)S(1)}, u32[]{:S(2)}) %copy-start.4) | copy-done | bytes 458776
  16.2 2.5 %collective-permute-done.7.refs_16_ = bf16[2,128,896]{2,1,0:T(8,128)(2,1)S(1)} collective-permute-done((bf16[2,128,896]{2,1,0:T(8,128)(2,1)S(1)}, bf16[2,128,896]{2,1,0:T(8,128)(2,1)S(1)}, u32[]{:S(2)}, u32[]{:S(2)}) %collective-permute-start.7) | collective-permute-done | bytes 458784 | tf_op jit(solution)/shard_map/ppermute | solution.py:357
  18.7 1.6 %collective-permute-start.9 = (bf16[2,128,896]{2,1,0:T(8,128)(2,1)S(1)}, bf16[2,128,896]{2,1,0:T(8,128)(2,1)S(1)}, u32[]{:S(2)}, u32[]{:S(2)}) collective-permute-start(bf16[2,128,896]{2,1,0:T(8,128)(2,1)S(1)} %collective-permute-done.7.refs_16_), channel_id=1, source_target_pairs={{0,4},{1,3},{4,8},{5,1},{8,12},{9,5},{12,14},{13,9},{14,10},{15,13... | collective-permute-start | bytes 1376264 | tf_op jit(solution)/shard_map/ppermute | solution.py:357
  20.3 0.0 collective-permute-start.10
  20.3 3.3 %collective-permute-done.2.refs_18_ = bf16[2,128,896]{2,1,0:T(8,128)(2,1)S(1)} collective-permute-done((bf16[2,128,896]{2,1,0:T(8,128)(2,1)S(1)}, bf16[2,128,896]{2,1,0:T(8,128)(2,1)S(1)}, u32[]{:S(2)}, u32[]{:S(2)}) %collective-permute-start.2) | collective-permute-done | bytes 458784 | tf_op jit(solution)/shard_map/ppermute | solution.py:357
  23.6 0.0 collective-permute-start.11
  23.6 0.0 collective-permute-done.3.refs_15_
  23.6 1.6 %collective-permute-start.4 = (bf16[2,128,896]{2,1,0:T(8,128)(2,1)S(1)}, bf16[2,128,896]{2,1,0:T(8,128)(2,1)S(1)}, u32[]{:S(2)}, u32[]{:S(2)}) collective-permute-start(bf16[2,128,896]{2,1,0:T(8,128)(2,1)S(1)} %collective-permute-done.2.refs_18_), channel_id=1, source_target_pairs={{0,4},{1,3},{4,8},{5,1},{8,12},{9,5},{12,14},{13,9},{14,10},{15,13... | collective-permute-start | bytes 1376264 | tf_op jit(solution)/shard_map/ppermute | solution.py:357
  25.2 3.3 %collective-permute-done.9.refs_20_ = bf16[2,128,896]{2,1,0:T(8,128)(2,1)S(1)} collective-permute-done((bf16[2,128,896]{2,1,0:T(8,128)(2,1)S(1)}, bf16[2,128,896]{2,1,0:T(8,128)(2,1)S(1)}, u32[]{:S(2)}, u32[]{:S(2)}) %collective-permute-start.9) | collective-permute-done | bytes 458784 | tf_op jit(solution)/shard_map/ppermute | solution.py:357
  28.5 0.0 collective-permute-start.12
  28.5 0.0 collective-permute-done.10.refs_17_
  28.5 0.0 collective-permute-done.11.refs_19_
  28.5 0.8 %copy-done.5 = bf16[2,128,896]{2,1,0:T(8,128)(2,1)} copy-done((bf16[2,128,896]{2,1,0:T(8,128)(2,1)}, bf16[2,128,896]{2,1,0:T(8,128)(2,1)S(1)}, u32[]{:S(2)}) %copy-start.5) | copy-done | bytes 458776
  29.3 0.8 %copy-done.6 = bf16[2,128,896]{2,1,0:T(8,128)(2,1)} copy-done((bf16[2,128,896]{2,1,0:T(8,128)(2,1)}, bf16[2,128,896]{2,1,0:T(8,128)(2,1)S(1)}, u32[]{:S(2)}) %copy-start.6) | copy-done | bytes 458776
  30.1 1.6 %collective-permute-start.13 = (bf16[2,128,896]{2,1,0:T(8,128)(2,1)S(1)}, bf16[2,128,896]{2,1,0:T(8,128)(2,1)}, u32[]{:S(2)}, u32[]{:S(2)}) collective-permute-start(bf16[2,128,896]{2,1,0:T(8,128)(2,1)S(1)} %collective-permute-done.9.refs_20_), channel_id=1, source_target_pairs={{0,4},{1,3},{4,8},{5,1},{8,12},{9,5},{12,14},{13,9},{14,10},{15,13... | collective-permute-start | bytes 1376264 | tf_op jit(solution)/shard_map/ppermute | solution.py:366
  31.7 0.0 copy-done.8
  31.7 0.0 copy-done.9
  31.7 3.6 %fold_queries.3 = (bf16[8,256,896]{2,1,0:T(8,128)(2,1)}, f32[8,896]{1,0:T(8,128)S(1)}) custom-call(bf16[256,2048]{1,0:T(8,128)(2,1)} %query_hbm.1, bf16[896,2048]{1,0:T(8,128)(2,1)} %key_hbm.3), custom_call_target="tpu_custom_call" | custom-call | flops 469762048 | bytes 6291456 | tf_op jit(solution)/shard_map/fold_queries/pallas_call | solution.py:81
  35.3 0.0 collective-permute-done.4.refs_22_
  35.3 1.9 %collective-permute-start.5 = (s32[2,4]{1,0:T(2,128)S(1)}, s32[2,4]{1,0:T(2,128)S(1)}, u32[]{:S(2)}, u32[]{:S(2)}) collective-permute-start(s32[2,4]{1,0:T(2,128)S(1)} %add_bitcast_fusion.refs_3_), channel_id=1, source_target_pairs={{0,1},{1,2},{2,3},{3,4},{4,5},{5,6},{6,7},{7,8},{8,9},{9,10},{10,1... | collective-permute-start | bytes 104 | tf_op jit(solution)/shard_map/ppermute | solution.py:361
  37.2 0.0 collective-permute-done.12.refs_21_
  37.2 0.0 copy-start.7
  37.2 3.8 %collective-permute-done.5.refs_2_ = s32[2,4]{1,0:T(2,128)S(1)} collective-permute-done((s32[2,4]{1,0:T(2,128)S(1)}, s32[2,4]{1,0:T(2,128)S(1)}, u32[]{:S(2)}, u32[]{:S(2)}) %collective-permute-start.5) | collective-permute-done | bytes 64 | tf_op jit(solution)/shard_map/ppermute | solution.py:361
  41.1 0.0 collective-permute-done.13.refs_24_
  41.1 0.0 copy-done.7
  41.1 0.0 collective-permute-start.15
  41.1 0.5 collective-permute-start.14
  41.6 1.6 %collective-permute-done.15.refs_25_ = bf16[2,128,896]{2,1,0:T(8,128)(2,1)} collective-permute-done((bf16[2,128,896]{2,1,0:T(8,128)(2,1)}, bf16[2,128,896]{2,1,0:T(8,128)(2,1)}, u32[]{:S(2)}, u32[]{:S(2)}) %collective-permute-start.15) | collective-permute-done | bytes 458784 | tf_op jit(solution)/shard_map/ppermute | solution.py:371
  43.2 0.4 collective-permute-done.14.refs_23_
  43.7 0.0 copy-done.2
  43.7 0.0 copy-done
  43.7 0.0 copy-done.1
  43.7 13.4 %attend_windows.1 = bf16[256,2048]{1,0:T(8,128)(2,1)} custom-call(s32[1]{0:T(128)} %bitcast.refs_0_, s32[8]{0:T(128)S(1)} %copy-done.2, s32[2,4]{1,0:T(2,128)S(1)} %collective-permute-done.5.refs_2_, s32[2,4]{1,0:T(2,128)S(1)} %add_bitcast_fusion.refs_3_, s32[4]{0:T(128)S(1)} %copy-done.1, bf16[8,256,896]{2,1,0:T(8,128)(2,1)} %get-tuple-element.20.refs_5_, ...), custom_call_target="tpu_custom_call" | custom-call | flops 4697620480 | bytes 16777216 | tf_op jit(solution)/shard_map/attend_windows/pallas_call | solution.py:284
  (8 shorter events, 0.0 us)
Async XLA Ops:
  0.0 43.7 %copy-start.2 = (s32[8]{0:T(128)S(1)}, s32[8]{0:T(128)}, u32[]{:S(2)}) copy-start(s32[8]{0:T(128)} %constant.8.clone.refs_1_) | copy-start | bytes 100
  0.0 43.7 %copy-start = (bf16[2,128,896]{2,1,0:T(8,128)(2,1)S(1)}, bf16[2,128,896]{2,1,0:T(8,128)(2,1)}, u32[]{:S(2)}) copy-start(bf16[2,128,896]{2,1,0:T(8,128)(2,1)} %refs_10_.1) | copy-start | bytes 1376260
  0.0 31.7 %copy-start.8 = (s32[4,2]{0,1:T(2,128)S(1)}, s32[4,2]{0,1:T(2,128)}, u32[]{:S(2)}) copy-start(s32[4,2]{0,1:T(2,128)} %param.13) | copy-start | bytes 100
  0.0 31.7 %copy-start.9 = (s32[4,2]{0,1:T(2,128)S(1)}, s32[4,2]{0,1:T(2,128)}, u32[]{:S(2)}) copy-start(s32[4,2]{0,1:T(2,128)} %param.12) | copy-start | bytes 100
  0.0 43.7 %copy-start.1 = (s32[4]{0:T(128)S(1)}, s32[4]{0:T(128)}, u32[]{:S(2)}) copy-start(s32[4]{0:T(128)} %refs_4_.1) | copy-start | bytes 52
  0.0 2.1 %collective-permute-start = (bf16[2,128,896]{2,1,0:T(8,128)(2,1)}, bf16[2,128,896]{2,1,0:T(8,128)(2,1)S(1)}, u32[]{:S(2)}, u32[]{:S(2)}) collective-permute-start(bf16[2,128,896]{2,1,0:T(8,128)(2,1)} %refs_10_.1), channel_id=1, source_target_pairs={{0,1},{1,0},{2,3},{3,2},{4,5},{5,4},{6,7},{7,6},{8,9},{9,8},{10,11... | collective-permute-start | bytes 1376264 | tf_op jit(solution)/shard_map/ppermute | solution.py:344
  0.1 8.7 %collective-permute-start.6 = (bf16[2,128,896]{2,1,0:T(8,128)(2,1)}, bf16[2,128,896]{2,1,0:T(8,128)(2,1)S(1)}, u32[]{:S(2)}, u32[]{:S(2)}) collective-permute-start(bf16[2,128,896]{2,1,0:T(8,128)(2,1)} %refs_10_.1), channel_id=1, source_target_pairs={{0,4},{1,3},{4,8},{5,1},{8,12},{9,5},{12,14},{13,9},{14,10},{15,13... | collective-permute-start | bytes 1376264 | tf_op jit(solution)/shard_map/ppermute | solution.py:357
  2.1 8.3 %copy-start.3 = (bf16[2,128,896]{2,1,0:T(8,128)(2,1)}, bf16[2,128,896]{2,1,0:T(8,128)(2,1)S(1)}, u32[]{:S(2)}) copy-start(bf16[2,128,896]{2,1,0:T(8,128)(2,1)S(1)} %collective-permute-done.refs_11_) | copy-start | bytes 1376260
  2.1 11.6 %collective-permute-start.1 = (bf16[2,128,896]{2,1,0:T(8,128)(2,1)S(1)}, bf16[2,128,896]{2,1,0:T(8,128)(2,1)S(1)}, u32[]{:S(2)}, u32[]{:S(2)}) collective-permute-start(bf16[2,128,896]{2,1,0:T(8,128)(2,1)S(1)} %collective-permute-done.refs_11_), channel_id=1, source_target_pairs={{0,4},{1,3},{4,8},{5,1},{8,12},{9,5},{12,14},{13,9},{14,10},{15,13... | collective-permute-start | bytes 1376264 | tf_op jit(solution)/shard_map/ppermute | solution.py:357
  8.9 6.5 %collective-permute-start.8 = (bf16[2,128,896]{2,1,0:T(8,128)(2,1)S(1)}, bf16[2,128,896]{2,1,0:T(8,128)(2,1)S(1)}, u32[]{:S(2)}, u32[]{:S(2)}) collective-permute-start(bf16[2,128,896]{2,1,0:T(8,128)(2,1)S(1)} %collective-permute-done.6.refs_12_), channel_id=1, source_target_pairs={{0,1},{1,0},{2,3},{3,2},{4,5},{5,4},{6,7},{7,6},{8,9},{9,8},{10,11... | collective-permute-start | bytes 1376264 | tf_op jit(solution)/shard_map/ppermute | solution.py:358
  8.9 9.8 %collective-permute-start.7 = (bf16[2,128,896]{2,1,0:T(8,128)(2,1)S(1)}, bf16[2,128,896]{2,1,0:T(8,128)(2,1)S(1)}, u32[]{:S(2)}, u32[]{:S(2)}) collective-permute-start(bf16[2,128,896]{2,1,0:T(8,128)(2,1)S(1)} %collective-permute-done.6.refs_12_), channel_id=1, source_target_pairs={{0,4},{1,3},{4,8},{5,1},{8,12},{9,5},{12,14},{13,9},{14,10},{15,13... | collective-permute-start | bytes 1376264 | tf_op jit(solution)/shard_map/ppermute | solution.py:357
  13.8 9.8 %collective-permute-start.2 = (bf16[2,128,896]{2,1,0:T(8,128)(2,1)S(1)}, bf16[2,128,896]{2,1,0:T(8,128)(2,1)S(1)}, u32[]{:S(2)}, u32[]{:S(2)}) collective-permute-start(bf16[2,128,896]{2,1,0:T(8,128)(2,1)S(1)} %collective-permute-done.1.refs_14_), channel_id=1, source_target_pairs={{0,4},{1,3},{4,8},{5,1},{8,12},{9,5},{12,14},{13,9},{14,10},{15,13... | collective-permute-start | bytes 1376264 | tf_op jit(solution)/shard_map/ppermute | solution.py:357
  15.3 8.3 %collective-permute-start.3 = (bf16[2,128,896]{2,1,0:T(8,128)(2,1)S(1)}, bf16[2,128,896]{2,1,0:T(8,128)(2,1)}, u32[]{:S(2)}, u32[]{:S(2)}) collective-permute-start(bf16[2,128,896]{2,1,0:T(8,128)(2,1)S(1)} %collective-permute-done.1.refs_14_), channel_id=1, source_target_pairs={{0,1},{1,0},{2,3},{3,2},{4,5},{5,4},{6,7},{7,6},{8,9},{9,8},{10,11... | collective-permute-start | bytes 1376264 | tf_op jit(solution)/shard_map/ppermute | solution.py:358
  15.3 0.8 %copy-start.4 = (bf16[2,128,896]{2,1,0:T(8,128)(2,1)}, bf16[2,128,896]{2,1,0:T(8,128)(2,1)S(1)}, u32[]{:S(2)}) copy-start(bf16[2,128,896]{2,1,0:T(8,128)(2,1)S(1)} %collective-permute-done.8.refs_13_) | copy-start | bytes 1376260
  18.7 9.8 %collective-permute-start.9 = (bf16[2,128,896]{2,1,0:T(8,128)(2,1)S(1)}, bf16[2,128,896]{2,1,0:T(8,128)(2,1)S(1)}, u32[]{:S(2)}, u32[]{:S(2)}) collective-permute-start(bf16[2,128,896]{2,1,0:T(8,128)(2,1)S(1)} %collective-permute-done.7.refs_16_), channel_id=1, source_target_pairs={{0,4},{1,3},{4,8},{5,1},{8,12},{9,5},{12,14},{13,9},{14,10},{15,13... | collective-permute-start | bytes 1376264 | tf_op jit(solution)/shard_map/ppermute | solution.py:357
  20.3 8.3 %collective-permute-start.10 = (bf16[2,128,896]{2,1,0:T(8,128)(2,1)S(1)}, bf16[2,128,896]{2,1,0:T(8,128)(2,1)S(1)}, u32[]{:S(2)}, u32[]{:S(2)}) collective-permute-start(bf16[2,128,896]{2,1,0:T(8,128)(2,1)S(1)} %collective-permute-done.7.refs_16_), channel_id=1, source_target_pairs={{0,1},{1,0},{2,3},{3,2},{4,5},{5,4},{6,7},{7,6},{8,9},{9,8},{10,11... | collective-permute-start | bytes 1376264 | tf_op jit(solution)/shard_map/ppermute | solution.py:358
  23.6 4.9 %collective-permute-start.11 = (bf16[2,128,896]{2,1,0:T(8,128)(2,1)S(1)}, bf16[2,128,896]{2,1,0:T(8,128)(2,1)S(1)}, u32[]{:S(2)}, u32[]{:S(2)}) collective-permute-start(bf16[2,128,896]{2,1,0:T(8,128)(2,1)S(1)} %collective-permute-done.2.refs_18_), channel_id=1, source_target_pairs={{0,1},{1,0},{2,3},{3,2},{4,5},{5,4},{6,7},{7,6},{8,9},{9,8},{10,11... | collective-permute-start | bytes 1376264 | tf_op jit(solution)/shard_map/ppermute | solution.py:358
  23.6 11.7 %collective-permute-start.4 = (bf16[2,128,896]{2,1,0:T(8,128)(2,1)S(1)}, bf16[2,128,896]{2,1,0:T(8,128)(2,1)S(1)}, u32[]{:S(2)}, u32[]{:S(2)}) collective-permute-start(bf16[2,128,896]{2,1,0:T(8,128)(2,1)S(1)} %collective-permute-done.2.refs_18_), channel_id=1, source_target_pairs={{0,4},{1,3},{4,8},{5,1},{8,12},{9,5},{12,14},{13,9},{14,10},{15,13... | collective-permute-start | bytes 1376264 | tf_op jit(solution)/shard_map/ppermute | solution.py:357
  28.5 8.7 %collective-permute-start.12 = (bf16[2,128,896]{2,1,0:T(8,128)(2,1)S(1)}, bf16[2,128,896]{2,1,0:T(8,128)(2,1)S(1)}, u32[]{:S(2)}, u32[]{:S(2)}) collective-permute-start(bf16[2,128,896]{2,1,0:T(8,128)(2,1)S(1)} %collective-permute-done.9.refs_20_), channel_id=1, source_target_pairs={{0,1},{1,0},{2,3},{3,2},{4,5},{5,4},{6,7},{7,6},{8,9},{9,8},{10,11... | collective-permute-start | bytes 1376264 | tf_op jit(solution)/shard_map/ppermute | solution.py:358
  28.5 0.8 %copy-start.5 = (bf16[2,128,896]{2,1,0:T(8,128)(2,1)}, bf16[2,128,896]{2,1,0:T(8,128)(2,1)S(1)}, u32[]{:S(2)}) copy-start(bf16[2,128,896]{2,1,0:T(8,128)(2,1)S(1)} %collective-permute-done.10.refs_17_) | copy-start | bytes 1376260
  29.3 0.8 %copy-start.6 = (bf16[2,128,896]{2,1,0:T(8,128)(2,1)}, bf16[2,128,896]{2,1,0:T(8,128)(2,1)S(1)}, u32[]{:S(2)}) copy-start(bf16[2,128,896]{2,1,0:T(8,128)(2,1)S(1)} %collective-permute-done.11.refs_19_) | copy-start | bytes 1376260
  30.1 11.0 %collective-permute-start.13 = (bf16[2,128,896]{2,1,0:T(8,128)(2,1)S(1)}, bf16[2,128,896]{2,1,0:T(8,128)(2,1)}, u32[]{:S(2)}, u32[]{:S(2)}) collective-permute-start(bf16[2,128,896]{2,1,0:T(8,128)(2,1)S(1)} %collective-permute-done.9.refs_20_), channel_id=1, source_target_pairs={{0,4},{1,3},{4,8},{5,1},{8,12},{9,5},{12,14},{13,9},{14,10},{15,13... | collective-permute-start | bytes 1376264 | tf_op jit(solution)/shard_map/ppermute | solution.py:366
  35.3 5.8 %collective-permute-start.5 = (s32[2,4]{1,0:T(2,128)S(1)}, s32[2,4]{1,0:T(2,128)S(1)}, u32[]{:S(2)}, u32[]{:S(2)}) collective-permute-start(s32[2,4]{1,0:T(2,128)S(1)} %add_bitcast_fusion.refs_3_), channel_id=1, source_target_pairs={{0,1},{1,2},{2,3},{3,4},{4,5},{5,6},{6,7},{7,8},{8,9},{9,10},{10,1... | collective-permute-start | bytes 104 | tf_op jit(solution)/shard_map/ppermute | solution.py:361
  37.2 3.9 %copy-start.7 = (bf16[2,128,896]{2,1,0:T(8,128)(2,1)}, bf16[2,128,896]{2,1,0:T(8,128)(2,1)S(1)}, u32[]{:S(2)}) copy-start(bf16[2,128,896]{2,1,0:T(8,128)(2,1)S(1)} %collective-permute-done.12.refs_21_) | copy-start | bytes 1376260
  41.1 2.2 %collective-permute-start.15 = (bf16[2,128,896]{2,1,0:T(8,128)(2,1)}, bf16[2,128,896]{2,1,0:T(8,128)(2,1)}, u32[]{:S(2)}, u32[]{:S(2)}) collective-permute-start(bf16[2,128,896]{2,1,0:T(8,128)(2,1)} %collective-permute-done.13.refs_24_), channel_id=1, source_target_pairs={{0,1},{1,0},{2,3},{3,2},{4,5},{5,4},{6,7},{7,6},{8,9},{9,8},{10,11... | collective-permute-start | bytes 1376264 | tf_op jit(solution)/shard_map/ppermute | solution.py:371
  41.1 2.6 %collective-permute-start.14 = (bf16[2,128,896]{2,1,0:T(8,128)(2,1)S(1)}, bf16[2,128,896]{2,1,0:T(8,128)(2,1)}, u32[]{:S(2)}, u32[]{:S(2)}) collective-permute-start(bf16[2,128,896]{2,1,0:T(8,128)(2,1)S(1)} %collective-permute-done.4.refs_22_), channel_id=1, source_target_pairs={{0,1},{1,0},{2,3},{3,2},{4,5},{5,4},{6,7},{7,6},{8,9},{9,8},{10,11... | collective-permute-start | bytes 1376264 | tf_op jit(solution)/shard_map/ppermute | solution.py:370

commit v18 on v17

--- a/solution.py
+++ b/solution.py
@@ -15,7 +15,7 @@
 SCALE = math.log2(math.e) / math.sqrt(HEAD_DIM)
 CORES = 2
 GROUP = 4
-FOLDS = 2
+FOLDS = 1
 MIB = 2**20
 
 
@@ -356,18 +356,17 @@
             sent = after([chains[chain]], others) if others else [chains[chain]]
             chains[chain] = onwards(sent[0])
             swaps.append(swapped(chains[chain]))
-            stores += [chains[chain], in_hbm(swaps[-1])]
+            stores += [chains[chain], in_hbm(swaps[-1]) if step + 2 < reach else swaps[-1]]
     asked = after([wanted], chains[1:])[0]
     before = lax.ppermute(asked, "seq", [(i, i + 1) for i in range(devices - 1)])
     places = jnp.asarray([ring.index(chip) for chip in range(size)], jnp.int32)
     plan = [lax.axis_index("seq").reshape(1), places, before, wanted]
     if size % 2 == 0:
-        sent = after([chains[0]], swaps[-4:-2]) if reach > 1 else [chains[0]]
-        last = onwards(sent[0])
+        last = onwards(chains[0])
         if reach:
             folds += [fold(part * half, half, *after([queries], [chains[0]]), w_key) for part in range(1, FOLDS)]
             others = [value for part in folds[1:] for value in part]
-            stores[-1] = swapped(after([chains[1]], [last, swaps[-2], before, *others])[0])
+            stores[-1] = swapped(after([chains[1]], [last, *swaps[-4:-1], before, *others])[0])
         stores += [last, swapped(last)]
     return attend(size, plan, doc_starts, folds, w_value, stores)
 

time: 57.6 us -> 61.3 us (1.064)
  the two profiles are of different devices: /device:TPU:18 before, /device:TPU:0 now
where the time goes in v18:
time: 61.3 us; the launch traced here: 61.1 us
  Pallas kernels  19.1 us (31%)
  starting transfers between devices  18 us (29%)
  waiting for transfers between devices  16.7 us (27%)
  local copies, waits for them, and re-layouts  7.05 us (12%)
    pallas_call x1, Pallas kernels, attend(): pl.pallas_call(functools.partial(attend_kernel, size), out_shape=jax.Shap...  14 us
    ppermute x6, starting transfers between devices, body(): chains[chain] = onwards(sent[0])  12.5 us
    ppermute x6, waiting for transfers between devices, body(): chains[chain] = onwards(sent[0])  12 us
    unnamed x28, local copies, waits for them, and re-layouts  7.05 us
    pallas_call x1, Pallas kernels, fold(): pl.pallas_call(functools.partial(fold_kernel, first), out_shape=(pltpu.HB...  5.05 us
    ppermute x1, waiting for transfers between devices, body(): last = onwards(chains[0])  3.19 us
    ppermute x1, starting transfers between devices, body(): last = onwards(chains[0])  2.08 us
    ppermute x1, starting transfers between devices, body(): lax.ppermute(asked, 'seq', [(i, i + 1) for i in range(devices - 1)])  1.82 us
  transfers between devices with their start and end apart: 16, of which 7 were waited for; matrix products, arithmetic and copies ran while one was open for 0% of the time, Pallas kernels for 8%

profile of v18, /device:TPU:0, one launch (start us, length us, event | category | flops | bytes accessed | tf_op | source)
XLA Modules:
  0.0 61.1 jit_solution(11128779930028802836)
XLA Ops:
  0.0 0.5 collective-permute-start
  0.5 2.6 %collective-permute-start.6 = (bf16[2,128,896]{2,1,0:T(8,128)(2,1)}, bf16[2,128,896]{2,1,0:T(8,128)(2,1)S(1)}, u32[]{:S(2)}, u32[]{:S(2)}) collective-permute-start(bf16[2,128,896]{2,1,0:T(8,128)(2,1)} %refs_8_.1), channel_id=1, source_target_pairs={{0,4},{1,3},{4,8},{5,1},{8,12},{9,5},{12,14},{13,9},{14,10},{15,13... | collective-permute-start | bytes 1376264 | tf_op jit(solution)/shard_map/ppermute | solution.py:357
  3.2 0.0 collective-permute-done.refs_9_
  3.2 2.0 %collective-permute-start.1 = (bf16[2,128,896]{2,1,0:T(8,128)(2,1)S(1)}, bf16[2,128,896]{2,1,0:T(8,128)(2,1)S(1)}, u32[]{:S(2)}, u32[]{:S(2)}) collective-permute-start(bf16[2,128,896]{2,1,0:T(8,128)(2,1)S(1)} %collective-permute-done.refs_9_), channel_id=1, source_target_pairs={{0,4},{1,3},{4,8},{5,1},{8,12},{9,5},{12,14},{13,9},{14,10},{15,13... | collective-permute-start | bytes 1376264 | tf_op jit(solution)/shard_map/ppermute | solution.py:357
  5.1 5.1 %fold_queries.1 = (bf16[16,256,896]{2,1,0:T(8,128)(2,1)}, f32[16,896]{1,0:T(8,128)S(1)}) custom-call(bf16[256,2048]{1,0:T(8,128)(2,1)} %query_hbm, bf16[896,2048]{1,0:T(8,128)(2,1)} %key_hbm.1), custom_call_target="tpu_custom_call" | custom-call | flops 939524096 | bytes 6291456 | tf_op jit(solution)/shard_map/fold_queries/pallas_call | solution.py:81
  10.2 0.0 collective-permute-done.6.refs_10_
  10.2 0.1 collective-permute-start.7
  10.3 1.6 %collective-permute-start.8 = (bf16[2,128,896]{2,1,0:T(8,128)(2,1)S(1)}, bf16[2,128,896]{2,1,0:T(8,128)(2,1)S(1)}, u32[]{:S(2)}, u32[]{:S(2)}) collective-permute-start(bf16[2,128,896]{2,1,0:T(8,128)(2,1)S(1)} %collective-permute-done.6.refs_10_), channel_id=1, source_target_pairs={{0,4},{1,3},{4,8},{5,1},{8,12},{9,5},{12,14},{13,9},{14,10},{15,13... | collective-permute-start | bytes 1376264 | tf_op jit(solution)/shard_map/ppermute | solution.py:357
  11.9 2.8 %collective-permute-done.1.refs_12_ = bf16[2,128,896]{2,1,0:T(8,128)(2,1)S(1)} collective-permute-done((bf16[2,128,896]{2,1,0:T(8,128)(2,1)S(1)}, bf16[2,128,896]{2,1,0:T(8,128)(2,1)S(1)}, u32[]{:S(2)}, u32[]{:S(2)}) %collective-permute-start.1) | collective-permute-done | bytes 458784 | tf_op jit(solution)/shard_map/ppermute | solution.py:357
  14.7 0.0 copy-done.9
  14.7 0.0 collective-permute-start.3
  14.7 2.1 %collective-permute-start.2 = (bf16[2,128,896]{2,1,0:T(8,128)(2,1)S(1)}, bf16[2,128,896]{2,1,0:T(8,128)(2,1)S(1)}, u32[]{:S(2)}, u32[]{:S(2)}) collective-permute-start(bf16[2,128,896]{2,1,0:T(8,128)(2,1)S(1)} %collective-permute-done.1.refs_12_), channel_id=1, source_target_pairs={{0,4},{1,3},{4,8},{5,1},{8,12},{9,5},{12,14},{13,9},{14,10},{15,13... | collective-permute-start | bytes 1376264 | tf_op jit(solution)/shard_map/ppermute | solution.py:357
  16.8 0.0 collective-permute-done.7.refs_11_
  16.8 0.8 %copy-done.10 = bf16[2,128,896]{2,1,0:T(8,128)(2,1)} copy-done((bf16[2,128,896]{2,1,0:T(8,128)(2,1)}, bf16[2,128,896]{2,1,0:T(8,128)(2,1)S(1)}, u32[]{:S(2)}) %copy-start.10) | copy-done | bytes 458776
  17.6 2.0 %collective-permute-done.8.refs_14_ = bf16[2,128,896]{2,1,0:T(8,128)(2,1)S(1)} collective-permute-done((bf16[2,128,896]{2,1,0:T(8,128)(2,1)S(1)}, bf16[2,128,896]{2,1,0:T(8,128)(2,1)S(1)}, u32[]{:S(2)}, u32[]{:S(2)}) %collective-permute-start.8) | collective-permute-done | bytes 458784 | tf_op jit(solution)/shard_map/ppermute | solution.py:357
  19.6 2.1 %collective-permute-start.11 = (bf16[2,128,896]{2,1,0:T(8,128)(2,1)S(1)}, bf16[2,128,896]{2,1,0:T(8,128)(2,1)S(1)}, u32[]{:S(2)}, u32[]{:S(2)}) collective-permute-start(bf16[2,128,896]{2,1,0:T(8,128)(2,1)S(1)} %collective-permute-done.8.refs_14_), channel_id=1, source_target_pairs={{0,4},{1,3},{4,8},{5,1},{8,12},{9,5},{12,14},{13,9},{14,10},{15,13... | collective-permute-start | bytes 1376264 | tf_op jit(solution)/shard_map/ppermute | solution.py:357
  21.7 0.0 collective-permute-done.3.refs_13_
  21.7 0.8 %copy-done.11 = bf16[2,128,896]{2,1,0:T(8,128)(2,1)} copy-done((bf16[2,128,896]{2,1,0:T(8,128)(2,1)}, bf16[2,128,896]{2,1,0:T(8,128)(2,1)S(1)}, u32[]{:S(2)}) %copy-start.11) | copy-done | bytes 458776
  22.5 2.0 %collective-permute-done.2.refs_16_ = bf16[2,128,896]{2,1,0:T(8,128)(2,1)S(1)} collective-permute-done((bf16[2,128,896]{2,1,0:T(8,128)(2,1)S(1)}, bf16[2,128,896]{2,1,0:T(8,128)(2,1)S(1)}, u32[]{:S(2)}, u32[]{:S(2)}) %collective-permute-start.2) | collective-permute-done | bytes 458784 | tf_op jit(solution)/shard_map/ppermute | solution.py:357
  24.5 2.1 %collective-permute-start.4 = (bf16[2,128,896]{2,1,0:T(8,128)(2,1)S(1)}, bf16[2,128,896]{2,1,0:T(8,128)(2,1)S(1)}, u32[]{:S(2)}, u32[]{:S(2)}) collective-permute-start(bf16[2,128,896]{2,1,0:T(8,128)(2,1)S(1)} %collective-permute-done.2.refs_16_), channel_id=1, source_target_pairs={{0,4},{1,3},{4,8},{5,1},{8,12},{9,5},{12,14},{13,9},{14,10},{15,13... | collective-permute-start | bytes 1376264 | tf_op jit(solution)/shard_map/ppermute | solution.py:357
  26.6 2.8 %collective-permute-done.11.refs_18_ = bf16[2,128,896]{2,1,0:T(8,128)(2,1)S(1)} collective-permute-done((bf16[2,128,896]{2,1,0:T(8,128)(2,1)S(1)}, bf16[2,128,896]{2,1,0:T(8,128)(2,1)S(1)}, u32[]{:S(2)}, u32[]{:S(2)}) %collective-permute-start.11) | collective-permute-done | bytes 458784 | tf_op jit(solution)/shard_map/ppermute | solution.py:357
  29.5 2.1 %collective-permute-start.13 = (bf16[2,128,896]{2,1,0:T(8,128)(2,1)S(1)}, bf16[2,128,896]{2,1,0:T(8,128)(2,1)}, u32[]{:S(2)}, u32[]{:S(2)}) collective-permute-start(bf16[2,128,896]{2,1,0:T(8,128)(2,1)S(1)} %collective-permute-done.11.refs_18_), channel_id=1, source_target_pairs={{0,4},{1,3},{4,8},{5,1},{8,12},{9,5},{12,14},{13,9},{14,10},{15,13... | collective-permute-start | bytes 1376264 | tf_op jit(solution)/shard_map/ppermute | solution.py:365
  31.5 0.0 collective-permute-start.9
  31.5 0.5 collective-permute-start.10
  32.0 0.0 collective-permute-start.12
  32.0 0.0 copy-done.12
  32.1 0.0 copy-done.13
  32.1 2.3 %collective-permute-done.4.refs_20_ = bf16[2,128,896]{2,1,0:T(8,128)(2,1)S(1)} collective-permute-done((bf16[2,128,896]{2,1,0:T(8,128)(2,1)S(1)}, bf16[2,128,896]{2,1,0:T(8,128)(2,1)S(1)}, u32[]{:S(2)}, u32[]{:S(2)}) %collective-permute-start.4) | collective-permute-done | bytes 458784 | tf_op jit(solution)/shard_map/ppermute | solution.py:357
  34.4 1.8 %collective-permute-start.5 = (s32[2,4]{1,0:T(2,128)S(1)}, s32[2,4]{1,0:T(2,128)S(1)}, u32[]{:S(2)}, u32[]{:S(2)}) collective-permute-start(s32[2,4]{1,0:T(2,128)S(1)} %add_bitcast_fusion.refs_3_), channel_id=1, source_target_pairs={{0,1},{1,2},{2,3},{3,4},{4,5},{5,6},{6,7},{7,8},{8,9},{9,10},{10,1... | collective-permute-start | bytes 104 | tf_op jit(solution)/shard_map/ppermute | solution.py:361
  36.2 3.2 %collective-permute-done.13.refs_22_ = bf16[2,128,896]{2,1,0:T(8,128)(2,1)} collective-permute-done((bf16[2,128,896]{2,1,0:T(8,128)(2,1)S(1)}, bf16[2,128,896]{2,1,0:T(8,128)(2,1)}, u32[]{:S(2)}, u32[]{:S(2)}) %collective-permute-start.13) | collective-permute-done | bytes 458784 | tf_op jit(solution)/shard_map/ppermute | solution.py:365
  39.4 0.0 collective-permute-start.15
  39.4 0.0 collective-permute-done.9.refs_15_
  39.4 0.8 %copy-done.1 = bf16[2,128,896]{2,1,0:T(8,128)(2,1)} copy-done((bf16[2,128,896]{2,1,0:T(8,128)(2,1)}, bf16[2,128,896]{2,1,0:T(8,128)(2,1)S(1)}, u32[]{:S(2)}) %copy-start.1) | copy-done | bytes 458776
  40.2 0.0 collective-permute-done.10.refs_17_
  40.2 0.8 %copy-done.3 = bf16[2,128,896]{2,1,0:T(8,128)(2,1)} copy-done((bf16[2,128,896]{2,1,0:T(8,128)(2,1)}, bf16[2,128,896]{2,1,0:T(8,128)(2,1)S(1)}, u32[]{:S(2)}) %copy-start.3) | copy-done | bytes 458776
  41.0 0.0 collective-permute-done.12.refs_19_
  41.0 0.8 %copy-done.5 = bf16[2,128,896]{2,1,0:T(8,128)(2,1)} copy-done((bf16[2,128,896]{2,1,0:T(8,128)(2,1)}, bf16[2,128,896]{2,1,0:T(8,128)(2,1)S(1)}, u32[]{:S(2)}) %copy-start.5) | copy-done | bytes 458776
  41.8 0.0 collective-permute-done.5.refs_2_
  41.8 0.5 collective-permute-start.14
  42.3 0.0 collective-permute-done.15.refs_23_
  42.3 1.6 %collective-permute-done.14.refs_21_ = bf16[2,128,896]{2,1,0:T(8,128)(2,1)} collective-permute-done((bf16[2,128,896]{2,1,0:T(8,128)(2,1)S(1)}, bf16[2,128,896]{2,1,0:T(8,128)(2,1)}, u32[]{:S(2)}, u32[]{:S(2)}) %collective-permute-start.14) | collective-permute-done | bytes 458784 | tf_op jit(solution)/shard_map/ppermute | solution.py:369
  43.8 0.0 copy-done.8
  43.9 0.0 copy-done
  43.9 0.0 copy-done.7
  43.9 1.0 %copy-done.2 = bf16[2,128,896]{2,1,0:T(8,128)(2,1)S(1)} copy-done((bf16[2,128,896]{2,1,0:T(8,128)(2,1)S(1)}, bf16[2,128,896]{2,1,0:T(8,128)(2,1)}, u32[]{:S(2)}) %copy-start.2) | copy-done | bytes 458776
  44.9 1.0 %copy-done.4 = bf16[2,128,896]{2,1,0:T(8,128)(2,1)S(1)} copy-done((bf16[2,128,896]{2,1,0:T(8,128)(2,1)S(1)}, bf16[2,128,896]{2,1,0:T(8,128)(2,1)}, u32[]{:S(2)}) %copy-start.4) | copy-done | bytes 458776
  45.9 1.0 %copy-done.6 = bf16[2,128,896]{2,1,0:T(8,128)(2,1)S(1)} copy-done((bf16[2,128,896]{2,1,0:T(8,128)(2,1)S(1)}, bf16[2,128,896]{2,1,0:T(8,128)(2,1)}, u32[]{:S(2)}) %copy-start.6) | copy-done | bytes 458776
  46.9 14.0 %attend_windows.1 = bf16[256,2048]{1,0:T(8,128)(2,1)} custom-call(s32[1]{0:T(128)} %bitcast.refs_0_, s32[8]{0:T(128)S(1)} %copy-done.8, s32[2,4]{1,0:T(2,128)S(1)} %collective-permute-done.5.refs_2_, s32[2,4]{1,0:T(2,128)S(1)} %add_bitcast_fusion.refs_3_, s32[4]{0:T(128)S(1)} %copy-done.7, bf16[16,256,896]{2,1,0:T(8,128)(2,1)} %get-tuple-element.16.refs_5_, ...), custom_call_target="tpu_custom_call" | custom-call | flops 4697620480 | bytes 16777216 | tf_op jit(solution)/shard_map/attend_windows/pallas_call | solution.py:284
  (15 shorter events, 0.0 us)
Async XLA Ops:
  0.0 43.8 %copy-start.8 = (s32[8]{0:T(128)S(1)}, s32[8]{0:T(128)}, u32[]{:S(2)}) copy-start(s32[8]{0:T(128)} %constant.8.clone.refs_1_) | copy-start | bytes 100
  0.0 43.9 %copy-start = (bf16[2,128,896]{2,1,0:T(8,128)(2,1)S(1)}, bf16[2,128,896]{2,1,0:T(8,128)(2,1)}, u32[]{:S(2)}) copy-start(bf16[2,128,896]{2,1,0:T(8,128)(2,1)} %refs_8_.1) | copy-start | bytes 1376260
  0.0 32.0 %copy-start.12 = (s32[4,2]{0,1:T(2,128)S(1)}, s32[4,2]{0,1:T(2,128)}, u32[]{:S(2)}) copy-start(s32[4,2]{0,1:T(2,128)} %param.13) | copy-start | bytes 100
  0.0 32.0 %copy-start.13 = (s32[4,2]{0,1:T(2,128)S(1)}, s32[4,2]{0,1:T(2,128)}, u32[]{:S(2)}) copy-start(s32[4,2]{0,1:T(2,128)} %param.12) | copy-start | bytes 100
  0.0 43.8 %copy-start.7 = (s32[4]{0:T(128)S(1)}, s32[4]{0:T(128)}, u32[]{:S(2)}) copy-start(s32[4]{0:T(128)} %refs_4_.1) | copy-start | bytes 52
  0.0 3.2 %collective-permute-start = (bf16[2,128,896]{2,1,0:T(8,128)(2,1)}, bf16[2,128,896]{2,1,0:T(8,128)(2,1)S(1)}, u32[]{:S(2)}, u32[]{:S(2)}) collective-permute-start(bf16[2,128,896]{2,1,0:T(8,128)(2,1)} %refs_8_.1), channel_id=1, source_target_pairs={{0,1},{1,0},{2,3},{3,2},{4,5},{5,4},{6,7},{7,6},{8,9},{9,8},{10,11... | collective-permute-start | bytes 1376264 | tf_op jit(solution)/shard_map/ppermute | solution.py:344
  0.5 9.7 %collective-permute-start.6 = (bf16[2,128,896]{2,1,0:T(8,128)(2,1)}, bf16[2,128,896]{2,1,0:T(8,128)(2,1)S(1)}, u32[]{:S(2)}, u32[]{:S(2)}) collective-permute-start(bf16[2,128,896]{2,1,0:T(8,128)(2,1)} %refs_8_.1), channel_id=1, source_target_pairs={{0,4},{1,3},{4,8},{5,1},{8,12},{9,5},{12,14},{13,9},{14,10},{15,13... | collective-permute-start | bytes 1376264 | tf_op jit(solution)/shard_map/ppermute | solution.py:357
  3.2 11.5 %copy-start.9 = (bf16[2,128,896]{2,1,0:T(8,128)(2,1)}, bf16[2,128,896]{2,1,0:T(8,128)(2,1)S(1)}, u32[]{:S(2)}) copy-start(bf16[2,128,896]{2,1,0:T(8,128)(2,1)S(1)} %collective-permute-done.refs_9_) | copy-start | bytes 1376260
  3.2 11.5 %collective-permute-start.1 = (bf16[2,128,896]{2,1,0:T(8,128)(2,1)S(1)}, bf16[2,128,896]{2,1,0:T(8,128)(2,1)S(1)}, u32[]{:S(2)}, u32[]{:S(2)}) collective-permute-start(bf16[2,128,896]{2,1,0:T(8,128)(2,1)S(1)} %collective-permute-done.refs_9_), channel_id=1, source_target_pairs={{0,4},{1,3},{4,8},{5,1},{8,12},{9,5},{12,14},{13,9},{14,10},{15,13... | collective-permute-start | bytes 1376264 | tf_op jit(solution)/shard_map/ppermute | solution.py:357
  10.2 6.6 %collective-permute-start.7 = (bf16[2,128,896]{2,1,0:T(8,128)(2,1)S(1)}, bf16[2,128,896]{2,1,0:T(8,128)(2,1)S(1)}, u32[]{:S(2)}, u32[]{:S(2)}) collective-permute-start(bf16[2,128,896]{2,1,0:T(8,128)(2,1)S(1)} %collective-permute-done.6.refs_10_), channel_id=1, source_target_pairs={{0,1},{1,0},{2,3},{3,2},{4,5},{5,4},{6,7},{7,6},{8,9},{9,8},{10,11... | collective-permute-start | bytes 1376264 | tf_op jit(solution)/shard_map/ppermute | solution.py:358
  10.3 9.3 %collective-permute-start.8 = (bf16[2,128,896]{2,1,0:T(8,128)(2,1)S(1)}, bf16[2,128,896]{2,1,0:T(8,128)(2,1)S(1)}, u32[]{:S(2)}, u32[]{:S(2)}) collective-permute-start(bf16[2,128,896]{2,1,0:T(8,128)(2,1)S(1)} %collective-permute-done.6.refs_10_), channel_id=1, source_target_pairs={{0,4},{1,3},{4,8},{5,1},{8,12},{9,5},{12,14},{13,9},{14,10},{15,13... | collective-permute-start | bytes 1376264 | tf_op jit(solution)/shard_map/ppermute | solution.py:357
  14.7 7.0 %collective-permute-start.3 = (bf16[2,128,896]{2,1,0:T(8,128)(2,1)S(1)}, bf16[2,128,896]{2,1,0:T(8,128)(2,1)S(1)}, u32[]{:S(2)}, u32[]{:S(2)}) collective-permute-start(bf16[2,128,896]{2,1,0:T(8,128)(2,1)S(1)} %collective-permute-done.1.refs_12_), channel_id=1, source_target_pairs={{0,1},{1,0},{2,3},{3,2},{4,5},{5,4},{6,7},{7,6},{8,9},{9,8},{10,11... | collective-permute-start | bytes 1376264 | tf_op jit(solution)/shard_map/ppermute | solution.py:358
  14.7 9.8 %collective-permute-start.2 = (bf16[2,128,896]{2,1,0:T(8,128)(2,1)S(1)}, bf16[2,128,896]{2,1,0:T(8,128)(2,1)S(1)}, u32[]{:S(2)}, u32[]{:S(2)}) collective-permute-start(bf16[2,128,896]{2,1,0:T(8,128)(2,1)S(1)} %collective-permute-done.1.refs_12_), channel_id=1, source_target_pairs={{0,4},{1,3},{4,8},{5,1},{8,12},{9,5},{12,14},{13,9},{14,10},{15,13... | collective-permute-start | bytes 1376264 | tf_op jit(solution)/shard_map/ppermute | solution.py:357
  16.8 0.8 %copy-start.10 = (bf16[2,128,896]{2,1,0:T(8,128)(2,1)}, bf16[2,128,896]{2,1,0:T(8,128)(2,1)S(1)}, u32[]{:S(2)}) copy-start(bf16[2,128,896]{2,1,0:T(8,128)(2,1)S(1)} %collective-permute-done.7.refs_11_) | copy-start | bytes 1376260
  19.6 9.8 %collective-permute-start.11 = (bf16[2,128,896]{2,1,0:T(8,128)(2,1)S(1)}, bf16[2,128,896]{2,1,0:T(8,128)(2,1)S(1)}, u32[]{:S(2)}, u32[]{:S(2)}) collective-permute-start(bf16[2,128,896]{2,1,0:T(8,128)(2,1)S(1)} %collective-permute-done.8.refs_14_), channel_id=1, source_target_pairs={{0,4},{1,3},{4,8},{5,1},{8,12},{9,5},{12,14},{13,9},{14,10},{15,13... | collective-permute-start | bytes 1376264 | tf_op jit(solution)/shard_map/ppermute | solution.py:357
  21.7 0.8 %copy-start.11 = (bf16[2,128,896]{2,1,0:T(8,128)(2,1)}, bf16[2,128,896]{2,1,0:T(8,128)(2,1)S(1)}, u32[]{:S(2)}) copy-start(bf16[2,128,896]{2,1,0:T(8,128)(2,1)S(1)} %collective-permute-done.3.refs_13_) | copy-start | bytes 1376260
  24.5 9.8 %collective-permute-start.4 = (bf16[2,128,896]{2,1,0:T(8,128)(2,1)S(1)}, bf16[2,128,896]{2,1,0:T(8,128)(2,1)S(1)}, u32[]{:S(2)}, u32[]{:S(2)}) collective-permute-start(bf16[2,128,896]{2,1,0:T(8,128)(2,1)S(1)} %collective-permute-done.2.refs_16_), channel_id=1, source_target_pairs={{0,4},{1,3},{4,8},{5,1},{8,12},{9,5},{12,14},{13,9},{14,10},{15,13... | collective-permute-start | bytes 1376264 | tf_op jit(solution)/shard_map/ppermute | solution.py:357
  29.5 9.9 %collective-permute-start.13 = (bf16[2,128,896]{2,1,0:T(8,128)(2,1)S(1)}, bf16[2,128,896]{2,1,0:T(8,128)(2,1)}, u32[]{:S(2)}, u32[]{:S(2)}) collective-permute-start(bf16[2,128,896]{2,1,0:T(8,128)(2,1)S(1)} %collective-permute-done.11.refs_18_), channel_id=1, source_target_pairs={{0,4},{1,3},{4,8},{5,1},{8,12},{9,5},{12,14},{13,9},{14,10},{15,13... | collective-permute-start | bytes 1376264 | tf_op jit(solution)/shard_map/ppermute | solution.py:365
  31.5 7.9 %collective-permute-start.9 = (bf16[2,128,896]{2,1,0:T(8,128)(2,1)S(1)}, bf16[2,128,896]{2,1,0:T(8,128)(2,1)S(1)}, u32[]{:S(2)}, u32[]{:S(2)}) collective-permute-start(bf16[2,128,896]{2,1,0:T(8,128)(2,1)S(1)} %collective-permute-done.8.refs_14_), channel_id=1, source_target_pairs={{0,1},{1,0},{2,3},{3,2},{4,5},{5,4},{6,7},{7,6},{8,9},{9,8},{10,11... | collective-permute-start | bytes 1376264 | tf_op jit(solution)/shard_map/ppermute | solution.py:358
  31.5 8.6 %collective-permute-start.10 = (bf16[2,128,896]{2,1,0:T(8,128)(2,1)S(1)}, bf16[2,128,896]{2,1,0:T(8,128)(2,1)S(1)}, u32[]{:S(2)}, u32[]{:S(2)}) collective-permute-start(bf16[2,128,896]{2,1,0:T(8,128)(2,1)S(1)} %collective-permute-done.2.refs_16_), channel_id=1, source_target_pairs={{0,1},{1,0},{2,3},{3,2},{4,5},{5,4},{6,7},{7,6},{8,9},{9,8},{10,11... | collective-permute-start | bytes 1376264 | tf_op jit(solution)/shard_map/ppermute | solution.py:358
  32.0 8.9 %collective-permute-start.12 = (bf16[2,128,896]{2,1,0:T(8,128)(2,1)S(1)}, bf16[2,128,896]{2,1,0:T(8,128)(2,1)S(1)}, u32[]{:S(2)}, u32[]{:S(2)}) collective-permute-start(bf16[2,128,896]{2,1,0:T(8,128)(2,1)S(1)} %collective-permute-done.11.refs_18_), channel_id=1, source_target_pairs={{0,1},{1,0},{2,3},{3,2},{4,5},{5,4},{6,7},{7,6},{8,9},{9,8},{10,11... | collective-permute-start | bytes 1376264 | tf_op jit(solution)/shard_map/ppermute | solution.py:358
  34.4 7.4 %collective-permute-start.5 = (s32[2,4]{1,0:T(2,128)S(1)}, s32[2,4]{1,0:T(2,128)S(1)}, u32[]{:S(2)}, u32[]{:S(2)}) collective-permute-start(s32[2,4]{1,0:T(2,128)S(1)} %add_bitcast_fusion.refs_3_), channel_id=1, source_target_pairs={{0,1},{1,2},{2,3},{3,4},{4,5},{5,6},{6,7},{7,8},{8,9},{9,10},{10,1... | collective-permute-start | bytes 104 | tf_op jit(solution)/shard_map/ppermute | solution.py:361
  39.4 2.9 %collective-permute-start.15 = (bf16[2,128,896]{2,1,0:T(8,128)(2,1)}, bf16[2,128,896]{2,1,0:T(8,128)(2,1)}, u32[]{:S(2)}, u32[]{:S(2)}) collective-permute-start(bf16[2,128,896]{2,1,0:T(8,128)(2,1)} %collective-permute-done.13.refs_22_), channel_id=1, source_target_pairs={{0,1},{1,0},{2,3},{3,2},{4,5},{5,4},{6,7},{7,6},{8,9},{9,8},{10,11... | collective-permute-start | bytes 1376264 | tf_op jit(solution)/shard_map/ppermute | solution.py:370
  39.4 0.8 %copy-start.1 = (bf16[2,128,896]{2,1,0:T(8,128)(2,1)}, bf16[2,128,896]{2,1,0:T(8,128)(2,1)S(1)}, u32[]{:S(2)}) copy-start(bf16[2,128,896]{2,1,0:T(8,128)(2,1)S(1)} %collective-permute-done.9.refs_15_) | copy-start | bytes 1376260
  40.2 0.8 %copy-start.3 = (bf16[2,128,896]{2,1,0:T(8,128)(2,1)}, bf16[2,128,896]{2,1,0:T(8,128)(2,1)S(1)}, u32[]{:S(2)}) copy-start(bf16[2,128,896]{2,1,0:T(8,128)(2,1)S(1)} %collective-permute-done.10.refs_17_) | copy-start | bytes 1376260
  41.0 0.8 %copy-start.5 = (bf16[2,128,896]{2,1,0:T(8,128)(2,1)}, bf16[2,128,896]{2,1,0:T(8,128)(2,1)S(1)}, u32[]{:S(2)}) copy-start(bf16[2,128,896]{2,1,0:T(8,128)(2,1)S(1)} %collective-permute-done.12.refs_19_) | copy-start | bytes 1376260
  41.8 2.1 %collective-permute-start.14 = (bf16[2,128,896]{2,1,0:T(8,128)(2,1)S(1)}, bf16[2,128,896]{2,1,0:T(8,128)(2,1)}, u32[]{:S(2)}, u32[]{:S(2)}) collective-permute-start(bf16[2,128,896]{2,1,0:T(8,128)(2,1)S(1)} %collective-permute-done.4.refs_20_), channel_id=1, source_target_pairs={{0,1},{1,0},{2,3},{3,2},{4,5},{5,4},{6,7},{7,6},{8,9},{9,8},{10,11... | collective-permute-start | bytes 1376264 | tf_op jit(solution)/shard_map/ppermute | solution.py:369
  43.9 1.0 %copy-start.2 = (bf16[2,128,896]{2,1,0:T(8,128)(2,1)S(1)}, bf16[2,128,896]{2,1,0:T(8,128)(2,1)}, u32[]{:S(2)}) copy-start(bf16[2,128,896]{2,1,0:T(8,128)(2,1)} %copy-done.1) | copy-start | bytes 1376260
  44.9 1.0 %copy-start.4 = (bf16[2,128,896]{2,1,0:T(8,128)(2,1)S(1)}, bf16[2,128,896]{2,1,0:T(8,128)(2,1)}, u32[]{:S(2)}) copy-start(bf16[2,128,896]{2,1,0:T(8,128)(2,1)} %copy-done.3) | copy-start | bytes 1376260
  45.9 1.0 %copy-start.6 = (bf16[2,128,896]{2,1,0:T(8,128)(2,1)S(1)}, bf16[2,128,896]{2,1,0:T(8,128)(2,1)}, u32[]{:S(2)}) copy-start(bf16[2,128,896]{2,1,0:T(8,128)(2,1)} %copy-done.5) | copy-start | bytes 1376260

commit v19 on v18

--- a/solution.py
+++ b/solution.py
@@ -356,8 +356,8 @@
             sent = after([chains[chain]], others) if others else [chains[chain]]
             chains[chain] = onwards(sent[0])
             swaps.append(swapped(chains[chain]))
-            stores += [chains[chain], in_hbm(swaps[-1]) if step + 2 < reach else swaps[-1]]
-    asked = after([wanted], chains[1:])[0]
+            stores += [chains[chain], in_hbm(swaps[-1])]
+    asked = after([wanted], [chains[1], *swaps[-4:-1]])[0]
     before = lax.ppermute(asked, "seq", [(i, i + 1) for i in range(devices - 1)])
     places = jnp.asarray([ring.index(chip) for chip in range(size)], jnp.int32)
     plan = [lax.axis_index("seq").reshape(1), places, before, wanted]
@@ -366,7 +366,7 @@
         if reach:
             folds += [fold(part * half, half, *after([queries], [chains[0]]), w_key) for part in range(1, FOLDS)]
             others = [value for part in folds[1:] for value in part]
-            stores[-1] = swapped(after([chains[1]], [last, *swaps[-4:-1], before, *others])[0])
+            stores[-1] = swapped(after([chains[1]], [last, before, *others])[0])
         stores += [last, swapped(last)]
     return attend(size, plan, doc_starts, folds, w_value, stores)
 

time: 61.3 us -> 55.5 us (0.905)
  local copies, waits for them, and re-layouts: 7.05 us -> 1.67 us
  waiting for transfers between devices: 16.7 us -> 17.7 us
    unnamed x28 -> x22, local copies, waits for them, and re-layouts: 7.05 us -> 1.67 us
    ppermute x1, waiting for transfers between devices: 0.01 us -> 1.64 us  [body(): stores += [last, swapped(last)]]
    ppermute x1, waiting for transfers between devices: 1.57 us -> 0.45 us  [body(): stores[-1] = swapped(after([chains[1]], [last, before, *others])[0])]
  transfers between devices with their start and end apart: 16 -> 16, of which waited for: 7 -> 8; matrix products, arithmetic and copies ran while one was open for 0% -> 0% of each run, Pallas kernels for 8% -> 9%
where the time goes in v19:
time: 55.5 us; the launch traced here: 55.6 us
  Pallas kernels  18.5 us (33%)
  waiting for transfers between devices  17.7 us (32%)
  starting transfers between devices  17.5 us (32%)
  local copies, waits for them, and re-layouts  1.67 us (3%)
    pallas_call x1, Pallas kernels, attend(): pl.pallas_call(functools.partial(attend_kernel, size), out_shape=jax.Shap...  13.4 us
    ppermute x6, starting transfers between devices, body(): chains[chain] = onwards(sent[0])  12.5 us
    ppermute x6, waiting for transfers between devices, body(): chains[chain] = onwards(sent[0])  12.4 us
    pallas_call x1, Pallas kernels, fold(): pl.pallas_call(functools.partial(fold_kernel, first), out_shape=(pltpu.HB...  5.05 us
    ppermute x1, waiting for transfers between devices, body(): last = onwards(chains[0])  3.16 us
    ppermute x1, starting transfers between devices, body(): last = onwards(chains[0])  2.08 us
    ppermute x1, starting transfers between devices, body(): lax.ppermute(asked, 'seq', [(i, i + 1) for i in range(devices - 1)])  1.83 us
    unnamed x22, local copies, waits for them, and re-layouts  1.67 us
  transfers between devices with their start and end apart: 16, of which 8 were waited for; matrix products, arithmetic and copies ran while one was open for 0% of the time, Pallas kernels for 9%

profile of v19, /device:TPU:0, one launch (start us, length us, event | category | flops | bytes accessed | tf_op | source)
XLA Modules:
  0.0 55.6 jit_solution(4757932303905565731)
XLA Ops:
  0.0 0.0 copy-start.2
  0.0 0.5 collective-permute-start
  0.5 2.6 %collective-permute-start.5 = (bf16[2,128,896]{2,1,0:T(8,128)(2,1)}, bf16[2,128,896]{2,1,0:T(8,128)(2,1)S(1)}, u32[]{:S(2)}, u32[]{:S(2)}) collective-permute-start(bf16[2,128,896]{2,1,0:T(8,128)(2,1)} %refs_8_.1), channel_id=1, source_target_pairs={{0,4},{1,3},{4,8},{5,1},{8,12},{9,5},{12,14},{13,9},{14,10},{15,13... | collective-permute-start | bytes 1376264 | tf_op jit(solution)/shard_map/ppermute | solution.py:357
  3.2 0.0 collective-permute-done.refs_9_
  3.2 2.0 %collective-permute-start.1 = (bf16[2,128,896]{2,1,0:T(8,128)(2,1)S(1)}, bf16[2,128,896]{2,1,0:T(8,128)(2,1)S(1)}, u32[]{:S(2)}, u32[]{:S(2)}) collective-permute-start(bf16[2,128,896]{2,1,0:T(8,128)(2,1)S(1)} %collective-permute-done.refs_9_), channel_id=1, source_target_pairs={{0,4},{1,3},{4,8},{5,1},{8,12},{9,5},{12,14},{13,9},{14,10},{15,13... | collective-permute-start | bytes 1376264 | tf_op jit(solution)/shard_map/ppermute | solution.py:357
  5.1 5.0 %fold_queries.1 = (bf16[16,256,896]{2,1,0:T(8,128)(2,1)}, f32[16,896]{1,0:T(8,128)S(1)}) custom-call(bf16[256,2048]{1,0:T(8,128)(2,1)} %query_hbm, bf16[896,2048]{1,0:T(8,128)(2,1)} %key_hbm.1), custom_call_target="tpu_custom_call" | custom-call | flops 939524096 | bytes 6291456 | tf_op jit(solution)/shard_map/fold_queries/pallas_call | solution.py:81
  10.2 0.0 collective-permute-done.5.refs_10_
  10.2 0.1 collective-permute-start.9
  10.3 1.6 %collective-permute-start.6 = (bf16[2,128,896]{2,1,0:T(8,128)(2,1)S(1)}, bf16[2,128,896]{2,1,0:T(8,128)(2,1)S(1)}, u32[]{:S(2)}, u32[]{:S(2)}) collective-permute-start(bf16[2,128,896]{2,1,0:T(8,128)(2,1)S(1)} %collective-permute-done.5.refs_10_), channel_id=1, source_target_pairs={{0,4},{1,3},{4,8},{5,1},{8,12},{9,5},{12,14},{13,9},{14,10},{15,13... | collective-permute-start | bytes 1376264 | tf_op jit(solution)/shard_map/ppermute | solution.py:357
  11.9 2.8 %collective-permute-done.1.refs_12_ = bf16[2,128,896]{2,1,0:T(8,128)(2,1)S(1)} collective-permute-done((bf16[2,128,896]{2,1,0:T(8,128)(2,1)S(1)}, bf16[2,128,896]{2,1,0:T(8,128)(2,1)S(1)}, u32[]{:S(2)}, u32[]{:S(2)}) %collective-permute-start.1) | collective-permute-done | bytes 458784 | tf_op jit(solution)/shard_map/ppermute | solution.py:357
  14.7 0.0 copy-done.3
  14.7 0.0 collective-permute-start.3
  14.7 2.1 %collective-permute-start.2 = (bf16[2,128,896]{2,1,0:T(8,128)(2,1)S(1)}, bf16[2,128,896]{2,1,0:T(8,128)(2,1)S(1)}, u32[]{:S(2)}, u32[]{:S(2)}) collective-permute-start(bf16[2,128,896]{2,1,0:T(8,128)(2,1)S(1)} %collective-permute-done.1.refs_12_), channel_id=1, source_target_pairs={{0,4},{1,3},{4,8},{5,1},{8,12},{9,5},{12,14},{13,9},{14,10},{15,13... | collective-permute-start | bytes 1376264 | tf_op jit(solution)/shard_map/ppermute | solution.py:357
  16.8 0.0 collective-permute-done.9.refs_11_
  16.8 0.8 %copy-done.4 = bf16[2,128,896]{2,1,0:T(8,128)(2,1)} copy-done((bf16[2,128,896]{2,1,0:T(8,128)(2,1)}, bf16[2,128,896]{2,1,0:T(8,128)(2,1)S(1)}, u32[]{:S(2)}) %copy-start.4) | copy-done | bytes 458776
  17.6 2.0 %collective-permute-done.6.refs_14_ = bf16[2,128,896]{2,1,0:T(8,128)(2,1)S(1)} collective-permute-done((bf16[2,128,896]{2,1,0:T(8,128)(2,1)S(1)}, bf16[2,128,896]{2,1,0:T(8,128)(2,1)S(1)}, u32[]{:S(2)}, u32[]{:S(2)}) %collective-permute-start.6) | collective-permute-done | bytes 458784 | tf_op jit(solution)/shard_map/ppermute | solution.py:357
  19.6 2.1 %collective-permute-start.10 = (bf16[2,128,896]{2,1,0:T(8,128)(2,1)S(1)}, bf16[2,128,896]{2,1,0:T(8,128)(2,1)S(1)}, u32[]{:S(2)}, u32[]{:S(2)}) collective-permute-start(bf16[2,128,896]{2,1,0:T(8,128)(2,1)S(1)} %collective-permute-done.6.refs_14_), channel_id=1, source_target_pairs={{0,4},{1,3},{4,8},{5,1},{8,12},{9,5},{12,14},{13,9},{14,10},{15,13... | collective-permute-start | bytes 1376264 | tf_op jit(solution)/shard_map/ppermute | solution.py:357
  21.7 0.0 collective-permute-start.7
  21.7 0.0 collective-permute-done.3.refs_13_
  21.7 0.8 %copy-done.5 = bf16[2,128,896]{2,1,0:T(8,128)(2,1)} copy-done((bf16[2,128,896]{2,1,0:T(8,128)(2,1)}, bf16[2,128,896]{2,1,0:T(8,128)(2,1)S(1)}, u32[]{:S(2)}) %copy-start.5) | copy-done | bytes 458776
  22.5 2.0 %collective-permute-done.2.refs_16_ = bf16[2,128,896]{2,1,0:T(8,128)(2,1)S(1)} collective-permute-done((bf16[2,128,896]{2,1,0:T(8,128)(2,1)S(1)}, bf16[2,128,896]{2,1,0:T(8,128)(2,1)S(1)}, u32[]{:S(2)}, u32[]{:S(2)}) %collective-permute-start.2) | collective-permute-done | bytes 458784 | tf_op jit(solution)/shard_map/ppermute | solution.py:357
  24.5 2.1 %collective-permute-start.4 = (bf16[2,128,896]{2,1,0:T(8,128)(2,1)S(1)}, bf16[2,128,896]{2,1,0:T(8,128)(2,1)S(1)}, u32[]{:S(2)}, u32[]{:S(2)}) collective-permute-start(bf16[2,128,896]{2,1,0:T(8,128)(2,1)S(1)} %collective-permute-done.2.refs_16_), channel_id=1, source_target_pairs={{0,4},{1,3},{4,8},{5,1},{8,12},{9,5},{12,14},{13,9},{14,10},{15,13... | collective-permute-start | bytes 1376264 | tf_op jit(solution)/shard_map/ppermute | solution.py:357
  26.6 0.0 collective-permute-start.8
  26.6 2.8 %collective-permute-done.10.refs_18_ = bf16[2,128,896]{2,1,0:T(8,128)(2,1)S(1)} collective-permute-done((bf16[2,128,896]{2,1,0:T(8,128)(2,1)S(1)}, bf16[2,128,896]{2,1,0:T(8,128)(2,1)S(1)}, u32[]{:S(2)}, u32[]{:S(2)}) %collective-permute-start.10) | collective-permute-done | bytes 458784 | tf_op jit(solution)/shard_map/ppermute | solution.py:357
  29.5 0.0 collective-permute-start.11
  29.5 2.1 %collective-permute-start.13 = (bf16[2,128,896]{2,1,0:T(8,128)(2,1)S(1)}, bf16[2,128,896]{2,1,0:T(8,128)(2,1)}, u32[]{:S(2)}, u32[]{:S(2)}) collective-permute-start(bf16[2,128,896]{2,1,0:T(8,128)(2,1)S(1)} %collective-permute-done.10.refs_18_), channel_id=1, source_target_pairs={{0,4},{1,3},{4,8},{5,1},{8,12},{9,5},{12,14},{13,9},{14,10},{15,13... | collective-permute-start | bytes 1376264 | tf_op jit(solution)/shard_map/ppermute | solution.py:365
  31.5 0.0 copy-done.9
  31.5 0.0 copy-done.10
  31.6 0.0 collective-permute-done.7.refs_15_
  31.6 0.0 copy-start.6
  31.6 2.8 %collective-permute-done.4.refs_20_ = bf16[2,128,896]{2,1,0:T(8,128)(2,1)S(1)} collective-permute-done((bf16[2,128,896]{2,1,0:T(8,128)(2,1)S(1)}, bf16[2,128,896]{2,1,0:T(8,128)(2,1)S(1)}, u32[]{:S(2)}, u32[]{:S(2)}) %collective-permute-start.4) | collective-permute-done | bytes 458784 | tf_op jit(solution)/shard_map/ppermute | solution.py:357
  34.4 0.0 collective-permute-done.8.refs_17_
  34.4 0.0 collective-permute-done.11.refs_19_
  34.4 0.0 copy-start.8
  34.4 1.8 %collective-permute-start.12 = (s32[2,4]{1,0:T(2,128)S(1)}, s32[2,4]{1,0:T(2,128)S(1)}, u32[]{:S(2)}, u32[]{:S(2)}) collective-permute-start(s32[2,4]{1,0:T(2,128)S(1)} %add_bitcast_fusion.refs_3_), channel_id=1, source_target_pairs={{0,1},{1,2},{2,3},{3,4},{4,5},{5,6},{6,7},{7,8},{8,9},{9,10},{10,1... | collective-permute-start | bytes 104 | tf_op jit(solution)/shard_map/ppermute | solution.py:361
  36.2 3.2 %collective-permute-done.13.refs_22_ = bf16[2,128,896]{2,1,0:T(8,128)(2,1)} collective-permute-done((bf16[2,128,896]{2,1,0:T(8,128)(2,1)S(1)}, bf16[2,128,896]{2,1,0:T(8,128)(2,1)}, u32[]{:S(2)}, u32[]{:S(2)}) %collective-permute-start.13) | collective-permute-done | bytes 458784 | tf_op jit(solution)/shard_map/ppermute | solution.py:365
  39.4 0.0 collective-permute-start.15
  39.4 0.0 collective-permute-done.12.refs_2_
  39.4 0.0 copy-done.6
  39.4 0.5 collective-permute-start.14
  39.9 0.0 copy-done.7
  39.9 0.0 copy-done.8
  39.9 1.6 %collective-permute-done.15.refs_23_ = bf16[2,128,896]{2,1,0:T(8,128)(2,1)} collective-permute-done((bf16[2,128,896]{2,1,0:T(8,128)(2,1)}, bf16[2,128,896]{2,1,0:T(8,128)(2,1)}, u32[]{:S(2)}, u32[]{:S(2)}) %collective-permute-start.15) | collective-permute-done | bytes 458784 | tf_op jit(solution)/shard_map/ppermute | solution.py:370
  41.6 0.4 collective-permute-done.14.refs_21_
  42.0 0.0 copy-done.2
  42.0 0.0 copy-done
  42.0 0.0 copy-done.1
  42.0 13.4 %attend_windows.1 = bf16[256,2048]{1,0:T(8,128)(2,1)} custom-call(s32[1]{0:T(128)} %bitcast.refs_0_, s32[8]{0:T(128)S(1)} %copy-done.2, s32[2,4]{1,0:T(2,128)S(1)} %collective-permute-done.12.refs_2_, s32[2,4]{1,0:T(2,128)S(1)} %add_bitcast_fusion.refs_3_, s32[4]{0:T(128)S(1)} %copy-done.1, bf16[16,256,896]{2,1,0:T(8,128)(2,1)} %get-tuple-element.15.refs_5_, ...), custom_call_target="tpu_custom_call" | custom-call | flops 4697620480 | bytes 16777216 | tf_op jit(solution)/shard_map/attend_windows/pallas_call | solution.py:284
  (9 shorter events, 0.0 us)
Async XLA Ops:
  0.0 42.0 %copy-start.2 = (s32[8]{0:T(128)S(1)}, s32[8]{0:T(128)}, u32[]{:S(2)}) copy-start(s32[8]{0:T(128)} %constant.8.clone.refs_1_) | copy-start | bytes 100
  0.0 42.0 %copy-start = (bf16[2,128,896]{2,1,0:T(8,128)(2,1)S(1)}, bf16[2,128,896]{2,1,0:T(8,128)(2,1)}, u32[]{:S(2)}) copy-start(bf16[2,128,896]{2,1,0:T(8,128)(2,1)} %refs_8_.1) | copy-start | bytes 1376260
  0.0 31.5 %copy-start.9 = (s32[4,2]{0,1:T(2,128)S(1)}, s32[4,2]{0,1:T(2,128)}, u32[]{:S(2)}) copy-start(s32[4,2]{0,1:T(2,128)} %param.13) | copy-start | bytes 100
  0.0 31.5 %copy-start.10 = (s32[4,2]{0,1:T(2,128)S(1)}, s32[4,2]{0,1:T(2,128)}, u32[]{:S(2)}) copy-start(s32[4,2]{0,1:T(2,128)} %param.12) | copy-start | bytes 100
  0.0 42.0 %copy-start.1 = (s32[4]{0:T(128)S(1)}, s32[4]{0:T(128)}, u32[]{:S(2)}) copy-start(s32[4]{0:T(128)} %refs_4_.1) | copy-start | bytes 52
  0.0 3.2 %collective-permute-start = (bf16[2,128,896]{2,1,0:T(8,128)(2,1)}, bf16[2,128,896]{2,1,0:T(8,128)(2,1)S(1)}, u32[]{:S(2)}, u32[]{:S(2)}) collective-permute-start(bf16[2,128,896]{2,1,0:T(8,128)(2,1)} %refs_8_.1), channel_id=1, source_target_pairs={{0,1},{1,0},{2,3},{3,2},{4,5},{5,4},{6,7},{7,6},{8,9},{9,8},{10,11... | collective-permute-start | bytes 1376264 | tf_op jit(solution)/shard_map/ppermute | solution.py:344
  0.5 9.7 %collective-permute-start.5 = (bf16[2,128,896]{2,1,0:T(8,128)(2,1)}, bf16[2,128,896]{2,1,0:T(8,128)(2,1)S(1)}, u32[]{:S(2)}, u32[]{:S(2)}) collective-permute-start(bf16[2,128,896]{2,1,0:T(8,128)(2,1)} %refs_8_.1), channel_id=1, source_target_pairs={{0,4},{1,3},{4,8},{5,1},{8,12},{9,5},{12,14},{13,9},{14,10},{15,13... | collective-permute-start | bytes 1376264 | tf_op jit(solution)/shard_map/ppermute | solution.py:357
  3.2 11.5 %copy-start.3 = (bf16[2,128,896]{2,1,0:T(8,128)(2,1)}, bf16[2,128,896]{2,1,0:T(8,128)(2,1)S(1)}, u32[]{:S(2)}) copy-start(bf16[2,128,896]{2,1,0:T(8,128)(2,1)S(1)} %collective-permute-done.refs_9_) | copy-start | bytes 1376260
  3.2 11.5 %collective-permute-start.1 = (bf16[2,128,896]{2,1,0:T(8,128)(2,1)S(1)}, bf16[2,128,896]{2,1,0:T(8,128)(2,1)S(1)}, u32[]{:S(2)}, u32[]{:S(2)}) collective-permute-start(bf16[2,128,896]{2,1,0:T(8,128)(2,1)S(1)} %collective-permute-done.refs_9_), channel_id=1, source_target_pairs={{0,4},{1,3},{4,8},{5,1},{8,12},{9,5},{12,14},{13,9},{14,10},{15,13... | collective-permute-start | bytes 1376264 | tf_op jit(solution)/shard_map/ppermute | solution.py:357
  10.2 6.6 %collective-permute-start.9 = (bf16[2,128,896]{2,1,0:T(8,128)(2,1)S(1)}, bf16[2,128,896]{2,1,0:T(8,128)(2,1)S(1)}, u32[]{:S(2)}, u32[]{:S(2)}) collective-permute-start(bf16[2,128,896]{2,1,0:T(8,128)(2,1)S(1)} %collective-permute-done.5.refs_10_), channel_id=1, source_target_pairs={{0,1},{1,0},{2,3},{3,2},{4,5},{5,4},{6,7},{7,6},{8,9},{9,8},{10,11... | collective-permute-start | bytes 1376264 | tf_op jit(solution)/shard_map/ppermute | solution.py:358
  10.3 9.3 %collective-permute-start.6 = (bf16[2,128,896]{2,1,0:T(8,128)(2,1)S(1)}, bf16[2,128,896]{2,1,0:T(8,128)(2,1)S(1)}, u32[]{:S(2)}, u32[]{:S(2)}) collective-permute-start(bf16[2,128,896]{2,1,0:T(8,128)(2,1)S(1)} %collective-permute-done.5.refs_10_), channel_id=1, source_target_pairs={{0,4},{1,3},{4,8},{5,1},{8,12},{9,5},{12,14},{13,9},{14,10},{15,13... | collective-permute-start | bytes 1376264 | tf_op jit(solution)/shard_map/ppermute | solution.py:357
  14.7 7.0 %collective-permute-start.3 = (bf16[2,128,896]{2,1,0:T(8,128)(2,1)S(1)}, bf16[2,128,896]{2,1,0:T(8,128)(2,1)S(1)}, u32[]{:S(2)}, u32[]{:S(2)}) collective-permute-start(bf16[2,128,896]{2,1,0:T(8,128)(2,1)S(1)} %collective-permute-done.1.refs_12_), channel_id=1, source_target_pairs={{0,1},{1,0},{2,3},{3,2},{4,5},{5,4},{6,7},{7,6},{8,9},{9,8},{10,11... | collective-permute-start | bytes 1376264 | tf_op jit(solution)/shard_map/ppermute | solution.py:358
  14.7 9.8 %collective-permute-start.2 = (bf16[2,128,896]{2,1,0:T(8,128)(2,1)S(1)}, bf16[2,128,896]{2,1,0:T(8,128)(2,1)S(1)}, u32[]{:S(2)}, u32[]{:S(2)}) collective-permute-start(bf16[2,128,896]{2,1,0:T(8,128)(2,1)S(1)} %collective-permute-done.1.refs_12_), channel_id=1, source_target_pairs={{0,4},{1,3},{4,8},{5,1},{8,12},{9,5},{12,14},{13,9},{14,10},{15,13... | collective-permute-start | bytes 1376264 | tf_op jit(solution)/shard_map/ppermute | solution.py:357
  16.8 0.8 %copy-start.4 = (bf16[2,128,896]{2,1,0:T(8,128)(2,1)}, bf16[2,128,896]{2,1,0:T(8,128)(2,1)S(1)}, u32[]{:S(2)}) copy-start(bf16[2,128,896]{2,1,0:T(8,128)(2,1)S(1)} %collective-permute-done.9.refs_11_) | copy-start | bytes 1376260
  19.6 9.8 %collective-permute-start.10 = (bf16[2,128,896]{2,1,0:T(8,128)(2,1)S(1)}, bf16[2,128,896]{2,1,0:T(8,128)(2,1)S(1)}, u32[]{:S(2)}, u32[]{:S(2)}) collective-permute-start(bf16[2,128,896]{2,1,0:T(8,128)(2,1)S(1)} %collective-permute-done.6.refs_14_), channel_id=1, source_target_pairs={{0,4},{1,3},{4,8},{5,1},{8,12},{9,5},{12,14},{13,9},{14,10},{15,13... | collective-permute-start | bytes 1376264 | tf_op jit(solution)/shard_map/ppermute | solution.py:357
  21.7 9.8 %collective-permute-start.7 = (bf16[2,128,896]{2,1,0:T(8,128)(2,1)S(1)}, bf16[2,128,896]{2,1,0:T(8,128)(2,1)S(1)}, u32[]{:S(2)}, u32[]{:S(2)}) collective-permute-start(bf16[2,128,896]{2,1,0:T(8,128)(2,1)S(1)} %collective-permute-done.6.refs_14_), channel_id=1, source_target_pairs={{0,1},{1,0},{2,3},{3,2},{4,5},{5,4},{6,7},{7,6},{8,9},{9,8},{10,11... | collective-permute-start | bytes 1376264 | tf_op jit(solution)/shard_map/ppermute | solution.py:358
  21.7 0.8 %copy-start.5 = (bf16[2,128,896]{2,1,0:T(8,128)(2,1)}, bf16[2,128,896]{2,1,0:T(8,128)(2,1)S(1)}, u32[]{:S(2)}) copy-start(bf16[2,128,896]{2,1,0:T(8,128)(2,1)S(1)} %collective-permute-done.3.refs_13_) | copy-start | bytes 1376260
  24.5 9.8 %collective-permute-start.4 = (bf16[2,128,896]{2,1,0:T(8,128)(2,1)S(1)}, bf16[2,128,896]{2,1,0:T(8,128)(2,1)S(1)}, u32[]{:S(2)}, u32[]{:S(2)}) collective-permute-start(bf16[2,128,896]{2,1,0:T(8,128)(2,1)S(1)} %collective-permute-done.2.refs_16_), channel_id=1, source_target_pairs={{0,4},{1,3},{4,8},{5,1},{8,12},{9,5},{12,14},{13,9},{14,10},{15,13... | collective-permute-start | bytes 1376264 | tf_op jit(solution)/shard_map/ppermute | solution.py:357
  26.6 7.8 %collective-permute-start.8 = (bf16[2,128,896]{2,1,0:T(8,128)(2,1)S(1)}, bf16[2,128,896]{2,1,0:T(8,128)(2,1)S(1)}, u32[]{:S(2)}, u32[]{:S(2)}) collective-permute-start(bf16[2,128,896]{2,1,0:T(8,128)(2,1)S(1)} %collective-permute-done.2.refs_16_), channel_id=1, source_target_pairs={{0,1},{1,0},{2,3},{3,2},{4,5},{5,4},{6,7},{7,6},{8,9},{9,8},{10,11... | collective-permute-start | bytes 1376264 | tf_op jit(solution)/shard_map/ppermute | solution.py:358
  29.5 4.9 %collective-permute-start.11 = (bf16[2,128,896]{2,1,0:T(8,128)(2,1)S(1)}, bf16[2,128,896]{2,1,0:T(8,128)(2,1)S(1)}, u32[]{:S(2)}, u32[]{:S(2)}) collective-permute-start(bf16[2,128,896]{2,1,0:T(8,128)(2,1)S(1)} %collective-permute-done.10.refs_18_), channel_id=1, source_target_pairs={{0,1},{1,0},{2,3},{3,2},{4,5},{5,4},{6,7},{7,6},{8,9},{9,8},{10,11... | collective-permute-start | bytes 1376264 | tf_op jit(solution)/shard_map/ppermute | solution.py:358
  29.5 9.9 %collective-permute-start.13 = (bf16[2,128,896]{2,1,0:T(8,128)(2,1)S(1)}, bf16[2,128,896]{2,1,0:T(8,128)(2,1)}, u32[]{:S(2)}, u32[]{:S(2)}) collective-permute-start(bf16[2,128,896]{2,1,0:T(8,128)(2,1)S(1)} %collective-permute-done.10.refs_18_), channel_id=1, source_target_pairs={{0,4},{1,3},{4,8},{5,1},{8,12},{9,5},{12,14},{13,9},{14,10},{15,13... | collective-permute-start | bytes 1376264 | tf_op jit(solution)/shard_map/ppermute | solution.py:365
  31.6 7.8 %copy-start.6 = (bf16[2,128,896]{2,1,0:T(8,128)(2,1)}, bf16[2,128,896]{2,1,0:T(8,128)(2,1)S(1)}, u32[]{:S(2)}) copy-start(bf16[2,128,896]{2,1,0:T(8,128)(2,1)S(1)} %collective-permute-done.7.refs_15_) | copy-start | bytes 1376260
  34.4 5.5 %copy-start.7 = (bf16[2,128,896]{2,1,0:T(8,128)(2,1)}, bf16[2,128,896]{2,1,0:T(8,128)(2,1)S(1)}, u32[]{:S(2)}) copy-start(bf16[2,128,896]{2,1,0:T(8,128)(2,1)S(1)} %collective-permute-done.8.refs_17_) | copy-start | bytes 1376260
  34.4 5.5 %copy-start.8 = (bf16[2,128,896]{2,1,0:T(8,128)(2,1)}, bf16[2,128,896]{2,1,0:T(8,128)(2,1)S(1)}, u32[]{:S(2)}) copy-start(bf16[2,128,896]{2,1,0:T(8,128)(2,1)S(1)} %collective-permute-done.11.refs_19_) | copy-start | bytes 1376260
  34.4 5.0 %collective-permute-start.12 = (s32[2,4]{1,0:T(2,128)S(1)}, s32[2,4]{1,0:T(2,128)S(1)}, u32[]{:S(2)}, u32[]{:S(2)}) collective-permute-start(s32[2,4]{1,0:T(2,128)S(1)} %add_bitcast_fusion.refs_3_), channel_id=1, source_target_pairs={{0,1},{1,2},{2,3},{3,4},{4,5},{5,6},{6,7},{7,8},{8,9},{9,10},{10,1... | collective-permute-start | bytes 104 | tf_op jit(solution)/shard_map/ppermute | solution.py:361
  39.4 2.2 %collective-permute-start.15 = (bf16[2,128,896]{2,1,0:T(8,128)(2,1)}, bf16[2,128,896]{2,1,0:T(8,128)(2,1)}, u32[]{:S(2)}, u32[]{:S(2)}) collective-permute-start(bf16[2,128,896]{2,1,0:T(8,128)(2,1)} %collective-permute-done.13.refs_22_), channel_id=1, source_target_pairs={{0,1},{1,0},{2,3},{3,2},{4,5},{5,4},{6,7},{7,6},{8,9},{9,8},{10,11... | collective-permute-start | bytes 1376264 | tf_op jit(solution)/shard_map/ppermute | solution.py:370
  39.4 2.6 %collective-permute-start.14 = (bf16[2,128,896]{2,1,0:T(8,128)(2,1)S(1)}, bf16[2,128,896]{2,1,0:T(8,128)(2,1)}, u32[]{:S(2)}, u32[]{:S(2)}) collective-permute-start(bf16[2,128,896]{2,1,0:T(8,128)(2,1)S(1)} %collective-permute-done.4.refs_20_), channel_id=1, source_target_pairs={{0,1},{1,0},{2,3},{3,2},{4,5},{5,4},{6,7},{7,6},{8,9},{9,8},{10,11... | collective-permute-start | bytes 1376264 | tf_op jit(solution)/shard_map/ppermute | solution.py:369

commit v20 on v19

--- a/solution.py
+++ b/solution.py
@@ -109,28 +109,37 @@
 
 def among(stores, first, source, act):
     if len(stores) == 1:
-        pl.when(source == first)(lambda: act(stores[0]))
+        act(stores[0])
         return
     half = len(stores) // 2
-    pl.when(source < first + half)(lambda: among(stores[:half], first, source, act))
-    pl.when(source >= first + half)(lambda: among(stores[half:], first + half, source, act))
+    lax.cond(
+        source < first + half,
+        lambda: among(stores[:half], first, source, act),
+        lambda: among(stores[half:], first + half, source, act),
+    )
+
+
+def split(value, count):
+    if count & (count - 1):
+        return lax.div(value, count), lax.rem(value, count)
+    return value >> (count.bit_length() - 1), value & (count - 1)
 
 
 def locate(request, plan_refs, size, stored):
     here_ref, place_ref, before_ref, wanted_ref = plan_refs
     window, part = divmod(request, 2)
     wanted = before_ref[part, before_ref.shape[1] - 1] if window == 0 else wanted_ref[part, window - 1]
-    owner, slot = wanted // stored, wanted % stored
+    owner, slot = split(wanted, stored)
+    chip, core = split(owner, CORES)
+    here_chip, here_core = split(here_ref[0], CORES)
     reach = (size - 1) // 2
     opposite = size - reach - 1
-    here = here_ref[0]
-    away = place_ref[here // CORES] - place_ref[owner // CORES]
+    away = place_ref[here_chip] - place_ref[chip]
     away = jnp.where(away < 0, away + size, away)
-    core = owner % CORES
     holder = jnp.where((away == 0) | ((away > reach) & (away <= opposite)), core, jnp.where(away <= reach, 0, 1))
     step = jnp.where(away <= opposite, away, size - away)
     arrival = jnp.where(away == 0, 0, 2 * step - 1 + jnp.where(core == holder, 0, 1))
-    return CORES * arrival + jnp.where(holder == here % CORES, 0, 1), slot
+    return CORES * arrival + jnp.where(holder == here_core, 0, 1), slot
 
 
 def weigh(scores):

time: 55.5 us -> 55.4 us (level)
  no operation moved by 1% of the time
where the time goes in v20:
time: 55.4 us
  Pallas kernels  18.3 us (33%)
  waiting for transfers between devices  17.7 us (32%)
  starting transfers between devices  17.5 us (32%)
  local copies, waits for them, and re-layouts  1.67 us (3%)
    pallas_call x1, Pallas kernels, attend(): pl.pallas_call(functools.partial(attend_kernel, size), out_shape=jax.Shap...  13.2 us
    ppermute x6, starting transfers between devices, body(): chains[chain] = onwards(sent[0])  12.5 us
    ppermute x6, waiting for transfers between devices, body(): chains[chain] = onwards(sent[0])  12.4 us
    pallas_call x1, Pallas kernels, fold(): pl.pallas_call(functools.partial(fold_kernel, first), out_shape=(pltpu.HB...  5.05 us
    ppermute x1, waiting for transfers between devices, body(): last = onwards(chains[0])  3.16 us
    ppermute x1, starting transfers between devices, body(): last = onwards(chains[0])  2.08 us
    ppermute x1, starting transfers between devices, body(): lax.ppermute(asked, 'seq', [(i, i + 1) for i in range(devices - 1)])  1.83 us
    unnamed x22, local copies, waits for them, and re-layouts  1.67 us
  transfers between devices with their start and end apart: 16, of which 8 were waited for; matrix products, arithmetic and copies ran while one was open for 0% of the time, Pallas kernels for 9%

profile of v20, /device:TPU:0, one launch (start us, length us, event | category | flops | bytes accessed | tf_op | source)
XLA Modules:
  0.0 55.4 jit_solution(4314913147676500712)
XLA Ops:
  0.0 0.0 copy-start.2
  0.0 0.5 collective-permute-start
  0.5 2.6 %collective-permute-start.5 = (bf16[2,128,896]{2,1,0:T(8,128)(2,1)}, bf16[2,128,896]{2,1,0:T(8,128)(2,1)S(1)}, u32[]{:S(2)}, u32[]{:S(2)}) collective-permute-start(bf16[2,128,896]{2,1,0:T(8,128)(2,1)} %refs_8_.1), channel_id=1, source_target_pairs={{0,4},{1,3},{4,8},{5,1},{8,12},{9,5},{12,14},{13,9},{14,10},{15,13... | collective-permute-start | bytes 1376264 | tf_op jit(solution)/shard_map/ppermute | solution.py:366
  3.2 0.0 collective-permute-done.refs_9_
  3.2 2.0 %collective-permute-start.1 = (bf16[2,128,896]{2,1,0:T(8,128)(2,1)S(1)}, bf16[2,128,896]{2,1,0:T(8,128)(2,1)S(1)}, u32[]{:S(2)}, u32[]{:S(2)}) collective-permute-start(bf16[2,128,896]{2,1,0:T(8,128)(2,1)S(1)} %collective-permute-done.refs_9_), channel_id=1, source_target_pairs={{0,4},{1,3},{4,8},{5,1},{8,12},{9,5},{12,14},{13,9},{14,10},{15,13... | collective-permute-start | bytes 1376264 | tf_op jit(solution)/shard_map/ppermute | solution.py:366
  5.1 5.0 %fold_queries.1 = (bf16[16,256,896]{2,1,0:T(8,128)(2,1)}, f32[16,896]{1,0:T(8,128)S(1)}) custom-call(bf16[256,2048]{1,0:T(8,128)(2,1)} %query_hbm, bf16[896,2048]{1,0:T(8,128)(2,1)} %key_hbm.1), custom_call_target="tpu_custom_call" | custom-call | flops 939524096 | bytes 6291456 | tf_op jit(solution)/shard_map/fold_queries/pallas_call | solution.py:81
  10.2 0.0 collective-permute-done.5.refs_10_
  10.2 0.1 collective-permute-start.9
  10.3 1.6 %collective-permute-start.6 = (bf16[2,128,896]{2,1,0:T(8,128)(2,1)S(1)}, bf16[2,128,896]{2,1,0:T(8,128)(2,1)S(1)}, u32[]{:S(2)}, u32[]{:S(2)}) collective-permute-start(bf16[2,128,896]{2,1,0:T(8,128)(2,1)S(1)} %collective-permute-done.5.refs_10_), channel_id=1, source_target_pairs={{0,4},{1,3},{4,8},{5,1},{8,12},{9,5},{12,14},{13,9},{14,10},{15,13... | collective-permute-start | bytes 1376264 | tf_op jit(solution)/shard_map/ppermute | solution.py:366
  11.9 2.8 %collective-permute-done.1.refs_12_ = bf16[2,128,896]{2,1,0:T(8,128)(2,1)S(1)} collective-permute-done((bf16[2,128,896]{2,1,0:T(8,128)(2,1)S(1)}, bf16[2,128,896]{2,1,0:T(8,128)(2,1)S(1)}, u32[]{:S(2)}, u32[]{:S(2)}) %collective-permute-start.1) | collective-permute-done | bytes 458784 | tf_op jit(solution)/shard_map/ppermute | solution.py:366
  14.7 0.0 copy-done.3
  14.7 0.0 collective-permute-start.3
  14.7 2.1 %collective-permute-start.2 = (bf16[2,128,896]{2,1,0:T(8,128)(2,1)S(1)}, bf16[2,128,896]{2,1,0:T(8,128)(2,1)S(1)}, u32[]{:S(2)}, u32[]{:S(2)}) collective-permute-start(bf16[2,128,896]{2,1,0:T(8,128)(2,1)S(1)} %collective-permute-done.1.refs_12_), channel_id=1, source_target_pairs={{0,4},{1,3},{4,8},{5,1},{8,12},{9,5},{12,14},{13,9},{14,10},{15,13... | collective-permute-start | bytes 1376264 | tf_op jit(solution)/shard_map/ppermute | solution.py:366
  16.8 0.0 collective-permute-done.9.refs_11_
  16.8 0.8 %copy-done.4 = bf16[2,128,896]{2,1,0:T(8,128)(2,1)} copy-done((bf16[2,128,896]{2,1,0:T(8,128)(2,1)}, bf16[2,128,896]{2,1,0:T(8,128)(2,1)S(1)}, u32[]{:S(2)}) %copy-start.4) | copy-done | bytes 458776
  17.6 2.0 %collective-permute-done.6.refs_14_ = bf16[2,128,896]{2,1,0:T(8,128)(2,1)S(1)} collective-permute-done((bf16[2,128,896]{2,1,0:T(8,128)(2,1)S(1)}, bf16[2,128,896]{2,1,0:T(8,128)(2,1)S(1)}, u32[]{:S(2)}, u32[]{:S(2)}) %collective-permute-start.6) | collective-permute-done | bytes 458784 | tf_op jit(solution)/shard_map/ppermute | solution.py:366
  19.6 2.1 %collective-permute-start.10 = (bf16[2,128,896]{2,1,0:T(8,128)(2,1)S(1)}, bf16[2,128,896]{2,1,0:T(8,128)(2,1)S(1)}, u32[]{:S(2)}, u32[]{:S(2)}) collective-permute-start(bf16[2,128,896]{2,1,0:T(8,128)(2,1)S(1)} %collective-permute-done.6.refs_14_), channel_id=1, source_target_pairs={{0,4},{1,3},{4,8},{5,1},{8,12},{9,5},{12,14},{13,9},{14,10},{15,13... | collective-permute-start | bytes 1376264 | tf_op jit(solution)/shard_map/ppermute | solution.py:366
  21.7 0.0 collective-permute-start.7
  21.7 0.0 collective-permute-done.3.refs_13_
  21.7 0.8 %copy-done.5 = bf16[2,128,896]{2,1,0:T(8,128)(2,1)} copy-done((bf16[2,128,896]{2,1,0:T(8,128)(2,1)}, bf16[2,128,896]{2,1,0:T(8,128)(2,1)S(1)}, u32[]{:S(2)}) %copy-start.5) | copy-done | bytes 458776
  22.5 2.0 %collective-permute-done.2.refs_16_ = bf16[2,128,896]{2,1,0:T(8,128)(2,1)S(1)} collective-permute-done((bf16[2,128,896]{2,1,0:T(8,128)(2,1)S(1)}, bf16[2,128,896]{2,1,0:T(8,128)(2,1)S(1)}, u32[]{:S(2)}, u32[]{:S(2)}) %collective-permute-start.2) | collective-permute-done | bytes 458784 | tf_op jit(solution)/shard_map/ppermute | solution.py:366
  24.5 2.1 %collective-permute-start.4 = (bf16[2,128,896]{2,1,0:T(8,128)(2,1)S(1)}, bf16[2,128,896]{2,1,0:T(8,128)(2,1)S(1)}, u32[]{:S(2)}, u32[]{:S(2)}) collective-permute-start(bf16[2,128,896]{2,1,0:T(8,128)(2,1)S(1)} %collective-permute-done.2.refs_16_), channel_id=1, source_target_pairs={{0,4},{1,3},{4,8},{5,1},{8,12},{9,5},{12,14},{13,9},{14,10},{15,13... | collective-permute-start | bytes 1376264 | tf_op jit(solution)/shard_map/ppermute | solution.py:366
  26.6 0.0 collective-permute-start.8
  26.6 2.8 %collective-permute-done.10.refs_18_ = bf16[2,128,896]{2,1,0:T(8,128)(2,1)S(1)} collective-permute-done((bf16[2,128,896]{2,1,0:T(8,128)(2,1)S(1)}, bf16[2,128,896]{2,1,0:T(8,128)(2,1)S(1)}, u32[]{:S(2)}, u32[]{:S(2)}) %collective-permute-start.10) | collective-permute-done | bytes 458784 | tf_op jit(solution)/shard_map/ppermute | solution.py:366
  29.5 0.0 collective-permute-start.11
  29.5 2.1 %collective-permute-start.13 = (bf16[2,128,896]{2,1,0:T(8,128)(2,1)S(1)}, bf16[2,128,896]{2,1,0:T(8,128)(2,1)}, u32[]{:S(2)}, u32[]{:S(2)}) collective-permute-start(bf16[2,128,896]{2,1,0:T(8,128)(2,1)S(1)} %collective-permute-done.10.refs_18_), channel_id=1, source_target_pairs={{0,4},{1,3},{4,8},{5,1},{8,12},{9,5},{12,14},{13,9},{14,10},{15,13... | collective-permute-start | bytes 1376264 | tf_op jit(solution)/shard_map/ppermute | solution.py:374
  31.5 0.0 copy-done.9
  31.5 0.0 copy-done.10
  31.6 0.0 collective-permute-done.7.refs_15_
  31.6 0.0 copy-start.6
  31.6 2.8 %collective-permute-done.4.refs_20_ = bf16[2,128,896]{2,1,0:T(8,128)(2,1)S(1)} collective-permute-done((bf16[2,128,896]{2,1,0:T(8,128)(2,1)S(1)}, bf16[2,128,896]{2,1,0:T(8,128)(2,1)S(1)}, u32[]{:S(2)}, u32[]{:S(2)}) %collective-permute-start.4) | collective-permute-done | bytes 458784 | tf_op jit(solution)/shard_map/ppermute | solution.py:366
  34.4 0.0 collective-permute-done.8.refs_17_
  34.4 0.0 collective-permute-done.11.refs_19_
  34.4 0.0 copy-start.8
  34.4 1.8 %collective-permute-start.12 = (s32[2,4]{1,0:T(2,128)S(1)}, s32[2,4]{1,0:T(2,128)S(1)}, u32[]{:S(2)}, u32[]{:S(2)}) collective-permute-start(s32[2,4]{1,0:T(2,128)S(1)} %add_bitcast_fusion.refs_3_), channel_id=1, source_target_pairs={{0,1},{1,2},{2,3},{3,4},{4,5},{5,6},{6,7},{7,8},{8,9},{9,10},{10,1... | collective-permute-start | bytes 104 | tf_op jit(solution)/shard_map/ppermute | solution.py:370
  36.2 3.2 %collective-permute-done.13.refs_22_ = bf16[2,128,896]{2,1,0:T(8,128)(2,1)} collective-permute-done((bf16[2,128,896]{2,1,0:T(8,128)(2,1)S(1)}, bf16[2,128,896]{2,1,0:T(8,128)(2,1)}, u32[]{:S(2)}, u32[]{:S(2)}) %collective-permute-start.13) | collective-permute-done | bytes 458784 | tf_op jit(solution)/shard_map/ppermute | solution.py:374
  39.4 0.0 collective-permute-start.15
  39.4 0.0 collective-permute-done.12.refs_2_
  39.4 0.0 copy-done.6
  39.4 0.5 collective-permute-start.14
  39.9 0.0 copy-done.7
  39.9 0.0 copy-done.8
  39.9 1.6 %collective-permute-done.15.refs_23_ = bf16[2,128,896]{2,1,0:T(8,128)(2,1)} collective-permute-done((bf16[2,128,896]{2,1,0:T(8,128)(2,1)}, bf16[2,128,896]{2,1,0:T(8,128)(2,1)}, u32[]{:S(2)}, u32[]{:S(2)}) %collective-permute-start.15) | collective-permute-done | bytes 458784 | tf_op jit(solution)/shard_map/ppermute | solution.py:379
  41.6 0.4 collective-permute-done.14.refs_21_
  42.0 0.0 copy-done.2
  42.0 0.0 copy-done
  42.0 0.0 copy-done.1
  42.0 13.2 %attend_windows.1 = bf16[256,2048]{1,0:T(8,128)(2,1)} custom-call(s32[1]{0:T(128)} %bitcast.refs_0_, s32[8]{0:T(128)S(1)} %copy-done.2, s32[2,4]{1,0:T(2,128)S(1)} %collective-permute-done.12.refs_2_, s32[2,4]{1,0:T(2,128)S(1)} %add_bitcast_fusion.refs_3_, s32[4]{0:T(128)S(1)} %copy-done.1, bf16[16,256,896]{2,1,0:T(8,128)(2,1)} %get-tuple-element.15.refs_5_, ...), custom_call_target="tpu_custom_call" | custom-call | flops 4697620480 | bytes 16777216 | tf_op jit(solution)/shard_map/attend_windows/pallas_call | solution.py:293
  (9 shorter events, 0.0 us)
Async XLA Ops:
  0.0 42.0 %copy-start.2 = (s32[8]{0:T(128)S(1)}, s32[8]{0:T(128)}, u32[]{:S(2)}) copy-start(s32[8]{0:T(128)} %constant.8.clone.refs_1_) | copy-start | bytes 100
  0.0 42.0 %copy-start = (bf16[2,128,896]{2,1,0:T(8,128)(2,1)S(1)}, bf16[2,128,896]{2,1,0:T(8,128)(2,1)}, u32[]{:S(2)}) copy-start(bf16[2,128,896]{2,1,0:T(8,128)(2,1)} %refs_8_.1) | copy-start | bytes 1376260
  0.0 31.5 %copy-start.9 = (s32[4,2]{0,1:T(2,128)S(1)}, s32[4,2]{0,1:T(2,128)}, u32[]{:S(2)}) copy-start(s32[4,2]{0,1:T(2,128)} %param.13) | copy-start | bytes 100
  0.0 31.5 %copy-start.10 = (s32[4,2]{0,1:T(2,128)S(1)}, s32[4,2]{0,1:T(2,128)}, u32[]{:S(2)}) copy-start(s32[4,2]{0,1:T(2,128)} %param.12) | copy-start | bytes 100
  0.0 42.0 %copy-start.1 = (s32[4]{0:T(128)S(1)}, s32[4]{0:T(128)}, u32[]{:S(2)}) copy-start(s32[4]{0:T(128)} %refs_4_.1) | copy-start | bytes 52
  0.0 3.2 %collective-permute-start = (bf16[2,128,896]{2,1,0:T(8,128)(2,1)}, bf16[2,128,896]{2,1,0:T(8,128)(2,1)S(1)}, u32[]{:S(2)}, u32[]{:S(2)}) collective-permute-start(bf16[2,128,896]{2,1,0:T(8,128)(2,1)} %refs_8_.1), channel_id=1, source_target_pairs={{0,1},{1,0},{2,3},{3,2},{4,5},{5,4},{6,7},{7,6},{8,9},{9,8},{10,11... | collective-permute-start | bytes 1376264 | tf_op jit(solution)/shard_map/ppermute | solution.py:353
  0.5 9.7 %collective-permute-start.5 = (bf16[2,128,896]{2,1,0:T(8,128)(2,1)}, bf16[2,128,896]{2,1,0:T(8,128)(2,1)S(1)}, u32[]{:S(2)}, u32[]{:S(2)}) collective-permute-start(bf16[2,128,896]{2,1,0:T(8,128)(2,1)} %refs_8_.1), channel_id=1, source_target_pairs={{0,4},{1,3},{4,8},{5,1},{8,12},{9,5},{12,14},{13,9},{14,10},{15,13... | collective-permute-start | bytes 1376264 | tf_op jit(solution)/shard_map/ppermute | solution.py:366
  3.2 11.5 %copy-start.3 = (bf16[2,128,896]{2,1,0:T(8,128)(2,1)}, bf16[2,128,896]{2,1,0:T(8,128)(2,1)S(1)}, u32[]{:S(2)}) copy-start(bf16[2,128,896]{2,1,0:T(8,128)(2,1)S(1)} %collective-permute-done.refs_9_) | copy-start | bytes 1376260
  3.2 11.5 %collective-permute-start.1 = (bf16[2,128,896]{2,1,0:T(8,128)(2,1)S(1)}, bf16[2,128,896]{2,1,0:T(8,128)(2,1)S(1)}, u32[]{:S(2)}, u32[]{:S(2)}) collective-permute-start(bf16[2,128,896]{2,1,0:T(8,128)(2,1)S(1)} %collective-permute-done.refs_9_), channel_id=1, source_target_pairs={{0,4},{1,3},{4,8},{5,1},{8,12},{9,5},{12,14},{13,9},{14,10},{15,13... | collective-permute-start | bytes 1376264 | tf_op jit(solution)/shard_map/ppermute | solution.py:366
  10.2 6.6 %collective-permute-start.9 = (bf16[2,128,896]{2,1,0:T(8,128)(2,1)S(1)}, bf16[2,128,896]{2,1,0:T(8,128)(2,1)S(1)}, u32[]{:S(2)}, u32[]{:S(2)}) collective-permute-start(bf16[2,128,896]{2,1,0:T(8,128)(2,1)S(1)} %collective-permute-done.5.refs_10_), channel_id=1, source_target_pairs={{0,1},{1,0},{2,3},{3,2},{4,5},{5,4},{6,7},{7,6},{8,9},{9,8},{10,11... | collective-permute-start | bytes 1376264 | tf_op jit(solution)/shard_map/ppermute | solution.py:367
  10.3 9.3 %collective-permute-start.6 = (bf16[2,128,896]{2,1,0:T(8,128)(2,1)S(1)}, bf16[2,128,896]{2,1,0:T(8,128)(2,1)S(1)}, u32[]{:S(2)}, u32[]{:S(2)}) collective-permute-start(bf16[2,128,896]{2,1,0:T(8,128)(2,1)S(1)} %collective-permute-done.5.refs_10_), channel_id=1, source_target_pairs={{0,4},{1,3},{4,8},{5,1},{8,12},{9,5},{12,14},{13,9},{14,10},{15,13... | collective-permute-start | bytes 1376264 | tf_op jit(solution)/shard_map/ppermute | solution.py:366
  14.7 7.0 %collective-permute-start.3 = (bf16[2,128,896]{2,1,0:T(8,128)(2,1)S(1)}, bf16[2,128,896]{2,1,0:T(8,128)(2,1)S(1)}, u32[]{:S(2)}, u32[]{:S(2)}) collective-permute-start(bf16[2,128,896]{2,1,0:T(8,128)(2,1)S(1)} %collective-permute-done.1.refs_12_), channel_id=1, source_target_pairs={{0,1},{1,0},{2,3},{3,2},{4,5},{5,4},{6,7},{7,6},{8,9},{9,8},{10,11... | collective-permute-start | bytes 1376264 | tf_op jit(solution)/shard_map/ppermute | solution.py:367
  14.7 9.8 %collective-permute-start.2 = (bf16[2,128,896]{2,1,0:T(8,128)(2,1)S(1)}, bf16[2,128,896]{2,1,0:T(8,128)(2,1)S(1)}, u32[]{:S(2)}, u32[]{:S(2)}) collective-permute-start(bf16[2,128,896]{2,1,0:T(8,128)(2,1)S(1)} %collective-permute-done.1.refs_12_), channel_id=1, source_target_pairs={{0,4},{1,3},{4,8},{5,1},{8,12},{9,5},{12,14},{13,9},{14,10},{15,13... | collective-permute-start | bytes 1376264 | tf_op jit(solution)/shard_map/ppermute | solution.py:366
  16.8 0.8 %copy-start.4 = (bf16[2,128,896]{2,1,0:T(8,128)(2,1)}, bf16[2,128,896]{2,1,0:T(8,128)(2,1)S(1)}, u32[]{:S(2)}) copy-start(bf16[2,128,896]{2,1,0:T(8,128)(2,1)S(1)} %collective-permute-done.9.refs_11_) | copy-start | bytes 1376260
  19.6 9.8 %collective-permute-start.10 = (bf16[2,128,896]{2,1,0:T(8,128)(2,1)S(1)}, bf16[2,128,896]{2,1,0:T(8,128)(2,1)S(1)}, u32[]{:S(2)}, u32[]{:S(2)}) collective-permute-start(bf16[2,128,896]{2,1,0:T(8,128)(2,1)S(1)} %collective-permute-done.6.refs_14_), channel_id=1, source_target_pairs={{0,4},{1,3},{4,8},{5,1},{8,12},{9,5},{12,14},{13,9},{14,10},{15,13... | collective-permute-start | bytes 1376264 | tf_op jit(solution)/shard_map/ppermute | solution.py:366
  21.7 9.8 %collective-permute-start.7 = (bf16[2,128,896]{2,1,0:T(8,128)(2,1)S(1)}, bf16[2,128,896]{2,1,0:T(8,128)(2,1)S(1)}, u32[]{:S(2)}, u32[]{:S(2)}) collective-permute-start(bf16[2,128,896]{2,1,0:T(8,128)(2,1)S(1)} %collective-permute-done.6.refs_14_), channel_id=1, source_target_pairs={{0,1},{1,0},{2,3},{3,2},{4,5},{5,4},{6,7},{7,6},{8,9},{9,8},{10,11... | collective-permute-start | bytes 1376264 | tf_op jit(solution)/shard_map/ppermute | solution.py:367
  21.7 0.8 %copy-start.5 = (bf16[2,128,896]{2,1,0:T(8,128)(2,1)}, bf16[2,128,896]{2,1,0:T(8,128)(2,1)S(1)}, u32[]{:S(2)}) copy-start(bf16[2,128,896]{2,1,0:T(8,128)(2,1)S(1)} %collective-permute-done.3.refs_13_) | copy-start | bytes 1376260
  24.5 9.8 %collective-permute-start.4 = (bf16[2,128,896]{2,1,0:T(8,128)(2,1)S(1)}, bf16[2,128,896]{2,1,0:T(8,128)(2,1)S(1)}, u32[]{:S(2)}, u32[]{:S(2)}) collective-permute-start(bf16[2,128,896]{2,1,0:T(8,128)(2,1)S(1)} %collective-permute-done.2.refs_16_), channel_id=1, source_target_pairs={{0,4},{1,3},{4,8},{5,1},{8,12},{9,5},{12,14},{13,9},{14,10},{15,13... | collective-permute-start | bytes 1376264 | tf_op jit(solution)/shard_map/ppermute | solution.py:366
  26.6 7.8 %collective-permute-start.8 = (bf16[2,128,896]{2,1,0:T(8,128)(2,1)S(1)}, bf16[2,128,896]{2,1,0:T(8,128)(2,1)S(1)}, u32[]{:S(2)}, u32[]{:S(2)}) collective-permute-start(bf16[2,128,896]{2,1,0:T(8,128)(2,1)S(1)} %collective-permute-done.2.refs_16_), channel_id=1, source_target_pairs={{0,1},{1,0},{2,3},{3,2},{4,5},{5,4},{6,7},{7,6},{8,9},{9,8},{10,11... | collective-permute-start | bytes 1376264 | tf_op jit(solution)/shard_map/ppermute | solution.py:367
  29.5 4.9 %collective-permute-start.11 = (bf16[2,128,896]{2,1,0:T(8,128)(2,1)S(1)}, bf16[2,128,896]{2,1,0:T(8,128)(2,1)S(1)}, u32[]{:S(2)}, u32[]{:S(2)}) collective-permute-start(bf16[2,128,896]{2,1,0:T(8,128)(2,1)S(1)} %collective-permute-done.10.refs_18_), channel_id=1, source_target_pairs={{0,1},{1,0},{2,3},{3,2},{4,5},{5,4},{6,7},{7,6},{8,9},{9,8},{10,11... | collective-permute-start | bytes 1376264 | tf_op jit(solution)/shard_map/ppermute | solution.py:367
  29.5 9.9 %collective-permute-start.13 = (bf16[2,128,896]{2,1,0:T(8,128)(2,1)S(1)}, bf16[2,128,896]{2,1,0:T(8,128)(2,1)}, u32[]{:S(2)}, u32[]{:S(2)}) collective-permute-start(bf16[2,128,896]{2,1,0:T(8,128)(2,1)S(1)} %collective-permute-done.10.refs_18_), channel_id=1, source_target_pairs={{0,4},{1,3},{4,8},{5,1},{8,12},{9,5},{12,14},{13,9},{14,10},{15,13... | collective-permute-start | bytes 1376264 | tf_op jit(solution)/shard_map/ppermute | solution.py:374
  31.6 7.8 %copy-start.6 = (bf16[2,128,896]{2,1,0:T(8,128)(2,1)}, bf16[2,128,896]{2,1,0:T(8,128)(2,1)S(1)}, u32[]{:S(2)}) copy-start(bf16[2,128,896]{2,1,0:T(8,128)(2,1)S(1)} %collective-permute-done.7.refs_15_) | copy-start | bytes 1376260
  34.4 5.5 %copy-start.7 = (bf16[2,128,896]{2,1,0:T(8,128)(2,1)}, bf16[2,128,896]{2,1,0:T(8,128)(2,1)S(1)}, u32[]{:S(2)}) copy-start(bf16[2,128,896]{2,1,0:T(8,128)(2,1)S(1)} %collective-permute-done.8.refs_17_) | copy-start | bytes 1376260
  34.4 5.5 %copy-start.8 = (bf16[2,128,896]{2,1,0:T(8,128)(2,1)}, bf16[2,128,896]{2,1,0:T(8,128)(2,1)S(1)}, u32[]{:S(2)}) copy-start(bf16[2,128,896]{2,1,0:T(8,128)(2,1)S(1)} %collective-permute-done.11.refs_19_) | copy-start | bytes 1376260
  34.4 5.0 %collective-permute-start.12 = (s32[2,4]{1,0:T(2,128)S(1)}, s32[2,4]{1,0:T(2,128)S(1)}, u32[]{:S(2)}, u32[]{:S(2)}) collective-permute-start(s32[2,4]{1,0:T(2,128)S(1)} %add_bitcast_fusion.refs_3_), channel_id=1, source_target_pairs={{0,1},{1,2},{2,3},{3,4},{4,5},{5,6},{6,7},{7,8},{8,9},{9,10},{10,1... | collective-permute-start | bytes 104 | tf_op jit(solution)/shard_map/ppermute | solution.py:370
  39.4 2.2 %collective-permute-start.15 = (bf16[2,128,896]{2,1,0:T(8,128)(2,1)}, bf16[2,128,896]{2,1,0:T(8,128)(2,1)}, u32[]{:S(2)}, u32[]{:S(2)}) collective-permute-start(bf16[2,128,896]{2,1,0:T(8,128)(2,1)} %collective-permute-done.13.refs_22_), channel_id=1, source_target_pairs={{0,1},{1,0},{2,3},{3,2},{4,5},{5,4},{6,7},{7,6},{8,9},{9,8},{10,11... | collective-permute-start | bytes 1376264 | tf_op jit(solution)/shard_map/ppermute | solution.py:379
  39.4 2.6 %collective-permute-start.14 = (bf16[2,128,896]{2,1,0:T(8,128)(2,1)S(1)}, bf16[2,128,896]{2,1,0:T(8,128)(2,1)}, u32[]{:S(2)}, u32[]{:S(2)}) collective-permute-start(bf16[2,128,896]{2,1,0:T(8,128)(2,1)S(1)} %collective-permute-done.4.refs_20_), channel_id=1, source_target_pairs={{0,1},{1,0},{2,3},{3,2},{4,5},{5,4},{6,7},{7,6},{8,9},{9,8},{10,11... | collective-permute-start | bytes 1376264 | tf_op jit(solution)/shard_map/ppermute | solution.py:378

commit v21 on v20

--- a/solution.py
+++ b/solution.py
@@ -177,12 +177,11 @@
         columns = group_columns(group)
         return pltpu.make_async_copy(out.at[:, columns], out_hbm.at[:, columns], group_sems.at[group, 2])
 
+    fetch_group(0)[0].start()
     for window in order:
         for request in (2 * window, 2 * window + 1):
             source, block = locate(request, plan_refs, size, stores[0].shape[0])
             among(stores, 0, source, lambda store: fetch(request, store, block).start())
-        if window == order[0]:
-            fetch_group(0)[0].start()
     fetch_group(0)[1].start()
     for group in range(1, groups):
         for copy in fetch_group(group):

time: 55.4 us -> 55.4 us (level)
  no operation moved by 1% of the time
where the time goes in v21:
time: 55.4 us
  Pallas kernels  18.3 us (33%)
  waiting for transfers between devices  17.7 us (32%)
  starting transfers between devices  17.5 us (32%)
  local copies, waits for them, and re-layouts  1.67 us (3%)
    pallas_call x1, Pallas kernels, attend(): pl.pallas_call(functools.partial(attend_kernel, size), out_shape=jax.Shap...  13.2 us
    ppermute x6, starting transfers between devices, body(): chains[chain] = onwards(sent[0])  12.5 us
    ppermute x6, waiting for transfers between devices, body(): chains[chain] = onwards(sent[0])  12.4 us
    pallas_call x1, Pallas kernels, fold(): pl.pallas_call(functools.partial(fold_kernel, first), out_shape=(pltpu.HB...  5.05 us
    ppermute x1, waiting for transfers between devices, body(): last = onwards(chains[0])  3.16 us
    ppermute x1, starting transfers between devices, body(): last = onwards(chains[0])  2.08 us
    ppermute x1, starting transfers between devices, body(): lax.ppermute(asked, 'seq', [(i, i + 1) for i in range(devices - 1)])  1.83 us
    unnamed x22, local copies, waits for them, and re-layouts  1.67 us
  transfers between devices with their start and end apart: 16, of which 8 were waited for; matrix products, arithmetic and copies ran while one was open for 0% of the time, Pallas kernels for 9%

profile of v21, /device:TPU:0, one launch (start us, length us, event | category | flops | bytes accessed | tf_op | source)
XLA Modules:
  0.0 55.4 jit_solution(8394997284785410906)
XLA Ops:
  0.0 0.0 copy-start.2
  0.0 0.5 collective-permute-start
  0.5 2.6 %collective-permute-start.5 = (bf16[2,128,896]{2,1,0:T(8,128)(2,1)}, bf16[2,128,896]{2,1,0:T(8,128)(2,1)S(1)}, u32[]{:S(2)}, u32[]{:S(2)}) collective-permute-start(bf16[2,128,896]{2,1,0:T(8,128)(2,1)} %refs_8_.1), channel_id=1, source_target_pairs={{0,4},{1,3},{4,8},{5,1},{8,12},{9,5},{12,14},{13,9},{14,10},{15,13... | collective-permute-start | bytes 1376264 | tf_op jit(solution)/shard_map/ppermute | solution.py:365
  3.2 0.0 collective-permute-done.refs_9_
  3.2 2.0 %collective-permute-start.1 = (bf16[2,128,896]{2,1,0:T(8,128)(2,1)S(1)}, bf16[2,128,896]{2,1,0:T(8,128)(2,1)S(1)}, u32[]{:S(2)}, u32[]{:S(2)}) collective-permute-start(bf16[2,128,896]{2,1,0:T(8,128)(2,1)S(1)} %collective-permute-done.refs_9_), channel_id=1, source_target_pairs={{0,4},{1,3},{4,8},{5,1},{8,12},{9,5},{12,14},{13,9},{14,10},{15,13... | collective-permute-start | bytes 1376264 | tf_op jit(solution)/shard_map/ppermute | solution.py:365
  5.1 5.0 %fold_queries.1 = (bf16[16,256,896]{2,1,0:T(8,128)(2,1)}, f32[16,896]{1,0:T(8,128)S(1)}) custom-call(bf16[256,2048]{1,0:T(8,128)(2,1)} %query_hbm, bf16[896,2048]{1,0:T(8,128)(2,1)} %key_hbm.1), custom_call_target="tpu_custom_call" | custom-call | flops 939524096 | bytes 6291456 | tf_op jit(solution)/shard_map/fold_queries/pallas_call | solution.py:81
  10.2 0.0 collective-permute-done.5.refs_10_
  10.2 0.1 collective-permute-start.9
  10.3 1.6 %collective-permute-start.6 = (bf16[2,128,896]{2,1,0:T(8,128)(2,1)S(1)}, bf16[2,128,896]{2,1,0:T(8,128)(2,1)S(1)}, u32[]{:S(2)}, u32[]{:S(2)}) collective-permute-start(bf16[2,128,896]{2,1,0:T(8,128)(2,1)S(1)} %collective-permute-done.5.refs_10_), channel_id=1, source_target_pairs={{0,4},{1,3},{4,8},{5,1},{8,12},{9,5},{12,14},{13,9},{14,10},{15,13... | collective-permute-start | bytes 1376264 | tf_op jit(solution)/shard_map/ppermute | solution.py:365
  11.9 2.8 %collective-permute-done.1.refs_12_ = bf16[2,128,896]{2,1,0:T(8,128)(2,1)S(1)} collective-permute-done((bf16[2,128,896]{2,1,0:T(8,128)(2,1)S(1)}, bf16[2,128,896]{2,1,0:T(8,128)(2,1)S(1)}, u32[]{:S(2)}, u32[]{:S(2)}) %collective-permute-start.1) | collective-permute-done | bytes 458784 | tf_op jit(solution)/shard_map/ppermute | solution.py:365
  14.7 0.0 copy-done.3
  14.7 0.0 collective-permute-start.3
  14.7 2.1 %collective-permute-start.2 = (bf16[2,128,896]{2,1,0:T(8,128)(2,1)S(1)}, bf16[2,128,896]{2,1,0:T(8,128)(2,1)S(1)}, u32[]{:S(2)}, u32[]{:S(2)}) collective-permute-start(bf16[2,128,896]{2,1,0:T(8,128)(2,1)S(1)} %collective-permute-done.1.refs_12_), channel_id=1, source_target_pairs={{0,4},{1,3},{4,8},{5,1},{8,12},{9,5},{12,14},{13,9},{14,10},{15,13... | collective-permute-start | bytes 1376264 | tf_op jit(solution)/shard_map/ppermute | solution.py:365
  16.8 0.0 collective-permute-done.9.refs_11_
  16.8 0.8 %copy-done.4 = bf16[2,128,896]{2,1,0:T(8,128)(2,1)} copy-done((bf16[2,128,896]{2,1,0:T(8,128)(2,1)}, bf16[2,128,896]{2,1,0:T(8,128)(2,1)S(1)}, u32[]{:S(2)}) %copy-start.4) | copy-done | bytes 458776
  17.6 2.0 %collective-permute-done.6.refs_14_ = bf16[2,128,896]{2,1,0:T(8,128)(2,1)S(1)} collective-permute-done((bf16[2,128,896]{2,1,0:T(8,128)(2,1)S(1)}, bf16[2,128,896]{2,1,0:T(8,128)(2,1)S(1)}, u32[]{:S(2)}, u32[]{:S(2)}) %collective-permute-start.6) | collective-permute-done | bytes 458784 | tf_op jit(solution)/shard_map/ppermute | solution.py:365
  19.6 2.1 %collective-permute-start.10 = (bf16[2,128,896]{2,1,0:T(8,128)(2,1)S(1)}, bf16[2,128,896]{2,1,0:T(8,128)(2,1)S(1)}, u32[]{:S(2)}, u32[]{:S(2)}) collective-permute-start(bf16[2,128,896]{2,1,0:T(8,128)(2,1)S(1)} %collective-permute-done.6.refs_14_), channel_id=1, source_target_pairs={{0,4},{1,3},{4,8},{5,1},{8,12},{9,5},{12,14},{13,9},{14,10},{15,13... | collective-permute-start | bytes 1376264 | tf_op jit(solution)/shard_map/ppermute | solution.py:365
  21.7 0.0 collective-permute-start.7
  21.7 0.0 collective-permute-done.3.refs_13_
  21.7 0.8 %copy-done.5 = bf16[2,128,896]{2,1,0:T(8,128)(2,1)} copy-done((bf16[2,128,896]{2,1,0:T(8,128)(2,1)}, bf16[2,128,896]{2,1,0:T(8,128)(2,1)S(1)}, u32[]{:S(2)}) %copy-start.5) | copy-done | bytes 458776
  22.5 2.0 %collective-permute-done.2.refs_16_ = bf16[2,128,896]{2,1,0:T(8,128)(2,1)S(1)} collective-permute-done((bf16[2,128,896]{2,1,0:T(8,128)(2,1)S(1)}, bf16[2,128,896]{2,1,0:T(8,128)(2,1)S(1)}, u32[]{:S(2)}, u32[]{:S(2)}) %collective-permute-start.2) | collective-permute-done | bytes 458784 | tf_op jit(solution)/shard_map/ppermute | solution.py:365
  24.5 2.1 %collective-permute-start.4 = (bf16[2,128,896]{2,1,0:T(8,128)(2,1)S(1)}, bf16[2,128,896]{2,1,0:T(8,128)(2,1)S(1)}, u32[]{:S(2)}, u32[]{:S(2)}) collective-permute-start(bf16[2,128,896]{2,1,0:T(8,128)(2,1)S(1)} %collective-permute-done.2.refs_16_), channel_id=1, source_target_pairs={{0,4},{1,3},{4,8},{5,1},{8,12},{9,5},{12,14},{13,9},{14,10},{15,13... | collective-permute-start | bytes 1376264 | tf_op jit(solution)/shard_map/ppermute | solution.py:365
  26.6 0.0 collective-permute-start.8
  26.6 2.8 %collective-permute-done.10.refs_18_ = bf16[2,128,896]{2,1,0:T(8,128)(2,1)S(1)} collective-permute-done((bf16[2,128,896]{2,1,0:T(8,128)(2,1)S(1)}, bf16[2,128,896]{2,1,0:T(8,128)(2,1)S(1)}, u32[]{:S(2)}, u32[]{:S(2)}) %collective-permute-start.10) | collective-permute-done | bytes 458784 | tf_op jit(solution)/shard_map/ppermute | solution.py:365
  29.5 0.0 collective-permute-start.11
  29.5 2.1 %collective-permute-start.13 = (bf16[2,128,896]{2,1,0:T(8,128)(2,1)S(1)}, bf16[2,128,896]{2,1,0:T(8,128)(2,1)}, u32[]{:S(2)}, u32[]{:S(2)}) collective-permute-start(bf16[2,128,896]{2,1,0:T(8,128)(2,1)S(1)} %collective-permute-done.10.refs_18_), channel_id=1, source_target_pairs={{0,4},{1,3},{4,8},{5,1},{8,12},{9,5},{12,14},{13,9},{14,10},{15,13... | collective-permute-start | bytes 1376264 | tf_op jit(solution)/shard_map/ppermute | solution.py:373
  31.5 0.0 copy-done.9
  31.5 0.0 copy-done.10
  31.6 0.0 collective-permute-done.7.refs_15_
  31.6 0.0 copy-start.6
  31.6 2.8 %collective-permute-done.4.refs_20_ = bf16[2,128,896]{2,1,0:T(8,128)(2,1)S(1)} collective-permute-done((bf16[2,128,896]{2,1,0:T(8,128)(2,1)S(1)}, bf16[2,128,896]{2,1,0:T(8,128)(2,1)S(1)}, u32[]{:S(2)}, u32[]{:S(2)}) %collective-permute-start.4) | collective-permute-done | bytes 458784 | tf_op jit(solution)/shard_map/ppermute | solution.py:365
  34.4 0.0 collective-permute-done.8.refs_17_
  34.4 0.0 collective-permute-done.11.refs_19_
  34.4 0.0 copy-start.8
  34.4 1.8 %collective-permute-start.12 = (s32[2,4]{1,0:T(2,128)S(1)}, s32[2,4]{1,0:T(2,128)S(1)}, u32[]{:S(2)}, u32[]{:S(2)}) collective-permute-start(s32[2,4]{1,0:T(2,128)S(1)} %add_bitcast_fusion.refs_3_), channel_id=1, source_target_pairs={{0,1},{1,2},{2,3},{3,4},{4,5},{5,6},{6,7},{7,8},{8,9},{9,10},{10,1... | collective-permute-start | bytes 104 | tf_op jit(solution)/shard_map/ppermute | solution.py:369
  36.2 3.2 %collective-permute-done.13.refs_22_ = bf16[2,128,896]{2,1,0:T(8,128)(2,1)} collective-permute-done((bf16[2,128,896]{2,1,0:T(8,128)(2,1)S(1)}, bf16[2,128,896]{2,1,0:T(8,128)(2,1)}, u32[]{:S(2)}, u32[]{:S(2)}) %collective-permute-start.13) | collective-permute-done | bytes 458784 | tf_op jit(solution)/shard_map/ppermute | solution.py:373
  39.4 0.0 collective-permute-start.15
  39.4 0.0 collective-permute-done.12.refs_2_
  39.4 0.0 copy-done.6
  39.4 0.5 collective-permute-start.14
  39.9 0.0 copy-done.7
  39.9 0.0 copy-done.8
  39.9 1.6 %collective-permute-done.15.refs_23_ = bf16[2,128,896]{2,1,0:T(8,128)(2,1)} collective-permute-done((bf16[2,128,896]{2,1,0:T(8,128)(2,1)}, bf16[2,128,896]{2,1,0:T(8,128)(2,1)}, u32[]{:S(2)}, u32[]{:S(2)}) %collective-permute-start.15) | collective-permute-done | bytes 458784 | tf_op jit(solution)/shard_map/ppermute | solution.py:378
  41.6 0.4 collective-permute-done.14.refs_21_
  42.0 0.0 copy-done.2
  42.0 0.0 copy-done
  42.0 0.0 copy-done.1
  42.0 13.2 %attend_windows.1 = bf16[256,2048]{1,0:T(8,128)(2,1)} custom-call(s32[1]{0:T(128)} %bitcast.refs_0_, s32[8]{0:T(128)S(1)} %copy-done.2, s32[2,4]{1,0:T(2,128)S(1)} %collective-permute-done.12.refs_2_, s32[2,4]{1,0:T(2,128)S(1)} %add_bitcast_fusion.refs_3_, s32[4]{0:T(128)S(1)} %copy-done.1, bf16[16,256,896]{2,1,0:T(8,128)(2,1)} %get-tuple-element.15.refs_5_, ...), custom_call_target="tpu_custom_call" | custom-call | flops 4697620480 | bytes 16777216 | tf_op jit(solution)/shard_map/attend_windows/pallas_call | solution.py:292
  (9 shorter events, 0.0 us)
Async XLA Ops:
  0.0 42.0 %copy-start.2 = (s32[8]{0:T(128)S(1)}, s32[8]{0:T(128)}, u32[]{:S(2)}) copy-start(s32[8]{0:T(128)} %constant.8.clone.refs_1_) | copy-start | bytes 100
  0.0 42.0 %copy-start = (bf16[2,128,896]{2,1,0:T(8,128)(2,1)S(1)}, bf16[2,128,896]{2,1,0:T(8,128)(2,1)}, u32[]{:S(2)}) copy-start(bf16[2,128,896]{2,1,0:T(8,128)(2,1)} %refs_8_.1) | copy-start | bytes 1376260
  0.0 31.5 %copy-start.9 = (s32[4,2]{0,1:T(2,128)S(1)}, s32[4,2]{0,1:T(2,128)}, u32[]{:S(2)}) copy-start(s32[4,2]{0,1:T(2,128)} %param.13) | copy-start | bytes 100
  0.0 31.5 %copy-start.10 = (s32[4,2]{0,1:T(2,128)S(1)}, s32[4,2]{0,1:T(2,128)}, u32[]{:S(2)}) copy-start(s32[4,2]{0,1:T(2,128)} %param.12) | copy-start | bytes 100
  0.0 42.0 %copy-start.1 = (s32[4]{0:T(128)S(1)}, s32[4]{0:T(128)}, u32[]{:S(2)}) copy-start(s32[4]{0:T(128)} %refs_4_.1) | copy-start | bytes 52
  0.0 3.2 %collective-permute-start = (bf16[2,128,896]{2,1,0:T(8,128)(2,1)}, bf16[2,128,896]{2,1,0:T(8,128)(2,1)S(1)}, u32[]{:S(2)}, u32[]{:S(2)}) collective-permute-start(bf16[2,128,896]{2,1,0:T(8,128)(2,1)} %refs_8_.1), channel_id=1, source_target_pairs={{0,1},{1,0},{2,3},{3,2},{4,5},{5,4},{6,7},{7,6},{8,9},{9,8},{10,11... | collective-permute-start | bytes 1376264 | tf_op jit(solution)/shard_map/ppermute | solution.py:352
  0.5 9.7 %collective-permute-start.5 = (bf16[2,128,896]{2,1,0:T(8,128)(2,1)}, bf16[2,128,896]{2,1,0:T(8,128)(2,1)S(1)}, u32[]{:S(2)}, u32[]{:S(2)}) collective-permute-start(bf16[2,128,896]{2,1,0:T(8,128)(2,1)} %refs_8_.1), channel_id=1, source_target_pairs={{0,4},{1,3},{4,8},{5,1},{8,12},{9,5},{12,14},{13,9},{14,10},{15,13... | collective-permute-start | bytes 1376264 | tf_op jit(solution)/shard_map/ppermute | solution.py:365
  3.2 11.5 %copy-start.3 = (bf16[2,128,896]{2,1,0:T(8,128)(2,1)}, bf16[2,128,896]{2,1,0:T(8,128)(2,1)S(1)}, u32[]{:S(2)}) copy-start(bf16[2,128,896]{2,1,0:T(8,128)(2,1)S(1)} %collective-permute-done.refs_9_) | copy-start | bytes 1376260
  3.2 11.5 %collective-permute-start.1 = (bf16[2,128,896]{2,1,0:T(8,128)(2,1)S(1)}, bf16[2,128,896]{2,1,0:T(8,128)(2,1)S(1)}, u32[]{:S(2)}, u32[]{:S(2)}) collective-permute-start(bf16[2,128,896]{2,1,0:T(8,128)(2,1)S(1)} %collective-permute-done.refs_9_), channel_id=1, source_target_pairs={{0,4},{1,3},{4,8},{5,1},{8,12},{9,5},{12,14},{13,9},{14,10},{15,13... | collective-permute-start | bytes 1376264 | tf_op jit(solution)/shard_map/ppermute | solution.py:365
  10.2 6.6 %collective-permute-start.9 = (bf16[2,128,896]{2,1,0:T(8,128)(2,1)S(1)}, bf16[2,128,896]{2,1,0:T(8,128)(2,1)S(1)}, u32[]{:S(2)}, u32[]{:S(2)}) collective-permute-start(bf16[2,128,896]{2,1,0:T(8,128)(2,1)S(1)} %collective-permute-done.5.refs_10_), channel_id=1, source_target_pairs={{0,1},{1,0},{2,3},{3,2},{4,5},{5,4},{6,7},{7,6},{8,9},{9,8},{10,11... | collective-permute-start | bytes 1376264 | tf_op jit(solution)/shard_map/ppermute | solution.py:366
  10.3 9.3 %collective-permute-start.6 = (bf16[2,128,896]{2,1,0:T(8,128)(2,1)S(1)}, bf16[2,128,896]{2,1,0:T(8,128)(2,1)S(1)}, u32[]{:S(2)}, u32[]{:S(2)}) collective-permute-start(bf16[2,128,896]{2,1,0:T(8,128)(2,1)S(1)} %collective-permute-done.5.refs_10_), channel_id=1, source_target_pairs={{0,4},{1,3},{4,8},{5,1},{8,12},{9,5},{12,14},{13,9},{14,10},{15,13... | collective-permute-start | bytes 1376264 | tf_op jit(solution)/shard_map/ppermute | solution.py:365
  14.7 7.0 %collective-permute-start.3 = (bf16[2,128,896]{2,1,0:T(8,128)(2,1)S(1)}, bf16[2,128,896]{2,1,0:T(8,128)(2,1)S(1)}, u32[]{:S(2)}, u32[]{:S(2)}) collective-permute-start(bf16[2,128,896]{2,1,0:T(8,128)(2,1)S(1)} %collective-permute-done.1.refs_12_), channel_id=1, source_target_pairs={{0,1},{1,0},{2,3},{3,2},{4,5},{5,4},{6,7},{7,6},{8,9},{9,8},{10,11... | collective-permute-start | bytes 1376264 | tf_op jit(solution)/shard_map/ppermute | solution.py:366
  14.7 9.8 %collective-permute-start.2 = (bf16[2,128,896]{2,1,0:T(8,128)(2,1)S(1)}, bf16[2,128,896]{2,1,0:T(8,128)(2,1)S(1)}, u32[]{:S(2)}, u32[]{:S(2)}) collective-permute-start(bf16[2,128,896]{2,1,0:T(8,128)(2,1)S(1)} %collective-permute-done.1.refs_12_), channel_id=1, source_target_pairs={{0,4},{1,3},{4,8},{5,1},{8,12},{9,5},{12,14},{13,9},{14,10},{15,13... | collective-permute-start | bytes 1376264 | tf_op jit(solution)/shard_map/ppermute | solution.py:365
  16.8 0.8 %copy-start.4 = (bf16[2,128,896]{2,1,0:T(8,128)(2,1)}, bf16[2,128,896]{2,1,0:T(8,128)(2,1)S(1)}, u32[]{:S(2)}) copy-start(bf16[2,128,896]{2,1,0:T(8,128)(2,1)S(1)} %collective-permute-done.9.refs_11_) | copy-start | bytes 1376260
  19.6 9.8 %collective-permute-start.10 = (bf16[2,128,896]{2,1,0:T(8,128)(2,1)S(1)}, bf16[2,128,896]{2,1,0:T(8,128)(2,1)S(1)}, u32[]{:S(2)}, u32[]{:S(2)}) collective-permute-start(bf16[2,128,896]{2,1,0:T(8,128)(2,1)S(1)} %collective-permute-done.6.refs_14_), channel_id=1, source_target_pairs={{0,4},{1,3},{4,8},{5,1},{8,12},{9,5},{12,14},{13,9},{14,10},{15,13... | collective-permute-start | bytes 1376264 | tf_op jit(solution)/shard_map/ppermute | solution.py:365
  21.7 9.8 %collective-permute-start.7 = (bf16[2,128,896]{2,1,0:T(8,128)(2,1)S(1)}, bf16[2,128,896]{2,1,0:T(8,128)(2,1)S(1)}, u32[]{:S(2)}, u32[]{:S(2)}) collective-permute-start(bf16[2,128,896]{2,1,0:T(8,128)(2,1)S(1)} %collective-permute-done.6.refs_14_), channel_id=1, source_target_pairs={{0,1},{1,0},{2,3},{3,2},{4,5},{5,4},{6,7},{7,6},{8,9},{9,8},{10,11... | collective-permute-start | bytes 1376264 | tf_op jit(solution)/shard_map/ppermute | solution.py:366
  21.7 0.8 %copy-start.5 = (bf16[2,128,896]{2,1,0:T(8,128)(2,1)}, bf16[2,128,896]{2,1,0:T(8,128)(2,1)S(1)}, u32[]{:S(2)}) copy-start(bf16[2,128,896]{2,1,0:T(8,128)(2,1)S(1)} %collective-permute-done.3.refs_13_) | copy-start | bytes 1376260
  24.5 9.8 %collective-permute-start.4 = (bf16[2,128,896]{2,1,0:T(8,128)(2,1)S(1)}, bf16[2,128,896]{2,1,0:T(8,128)(2,1)S(1)}, u32[]{:S(2)}, u32[]{:S(2)}) collective-permute-start(bf16[2,128,896]{2,1,0:T(8,128)(2,1)S(1)} %collective-permute-done.2.refs_16_), channel_id=1, source_target_pairs={{0,4},{1,3},{4,8},{5,1},{8,12},{9,5},{12,14},{13,9},{14,10},{15,13... | collective-permute-start | bytes 1376264 | tf_op jit(solution)/shard_map/ppermute | solution.py:365
  26.6 7.8 %collective-permute-start.8 = (bf16[2,128,896]{2,1,0:T(8,128)(2,1)S(1)}, bf16[2,128,896]{2,1,0:T(8,128)(2,1)S(1)}, u32[]{:S(2)}, u32[]{:S(2)}) collective-permute-start(bf16[2,128,896]{2,1,0:T(8,128)(2,1)S(1)} %collective-permute-done.2.refs_16_), channel_id=1, source_target_pairs={{0,1},{1,0},{2,3},{3,2},{4,5},{5,4},{6,7},{7,6},{8,9},{9,8},{10,11... | collective-permute-start | bytes 1376264 | tf_op jit(solution)/shard_map/ppermute | solution.py:366
  29.5 4.9 %collective-permute-start.11 = (bf16[2,128,896]{2,1,0:T(8,128)(2,1)S(1)}, bf16[2,128,896]{2,1,0:T(8,128)(2,1)S(1)}, u32[]{:S(2)}, u32[]{:S(2)}) collective-permute-start(bf16[2,128,896]{2,1,0:T(8,128)(2,1)S(1)} %collective-permute-done.10.refs_18_), channel_id=1, source_target_pairs={{0,1},{1,0},{2,3},{3,2},{4,5},{5,4},{6,7},{7,6},{8,9},{9,8},{10,11... | collective-permute-start | bytes 1376264 | tf_op jit(solution)/shard_map/ppermute | solution.py:366
  29.5 9.9 %collective-permute-start.13 = (bf16[2,128,896]{2,1,0:T(8,128)(2,1)S(1)}, bf16[2,128,896]{2,1,0:T(8,128)(2,1)}, u32[]{:S(2)}, u32[]{:S(2)}) collective-permute-start(bf16[2,128,896]{2,1,0:T(8,128)(2,1)S(1)} %collective-permute-done.10.refs_18_), channel_id=1, source_target_pairs={{0,4},{1,3},{4,8},{5,1},{8,12},{9,5},{12,14},{13,9},{14,10},{15,13... | collective-permute-start | bytes 1376264 | tf_op jit(solution)/shard_map/ppermute | solution.py:373
  31.6 7.8 %copy-start.6 = (bf16[2,128,896]{2,1,0:T(8,128)(2,1)}, bf16[2,128,896]{2,1,0:T(8,128)(2,1)S(1)}, u32[]{:S(2)}) copy-start(bf16[2,128,896]{2,1,0:T(8,128)(2,1)S(1)} %collective-permute-done.7.refs_15_) | copy-start | bytes 1376260
  34.4 5.5 %copy-start.7 = (bf16[2,128,896]{2,1,0:T(8,128)(2,1)}, bf16[2,128,896]{2,1,0:T(8,128)(2,1)S(1)}, u32[]{:S(2)}) copy-start(bf16[2,128,896]{2,1,0:T(8,128)(2,1)S(1)} %collective-permute-done.8.refs_17_) | copy-start | bytes 1376260
  34.4 5.5 %copy-start.8 = (bf16[2,128,896]{2,1,0:T(8,128)(2,1)}, bf16[2,128,896]{2,1,0:T(8,128)(2,1)S(1)}, u32[]{:S(2)}) copy-start(bf16[2,128,896]{2,1,0:T(8,128)(2,1)S(1)} %collective-permute-done.11.refs_19_) | copy-start | bytes 1376260
  34.4 5.0 %collective-permute-start.12 = (s32[2,4]{1,0:T(2,128)S(1)}, s32[2,4]{1,0:T(2,128)S(1)}, u32[]{:S(2)}, u32[]{:S(2)}) collective-permute-start(s32[2,4]{1,0:T(2,128)S(1)} %add_bitcast_fusion.refs_3_), channel_id=1, source_target_pairs={{0,1},{1,2},{2,3},{3,4},{4,5},{5,6},{6,7},{7,8},{8,9},{9,10},{10,1... | collective-permute-start | bytes 104 | tf_op jit(solution)/shard_map/ppermute | solution.py:369
  39.4 2.2 %collective-permute-start.15 = (bf16[2,128,896]{2,1,0:T(8,128)(2,1)}, bf16[2,128,896]{2,1,0:T(8,128)(2,1)}, u32[]{:S(2)}, u32[]{:S(2)}) collective-permute-start(bf16[2,128,896]{2,1,0:T(8,128)(2,1)} %collective-permute-done.13.refs_22_), channel_id=1, source_target_pairs={{0,1},{1,0},{2,3},{3,2},{4,5},{5,4},{6,7},{7,6},{8,9},{9,8},{10,11... | collective-permute-start | bytes 1376264 | tf_op jit(solution)/shard_map/ppermute | solution.py:378
  39.4 2.6 %collective-permute-start.14 = (bf16[2,128,896]{2,1,0:T(8,128)(2,1)S(1)}, bf16[2,128,896]{2,1,0:T(8,128)(2,1)}, u32[]{:S(2)}, u32[]{:S(2)}) collective-permute-start(bf16[2,128,896]{2,1,0:T(8,128)(2,1)S(1)} %collective-permute-done.4.refs_20_), channel_id=1, source_target_pairs={{0,1},{1,0},{2,3},{3,2},{4,5},{5,4},{6,7},{7,6},{8,9},{9,8},{10,11... | collective-permute-start | bytes 1376264 | tf_op jit(solution)/shard_map/ppermute | solution.py:377
